TPU v7x, 128 devices: a whole 4x4x4 slice. The times are simulated.
128 devices in a mesh: occ: 4 (over z_hi, core), vir: 32 (over x, z_lo, y).
Axes of the slice: x: 4, y: 4, z: 4 (z_hi: 2, z_lo: 2; z = z_hi * 2 + z_lo), core: 2. Of those that a mesh axis runs over, the one named last changes fastest.
Arguments:
- cholesky: bfloat16 [256, 256, 128], P(None, 'vir'), may hold values from -6 to 6
- amplitudes: bfloat16 [256, 8, 128, 128], P('occ'), may hold values from -0.0029296875 to 0.0029296875
- mirror: int32 [256], P('occ'), may hold values from 0 to 63, as said below
Outputs:
- residual: float32 [256, 256, 32], P('occ', 'vir')
Inputs may be any that keep to these rules, and one draw needn't show every extreme that they name: Pair rows on each occ device are sorted by class, 8 of each class. mirror[r] on occ device p is a row of occ device p XOR 1 within the same class block, and the mirror of that row is r.
All inputs are finite; a program needn't handle non-finite values.
Results may differ from a plain program's by a relative error of at most 0.0029.
Values may be sent and summed in bfloat16 or wider, within the bound.
No kernel may reach another device: no remote copies, remote signals or barrier semaphores. Data moves between devices by JAX's collectives and lax.ppermute only.
A program may use at most 256 MiB of HBM per device.

v0:
```python
import jax
import jax.numpy as jnp
from jax import lax
from jax.sharding import PartitionSpec as P

IRREPS = 8


def from_partner(value, axis, distance):
    mask = 2**distance
    pairs = [(source, source ^ mask) for source in range(lax.axis_size(axis))]
    return lax.ppermute(value, axis, pairs)


def shards(cholesky, amplitudes, mirror):
    vectors, a_rows, orbitals = cholesky.shape
    vir_count = lax.axis_size("vir")
    per_irrep = vir_count // IRREPS
    window = a_rows * per_irrep
    irrep_one = lax.axis_index("vir") // per_irrep
    pair_rows = amplitudes.shape[0]
    per_class = pair_rows // IRREPS
    own_tiles = lax.dynamic_index_in_dim(amplitudes, irrep_one, 1, keepdims=False)
    gathered = lax.all_gather(cholesky, "vir", axis=1, tiled=True)
    result = jnp.zeros((pair_rows, a_rows, window), jnp.float32)
    for irrep_two in range(IRREPS):
        b_block = gathered[:, irrep_two * window : (irrep_two + 1) * window, :]
        v_slab = jnp.einsum(
            "lac,lbd->abcd", cholesky, b_block, preferred_element_type=jnp.float32
        ).astype(jnp.bfloat16)
        row_start = (irrep_one ^ irrep_two) * per_class
        amp_tiles = lax.dynamic_slice_in_dim(own_tiles, row_start, per_class, 0)
        contrib = jnp.einsum("abcd,kcd->kab", v_slab, amp_tiles, preferred_element_type=jnp.float32)
        result = lax.dynamic_update_slice_in_dim(result, contrib, row_start, 0)
    grouped = result.reshape(IRREPS, per_class, a_rows, per_irrep, a_rows)
    outgoing = jnp.stack(
        [
            jnp.transpose(
                lax.dynamic_index_in_dim(grouped, irrep_one ^ dest_irrep, 0, keepdims=False),
                (2, 0, 1, 3),
            )
            for dest_irrep in range(IRREPS)
        ],
        axis=0,
    ).reshape(vir_count, per_class, a_rows, a_rows)
    received = lax.all_to_all(outgoing, "vir", split_axis=0, concat_axis=0, tiled=True)
    received = from_partner(received, "occ", 0)
    arrived = received.reshape(IRREPS, per_irrep, per_class, a_rows, a_rows)
    pieces = []
    for pair_class in range(IRREPS):
        block_in = lax.dynamic_index_in_dim(arrived, irrep_one ^ pair_class, 0, keepdims=False)
        pieces.append(jnp.transpose(block_in, (1, 3, 0, 2)).reshape(per_class, a_rows, window))
    mirrored = jnp.concatenate(pieces, axis=0)
    return result + jnp.take(mirrored, mirror, axis=0)


def solution(mesh):
    placed = (P(None, "vir", None), P("occ", None, None, None), P("occ"))
    return jax.shard_map(
        shards, mesh=mesh, in_specs=placed, out_specs=P("occ", "vir", None), check_vma=False
    )
```

profile of v0, /device:TPU:0, one launch (start us, length us, event | category | flops | bytes accessed | tf_op | source)
XLA Modules:
  0.0 453.3 jit_solution(486611229945572093)
XLA Ops:
  10.9 193.7 %all-gather.2.cloned.1.call-done = bf16[256,256,128]{2,0,1:T(8,128)(2,1)} async-done(((bf16[256,8,128]{2,0,1:T(8,128)(2,1)}), bf16[256,256,128]{2,0,1:T(8,128)(2,1)}) %all-gather.2.cloned.1.call-update) | async-done | bytes 16777232 | tf_op jit(solution)/shard_map/all_gather | solution.py:24
  204.6 7.3 %convert_bitcast_fusion.7 = bf16[8,32,128,128]{2,3,0,1:T(8,128)(2,1)} fusion(bf16[256,256,128]{2,0,1:T(8,128)(2,1)} %all-gather.2.cloned.1.call-done, bf16[256,8,128]{2,1,0:T(8,128)(2,1)} %param.3), kind=kOutput, calls=%fused_computation.8 | convolution fusion | flops 2151677952 | bytes 11010048 | tf_op jit(solution)/shard_map/lac,lbd->abcd/dot_general | solution.py:28
  211.9 12.9 %copy.267 = bf16[8,32,128,128]{3,1,2,0:T(8,128)(2,1)} copy(bf16[8,32,128,128]{2,3,0,1:T(8,128)(2,1)} %convert_bitcast_fusion.7) | data formatting | bytes 16777216 | tf_op jit(solution)/shard_map/convert_element_type | solution.py:30
  224.8 7.2 %convert_bitcast_fusion.6 = bf16[8,32,128,128]{2,3,0,1:T(8,128)(2,1)} fusion(bf16[256,256,128]{2,0,1:T(8,128)(2,1)} %all-gather.2.cloned.1.call-done, bf16[256,8,128]{2,1,0:T(8,128)(2,1)S(1)} %copy-done), kind=kOutput, calls=%fused_computation.7 | convolution fusion | flops 2151677952 | bytes 11010048 | tf_op jit(solution)/shard_map/lac,lbd->abcd/dot_general | solution.py:28
  232.1 12.5 %copy.272 = bf16[8,32,128,128]{3,1,2,0:T(8,128)(2,1)} copy(bf16[8,32,128,128]{2,3,0,1:T(8,128)(2,1)} %convert_bitcast_fusion.6) | data formatting | bytes 16777216 | tf_op jit(solution)/shard_map/convert_element_type | solution.py:30
  244.6 7.2 %convert_bitcast_fusion.5 = bf16[8,32,128,128]{2,3,0,1:T(8,128)(2,1)} fusion(bf16[256,256,128]{2,0,1:T(8,128)(2,1)} %all-gather.2.cloned.1.call-done, bf16[256,8,128]{2,1,0:T(8,128)(2,1)S(1)} %copy-done), kind=kOutput, calls=%fused_computation.6 | convolution fusion | flops 2151677952 | bytes 11010048 | tf_op jit(solution)/shard_map/lac,lbd->abcd/dot_general | solution.py:28
  251.7 12.7 %copy.277 = bf16[8,32,128,128]{3,1,2,0:T(8,128)(2,1)} copy(bf16[8,32,128,128]{2,3,0,1:T(8,128)(2,1)} %convert_bitcast_fusion.5) | data formatting | bytes 16777216 | tf_op jit(solution)/shard_map/convert_element_type | solution.py:30
  264.5 7.2 %convert_bitcast_fusion.4 = bf16[8,32,128,128]{2,3,0,1:T(8,128)(2,1)} fusion(bf16[256,256,128]{2,0,1:T(8,128)(2,1)} %all-gather.2.cloned.1.call-done, bf16[256,8,128]{2,1,0:T(8,128)(2,1)S(1)} %copy-done), kind=kOutput, calls=%fused_computation.5 | convolution fusion | flops 2151677952 | bytes 11010048 | tf_op jit(solution)/shard_map/lac,lbd->abcd/dot_general | solution.py:28
  271.7 12.6 %copy.282 = bf16[8,32,128,128]{3,1,2,0:T(8,128)(2,1)} copy(bf16[8,32,128,128]{2,3,0,1:T(8,128)(2,1)} %convert_bitcast_fusion.4) | data formatting | bytes 16777216 | tf_op jit(solution)/shard_map/convert_element_type | solution.py:30
  284.3 7.2 %convert_bitcast_fusion.3 = bf16[8,32,128,128]{2,3,0,1:T(8,128)(2,1)} fusion(bf16[256,256,128]{2,0,1:T(8,128)(2,1)} %all-gather.2.cloned.1.call-done, bf16[256,8,128]{2,1,0:T(8,128)(2,1)S(1)} %copy-done), kind=kOutput, calls=%fused_computation.4 | convolution fusion | flops 2151677952 | bytes 11010048 | tf_op jit(solution)/shard_map/lac,lbd->abcd/dot_general | solution.py:28
  291.5 12.8 %copy.287 = bf16[8,32,128,128]{3,1,2,0:T(8,128)(2,1)} copy(bf16[8,32,128,128]{2,3,0,1:T(8,128)(2,1)} %convert_bitcast_fusion.3) | data formatting | bytes 16777216 | tf_op jit(solution)/shard_map/convert_element_type | solution.py:30
  304.3 7.2 %convert_bitcast_fusion.2 = bf16[8,32,128,128]{2,3,0,1:T(8,128)(2,1)} fusion(bf16[256,256,128]{2,0,1:T(8,128)(2,1)} %all-gather.2.cloned.1.call-done, bf16[256,8,128]{2,1,0:T(8,128)(2,1)S(1)} %copy-done), kind=kOutput, calls=%fused_computation.3 | convolution fusion | flops 2151677952 | bytes 11010048 | tf_op jit(solution)/shard_map/lac,lbd->abcd/dot_general | solution.py:28
  311.5 12.5 %copy.292 = bf16[8,32,128,128]{3,1,2,0:T(8,128)(2,1)} copy(bf16[8,32,128,128]{2,3,0,1:T(8,128)(2,1)} %convert_bitcast_fusion.2) | data formatting | bytes 16777216 | tf_op jit(solution)/shard_map/convert_element_type | solution.py:30
  324.0 7.3 %convert_bitcast_fusion.1 = bf16[8,32,128,128]{2,3,0,1:T(8,128)(2,1)} fusion(bf16[256,256,128]{2,0,1:T(8,128)(2,1)} %all-gather.2.cloned.1.call-done, bf16[256,8,128]{2,1,0:T(8,128)(2,1)S(1)} %copy-done), kind=kOutput, calls=%fused_computation.2 | convolution fusion | flops 2151677952 | bytes 11010048 | tf_op jit(solution)/shard_map/lac,lbd->abcd/dot_general | solution.py:28
  331.3 12.4 %copy.297 = bf16[8,32,128,128]{3,1,2,0:T(8,128)(2,1)} copy(bf16[8,32,128,128]{2,3,0,1:T(8,128)(2,1)} %convert_bitcast_fusion.1) | data formatting | bytes 16777216 | tf_op jit(solution)/shard_map/convert_element_type | solution.py:30
  343.7 7.3 %convert_bitcast_fusion = bf16[8,32,128,128]{2,3,0,1:T(8,128)(2,1)} fusion(bf16[256,256,128]{2,0,1:T(8,128)(2,1)} %all-gather.2.cloned.1.call-done, bf16[256,8,128]{2,1,0:T(8,128)(2,1)S(1)} %copy-done), kind=kOutput, calls=%fused_computation.1 | convolution fusion | flops 2151677952 | bytes 11010048 | tf_op jit(solution)/shard_map/lac,lbd->abcd/dot_general | solution.py:28
  351.0 13.1 %copy.302 = bf16[8,32,128,128]{3,1,2,0:T(8,128)(2,1)} copy(bf16[8,32,128,128]{2,3,0,1:T(8,128)(2,1)} %convert_bitcast_fusion) | data formatting | bytes 16777216 | tf_op jit(solution)/shard_map/convert_element_type | solution.py:30
  364.1 9.0 %convolution_bitcast_fusion.7 = f32[8,8,32]{2,0,1:T(8,128)S(1)} fusion(bf16[8,32,128,128]{3,1,2,0:T(8,128)(2,1)} %copy.267, bf16[8,1,128,128]{3,2,1,0:T(8,128)(2,1)S(1)} %get-tuple-element.11), kind=kOutput, calls=%fused_computation.24 | convolution fusion | flops 67108864 | bytes 8658944 | tf_op jit(solution)/shard_map/abcd,kcd->kab/dot_general | solution.py:33
  373.2 9.0 %convolution_bitcast_fusion.6 = f32[8,8,32]{2,0,1:T(8,128)S(1)} fusion(bf16[8,32,128,128]{3,1,2,0:T(8,128)(2,1)} %copy.272, bf16[8,1,128,128]{3,2,1,0:T(8,128)(2,1)S(1)} %get-tuple-element.10), kind=kOutput, calls=%fused_computation.23 | convolution fusion | flops 67108864 | bytes 8658944 | tf_op jit(solution)/shard_map/abcd,kcd->kab/dot_general | solution.py:33
  382.2 9.0 %convolution_bitcast_fusion.5 = f32[8,8,32]{2,0,1:T(8,128)S(1)} fusion(bf16[8,32,128,128]{3,1,2,0:T(8,128)(2,1)} %copy.277, bf16[8,1,128,128]{3,2,1,0:T(8,128)(2,1)S(1)} %get-tuple-element.9), kind=kOutput, calls=%fused_computation.22 | convolution fusion | flops 67108864 | bytes 8658944 | tf_op jit(solution)/shard_map/abcd,kcd->kab/dot_general | solution.py:33
  391.3 5.5 %convolution_bitcast_fusion.4 = f32[8,8,32]{2,0,1:T(8,128)S(1)} fusion(bf16[8,32,128,128]{3,1,2,0:T(8,128)(2,1)S(1)} %bitcast.245, bf16[8,1,128,128]{3,2,1,0:T(8,128)(2,1)S(1)} %get-tuple-element.8), kind=kOutput, calls=%fused_computation.21 | convolution fusion | flops 67108864 | bytes 8658944 | tf_op jit(solution)/shard_map/abcd,kcd->kab/dot_general | solution.py:33
  396.9 5.6 %convolution_bitcast_fusion.3 = f32[8,8,32]{2,0,1:T(8,128)S(1)} fusion(bf16[8,32,128,128]{3,1,2,0:T(8,128)(2,1)S(1)} %bitcast.243, bf16[8,1,128,128]{3,2,1,0:T(8,128)(2,1)S(1)} %get-tuple-element.7), kind=kOutput, calls=%fused_computation.20 | convolution fusion | flops 67108864 | bytes 8658944 | tf_op jit(solution)/shard_map/abcd,kcd->kab/dot_general | solution.py:33
  402.6 5.5 %convolution_bitcast_fusion.2 = f32[8,8,32]{2,0,1:T(8,128)S(1)} fusion(bf16[8,32,128,128]{3,1,2,0:T(8,128)(2,1)S(1)} %bitcast.241, bf16[8,1,128,128]{3,2,1,0:T(8,128)(2,1)S(1)} %get-tuple-element.6), kind=kOutput, calls=%fused_computation.19 | convolution fusion | flops 67108864 | bytes 8658944 | tf_op jit(solution)/shard_map/abcd,kcd->kab/dot_general | solution.py:33
  429.0 8.5 %all-to-all-done = f32[32,1,512]{2,1,0:T(1,128)S(1)} async-done(((f32[32,1,512]{2,1,0:T(1,128)}), f32[32,1,512]{2,1,0:T(1,128)S(1)}, u32[]{:S(2)}, u32[]{:S(2)}) %all-to-all-start) | async-done | bytes 65568 | tf_op jit(solution)/shard_map/all_to_all | solution.py:46
  (104 shorter events, 33.6 us)
Async XLA Ops:
  6.5 198.1 %all-gather.2.cloned.1.call-start = ((), (), s32[]{:S(2)}) async-start(), calls=%async_computation.1 | async-start | bytes 17301504 | tf_op jit(solution)/shard_map/all_gather | solution.py:24
  211.9 12.9 %copy-start = (bf16[256,8,128]{2,1,0:T(8,128)(2,1)S(1)}, bf16[256,8,128]{2,1,0:T(8,128)(2,1)}, u32[]{:S(2)}) copy-start(bf16[256,8,128]{2,1,0:T(8,128)(2,1)} %param.3) | copy-start | bytes 1572868
  364.1 27.2 %slice-start.8 = ((s8[8388608]{0:T(1024)(128)(4,1)}), s8[4194304]{0:T(1024)(128)(4,1)S(1)}, s32[]{:S(2)}) async-start(s8[8388608]{0:T(1024)(128)(4,1)} %bitcast.244), calls=%async_computation.10 | async-start | bytes 8388608
  373.2 18.1 %slice-start.9 = ((s8[8388608]{0:T(1024)(128)(4,1)}), s8[4194304]{0:T(1024)(128)(4,1)S(1)}, s32[]{:S(2)}) async-start(s8[8388608]{0:T(1024)(128)(4,1)} %bitcast.244), calls=%async_computation.11 | async-start | bytes 8388608
  373.2 23.7 %slice-start.6 = ((s8[8388608]{0:T(1024)(128)(4,1)}), s8[4194304]{0:T(1024)(128)(4,1)S(1)}, s32[]{:S(2)}) async-start(s8[8388608]{0:T(1024)(128)(4,1)} %bitcast.242), calls=%async_computation.8 | async-start | bytes 8388608
  382.2 14.6 %slice-start.7 = ((s8[8388608]{0:T(1024)(128)(4,1)}), s8[4194304]{0:T(1024)(128)(4,1)S(1)}, s32[]{:S(2)}) async-start(s8[8388608]{0:T(1024)(128)(4,1)} %bitcast.242), calls=%async_computation.9 | async-start | bytes 8388608
  391.3 11.3 %slice-start.4 = ((s8[8388608]{0:T(1024)(128)(4,1)}), s8[4194304]{0:T(1024)(128)(4,1)S(1)}, s32[]{:S(2)}) async-start(s8[8388608]{0:T(1024)(128)(4,1)} %bitcast.240), calls=%async_computation.6 | async-start | bytes 8388608
  396.8 5.8 %slice-start.5 = ((s8[8388608]{0:T(1024)(128)(4,1)}), s8[4194304]{0:T(1024)(128)(4,1)S(1)}, s32[]{:S(2)}) async-start(s8[8388608]{0:T(1024)(128)(4,1)} %bitcast.240), calls=%async_computation.7 | async-start | bytes 8388608
  396.8 11.3 %slice-start.2 = ((s8[8388608]{0:T(1024)(128)(4,1)}), s8[4194304]{0:T(1024)(128)(4,1)S(1)}, s32[]{:S(2)}) async-start(s8[8388608]{0:T(1024)(128)(4,1)} %bitcast.238), calls=%async_computation.4 | async-start | bytes 8388608
  402.6 5.6 %slice-start.3 = ((s8[8388608]{0:T(1024)(128)(4,1)}), s8[4194304]{0:T(1024)(128)(4,1)S(1)}, s32[]{:S(2)}) async-start(s8[8388608]{0:T(1024)(128)(4,1)} %bitcast.238), calls=%async_computation.5 | async-start | bytes 8388608
  402.6 11.1 %slice-start = ((s8[8388608]{0:T(1024)(128)(4,1)}), s8[4194304]{0:T(1024)(128)(4,1)S(1)}, s32[]{:S(2)}) async-start(s8[8388608]{0:T(1024)(128)(4,1)} %bitcast.236), calls=%async_computation.2 | async-start | bytes 8388608
  408.2 5.5 %slice-start.1 = ((s8[8388608]{0:T(1024)(128)(4,1)}), s8[4194304]{0:T(1024)(128)(4,1)S(1)}, s32[]{:S(2)}) async-start(s8[8388608]{0:T(1024)(128)(4,1)} %bitcast.236), calls=%async_computation.3 | async-start | bytes 8388608
  413.7 15.3 %copy-start.1 = (s32[64]{0:T(128)S(1)}, s32[64]{0:T(128)}, u32[]{:S(2)}) copy-start(s32[64]{0:T(128)} %param.5) | copy-start | bytes 772
  423.6 13.9 %all-to-all-start = ((f32[32,1,512]{2,1,0:T(1,128)}), f32[32,1,512]{2,1,0:T(1,128)S(1)}, u32[]{:S(2)}, u32[]{:S(2)}) async-start(f32[32,1,512]{2,1,0:T(1,128)} %reshape.98), calls=%async_computation | async-start | bytes 131072 | tf_op jit(solution)/shard_map/all_to_all | solution.py:46
  439.9 1.6 collective-permute-start
Sparse Core Ops, SparseCore 0:
  9.0 195.5 all-gather.1
where the time goes:
time: 460 us; the launch traced here: 453 us
  waiting for transfers between devices  204 us (44%)
  local copies, waits for them, and re-layouts  116 us (25%)
  matrix products  113 us (25%)
  between operations  14.4 us (3%)
  starting transfers between devices  5.43 us (1%)
    all_gather x1, waiting for transfers between devices, shards(): gathered = lax.all_gather(cholesky, 'vir', axis=1, tiled=True)  194 us
    convert_element_type x8, local copies, waits for them, and re-layouts, shards(): v_slab = jnp.einsum('lac,lbd->abcd', cholesky, b_block, preferred_element...  102 us
    dot_general x8, matrix products, shards(): jnp.einsum('lac,lbd->abcd', cholesky, b_block, preferred_element_type=jnp...  57.9 us
    dot_general x8, matrix products, shards(): jnp.einsum('abcd,kcd->kab', v_slab, amp_tiles, preferred_element_type=jnp...  54.6 us
  transfers between devices with their start and end apart: 3, of which 3 were waited for; matrix products, arithmetic and copies ran while one was open for 1% of the time, Pallas kernels for 0%

commit v1 on v0

v1 whole, which is shorter than its diff:
```python
import functools

import jax
import jax.numpy as jnp
from jax import lax
from jax.experimental import pallas as pl
from jax.experimental.pallas import tpu as pltpu
from jax.sharding import PartitionSpec as P

IRREPS = 8
CLS = 8
NT = (((1,), (1,)), ((), ()))
BF16 = jnp.bfloat16
F32 = jnp.float32


def permute(value, move):
    pairs = []
    for occ in range(4):
        for vir in range(32):
            to_occ, to_vir = move(occ, vir)
            pairs.append((occ * 32 + vir, to_occ * 32 + to_vir))
    return lax.ppermute(value, ("occ", "vir"), pairs)


def over_y(value, k):
    return permute(value, lambda occ, vir: (occ, vir ^ k))


def over_x(value, k):
    return permute(value, lambda occ, vir: (occ, vir ^ (8 * k)))


def over_z(value):
    return permute(value, lambda occ, vir: (occ ^ (2 if occ & 1 else 0), vir ^ 4))


def to_sibling(value):
    return permute(value, lambda occ, vir: (occ ^ 1, vir))


def fill_positions(odd, mirror_ref, rows_ref):
    def step(i, _):
        rows_ref[jnp.where(odd == 1, mirror_ref[i], i)] = i
        return 0

    lax.fori_loop(0, IRREPS * CLS, step, 0)


def spec(space):
    return pl.BlockSpec(memory_space=space)


def pack_kernel(place_ref, mirror_ref, amp_ref, out_ref, rows_ref, sem):
    h = place_ref[0]
    fill_positions(place_ref[2], mirror_ref, rows_ref)

    def step(i, _):
        pltpu.make_async_copy(amp_ref.at[rows_ref[i], h ^ (i // CLS)], out_ref.at[i], sem).start()
        return 0

    lax.fori_loop(0, IRREPS * CLS, step, 0)
    pltpu.make_async_copy(out_ref, out_ref, sem).wait()


def pack_tiles(place, mirror, amplitudes):
    return pl.pallas_call(
        pack_kernel,
        out_shape=jax.ShapeDtypeStruct((IRREPS * CLS, 128, 128), BF16),
        in_specs=[spec(pltpu.SMEM), spec(pltpu.SMEM), spec(pl.ANY)],
        out_specs=spec(pl.ANY),
        scratch_shapes=[pltpu.SMEM((IRREPS * CLS,), jnp.int32), pltpu.SemaphoreType.DMA],
        name="pack_tiles",
    )(place, mirror, amplitudes)


def rows_kernel(place_ref, r0_ref, r1_ref, r2_ref, r3_ref, mine_ref, other_ref, all_ref):
    y, core = place_ref[1], place_ref[2]
    for k, ref in enumerate((r0_ref, r1_ref, r2_ref, r3_ref)):
        all_ref[k] = ref[...]
    for half, out_ref in enumerate((mine_ref, other_ref)):
        base = (half ^ core) * 256

        def step(i, _):
            parts = []
            for q in range(4):
                start = pl.multiple_of(base + i * 16, 16)
                parts.append(all_ref[q ^ y, pl.ds(start, 16), :].astype(F32))
            both = [p[0:8] for p in parts] + [p[8:16] for p in parts]
            out_ref[pl.ds(pl.multiple_of(i * 64, 64), 64), :] = jnp.concatenate(both, axis=0).astype(BF16)
            return 0

        lax.fori_loop(0, 16, step, 0, unroll=4)


def order_rows(place, quarters):
    half = jax.ShapeDtypeStruct((1024, 128), BF16)
    return pl.pallas_call(
        rows_kernel,
        out_shape=(half, half),
        in_specs=[spec(pltpu.SMEM)] + [spec(pltpu.VMEM)] * 4,
        out_specs=(spec(pltpu.VMEM), spec(pltpu.VMEM)),
        scratch_shapes=[pltpu.VMEM((4, 512, 128), BF16)],
        name="order_rows",
    )(place, *quarters)


CHUNK = 16


def ladder_kernel(classes, carried, *refs):
    n = len(classes)
    place_ref, mirror_ref, amp_ref, tp_ref, mine_ref, other_ref = refs[:6]
    refs = refs[6:]
    peers, refs = refs[: 2 * n], refs[2 * n :]
    if carried:
        carry_ref, refs = refs[0], refs[1:]
    out_ref, rows_ref, own_s, b_s, t_s, tp_s, w_s, r_s, own_sem, b_sem, t_sem, tp_sem = refs
    h, y = place_ref[0], place_ref[1]
    fill_positions(place_ref[2], mirror_ref, rows_ref)

    own = [
        pltpu.make_async_copy(mine_ref, own_s.at[0], own_sem.at[0]),
        pltpu.make_async_copy(other_ref, own_s.at[1], own_sem.at[1]),
    ]
    for i, g in enumerate(classes):
        def tile(j, _):
            pltpu.make_async_copy(amp_ref.at[rows_ref[g * CLS + j], h], t_s.at[i, j], t_sem.at[i]).start()
            return 0

        lax.fori_loop(0, CLS, tile, 0)
        pltpu.make_async_copy(tp_ref.at[pl.ds(g * CLS, CLS)], tp_s.at[i], tp_sem.at[i]).start()
        if i == 0:
            for copy in own:
                copy.start()
        for half in range(2):
            pltpu.make_async_copy(peers[2 * i + half], b_s.at[i, half], b_sem.at[i, half]).start()
    for copy in own:
        copy.wait()

    rows = CHUNK * 32

    def one_class(i, _):
        pltpu.make_async_copy(t_s.at[i], t_s.at[i], t_sem.at[i]).wait()
        pltpu.make_async_copy(tp_s.at[i], tp_s.at[i], tp_sem.at[i]).wait()
        for half in range(2):
            pltpu.make_async_copy(b_s.at[i, half], b_s.at[i, half], b_sem.at[i, half]).wait()
        for j in range(CLS):
            w_s[0:128, j * 128 : (j + 1) * 128] = t_s[i, j]
            w_s[128:256, j * 128 : (j + 1) * 128] = tp_s[i, j].T
        r_s[i] = jnp.zeros((256, 32), F32)

        def chunk(n_chunk, _):
            half = n_chunk // (32 // CHUNK)
            start = pl.multiple_of((n_chunk % (32 // CHUNK)) * rows, rows)
            own_rows = own_s[half, pl.ds(start, rows), :]
            lhs = jnp.concatenate([own_rows, own_rows], axis=1)
            x = jnp.dot(lhs, w_s[...], preferred_element_type=F32).astype(BF16)
            b = b_s[i, half, pl.ds(start, rows), :]
            x2 = jnp.concatenate(
                [
                    jnp.concatenate(
                        [x[l * 32 : (l + 1) * 32, j * 128 : (j + 1) * 128] for l in range(CHUNK)], axis=1
                    )
                    for j in range(CLS)
                ],
                axis=0,
            )
            bt = jnp.concatenate([b[l * 32 : (l + 1) * 32] for l in range(CHUNK)], axis=1)
            r_s[i] += lax.dot_general(x2, bt, NT, preferred_element_type=F32)
            return 0

        lax.fori_loop(0, 64 // CHUNK, chunk, 0)
        return 0

    lax.fori_loop(0, n, one_class, 0)
    for q in range(4):
        blocks = []
        for i in range(n):
            r = r_s[i]
            blocks.append(
                jnp.concatenate([r[j * 32 + q * 8 : j * 32 + q * 8 + 8] for j in range(CLS)], axis=0)
            )
        if carried:
            blocks = [carry_ref[q ^ y]] + blocks
        out_ref[q ^ y] = jnp.concatenate(blocks, axis=1) if len(blocks) > 1 else blocks[0]


def ladder(classes, place, mirror, amplitudes, received, own, peers, carry=None):
    n = len(classes)
    lanes = 32 * (n + (carry is not None))
    operands = [place, mirror, amplitudes, received, *own, *[half for peer in peers for half in peer]]
    in_specs = [spec(pltpu.SMEM)] * 2 + [spec(pl.ANY)] * (len(operands) - 2)
    if carry is not None:
        operands.append(carry)
        in_specs.append(spec(pltpu.VMEM))
    return pl.pallas_call(
        functools.partial(ladder_kernel, classes, carry is not None),
        out_shape=jax.ShapeDtypeStruct((4, 64, lanes), F32),
        in_specs=in_specs,
        out_specs=spec(pltpu.VMEM),
        scratch_shapes=[
            pltpu.SMEM((IRREPS * CLS,), jnp.int32),
            pltpu.VMEM((2, 1024, 128), BF16),
            pltpu.VMEM((n, 2, 1024, 128), BF16),
            pltpu.VMEM((n, CLS, 128, 128), BF16),
            pltpu.VMEM((n, CLS, 128, 128), BF16),
            pltpu.VMEM((256, 1024), BF16),
            pltpu.VMEM((n, 256, 32), F32),
            pltpu.SemaphoreType.DMA((2,)),
            pltpu.SemaphoreType.DMA((n, 2)),
            pltpu.SemaphoreType.DMA((n,)),
            pltpu.SemaphoreType.DMA((n,)),
        ],
        compiler_params=pltpu.CompilerParams(vmem_limit_bytes=40 * 2**20),
        cost_estimate=pl.CostEstimate(
            flops=n * 2**31, transcendentals=0, bytes_accessed=n * 2**20
        ),
        name="ladder_" + "_".join(str(g) for g in classes),
    )(*operands)


def finish_kernel(orders, place_ref, mirror_ref, *refs):
    parts, out_ref, rows_ref = refs[:-2], refs[-2], refs[-1]
    fill_positions(place_ref[2], mirror_ref, rows_ref)
    for n, order in enumerate(orders):
        own, rest = parts[4 * n], parts[4 * n + 1 : 4 * n + 4]
        total = own[0]
        for ref in rest:
            total = total + ref[...]
        for lane, g in enumerate(order):
            for j in range(CLS):
                out_ref[rows_ref[g * CLS + j]] = total[j * 8 : (j + 1) * 8, lane * 32 : (lane + 1) * 32]


def finish(orders, place, mirror, parts):
    return pl.pallas_call(
        functools.partial(finish_kernel, orders),
        out_shape=jax.ShapeDtypeStruct((64, 8, 32), F32),
        in_specs=[spec(pltpu.SMEM)] * 2 + [spec(pltpu.VMEM)] * len(parts),
        out_specs=spec(pltpu.VMEM),
        scratch_shapes=[pltpu.SMEM((IRREPS * CLS,), jnp.int32)],
        name="finish",
    )(place, mirror, *parts)


def shards(cholesky, amplitudes, mirror):
    vir = lax.axis_index("vir")
    core = lax.axis_index("occ") % 2
    h, y = vir // 4, vir % 4
    place = jnp.stack([h, y, core]).astype(jnp.int32)

    by_chunk = cholesky.reshape(4, 512, 128)
    quarters = [lax.dynamic_index_in_dim(by_chunk, y, 0, keepdims=False)]
    for k in range(1, 4):
        quarters.append(over_y(lax.dynamic_index_in_dim(by_chunk, y ^ k, 0, keepdims=False), k))
    received = to_sibling(pack_tiles(place, mirror, amplitudes))
    mine, other = order_rows(place, quarters)

    halves = {0: (mine, other)}
    direct = {1: over_z(mine), 2: over_x(mine, 1), 4: over_x(mine, 2), 6: over_x(mine, 3)}
    for g in (2, 4, 6):
        direct[g + 1] = over_z(direct[g])
    for g in range(1, 8):
        halves[g] = (direct[g], to_sibling(direct[g]))

    def run(classes, carry=None):
        return ladder(
            classes, place, mirror, amplitudes, received, halves[0], [halves[g] for g in classes], carry
        )

    first = run((0,))
    near = run((1, 2, 4, 6))
    far = run((3, 5, 7), first)
    parts = []
    for block in (near, far):
        parts.append(block)
        for k in range(1, 4):
            parts.append(over_y(block[k], k))
    return finish(((1, 2, 4, 6), (0, 3, 5, 7)), place, mirror, parts)


def solution(mesh):
    placed = (P(None, "vir", None), P("occ", None, None, None), P("occ"))
    return jax.shard_map(
        shards, mesh=mesh, in_specs=placed, out_specs=P("occ", "vir", None), check_vma=False
    )
```

time: 460 us -> 169 us (0.37); the launches traced: 453 us -> 169 us
  waiting for transfers between devices: 204 us -> 33.2 us
  matrix products: 113 us -> 0 us
  local copies, waits for them, and re-layouts: 116 us -> 5.63 us
  Pallas kernels: 0 us -> 102 us
  starting transfers between devices: 5.43 us -> 26.8 us
  between operations: 14.4 us -> 0.25 us
    all_gather x1 -> x0, waiting for transfers between devices: 194 us -> none  [shards(): gathered = lax.all_gather(cholesky, 'vir', axis=1, tiled=True)]
    dot_general x16 -> x0, matrix products: 113 us -> none  [the longest x8 57.9 us: shards(): jnp.einsum('lac,lbd->abcd', cholesky, b_block, preferred_element_type=jnp...]
    pallas_call x0 -> x6, Pallas kernels: none -> 102 us  [the longest x1 66.1 us: pack_tiles(): pl.pallas_call(pack_kernel, out_shape=jax.ShapeDtypeStruct((IRREPS * CLS,...]
    convert_element_type x8 -> x0, local copies, waits for them, and re-layouts: 102 us -> none  [shards(): v_slab = jnp.einsum('lac,lbd->abcd', cholesky, b_block, preferred_element...]
    ppermute x1 -> x24, waiting for transfers between devices: 1.51 us -> 33.2 us  [permute(): return lax.ppermute(value, ('occ', 'vir'), pairs)]
    ppermute x1 -> x24, starting transfers between devices: 0.04 us -> 26.8 us  [permute(): return lax.ppermute(value, ('occ', 'vir'), pairs)]
    all_to_all x1 -> x0, waiting for transfers between devices: 8.47 us -> none  [shards(): lax.all_to_all(outgoing, 'vir', split_axis=0, concat_axis=0, tiled=True)]
    all_to_all x1 -> x0, starting transfers between devices: 5.38 us -> none  [shards(): lax.all_to_all(outgoing, 'vir', split_axis=0, concat_axis=0, tiled=True)]
  transfers between devices with their start and end apart: 3 -> 24, of which waited for: 3 -> 11; matrix products, arithmetic and copies ran while one was open for 1% -> 0% of each run, Pallas kernels for 0% -> 20%
where the time goes in v1:
time: 169 us
  Pallas kernels  102 us (60%)
  waiting for transfers between devices  33.2 us (20%)
  starting transfers between devices  26.8 us (16%)
  local copies, waits for them, and re-layouts  5.63 us (3%)
    pallas_call x1, Pallas kernels, pack_tiles(): pl.pallas_call(pack_kernel, out_shape=jax.ShapeDtypeStruct((IRREPS * CLS,...  66.1 us
    ppermute x24, waiting for transfers between devices, permute(): return lax.ppermute(value, ('occ', 'vir'), pairs)  33.2 us
    pallas_call x3, Pallas kernels, ladder(): pl.pallas_call(functools.partial(ladder_kernel, classes, carry is not Non...  31.3 us
    ppermute x24, starting transfers between devices, permute(): return lax.ppermute(value, ('occ', 'vir'), pairs)  26.8 us
  transfers between devices with their start and end apart: 24, of which 11 were waited for; matrix products, arithmetic and copies ran while one was open for 0% of the time, Pallas kernels for 20%

profile of v1, /device:TPU:0, one launch (start us, length us, event | category | flops | bytes accessed | tf_op | source)
XLA Modules:
  0.0 168.6 jit_solution(11599838450051943609)
XLA Ops:
  0.7 66.1 %pack_tiles.1 = bf16[64,128,128]{2,1,0:T(8,128)(2,1)} custom-call(s32[3]{0:T(128)} %pad_add_fusion.place_ref.refs_0_, s32[64]{0:T(128)} %mirror_ref.3, bf16[64,8,128,128]{3,2,1,0:T(8,128)(2,1)} %refs_2_.5), custom_call_target="tpu_custom_call" | custom-call | tf_op jit(solution)/shard_map/pack_tiles/pallas_call | solution.py:67
  67.5 1.7 collective-permute-start.1
  69.2 2.9 %collective-permute-start.2 = (bf16[512,128]{1,0:T(8,128)(2,1)S(1)}, bf16[512,128]{1,0:T(8,128)(2,1)S(1)}, u32[]{:S(2)}, u32[]{:S(2)}) collective-permute-start(bf16[512,128]{1,0:T(8,128)(2,1)S(1)} %get-tuple-element.10), channel_id=1, source_target_pairs={{0,2},{1,3},{2,0},{3,1},{4,6},{5,7},{6,4},{7,5},{8,10},{9,11},{10,... | collective-permute-start | bytes 393224 | tf_op jit(solution)/shard_map/ppermute | solution.py:23
  73.8 5.1 %collective-permute-done.2.r2_ref = bf16[512,128]{1,0:T(8,128)(2,1)S(1)} collective-permute-done((bf16[512,128]{1,0:T(8,128)(2,1)S(1)}, bf16[512,128]{1,0:T(8,128)(2,1)S(1)}, u32[]{:S(2)}, u32[]{:S(2)}) %collective-permute-start.2) | collective-permute-done | bytes 131104 | tf_op jit(solution)/shard_map/ppermute | solution.py:23
  78.9 2.4 %collective-permute-done.3.r3_ref = bf16[512,128]{1,0:T(8,128)(2,1)S(1)} collective-permute-done((bf16[512,128]{1,0:T(8,128)(2,1)S(1)}, bf16[512,128]{1,0:T(8,128)(2,1)S(1)}, u32[]{:S(2)}, u32[]{:S(2)}) %collective-permute-start.3) | collective-permute-done | bytes 131104 | tf_op jit(solution)/shard_map/ppermute | solution.py:23
  81.9 2.2 %order_rows.1 = (bf16[1024,128]{1,0:T(8,128)(2,1)}, bf16[1024,128]{1,0:T(8,128)(2,1)}) custom-call(s32[3]{0:T(128)} %pad_add_fusion.place_ref.refs_0_, bf16[512,128]{1,0:T(8,128)(2,1)} %get-tuple-element.12.r0_ref, bf16[512,128]{1,0:T(8,128)(2,1)} %copy-done.7, bf16[512,128]{1,0:T(8,128)(2,1)} %copy-done.8, bf16[512,128]{1,0:T(8,128)(2,1)} %copy-done.9), custom_call_target="tpu_custom_call" | custom-call | tf_op jit(solution)/shard_map/order_rows/pallas_call | solution.py:98
  84.1 1.9 %collective-permute-start.4 = (bf16[1024,128]{1,0:T(8,128)(2,1)}, bf16[1024,128]{1,0:T(8,128)(2,1)S(1)}, u32[]{:S(2)}, u32[]{:S(2)}) collective-permute-start(bf16[1024,128]{1,0:T(8,128)(2,1)} %get-tuple-element.7.refs_4_.refs_6_), channel_id=1, source_target_pairs={{0,4},{1,5},{2,6},{3,7},{4,0},{5,1},{6,2},{7,3},{8,12},{9,13},{10,... | collective-permute-start | bytes 786440 | tf_op jit(solution)/shard_map/ppermute | solution.py:23
  87.5 2.7 %collective-permute-start.8 = (bf16[1024,128]{1,0:T(8,128)(2,1)}, bf16[1024,128]{1,0:T(8,128)(2,1)S(1)}, u32[]{:S(2)}, u32[]{:S(2)}) collective-permute-start(bf16[1024,128]{1,0:T(8,128)(2,1)} %get-tuple-element.7.refs_4_.refs_6_), channel_id=1, source_target_pairs={{0,16},{1,17},{2,18},{3,19},{4,20},{5,21},{6,22},{7,23},{8,24},{9,... | collective-permute-start | bytes 786440 | tf_op jit(solution)/shard_map/ppermute | solution.py:23
  91.6 3.3 %collective-permute-done.6.refs_8_ = bf16[1024,128]{1,0:T(8,128)(2,1)S(1)} collective-permute-done((bf16[1024,128]{1,0:T(8,128)(2,1)}, bf16[1024,128]{1,0:T(8,128)(2,1)S(1)}, u32[]{:S(2)}, u32[]{:S(2)}) %collective-permute-start.6) | collective-permute-done | bytes 262176 | tf_op jit(solution)/shard_map/ppermute | solution.py:23
  96.1 6.7 %collective-permute-done.8.refs_10_ = bf16[1024,128]{1,0:T(8,128)(2,1)S(1)} collective-permute-done((bf16[1024,128]{1,0:T(8,128)(2,1)}, bf16[1024,128]{1,0:T(8,128)(2,1)S(1)}, u32[]{:S(2)}, u32[]{:S(2)}) %collective-permute-start.8) | collective-permute-done | bytes 262176 | tf_op jit(solution)/shard_map/ppermute | solution.py:23
  103.2 3.3 %collective-permute-done.10.refs_12_ = bf16[1024,128]{1,0:T(8,128)(2,1)S(1)} collective-permute-done((bf16[1024,128]{1,0:T(8,128)(2,1)}, bf16[1024,128]{1,0:T(8,128)(2,1)S(1)}, u32[]{:S(2)}, u32[]{:S(2)}) %collective-permute-start.10) | collective-permute-done | bytes 262176 | tf_op jit(solution)/shard_map/ppermute | solution.py:23
  106.4 2.0 %collective-permute-start.17 = (bf16[1024,128]{1,0:T(8,128)(2,1)S(1)}, bf16[1024,128]{1,0:T(8,128)(2,1)S(1)}, u32[]{:S(2)}, u32[]{:S(2)}) collective-permute-start(bf16[1024,128]{1,0:T(8,128)(2,1)S(1)} %collective-permute-done.8.refs_10_), channel_id=1, source_target_pairs={{0,4},{1,5},{2,6},{3,7},{4,0},{5,1},{6,2},{7,3},{8,12},{9,13},{10,... | collective-permute-start | bytes 786440 | tf_op jit(solution)/shard_map/ppermute | solution.py:23
  109.3 3.5 %collective-permute-done.15.refs_6_ = bf16[1024,128]{1,0:T(8,128)(2,1)S(1)} collective-permute-done((bf16[1024,128]{1,0:T(8,128)(2,1)S(1)}, bf16[1024,128]{1,0:T(8,128)(2,1)S(1)}, u32[]{:S(2)}, u32[]{:S(2)}) %collective-permute-start.15) | collective-permute-done | bytes 262176 | tf_op jit(solution)/shard_map/ppermute | solution.py:23
  113.0 2.6 %collective-permute-done.17.refs_8_ = bf16[1024,128]{1,0:T(8,128)(2,1)S(1)} collective-permute-done((bf16[1024,128]{1,0:T(8,128)(2,1)S(1)}, bf16[1024,128]{1,0:T(8,128)(2,1)S(1)}, u32[]{:S(2)}, u32[]{:S(2)}) %collective-permute-start.17) | collective-permute-done | bytes 262176 | tf_op jit(solution)/shard_map/ppermute | solution.py:23
  115.8 2.6 %collective-permute-done.19.refs_10_ = bf16[1024,128]{1,0:T(8,128)(2,1)S(1)} collective-permute-done((bf16[1024,128]{1,0:T(8,128)(2,1)S(1)}, bf16[1024,128]{1,0:T(8,128)(2,1)S(1)}, u32[]{:S(2)}, u32[]{:S(2)}) %collective-permute-start.19) | collective-permute-done | bytes 262176 | tf_op jit(solution)/shard_map/ppermute | solution.py:23
  120.5 14.6 %ladder_1_2_4_6.1.refs_0_ = f32[4,64,128]{2,1,0:T(8,128)S(1)} custom-call(s32[3]{0:T(128)S(1)} %copy-done.4, s32[64]{0:T(128)S(1)} %copy-done.5, bf16[64,8,128,128]{3,2,1,0:T(8,128)(2,1)} %refs_2_.5, bf16[64,128,128]{2,1,0:T(8,128)(2,1)S(1)} %collective-permute-done.refs_3_, bf16[1024,128]{1,0:T(8,128)(2,1)S(1)} %copy-done, bf16[1024,128]{1,0:T(8,128)(2,1)S(1)} %copy-done.1, ...), custom_call_target="tpu_custom_call" | custom-call | flops 8589934592 | bytes 4194304 | tf_op jit(solution)/shard_map/ladder_1_2_4_6/pallas_call | solution.py:197
  135.3 1.7 collective-permute-start.13
  137.0 5.2 %ladder_0.1.refs_12_ = f32[4,64,32]{2,1,0:T(8,128)S(1)} custom-call(s32[3]{0:T(128)S(1)} %copy-done.4, s32[64]{0:T(128)S(1)} %copy-done.5, bf16[64,8,128,128]{3,2,1,0:T(8,128)(2,1)} %refs_2_.5, bf16[64,128,128]{2,1,0:T(8,128)(2,1)S(1)} %collective-permute-done.refs_3_, bf16[1024,128]{1,0:T(8,128)(2,1)S(1)} %copy-done, bf16[1024,128]{1,0:T(8,128)(2,1)S(1)} %copy-done.1, ...), custom_call_target="tpu_custom_call" | custom-call | flops 2147483648 | bytes 1048576 | tf_op jit(solution)/shard_map/ladder_0/pallas_call | solution.py:197
  142.1 3.1 %collective-permute-start.14 = (f32[64,128]{1,0:T(8,128)S(1)}, f32[64,128]{1,0:T(8,128)S(1)}, u32[]{:S(2)}, u32[]{:S(2)}) collective-permute-start(f32[64,128]{1,0:T(8,128)S(1)} %get-tuple-element.16), channel_id=1, source_target_pairs={{0,3},{1,2},{2,1},{3,0},{4,7},{5,6},{6,5},{7,4},{8,11},{9,10},{10,... | collective-permute-start | bytes 98312 | tf_op jit(solution)/shard_map/ppermute | solution.py:23
  145.3 11.5 %ladder_3_5_7.1.refs_4_ = f32[4,64,128]{2,1,0:T(8,128)S(1)} custom-call(s32[3]{0:T(128)S(1)} %copy-done.4, s32[64]{0:T(128)S(1)} %copy-done.5, bf16[64,8,128,128]{3,2,1,0:T(8,128)(2,1)} %refs_2_.5, bf16[64,128,128]{2,1,0:T(8,128)(2,1)S(1)} %collective-permute-done.refs_3_, bf16[1024,128]{1,0:T(8,128)(2,1)S(1)} %copy-done, bf16[1024,128]{1,0:T(8,128)(2,1)S(1)} %copy-done.1, ...), custom_call_target="tpu_custom_call" | custom-call | flops 6442450944 | bytes 3145728 | tf_op jit(solution)/shard_map/ladder_3_5_7/pallas_call | solution.py:197
  156.9 1.7 collective-permute-start.22
  158.6 3.0 %collective-permute-start.23 = (f32[64,128]{1,0:T(8,128)S(1)}, f32[64,128]{1,0:T(8,128)S(1)}, u32[]{:S(2)}, u32[]{:S(2)}) collective-permute-start(f32[64,128]{1,0:T(8,128)S(1)} %get-tuple-element.13), channel_id=1, source_target_pairs={{0,3},{1,2},{2,1},{3,0},{4,7},{5,6},{6,5},{7,4},{8,11},{9,10},{10,... | collective-permute-start | bytes 98312 | tf_op jit(solution)/shard_map/ppermute | solution.py:23
  164.4 2.5 %finish.1 = f32[64,8,32]{2,1,0:T(8,128)} custom-call(s32[3]{0:T(128)} %pad_add_fusion.place_ref.refs_0_, s32[64]{0:T(128)} %mirror_ref.3, f32[4,64,128]{2,1,0:T(8,128)} %copy-done.2, f32[64,128]{1,0:T(8,128)} %copy-done.10, f32[64,128]{1,0:T(8,128)} %copy-done.11, f32[64,128]{1,0:T(8,128)} %copy-done.12, f32[4,64,128]{2,1,0:T(8,128)} %copy-done.3, ...), custom_call_target="tpu_custom_call" | custom-call | tf_op jit(solution)/shard_map/finish/pallas_call | solution.py:237
  166.8 1.7 %copy.4 = f32[64,8,32]{0,2,1:T(8,128)} copy(f32[64,8,32]{2,1,0:T(8,128)} %finish.1) | data formatting | bytes 131072 | tf_op jit(solution)/shard_map/finish/pallas_call | solution.py:237
  (67 shorter events, 14.3 us)
Async XLA Ops:
  66.7 51.9 %collective-permute-start = (bf16[64,128,128]{2,1,0:T(8,128)(2,1)}, bf16[64,128,128]{2,1,0:T(8,128)(2,1)S(1)}, u32[]{:S(2)}, u32[]{:S(2)}) collective-permute-start(bf16[64,128,128]{2,1,0:T(8,128)(2,1)} %pack_tiles.1), channel_id=1, source_target_pairs={{0,32},{1,33},{2,34},{3,35},{4,36},{5,37},{6,38},{7,39},{8,40},{9,... | collective-permute-start | bytes 6291464 | tf_op jit(solution)/shard_map/ppermute | solution.py:23
  67.5 6.2 %collective-permute-start.1 = (bf16[512,128]{1,0:T(8,128)(2,1)S(1)}, bf16[512,128]{1,0:T(8,128)(2,1)S(1)}, u32[]{:S(2)}, u32[]{:S(2)}) collective-permute-start(bf16[512,128]{1,0:T(8,128)(2,1)S(1)} %get-tuple-element.11), channel_id=1, source_target_pairs={{0,1},{1,0},{2,3},{3,2},{4,5},{5,4},{6,7},{7,6},{8,9},{9,8},{10,11... | collective-permute-start | bytes 393224 | tf_op jit(solution)/shard_map/ppermute | solution.py:23
  69.2 9.6 %collective-permute-start.2 = (bf16[512,128]{1,0:T(8,128)(2,1)S(1)}, bf16[512,128]{1,0:T(8,128)(2,1)S(1)}, u32[]{:S(2)}, u32[]{:S(2)}) collective-permute-start(bf16[512,128]{1,0:T(8,128)(2,1)S(1)} %get-tuple-element.10), channel_id=1, source_target_pairs={{0,2},{1,3},{2,0},{3,1},{4,6},{5,7},{6,4},{7,5},{8,10},{9,11},{10,... | collective-permute-start | bytes 393224 | tf_op jit(solution)/shard_map/ppermute | solution.py:23
  72.1 9.2 %collective-permute-start.3 = (bf16[512,128]{1,0:T(8,128)(2,1)S(1)}, bf16[512,128]{1,0:T(8,128)(2,1)S(1)}, u32[]{:S(2)}, u32[]{:S(2)}) collective-permute-start(bf16[512,128]{1,0:T(8,128)(2,1)S(1)} %get-tuple-element.9), channel_id=1, source_target_pairs={{0,3},{1,2},{2,1},{3,0},{4,7},{5,6},{6,5},{7,4},{8,11},{9,10},{10,... | collective-permute-start | bytes 393224 | tf_op jit(solution)/shard_map/ppermute | solution.py:23
  84.1 6.6 %collective-permute-start.4 = (bf16[1024,128]{1,0:T(8,128)(2,1)}, bf16[1024,128]{1,0:T(8,128)(2,1)S(1)}, u32[]{:S(2)}, u32[]{:S(2)}) collective-permute-start(bf16[1024,128]{1,0:T(8,128)(2,1)} %get-tuple-element.7.refs_4_.refs_6_), channel_id=1, source_target_pairs={{0,4},{1,5},{2,6},{3,7},{4,0},{5,1},{6,2},{7,3},{8,12},{9,13},{10,... | collective-permute-start | bytes 786440 | tf_op jit(solution)/shard_map/ppermute | solution.py:23
  86.0 8.9 %collective-permute-start.6 = (bf16[1024,128]{1,0:T(8,128)(2,1)}, bf16[1024,128]{1,0:T(8,128)(2,1)S(1)}, u32[]{:S(2)}, u32[]{:S(2)}) collective-permute-start(bf16[1024,128]{1,0:T(8,128)(2,1)} %get-tuple-element.7.refs_4_.refs_6_), channel_id=1, source_target_pairs={{0,8},{1,9},{2,10},{3,11},{4,12},{5,13},{6,14},{7,15},{8,0},{9,1},... | collective-permute-start | bytes 786440 | tf_op jit(solution)/shard_map/ppermute | solution.py:23
  87.5 15.3 %collective-permute-start.8 = (bf16[1024,128]{1,0:T(8,128)(2,1)}, bf16[1024,128]{1,0:T(8,128)(2,1)S(1)}, u32[]{:S(2)}, u32[]{:S(2)}) collective-permute-start(bf16[1024,128]{1,0:T(8,128)(2,1)} %get-tuple-element.7.refs_4_.refs_6_), channel_id=1, source_target_pairs={{0,16},{1,17},{2,18},{3,19},{4,20},{5,21},{6,22},{7,23},{8,24},{9,... | collective-permute-start | bytes 786440 | tf_op jit(solution)/shard_map/ppermute | solution.py:23
  90.2 16.2 %collective-permute-start.10 = (bf16[1024,128]{1,0:T(8,128)(2,1)}, bf16[1024,128]{1,0:T(8,128)(2,1)S(1)}, u32[]{:S(2)}, u32[]{:S(2)}) collective-permute-start(bf16[1024,128]{1,0:T(8,128)(2,1)} %get-tuple-element.7.refs_4_.refs_6_), channel_id=1, source_target_pairs={{0,24},{1,25},{2,26},{3,27},{4,28},{5,29},{6,30},{7,31},{8,16},{9,... | collective-permute-start | bytes 786440 | tf_op jit(solution)/shard_map/ppermute | solution.py:23
  90.7 15.7 %collective-permute-start.5 = (bf16[1024,128]{1,0:T(8,128)(2,1)S(1)}, bf16[1024,128]{1,0:T(8,128)(2,1)S(1)}, u32[]{:S(2)}, u32[]{:S(2)}) collective-permute-start(bf16[1024,128]{1,0:T(8,128)(2,1)S(1)} %collective-permute-done.4.refs_6_), channel_id=1, source_target_pairs={{0,32},{1,33},{2,34},{3,35},{4,36},{5,37},{6,38},{7,39},{8,40},{9,... | collective-permute-start | bytes 786440 | tf_op jit(solution)/shard_map/ppermute | solution.py:23
  94.9 13.6 %collective-permute-start.7 = (bf16[1024,128]{1,0:T(8,128)(2,1)S(1)}, bf16[1024,128]{1,0:T(8,128)(2,1)S(1)}, u32[]{:S(2)}, u32[]{:S(2)}) collective-permute-start(bf16[1024,128]{1,0:T(8,128)(2,1)S(1)} %collective-permute-done.6.refs_8_), channel_id=1, source_target_pairs={{0,32},{1,33},{2,34},{3,35},{4,36},{5,37},{6,38},{7,39},{8,40},{9,... | collective-permute-start | bytes 786440 | tf_op jit(solution)/shard_map/ppermute | solution.py:23
  102.8 5.8 %collective-permute-start.9 = (bf16[1024,128]{1,0:T(8,128)(2,1)S(1)}, bf16[1024,128]{1,0:T(8,128)(2,1)S(1)}, u32[]{:S(2)}, u32[]{:S(2)}) collective-permute-start(bf16[1024,128]{1,0:T(8,128)(2,1)S(1)} %collective-permute-done.8.refs_10_), channel_id=1, source_target_pairs={{0,32},{1,33},{2,34},{3,35},{4,36},{5,37},{6,38},{7,39},{8,40},{9,... | collective-permute-start | bytes 786440 | tf_op jit(solution)/shard_map/ppermute | solution.py:23
  106.4 6.4 %collective-permute-start.15 = (bf16[1024,128]{1,0:T(8,128)(2,1)S(1)}, bf16[1024,128]{1,0:T(8,128)(2,1)S(1)}, u32[]{:S(2)}, u32[]{:S(2)}) collective-permute-start(bf16[1024,128]{1,0:T(8,128)(2,1)S(1)} %collective-permute-done.6.refs_8_), channel_id=1, source_target_pairs={{0,4},{1,5},{2,6},{3,7},{4,0},{5,1},{6,2},{7,3},{8,12},{9,13},{10,... | collective-permute-start | bytes 786440 | tf_op jit(solution)/shard_map/ppermute | solution.py:23
  106.4 9.2 %collective-permute-start.17 = (bf16[1024,128]{1,0:T(8,128)(2,1)S(1)}, bf16[1024,128]{1,0:T(8,128)(2,1)S(1)}, u32[]{:S(2)}, u32[]{:S(2)}) collective-permute-start(bf16[1024,128]{1,0:T(8,128)(2,1)S(1)} %collective-permute-done.8.refs_10_), channel_id=1, source_target_pairs={{0,4},{1,5},{2,6},{3,7},{4,0},{5,1},{6,2},{7,3},{8,12},{9,13},{10,... | collective-permute-start | bytes 786440 | tf_op jit(solution)/shard_map/ppermute | solution.py:23
  108.5 10.0 %collective-permute-start.19 = (bf16[1024,128]{1,0:T(8,128)(2,1)S(1)}, bf16[1024,128]{1,0:T(8,128)(2,1)S(1)}, u32[]{:S(2)}, u32[]{:S(2)}) collective-permute-start(bf16[1024,128]{1,0:T(8,128)(2,1)S(1)} %collective-permute-done.10.refs_12_), channel_id=1, source_target_pairs={{0,4},{1,5},{2,6},{3,7},{4,0},{5,1},{6,2},{7,3},{8,12},{9,13},{10,... | collective-permute-start | bytes 786440 | tf_op jit(solution)/shard_map/ppermute | solution.py:23
  108.6 10.0 %collective-permute-start.11 = (bf16[1024,128]{1,0:T(8,128)(2,1)S(1)}, bf16[1024,128]{1,0:T(8,128)(2,1)S(1)}, u32[]{:S(2)}, u32[]{:S(2)}) collective-permute-start(bf16[1024,128]{1,0:T(8,128)(2,1)S(1)} %collective-permute-done.10.refs_12_), channel_id=1, source_target_pairs={{0,32},{1,33},{2,34},{3,35},{4,36},{5,37},{6,38},{7,39},{8,40},{9,... | collective-permute-start | bytes 786440 | tf_op jit(solution)/shard_map/ppermute | solution.py:23
  112.8 29.3 %collective-permute-start.16 = (bf16[1024,128]{1,0:T(8,128)(2,1)S(1)}, bf16[1024,128]{1,0:T(8,128)(2,1)S(1)}, u32[]{:S(2)}, u32[]{:S(2)}) collective-permute-start(bf16[1024,128]{1,0:T(8,128)(2,1)S(1)} %collective-permute-done.15.refs_6_), channel_id=1, source_target_pairs={{0,32},{1,33},{2,34},{3,35},{4,36},{5,37},{6,38},{7,39},{8,40},{9,... | collective-permute-start | bytes 786440 | tf_op jit(solution)/shard_map/ppermute | solution.py:23
  115.6 29.6 %collective-permute-start.18 = (bf16[1024,128]{1,0:T(8,128)(2,1)S(1)}, bf16[1024,128]{1,0:T(8,128)(2,1)S(1)}, u32[]{:S(2)}, u32[]{:S(2)}) collective-permute-start(bf16[1024,128]{1,0:T(8,128)(2,1)S(1)} %collective-permute-done.17.refs_8_), channel_id=1, source_target_pairs={{0,32},{1,33},{2,34},{3,35},{4,36},{5,37},{6,38},{7,39},{8,40},{9,... | collective-permute-start | bytes 786440 | tf_op jit(solution)/shard_map/ppermute | solution.py:23
  118.4 26.8 %collective-permute-start.20 = (bf16[1024,128]{1,0:T(8,128)(2,1)S(1)}, bf16[1024,128]{1,0:T(8,128)(2,1)S(1)}, u32[]{:S(2)}, u32[]{:S(2)}) collective-permute-start(bf16[1024,128]{1,0:T(8,128)(2,1)S(1)} %collective-permute-done.19.refs_10_), channel_id=1, source_target_pairs={{0,32},{1,33},{2,34},{3,35},{4,36},{5,37},{6,38},{7,39},{8,40},{9,... | collective-permute-start | bytes 786440 | tf_op jit(solution)/shard_map/ppermute | solution.py:23
  135.2 23.4 %collective-permute-start.12 = (f32[64,128]{1,0:T(8,128)S(1)}, f32[64,128]{1,0:T(8,128)S(1)}, u32[]{:S(2)}, u32[]{:S(2)}) collective-permute-start(f32[64,128]{1,0:T(8,128)S(1)} %get-tuple-element.18), channel_id=1, source_target_pairs={{0,1},{1,0},{2,3},{3,2},{4,5},{5,4},{6,7},{7,6},{8,9},{9,8},{10,11... | collective-permute-start | bytes 98312 | tf_op jit(solution)/shard_map/ppermute | solution.py:23
  135.3 26.3 %collective-permute-start.13 = (f32[64,128]{1,0:T(8,128)S(1)}, f32[64,128]{1,0:T(8,128)S(1)}, u32[]{:S(2)}, u32[]{:S(2)}) collective-permute-start(f32[64,128]{1,0:T(8,128)S(1)} %get-tuple-element.17), channel_id=1, source_target_pairs={{0,2},{1,3},{2,0},{3,1},{4,6},{5,7},{6,4},{7,5},{8,10},{9,11},{10,... | collective-permute-start | bytes 98312 | tf_op jit(solution)/shard_map/ppermute | solution.py:23
  142.1 19.5 %collective-permute-start.14 = (f32[64,128]{1,0:T(8,128)S(1)}, f32[64,128]{1,0:T(8,128)S(1)}, u32[]{:S(2)}, u32[]{:S(2)}) collective-permute-start(f32[64,128]{1,0:T(8,128)S(1)} %get-tuple-element.16), channel_id=1, source_target_pairs={{0,3},{1,2},{2,1},{3,0},{4,7},{5,6},{6,5},{7,4},{8,11},{9,10},{10,... | collective-permute-start | bytes 98312 | tf_op jit(solution)/shard_map/ppermute | solution.py:23
  156.8 4.8 %collective-permute-start.21 = (f32[64,128]{1,0:T(8,128)S(1)}, f32[64,128]{1,0:T(8,128)S(1)}, u32[]{:S(2)}, u32[]{:S(2)}) collective-permute-start(f32[64,128]{1,0:T(8,128)S(1)} %get-tuple-element.15), channel_id=1, source_target_pairs={{0,1},{1,0},{2,3},{3,2},{4,5},{5,4},{6,7},{7,6},{8,9},{9,8},{10,11... | collective-permute-start | bytes 98312 | tf_op jit(solution)/shard_map/ppermute | solution.py:23
  156.9 5.5 %collective-permute-start.22 = (f32[64,128]{1,0:T(8,128)S(1)}, f32[64,128]{1,0:T(8,128)S(1)}, u32[]{:S(2)}, u32[]{:S(2)}) collective-permute-start(f32[64,128]{1,0:T(8,128)S(1)} %get-tuple-element.14), channel_id=1, source_target_pairs={{0,2},{1,3},{2,0},{3,1},{4,6},{5,7},{6,4},{7,5},{8,10},{9,11},{10,... | collective-permute-start | bytes 98312 | tf_op jit(solution)/shard_map/ppermute | solution.py:23
  158.6 5.1 %collective-permute-start.23 = (f32[64,128]{1,0:T(8,128)S(1)}, f32[64,128]{1,0:T(8,128)S(1)}, u32[]{:S(2)}, u32[]{:S(2)}) collective-permute-start(f32[64,128]{1,0:T(8,128)S(1)} %get-tuple-element.13), channel_id=1, source_target_pairs={{0,3},{1,2},{2,1},{3,0},{4,7},{5,6},{6,5},{7,4},{8,11},{9,10},{10,... | collective-permute-start | bytes 98312 | tf_op jit(solution)/shard_map/ppermute | solution.py:23
  (16 other events, 341.9 us)

commit v2 on v0

v2 whole, which is shorter than its diff:
```python
import functools

import jax
import jax.numpy as jnp
from jax import lax
from jax.experimental import pallas as pl
from jax.experimental.pallas import tpu as pltpu
from jax.sharding import PartitionSpec as P

IRREPS = 8
CLS = 8
ROWS = IRREPS * CLS
NT = (((1,), (1,)), ((), ()))
TN = (((0,), (0,)), ((), ()))
BF16 = jnp.bfloat16
F32 = jnp.float32
MIB = 2**20


def permute(value, move):
    pairs = []
    for occ in range(4):
        for vir in range(32):
            to_occ, to_vir = move(occ, vir)
            pairs.append((occ * 32 + vir, to_occ * 32 + to_vir))
    return lax.ppermute(value, ("occ", "vir"), pairs)


def over_y(value, k):
    return permute(value, lambda occ, vir: (occ, vir ^ k))


def over_x(value, even, odd):
    return permute(value, lambda occ, vir: (occ, vir ^ (8 * (odd if occ & 1 else even))))


def over_z(value):
    return permute(value, lambda occ, vir: (occ ^ (2 if occ & 1 else 0), vir ^ 4))


def to_sibling(value):
    return permute(value, lambda occ, vir: (occ ^ 1, vir))


def spec(space):
    return pl.BlockSpec(memory_space=space)


def params(mib):
    return pltpu.CompilerParams(vmem_limit_bytes=mib * MIB)


def place():
    vir, core = lax.axis_index("vir"), lax.axis_index("occ") & 1
    return lax.shift_right_logical(vir, 2), vir & 3, core


def fill_positions(core, mirror_ref, rows_ref):
    def step(i, _):
        rows_ref[jnp.where(core == 1, mirror_ref[i], i)] = i
        return 0

    lax.fori_loop(0, ROWS, step, 0, unroll=8)


def pack_kernel(mirror_ref, amp_ref, out_ref, rows_ref, tiles, sems):
    h, _, core = place()
    fill_positions(core, mirror_ref, rows_ref)
    for g in range(IRREPS):
        for j in range(CLS):
            source = amp_ref.at[rows_ref[g * CLS + j], h ^ g]
            pltpu.make_async_copy(source, tiles.at[g, j], sems.at[g]).start()

    def one_class(g, _):
        pltpu.make_async_copy(tiles.at[g], tiles.at[g], sems.at[g]).wait()
        for j in range(CLS):
            out_ref[g, :, j * 128 : (j + 1) * 128] = tiles[g, j].T
        return 0

    lax.fori_loop(0, IRREPS, one_class, 0)


def pack_tiles(mirror, amplitudes):
    return pl.pallas_call(
        pack_kernel,
        out_shape=jax.ShapeDtypeStruct((IRREPS, 128, CLS * 128), BF16),
        in_specs=[spec(pltpu.SMEM), spec(pl.ANY)],
        out_specs=spec(pltpu.VMEM),
        scratch_shapes=[
            pltpu.SMEM((ROWS,), jnp.int32),
            pltpu.VMEM((IRREPS, CLS, 128, 128), BF16),
            pltpu.SemaphoreType.DMA((IRREPS,)),
        ],
        compiler_params=params(8),
        name="pack_tiles",
    )(mirror, amplitudes)


def rows_kernel(quarters_ref, all_ref, mine_ref):
    core = place()[2]

    def step(i, _):
        start = pl.multiple_of(i * 16, 16)
        parts = [quarters_ref[q, pl.ds(start, 16), :].astype(F32) for q in range(4)]
        both = [p[0:8] for p in parts] + [p[8:16] for p in parts]
        all_ref[pl.ds(pl.multiple_of(i * 64, 64), 64), :] = jnp.concatenate(both, axis=0).astype(BF16)
        return 0

    lax.fori_loop(0, 32, step, 0, unroll=8)
    mine_ref[...] = all_ref[pl.ds(pl.multiple_of(core * 1024, 1024), 1024), :]


def order_rows(quarters):
    return pl.pallas_call(
        rows_kernel,
        out_shape=(jax.ShapeDtypeStruct((2048, 128), BF16), jax.ShapeDtypeStruct((1024, 128), BF16)),
        in_specs=[spec(pltpu.VMEM)],
        out_specs=(spec(pltpu.VMEM), spec(pltpu.VMEM)),
        compiler_params=params(6),
        name="order_rows",
    )(quarters)


def ladder_kernel(classes, blocks, carried, *refs):
    n = len(classes)
    mirror_ref, amp_ref, tp_ref, own_ref = refs[:4]
    refs = refs[4:]
    peers, refs = refs[: 2 * len(blocks)], refs[2 * len(blocks) :]
    carry, refs = refs[:carried], refs[carried:]
    out_ref, rows_ref, own_s, b_s, w_s, x_s, r_s, own_sem, b_sem, t_sem, tp_sem = refs
    h, y, core = place()
    fill_positions(core, mirror_ref, rows_ref)

    own_copy = pltpu.make_async_copy(own_ref, own_s, own_sem)
    for i, g in enumerate(classes):
        for j in range(CLS):
            source = amp_ref.at[rows_ref[g * CLS + j], h]
            lanes = pl.ds(j * 128, 128)
            pltpu.make_async_copy(source, w_s.at[i, pl.ds(0, 128), lanes], t_sem.at[i]).start()
        pltpu.make_async_copy(tp_ref.at[g], w_s.at[i, pl.ds(128, 128)], tp_sem.at[i]).start()
        if i == 0:
            own_copy.start()
    copies = {}
    for k, block in enumerate(blocks):
        first, second = peers[2 * k], peers[2 * k + 1]
        if len(block) == 2:
            i = classes.index(block[0])
            pltpu.make_async_copy(first, b_s.at[i + core], b_sem.at[i, 0]).start()
            pltpu.make_async_copy(second, b_s.at[i + 1 - core], b_sem.at[i, 1]).start()
        else:
            i = classes.index(block[0])
            for half, ref in ((core, first), (1 - core, second)):
                target = b_s.at[i, pl.ds(pl.multiple_of(half * 1024, 1024), 1024)]
                pltpu.make_async_copy(ref, target, b_sem.at[i, 0 if ref is first else 1]).start()
        copies[i] = (first, second)

    def wait_weights(i):
        pltpu.make_async_copy(w_s.at[i, pl.ds(0, 128)], w_s.at[i, pl.ds(0, 128)], t_sem.at[i]).wait()
        pltpu.make_async_copy(tp_ref.at[classes[i]], w_s.at[i, pl.ds(128, 128)], tp_sem.at[i]).wait()

    def wait_peers(i):
        if i in copies:
            for k, ref in enumerate(copies[i]):
                rows = ref.shape[0]
                pltpu.make_async_copy(ref, b_s.at[i, pl.ds(0, rows)], b_sem.at[i, k]).wait()

    own_copy.wait()
    for i in range(n + 1):
        if i < n:
            wait_weights(i)
        if i > 0:
            wait_peers(i - 1)
        total = None
        for pair in range(4):
            for part in range(4):
                if i < n:
                    own = own_s[part * 512 : (part + 1) * 512, :]
                    lhs = jnp.concatenate([own, own], axis=1)
                    weights = w_s[i, :, pair * 256 : (pair + 1) * 256]
                    x = jnp.dot(lhs, weights, preferred_element_type=F32).astype(BF16)
                    for k in range(2):
                        j = pair * 2 + k
                        for l in range(16):
                            lane = (part * 16 + l) * 128
                            x_s[i % 2, j * 32 : (j + 1) * 32, lane : lane + 128] = x[
                                l * 32 : (l + 1) * 32, k * 128 : (k + 1) * 128
                            ]
                if i > 0:
                    step = pair * 4 + part
                    source = own_s if classes[i - 1] == 0 else b_s.at[i - 1]
                    b = source[step * 128 : (step + 1) * 128, :]
                    bt = jnp.concatenate([b[l * 32 : (l + 1) * 32] for l in range(4)], axis=1)
                    x2 = x_s[(i - 1) % 2, :, step * 512 : (step + 1) * 512]
                    term = lax.dot_general(x2, bt, NT, preferred_element_type=F32)
                    total = term if total is None else total + term
        if i > 0:
            r_s[i - 1] = total
    for q in range(4):
        columns = [ref[q ^ y] for ref in carry]
        for i in range(n):
            r = r_s[i]
            columns.append(
                jnp.concatenate([r[j * 32 + q * 8 : j * 32 + q * 8 + 8] for j in range(CLS)], axis=0)
            )
        out_ref[q ^ y] = jnp.concatenate(columns, axis=1) if len(columns) > 1 else columns[0]


def ladder(classes, mirror, amplitudes, received, own, blocks, peers, carry=()):
    n = len(classes)
    lanes = 32 * n + sum(c.shape[2] for c in carry)
    operands = [mirror, amplitudes, received, own, *peers, *carry]
    in_specs = [spec(pltpu.SMEM)] + [spec(pl.ANY)] * (3 + len(peers)) + [spec(pltpu.VMEM)] * len(carry)
    return pl.pallas_call(
        functools.partial(ladder_kernel, classes, blocks, len(carry)),
        out_shape=jax.ShapeDtypeStruct((4, 64, lanes), F32),
        in_specs=in_specs,
        out_specs=spec(pltpu.VMEM),
        scratch_shapes=[
            pltpu.SMEM((ROWS,), jnp.int32),
            pltpu.VMEM((2048, 128), BF16),
            pltpu.VMEM((n, 2048, 128), BF16),
            pltpu.VMEM((n, 256, 1024), BF16),
            pltpu.VMEM((2, 256, 8192), BF16),
            pltpu.VMEM((n, 256, 32), F32),
            pltpu.SemaphoreType.DMA,
            pltpu.SemaphoreType.DMA((n, 2)),
            pltpu.SemaphoreType.DMA((n,)),
            pltpu.SemaphoreType.DMA((n,)),
        ],
        compiler_params=params(36),
        cost_estimate=pl.CostEstimate(flops=n * 2**31, transcendentals=0, bytes_accessed=n * 2**20),
        name="ladder_" + "_".join(str(g) for g in classes),
    )(*operands)


def finish_kernel(order, mirror_ref, own_ref, r1_ref, r2_ref, r3_ref, out_ref, sum_s, pos_s):
    core = place()[2]
    total = own_ref[0] + r1_ref[...] + r2_ref[...] + r3_ref[...]
    sum_s[0] = total[:, 0:128]
    sum_s[1] = total[:, 128:256]
    for a8 in range(8):
        for k in range(2):
            strip = sum_s[k, pl.ds(a8, CLS, stride=8), :]
            for c in range(4):
                g = order[k * 4 + c]
                pos_s[g * CLS : (g + 1) * CLS, a8 * 32 : (a8 + 1) * 32] = strip[:, c * 32 : (c + 1) * 32]
    lane = lax.broadcasted_iota(jnp.int32, (ROWS, ROWS), 1)
    position = jnp.where(core == 1, jnp.broadcast_to(mirror_ref[...], (ROWS, ROWS)), lane)
    move = (lax.broadcasted_iota(jnp.int32, (ROWS, ROWS), 0) == position).astype(F32)
    out = lax.dot_general(
        pos_s[...], move, TN, preferred_element_type=F32, precision=lax.Precision.HIGHEST
    )
    out_ref[...] = out.reshape(8, 32, ROWS)


def finish(order, mirror, parts):
    out = pl.pallas_call(
        functools.partial(finish_kernel, order),
        out_shape=jax.ShapeDtypeStruct((8, 32, ROWS), F32),
        in_specs=[spec(pltpu.VMEM)] * 5,
        out_specs=spec(pltpu.VMEM),
        scratch_shapes=[pltpu.VMEM((2, 64, 128), F32), pltpu.VMEM((ROWS, 256), F32)],
        compiler_params=params(6),
        name="finish",
    )(mirror.reshape(1, ROWS), *parts)
    return jnp.transpose(out, (2, 0, 1))


def shards(cholesky, amplitudes, mirror):
    core = lax.axis_index("occ") & 1

    received = to_sibling(pack_tiles(mirror, amplitudes))
    quarters = lax.all_to_all(
        cholesky.reshape(4, 512, 128),
        "vir",
        0,
        0,
        axis_index_groups=[[4 * h + y for y in range(4)] for h in range(IRREPS)],
        tiled=True,
    )
    own, mine = order_rows(quarters)

    x1 = over_x(own, 1, 3)
    z0 = over_z(mine)
    x1_twin, z0_twin = to_sibling(x1), to_sibling(z0)
    x2 = over_x(lax.dynamic_slice_in_dim(x1, core * 1024, 1024, 0), 3, 1)
    zx1 = over_z(x1)
    x2_twin, zx1_twin = to_sibling(x2), to_sibling(zx1)
    zx2 = over_z(x2)
    zx2_twin = to_sibling(zx2)

    common = (mirror, amplitudes, received, own)
    first = ladder((0,), *common, (), ())
    near = ladder((1, 2, 6), *common, ((1,), (2, 6)), (z0, z0_twin, x1, x1_twin), (first,))
    far = ladder(
        (3, 7, 4, 5), *common, ((3, 7), (4,), (5,)), (zx1, zx1_twin, x2, x2_twin, zx2, zx2_twin), (near,)
    )
    parts = [far] + [over_y(far[k], k) for k in range(1, 4)]
    return finish((0, 1, 2, 6, 3, 7, 4, 5), mirror, parts)


def solution(mesh):
    placed = (P(None, "vir", None), P("occ", None, None, None), P("occ"))
    return jax.shard_map(
        shards, mesh=mesh, in_specs=placed, out_specs=P("occ", "vir", None), check_vma=False
    )
```

time: 460 us -> 95 us (0.21); the launches traced: 453 us -> 94.5 us
  waiting for transfers between devices: 204 us -> 22 us
  matrix products: 113 us -> 0 us
  local copies, waits for them, and re-layouts: 116 us -> 6.47 us
  Pallas kernels: 0 us -> 37.5 us
  blocking collectives: 0 us -> 14.5 us
  between operations: 14.4 us -> 0.13 us
  starting transfers between devices: 5.43 us -> 14 us
    all_gather x1 -> x0, waiting for transfers between devices: 194 us -> none  [shards(): gathered = lax.all_gather(cholesky, 'vir', axis=1, tiled=True)]
    dot_general x16 -> x0, matrix products: 113 us -> none  [the longest x8 57.9 us: shards(): jnp.einsum('lac,lbd->abcd', cholesky, b_block, preferred_element_type=jnp...]
    convert_element_type x8 -> x0, local copies, waits for them, and re-layouts: 102 us -> none  [shards(): v_slab = jnp.einsum('lac,lbd->abcd', cholesky, b_block, preferred_element...]
    pallas_call x0 -> x6, Pallas kernels: none -> 37.5 us  [the longest x3 30.2 us: ladder(): pl.pallas_call(functools.partial(ladder_kernel, classes, blocks, len(carr...]
    ppermute x1 -> x14, waiting for transfers between devices: 1.51 us -> 22 us  [permute(): return lax.ppermute(value, ('occ', 'vir'), pairs)]
    all_to_all x0 -> x1, blocking collectives: none -> 14.5 us  [shards(): lax.all_to_all(cholesky.reshape(4, 512, 128), 'vir', 0, 0, axis_index_gro...]
    ppermute x1 -> x14, starting transfers between devices: 0.04 us -> 14 us  [permute(): return lax.ppermute(value, ('occ', 'vir'), pairs)]
    all_to_all x1 -> x0, waiting for transfers between devices: 8.47 us -> none  [shards(): lax.all_to_all(outgoing, 'vir', split_axis=0, concat_axis=0, tiled=True)]
  transfers between devices with their start and end apart: 3 -> 14, of which waited for: 3 -> 7; matrix products, arithmetic and copies ran while one was open for 1% -> 0% of each run, Pallas kernels for 0% -> 18%
where the time goes in v2:
time: 95 us; the launch traced here: 94.5 us
  Pallas kernels  37.5 us (39%)
  waiting for transfers between devices  22 us (23%)
  blocking collectives  14.5 us (15%)
  starting transfers between devices  14 us (15%)
  local copies, waits for them, and re-layouts  6.47 us (7%)
    pallas_call x3, Pallas kernels, ladder(): pl.pallas_call(functools.partial(ladder_kernel, classes, blocks, len(carr...  30.2 us
    ppermute x14, waiting for transfers between devices, permute(): return lax.ppermute(value, ('occ', 'vir'), pairs)  22 us
    all_to_all x1, blocking collectives, shards(): lax.all_to_all(cholesky.reshape(4, 512, 128), 'vir', 0, 0, axis_index_gro...  14.5 us
    ppermute x14, starting transfers between devices, permute(): return lax.ppermute(value, ('occ', 'vir'), pairs)  14 us
    unnamed x8, local copies, waits for them, and re-layouts  6.43 us
    pallas_call x1, Pallas kernels, pack_tiles(): pl.pallas_call(pack_kernel, out_shape=jax.ShapeDtypeStruct((IRREPS, 128,...  6.07 us
  transfers between devices with their start and end apart: 14, of which 7 were waited for; matrix products, arithmetic and copies ran while one was open for 0% of the time, Pallas kernels for 18%

profile of v2, /device:TPU:0, one launch (start us, length us, event | category | flops | bytes accessed | tf_op | source)
XLA Modules:
  0.0 94.5 jit_solution(2659693351732677810)
XLA Ops:
  0.0 5.8 %copy-done = bf16[64,8,128,128]{3,2,1,0:T(8,128)(2,1)S(1)} copy-done((bf16[64,8,128,128]{3,2,1,0:T(8,128)(2,1)S(1)}, bf16[64,8,128,128]{3,2,1,0:T(8,128)(2,1)}, u32[]{:S(2)}) %copy-start) | copy-done | bytes 16777240
  5.8 0.7 copy-done.1
  6.4 6.1 %pack_tiles.1 = bf16[8,128,1024]{2,1,0:T(8,128)(2,1)} custom-call(s32[64]{0:T(128)S(1)} %copy-done.1, bf16[64,8,128,128]{3,2,1,0:T(8,128)(2,1)S(1)} %copy-done), custom_call_target="tpu_custom_call" | custom-call | tf_op jit(solution)/shard_map/pack_tiles/pallas_call | solution.py:84
  12.6 14.5 %all_to_all.5.quarters_ref = bf16[4,512,128]{2,1,0:T(8,128)(2,1)S(1)} all-to-all(bf16[4,512,128]{2,1,0:T(8,128)(2,1)S(1)} %bitcast.10), channel_id=1, replica_groups={{0,1,2,3},{4,5,6,7},{8,9,10,11},{12,13,14,15},{16,17,18,19},{20,21,22,2..., dimensions={0} | all-to-all | bytes 1048576 | tf_op jit(solution)/shard_map/all_to_all | solution.py:273
  27.2 1.6 %collective-permute-start.1 = (bf16[2048,128]{1,0:T(8,128)(2,1)S(1)}, bf16[2048,128]{1,0:T(8,128)(2,1)S(1)}, u32[]{:S(2)}, u32[]{:S(2)}) collective-permute-start(bf16[2048,128]{1,0:T(8,128)(2,1)S(1)} %get-tuple-element.7.refs_3_), channel_id=1, source_target_pairs={{0,8},{1,9},{2,10},{3,11},{4,12},{5,13},{6,14},{7,15},{8,0},{9,1},... | collective-permute-start | bytes 1572872 | tf_op jit(solution)/shard_map/ppermute | solution.py:26
  28.8 7.7 %collective-permute-done.1.refs_6_ = bf16[2048,128]{1,0:T(8,128)(2,1)S(1)} collective-permute-done((bf16[2048,128]{1,0:T(8,128)(2,1)S(1)}, bf16[2048,128]{1,0:T(8,128)(2,1)S(1)}, u32[]{:S(2)}, u32[]{:S(2)}) %collective-permute-start.1) | collective-permute-done | bytes 524320 | tf_op jit(solution)/shard_map/ppermute | solution.py:26
  36.5 2.8 %collective-permute-start.4 = (bf16[1024,128]{1,0:T(8,128)(2,1)S(1)}, bf16[1024,128]{1,0:T(8,128)(2,1)S(1)}, u32[]{:S(2)}, u32[]{:S(2)}) collective-permute-start(bf16[1024,128]{1,0:T(8,128)(2,1)S(1)} %constant_dynamic-slice_fusion), channel_id=1, source_target_pairs={{0,24},{1,25},{2,26},{3,27},{4,28},{5,29},{6,30},{7,31},{8,16},{9,... | collective-permute-start | bytes 786440 | tf_op jit(solution)/shard_map/ppermute | solution.py:26
  39.4 1.9 %collective-permute-start.2 = (bf16[2048,128]{1,0:T(8,128)(2,1)S(1)}, bf16[2048,128]{1,0:T(8,128)(2,1)S(1)}, u32[]{:S(2)}, u32[]{:S(2)}) collective-permute-start(bf16[2048,128]{1,0:T(8,128)(2,1)S(1)} %collective-permute-done.1.refs_6_), channel_id=1, source_target_pairs={{0,4},{1,5},{2,6},{3,7},{4,0},{5,1},{6,2},{7,3},{8,12},{9,13},{10,... | collective-permute-start | bytes 1572872 | tf_op jit(solution)/shard_map/ppermute | solution.py:26
  41.4 2.8 %collective-permute-done.4.refs_6_ = bf16[1024,128]{1,0:T(8,128)(2,1)S(1)} collective-permute-done((bf16[1024,128]{1,0:T(8,128)(2,1)S(1)}, bf16[1024,128]{1,0:T(8,128)(2,1)S(1)}, u32[]{:S(2)}, u32[]{:S(2)}) %collective-permute-start.4) | collective-permute-done | bytes 262176 | tf_op jit(solution)/shard_map/ppermute | solution.py:26
  44.2 1.9 %collective-permute-start.6 = (bf16[1024,128]{1,0:T(8,128)(2,1)S(1)}, bf16[1024,128]{1,0:T(8,128)(2,1)S(1)}, u32[]{:S(2)}, u32[]{:S(2)}) collective-permute-start(bf16[1024,128]{1,0:T(8,128)(2,1)S(1)} %collective-permute-done.4.refs_6_), channel_id=1, source_target_pairs={{0,4},{1,5},{2,6},{3,7},{4,0},{5,1},{6,2},{7,3},{8,12},{9,13},{10,... | collective-permute-start | bytes 786440 | tf_op jit(solution)/shard_map/ppermute | solution.py:26
  46.1 5.2 %collective-permute-done.8.refs_4_ = bf16[1024,128]{1,0:T(8,128)(2,1)S(1)} collective-permute-done((bf16[1024,128]{1,0:T(8,128)(2,1)S(1)}, bf16[1024,128]{1,0:T(8,128)(2,1)S(1)}, u32[]{:S(2)}, u32[]{:S(2)}) %collective-permute-start.8) | collective-permute-done | bytes 262176 | tf_op jit(solution)/shard_map/ppermute | solution.py:26
  51.4 2.8 %collective-permute-done.6.refs_8_ = bf16[1024,128]{1,0:T(8,128)(2,1)S(1)} collective-permute-done((bf16[1024,128]{1,0:T(8,128)(2,1)S(1)}, bf16[1024,128]{1,0:T(8,128)(2,1)S(1)}, u32[]{:S(2)}, u32[]{:S(2)}) %collective-permute-start.6) | collective-permute-done | bytes 262176 | tf_op jit(solution)/shard_map/ppermute | solution.py:26
  54.2 0.5 collective-permute-start.7
  54.7 0.3 collective-permute-start.3
  54.9 5.8 %ladder_0.1.refs_8_ = f32[4,64,32]{2,1,0:T(8,128)S(1)} custom-call(s32[64]{0:T(128)S(1)} %copy-done.2, bf16[64,8,128,128]{3,2,1,0:T(8,128)(2,1)} %refs_1_.5, bf16[8,128,1024]{2,1,0:T(8,128)(2,1)S(1)} %collective-permute-done.refs_2_, bf16[2048,128]{1,0:T(8,128)(2,1)S(1)} %get-tuple-element.7.refs_3_), custom_call_target="tpu_custom_call" | custom-call | flops 2147483648 | bytes 1048576 | tf_op jit(solution)/shard_map/ladder_0/pallas_call | solution.py:213
  60.8 11.0 %ladder_1_2_6.1.refs_10_ = f32[4,64,128]{2,1,0:T(8,128)S(1)} custom-call(s32[64]{0:T(128)S(1)} %copy-done.2, bf16[64,8,128,128]{3,2,1,0:T(8,128)(2,1)} %refs_1_.5, bf16[8,128,1024]{2,1,0:T(8,128)(2,1)S(1)} %collective-permute-done.refs_2_, bf16[2048,128]{1,0:T(8,128)(2,1)S(1)} %get-tuple-element.7.refs_3_, ...), custom_call_target="tpu_custom_call" | custom-call | flops 6442450944 | bytes 3145728 | tf_op jit(solution)/shard_map/ladder_1_2_6/pallas_call | solution.py:213
  71.8 13.5 %ladder_3_7_4_5.1.own_ref = f32[4,64,256]{2,1,0:T(8,128)S(1)} custom-call(s32[64]{0:T(128)S(1)} %copy-done.2, bf16[64,8,128,128]{3,2,1,0:T(8,128)(2,1)} %refs_1_.5, bf16[8,128,1024]{2,1,0:T(8,128)(2,1)S(1)} %collective-permute-done.refs_2_, bf16[2048,128]{1,0:T(8,128)(2,1)S(1)} %get-tuple-element.7.refs_3_, ...), custom_call_target="tpu_custom_call" | custom-call | flops 8589934592 | bytes 4194304 | tf_op jit(solution)/shard_map/ladder_3_7_4_5/pallas_call | solution.py:213
  85.3 0.6 collective-permute-start.11
  85.9 2.1 %collective-permute-start.12 = (f32[64,256]{1,0:T(8,128)S(1)}, f32[64,256]{1,0:T(8,128)S(1)}, u32[]{:S(2)}, u32[]{:S(2)}) collective-permute-start(f32[64,256]{1,0:T(8,128)S(1)} %get-tuple-element.10), channel_id=1, source_target_pairs={{0,2},{1,3},{2,0},{3,1},{4,6},{5,7},{6,4},{7,5},{8,10},{9,11},{10,... | collective-permute-start | bytes 196616 | tf_op jit(solution)/shard_map/ppermute | solution.py:26
  88.0 2.1 %collective-permute-start.13 = (f32[64,256]{1,0:T(8,128)S(1)}, f32[64,256]{1,0:T(8,128)S(1)}, u32[]{:S(2)}, u32[]{:S(2)}) collective-permute-start(f32[64,256]{1,0:T(8,128)S(1)} %get-tuple-element.9), channel_id=1, source_target_pairs={{0,3},{1,2},{2,1},{3,0},{4,7},{5,6},{6,5},{7,4},{8,11},{9,10},{10,... | collective-permute-start | bytes 196616 | tf_op jit(solution)/shard_map/ppermute | solution.py:26
  90.0 0.2 collective-permute-done.11.r1_ref
  90.3 1.4 %collective-permute-done.12.r2_ref = f32[64,256]{1,0:T(8,128)S(1)} collective-permute-done((f32[64,256]{1,0:T(8,128)S(1)}, f32[64,256]{1,0:T(8,128)S(1)}, u32[]{:S(2)}, u32[]{:S(2)}) %collective-permute-start.12) | collective-permute-done | bytes 65568 | tf_op jit(solution)/shard_map/ppermute | solution.py:26
  91.7 1.8 %collective-permute-done.13.r3_ref = f32[64,256]{1,0:T(8,128)S(1)} collective-permute-done((f32[64,256]{1,0:T(8,128)S(1)}, f32[64,256]{1,0:T(8,128)S(1)}, u32[]{:S(2)}, u32[]{:S(2)}) %collective-permute-start.13) | collective-permute-done | bytes 65568 | tf_op jit(solution)/shard_map/ppermute | solution.py:26
  93.5 1.1 %finish.1 = f32[8,32,64]{2,1,0:T(8,128)} custom-call(s32[1,64]{1,0:T(1,128)S(1)} %bitcast.9, f32[4,64,256]{2,1,0:T(8,128)S(1)} %ladder_3_7_4_5.1.own_ref, f32[64,256]{1,0:T(8,128)S(1)} %collective-permute-done.11.r1_ref, f32[64,256]{1,0:T(8,128)S(1)} %collective-permute-done.12.r2_ref, f32[64,256]{1,0:T(8,128)S(1)} %collective-permute-done.13.r3_ref), custom_call_target="tpu_custom_call" | custom-call | tf_op jit(solution)/shard_map/finish/pallas_call | solution.py:257
  (21 shorter events, 0.4 us)
Async XLA Ops:
  0.0 5.8 %copy-start = (bf16[64,8,128,128]{3,2,1,0:T(8,128)(2,1)S(1)}, bf16[64,8,128,128]{3,2,1,0:T(8,128)(2,1)}, u32[]{:S(2)}) copy-start(bf16[64,8,128,128]{3,2,1,0:T(8,128)(2,1)} %refs_1_.5) | copy-start | bytes 50331652
  5.8 0.7 copy-start.1
  6.4 6.2 %copy-start.3 = (bf16[256,8,128]{2,1,0:T(8,128)(2,1)S(1)}, bf16[256,8,128]{2,1,0:T(8,128)(2,1)}, u32[]{:S(2)}) copy-start(bf16[256,8,128]{2,1,0:T(8,128)(2,1)} %param.3) | copy-start | bytes 1572868
  12.5 42.4 %copy-start.2 = (s32[64]{0:T(128)S(1)}, s32[64]{0:T(128)}, u32[]{:S(2)}) copy-start(s32[64]{0:T(128)} %refs_0_.5) | copy-start | bytes 772
  12.5 42.2 %collective-permute-start = (bf16[8,128,1024]{2,1,0:T(8,128)(2,1)}, bf16[8,128,1024]{2,1,0:T(8,128)(2,1)S(1)}, u32[]{:S(2)}, u32[]{:S(2)}) collective-permute-start(bf16[8,128,1024]{2,1,0:T(8,128)(2,1)} %pack_tiles.1), channel_id=1, source_target_pairs={{0,32},{1,33},{2,34},{3,35},{4,36},{5,37},{6,38},{7,39},{8,40},{9,... | collective-permute-start | bytes 6291464 | tf_op jit(solution)/shard_map/ppermute | solution.py:26
  27.2 9.3 %collective-permute-start.1 = (bf16[2048,128]{1,0:T(8,128)(2,1)S(1)}, bf16[2048,128]{1,0:T(8,128)(2,1)S(1)}, u32[]{:S(2)}, u32[]{:S(2)}) collective-permute-start(bf16[2048,128]{1,0:T(8,128)(2,1)S(1)} %get-tuple-element.7.refs_3_), channel_id=1, source_target_pairs={{0,8},{1,9},{2,10},{3,11},{4,12},{5,13},{6,14},{7,15},{8,0},{9,1},... | collective-permute-start | bytes 1572872 | tf_op jit(solution)/shard_map/ppermute | solution.py:26
  36.5 7.7 %collective-permute-start.4 = (bf16[1024,128]{1,0:T(8,128)(2,1)S(1)}, bf16[1024,128]{1,0:T(8,128)(2,1)S(1)}, u32[]{:S(2)}, u32[]{:S(2)}) collective-permute-start(bf16[1024,128]{1,0:T(8,128)(2,1)S(1)} %constant_dynamic-slice_fusion), channel_id=1, source_target_pairs={{0,24},{1,25},{2,26},{3,27},{4,28},{5,29},{6,30},{7,31},{8,16},{9,... | collective-permute-start | bytes 786440 | tf_op jit(solution)/shard_map/ppermute | solution.py:26
  39.4 14.8 %collective-permute-start.2 = (bf16[2048,128]{1,0:T(8,128)(2,1)S(1)}, bf16[2048,128]{1,0:T(8,128)(2,1)S(1)}, u32[]{:S(2)}, u32[]{:S(2)}) collective-permute-start(bf16[2048,128]{1,0:T(8,128)(2,1)S(1)} %collective-permute-done.1.refs_6_), channel_id=1, source_target_pairs={{0,4},{1,5},{2,6},{3,7},{4,0},{5,1},{6,2},{7,3},{8,12},{9,13},{10,... | collective-permute-start | bytes 1572872 | tf_op jit(solution)/shard_map/ppermute | solution.py:26
  41.3 10.1 %collective-permute-start.8 = (bf16[1024,128]{1,0:T(8,128)(2,1)S(1)}, bf16[1024,128]{1,0:T(8,128)(2,1)S(1)}, u32[]{:S(2)}, u32[]{:S(2)}) collective-permute-start(bf16[1024,128]{1,0:T(8,128)(2,1)S(1)} %get-tuple-element.8), channel_id=1, source_target_pairs={{0,4},{1,5},{2,6},{3,7},{4,0},{5,1},{6,2},{7,3},{8,12},{9,13},{10,... | collective-permute-start | bytes 786440 | tf_op jit(solution)/shard_map/ppermute | solution.py:26
  41.4 19.4 %collective-permute-start.10 = (bf16[2048,128]{1,0:T(8,128)(2,1)S(1)}, bf16[2048,128]{1,0:T(8,128)(2,1)S(1)}, u32[]{:S(2)}, u32[]{:S(2)}) collective-permute-start(bf16[2048,128]{1,0:T(8,128)(2,1)S(1)} %collective-permute-done.1.refs_6_), channel_id=1, source_target_pairs={{0,32},{1,33},{2,34},{3,35},{4,36},{5,37},{6,38},{7,39},{8,40},{9,... | collective-permute-start | bytes 1572872 | tf_op jit(solution)/shard_map/ppermute | solution.py:26
  44.2 10.0 %collective-permute-start.6 = (bf16[1024,128]{1,0:T(8,128)(2,1)S(1)}, bf16[1024,128]{1,0:T(8,128)(2,1)S(1)}, u32[]{:S(2)}, u32[]{:S(2)}) collective-permute-start(bf16[1024,128]{1,0:T(8,128)(2,1)S(1)} %collective-permute-done.4.refs_6_), channel_id=1, source_target_pairs={{0,4},{1,5},{2,6},{3,7},{4,0},{5,1},{6,2},{7,3},{8,12},{9,13},{10,... | collective-permute-start | bytes 786440 | tf_op jit(solution)/shard_map/ppermute | solution.py:26
  51.4 9.4 %collective-permute-start.9 = (bf16[1024,128]{1,0:T(8,128)(2,1)S(1)}, bf16[1024,128]{1,0:T(8,128)(2,1)S(1)}, u32[]{:S(2)}, u32[]{:S(2)}) collective-permute-start(bf16[1024,128]{1,0:T(8,128)(2,1)S(1)} %collective-permute-done.8.refs_4_), channel_id=1, source_target_pairs={{0,32},{1,33},{2,34},{3,35},{4,36},{5,37},{6,38},{7,39},{8,40},{9,... | collective-permute-start | bytes 786440 | tf_op jit(solution)/shard_map/ppermute | solution.py:26
  54.2 17.6 %collective-permute-start.5 = (bf16[1024,128]{1,0:T(8,128)(2,1)S(1)}, bf16[1024,128]{1,0:T(8,128)(2,1)S(1)}, u32[]{:S(2)}, u32[]{:S(2)}) collective-permute-start(bf16[1024,128]{1,0:T(8,128)(2,1)S(1)} %collective-permute-done.4.refs_6_), channel_id=1, source_target_pairs={{0,32},{1,33},{2,34},{3,35},{4,36},{5,37},{6,38},{7,39},{8,40},{9,... | collective-permute-start | bytes 786440 | tf_op jit(solution)/shard_map/ppermute | solution.py:26
  54.2 17.6 %collective-permute-start.7 = (bf16[1024,128]{1,0:T(8,128)(2,1)S(1)}, bf16[1024,128]{1,0:T(8,128)(2,1)S(1)}, u32[]{:S(2)}, u32[]{:S(2)}) collective-permute-start(bf16[1024,128]{1,0:T(8,128)(2,1)S(1)} %collective-permute-done.6.refs_8_), channel_id=1, source_target_pairs={{0,32},{1,33},{2,34},{3,35},{4,36},{5,37},{6,38},{7,39},{8,40},{9,... | collective-permute-start | bytes 786440 | tf_op jit(solution)/shard_map/ppermute | solution.py:26
  54.7 17.1 %collective-permute-start.3 = (bf16[2048,128]{1,0:T(8,128)(2,1)S(1)}, bf16[2048,128]{1,0:T(8,128)(2,1)S(1)}, u32[]{:S(2)}, u32[]{:S(2)}) collective-permute-start(bf16[2048,128]{1,0:T(8,128)(2,1)S(1)} %collective-permute-done.2.refs_4_), channel_id=1, source_target_pairs={{0,32},{1,33},{2,34},{3,35},{4,36},{5,37},{6,38},{7,39},{8,40},{9,... | collective-permute-start | bytes 1572872 | tf_op jit(solution)/shard_map/ppermute | solution.py:26
  85.3 5.0 %collective-permute-start.11 = (f32[64,256]{1,0:T(8,128)S(1)}, f32[64,256]{1,0:T(8,128)S(1)}, u32[]{:S(2)}, u32[]{:S(2)}) collective-permute-start(f32[64,256]{1,0:T(8,128)S(1)} %get-tuple-element.11), channel_id=1, source_target_pairs={{0,1},{1,0},{2,3},{3,2},{4,5},{5,4},{6,7},{7,6},{8,9},{9,8},{10,11... | collective-permute-start | bytes 196616 | tf_op jit(solution)/shard_map/ppermute | solution.py:26
  85.9 5.8 %collective-permute-start.12 = (f32[64,256]{1,0:T(8,128)S(1)}, f32[64,256]{1,0:T(8,128)S(1)}, u32[]{:S(2)}, u32[]{:S(2)}) collective-permute-start(f32[64,256]{1,0:T(8,128)S(1)} %get-tuple-element.10), channel_id=1, source_target_pairs={{0,2},{1,3},{2,0},{3,1},{4,6},{5,7},{6,4},{7,5},{8,10},{9,11},{10,... | collective-permute-start | bytes 196616 | tf_op jit(solution)/shard_map/ppermute | solution.py:26
  88.0 5.5 %collective-permute-start.13 = (f32[64,256]{1,0:T(8,128)S(1)}, f32[64,256]{1,0:T(8,128)S(1)}, u32[]{:S(2)}, u32[]{:S(2)}) collective-permute-start(f32[64,256]{1,0:T(8,128)S(1)} %get-tuple-element.9), channel_id=1, source_target_pairs={{0,3},{1,2},{2,1},{3,0},{4,7},{5,6},{6,5},{7,4},{8,11},{9,10},{10,... | collective-permute-start | bytes 196616 | tf_op jit(solution)/shard_map/ppermute | solution.py:26

commit v3 on v0

v3 whole, which is shorter than its diff:
```python
import functools

import jax
import jax.numpy as jnp
from jax import lax
from jax.experimental import pallas as pl
from jax.experimental.pallas import tpu as pltpu
from jax.sharding import PartitionSpec as P

IRREPS = 8
CLS = 8
ROWS = IRREPS * CLS
NT = (((1,), (1,)), ((), ()))
BF16 = jnp.bfloat16
F32 = jnp.float32
MIB = 2**20


def permute(value, move):
    pairs = []
    for occ in range(4):
        for vir in range(32):
            to_occ, to_vir = move(occ, vir)
            pairs.append((occ * 32 + vir, to_occ * 32 + to_vir))
    return lax.ppermute(value, ("occ", "vir"), pairs)


def over_y(value, k):
    return permute(value, lambda occ, vir: (occ, vir ^ k))


def over_x(value, even, odd):
    return permute(value, lambda occ, vir: (occ, vir ^ (8 * (odd if occ & 1 else even))))


def over_z(value):
    return permute(value, lambda occ, vir: (occ ^ (2 if occ & 1 else 0), vir ^ 4))


def to_sibling(value):
    return permute(value, lambda occ, vir: (occ ^ 1, vir))


def spec(space):
    return pl.BlockSpec(memory_space=space)


def params(mib):
    return pltpu.CompilerParams(vmem_limit_bytes=mib * MIB)


def place():
    vir, core = lax.axis_index("vir"), lax.axis_index("occ") & 1
    return lax.shift_right_logical(vir, 2), vir & 3, core


def pack_kernel(mirror_ref, amp_ref, own_ref, out_ref, sems, own_sems):
    h = place()[0]
    for g in range(IRREPS):
        for j in range(CLS):
            row = g * CLS + j
            target = out_ref.at[g, mirror_ref[row] - g * CLS]
            pltpu.make_async_copy(amp_ref.at[row, h ^ g], target, sems.at[g]).start()
    own_copies = []
    for g in range(IRREPS):
        source = amp_ref.at[pl.ds(g * CLS, CLS), h]
        own_copies.append(pltpu.make_async_copy(source, own_ref.at[g], own_sems.at[g]))
        own_copies[-1].start()
    for g in range(IRREPS):
        pltpu.make_async_copy(out_ref.at[g], out_ref.at[g], sems.at[g]).wait()
    for copy in own_copies:
        copy.wait()


def pack_tiles(mirror, amplitudes):
    shape = (IRREPS, CLS, 128, 128)
    return pl.pallas_call(
        pack_kernel,
        out_shape=(jax.ShapeDtypeStruct(shape, BF16), jax.ShapeDtypeStruct(shape, BF16)),
        in_specs=[spec(pltpu.SMEM), spec(pltpu.HBM)],
        out_specs=(spec(pltpu.VMEM), spec(pltpu.VMEM)),
        scratch_shapes=[
            pltpu.SemaphoreType.DMA((IRREPS,)),
            pltpu.SemaphoreType.DMA((IRREPS,)),
        ],
        compiler_params=params(46),
        name="pack_tiles",
    )(mirror, amplitudes)


def rows_kernel(r0_ref, r1_ref, r2_ref, r3_ref, _, out_ref, all_ref):
    y = place()[1]
    for k, ref in enumerate((r0_ref, r1_ref, r2_ref, r3_ref)):
        all_ref[k ^ y] = ref[...]

    def step(i, _):
        start = pl.multiple_of(i * 16, 16)
        parts = [all_ref[q, pl.ds(start, 16), :].astype(F32) for q in range(4)]
        both = [p[0:8] for p in parts] + [p[8:16] for p in parts]
        out_ref[pl.ds(pl.multiple_of(i * 64, 64), 64), :] = jnp.concatenate(both, axis=0).astype(BF16)
        return 0

    lax.fori_loop(0, 32, step, 0, unroll=8)


def order_rows(quarters, token):
    return pl.pallas_call(
        rows_kernel,
        out_shape=jax.ShapeDtypeStruct((2048, 128), BF16),
        in_specs=[spec(pltpu.VMEM)] * 4 + [spec(pl.ANY)],
        out_specs=spec(pltpu.VMEM),
        scratch_shapes=[pltpu.VMEM((4, 512, 128), BF16)],
        compiler_params=params(6),
        name="order_rows",
    )(*quarters, token)


def relay(values, tokens):
    n = len(values)
    outs = pl.pallas_call(
        lambda *refs: None,
        out_shape=tuple(jax.ShapeDtypeStruct(v.shape, v.dtype) for v in values),
        in_specs=[spec(pl.ANY)] * (n + len(tokens)),
        out_specs=tuple(spec(pl.ANY) for _ in values),
        input_output_aliases={i: i for i in range(n)},
        compiler_params=params(1),
        name="relay",
    )(*values, *tokens)
    return outs


def half_kernel(value_ref, _, out_ref):
    core = place()[2]
    out_ref[...] = value_ref[pl.ds(pl.multiple_of(core * 1024, 1024), 1024), :]


def own_half(value, token):
    return pl.pallas_call(
        half_kernel,
        out_shape=jax.ShapeDtypeStruct((1024, 128), BF16),
        in_specs=[spec(pltpu.VMEM), spec(pl.ANY)],
        out_specs=spec(pltpu.VMEM),
        compiler_params=params(2),
        name="own_half",
    )(value, token)


def stage1_kernel(groups, tokens, own_ref, t_ref, tp_ref, *refs):
    places = [(ref, i, g) for ref, group in zip(refs[tokens:], groups) for i, g in enumerate(group)]
    for x_ref, i, g in places:
        for pair in range(4):
            j0, j1 = 2 * pair, 2 * pair + 1
            upper = jnp.concatenate([t_ref[g, j0], t_ref[g, j1]], axis=1)
            lower = jnp.concatenate([tp_ref[g, j0].T, tp_ref[g, j1].T], axis=1)
            weights = jnp.concatenate([upper, lower], axis=0)
            for part in range(4):
                own = own_ref[part * 512 : (part + 1) * 512, :]
                lhs = jnp.concatenate([own, own], axis=1)
                x = jnp.dot(lhs, weights, preferred_element_type=F32).astype(BF16)
                for k in range(2):
                    j = 2 * pair + k
                    for l in range(16):
                        lane = (part * 16 + l) * 128
                        x_ref[i, j * 32 : (j + 1) * 32, lane : lane + 128] = x[
                            l * 32 : (l + 1) * 32, k * 128 : (k + 1) * 128
                        ]


def stage1(groups, own, tiles, received, tokens=()):
    n = sum(len(group) for group in groups)
    return pl.pallas_call(
        functools.partial(stage1_kernel, groups, len(tokens)),
        out_shape=tuple(jax.ShapeDtypeStruct((len(group), 256, 8192), BF16) for group in groups),
        in_specs=[spec(pltpu.VMEM)] * 3 + [spec(pl.ANY)] * len(tokens),
        out_specs=tuple(spec(pltpu.VMEM) for _ in groups),
        compiler_params=params(8),
        cost_estimate=pl.CostEstimate(flops=n * 2**30, transcendentals=0, bytes_accessed=n * 2**18),
        name="stage1_" + "_".join(str(g) for group in groups for g in group),
    )(own, tiles, received, *tokens)


def stage2_kernel(blocks, n_x, n_b, carried, tokens, n, *refs):
    x_refs, refs = refs[:n_x], refs[n_x:]
    b_refs, refs = refs[:n_b], refs[n_b:]
    carry, refs = refs[:carried], refs[carried:]
    out_ref, r_s = refs[tokens:]
    _, y, core = place()

    def contract(x_ref, index, lane0, b_ref, rows):
        total = None
        for step in range(rows // 128):
            b = b_ref[step * 128 : (step + 1) * 128, :]
            bt = jnp.concatenate([b[l * 32 : (l + 1) * 32] for l in range(4)], axis=1)
            lane = lane0 + step * 512
            if not isinstance(lane, int):
                lane = pl.multiple_of(lane, 512)
            x = x_ref[index, :, pl.ds(lane, 512)]
            term = lax.dot_general(x, bt, NT, preferred_element_type=F32)
            total = term if total is None else total + term
        return total

    at = 0
    for kind, *slots in blocks:
        if kind == "all":
            ((k, index, to),) = slots
            r_s[to] = contract(x_refs[k], index, 0, b_refs[at], 2048)
            at += 1
        elif kind == "swap":
            (k, first, to_first), (_, second, to_second) = slots
            odd = core == 1
            r_s[jnp.where(odd, to_second, to_first)] = contract(
                x_refs[k], jnp.where(odd, second, first), 0, b_refs[at], 2048
            )
            r_s[jnp.where(odd, to_first, to_second)] = contract(
                x_refs[k], jnp.where(odd, first, second), 0, b_refs[at + 1], 2048
            )
            at += 2
        else:
            ((k, index, to),) = slots
            mine = contract(x_refs[k], index, core * 4096, b_refs[at], 1024)
            r_s[to] = mine + contract(x_refs[k], index, (1 - core) * 4096, b_refs[at + 1], 1024)
            at += 2
    for q in range(4):
        columns = [ref[q ^ y] for ref in carry]
        for i in range(n):
            r = r_s[i]
            columns.append(
                jnp.concatenate([r[j * 32 + q * 8 : j * 32 + q * 8 + 8] for j in range(CLS)], axis=0)
            )
        out_ref[q ^ y] = jnp.concatenate(columns, axis=1) if len(columns) > 1 else columns[0]


def stage2(name, n, blocks, xs, bs, carry=(), tokens=()):
    lanes = 32 * n + sum(c.shape[2] for c in carry)
    kernel = functools.partial(stage2_kernel, blocks, len(xs), len(bs), len(carry), len(tokens), n)
    return pl.pallas_call(
        kernel,
        out_shape=jax.ShapeDtypeStruct((4, 64, lanes), F32),
        in_specs=[spec(pltpu.VMEM)] * (len(xs) + len(bs) + len(carry)) + [spec(pl.ANY)] * len(tokens),
        out_specs=spec(pltpu.VMEM),
        scratch_shapes=[pltpu.VMEM((n, 256, 32), F32)],
        compiler_params=params(8),
        cost_estimate=pl.CostEstimate(flops=n * 2**30, transcendentals=0, bytes_accessed=n * 2**18),
        name="stage2_" + name,
    )(*xs, *bs, *carry, *tokens)


def finish_kernel(order, own_ref, r1_ref, r2_ref, r3_ref, out_ref, sum_s, pos_s):
    total = own_ref[0] + r1_ref[...] + r2_ref[...] + r3_ref[...]
    sum_s[0] = total[:, 0:128]
    sum_s[1] = total[:, 128:256]
    for a8 in range(8):
        for k in range(2):
            strip = sum_s[k, pl.ds(a8, CLS, stride=8), :]
            for c in range(4):
                g = order[k * 4 + c]
                pos_s[g * CLS : (g + 1) * CLS, a8 * 32 : (a8 + 1) * 32] = strip[:, c * 32 : (c + 1) * 32]
    out_ref[...] = pos_s[...].T.reshape(8, 32, ROWS)


def finish(order, parts):
    out = pl.pallas_call(
        functools.partial(finish_kernel, order),
        out_shape=jax.ShapeDtypeStruct((8, 32, ROWS), F32),
        in_specs=[spec(pltpu.VMEM)] * 4,
        out_specs=spec(pltpu.VMEM),
        scratch_shapes=[pltpu.VMEM((2, 64, 128), F32), pltpu.VMEM((ROWS, 256), F32)],
        compiler_params=params(6),
        name="finish",
    )(*parts)
    return jnp.transpose(out, (2, 0, 1))


def shards(cholesky, amplitudes, mirror):
    y = lax.axis_index("vir") & 3

    by_chunk = cholesky.reshape(4, 512, 128)
    quarters = [lax.dynamic_index_in_dim(by_chunk, y ^ k, 0, keepdims=False) for k in range(4)]
    quarters = [quarters[0]] + [over_y(quarters[k], k) for k in range(1, 4)]
    tiles, outgoing = pack_tiles(mirror, amplitudes)
    received = to_sibling(outgoing)
    own = order_rows(quarters, received)

    x1 = over_x(own, 1, 3)
    z0 = over_z(own)
    xc0, xc1, xc26, xc4 = stage1(((0,), (1,), (2, 6), (4,)), own, tiles, received)
    x1, z0 = relay((x1, z0), (xc0,))
    x1_twin = to_sibling(x1)
    x2 = over_x(own_half(x1, xc0), 3, 1)
    zx1 = over_z(x1)
    near = stage2(
        "near", 4, (("all", (0, 0, 0)), ("all", (1, 0, 1)), ("swap", (2, 0, 2), (2, 1, 3))),
        (xc0, xc1, xc26), (own, z0, x1, x1_twin),
    )
    x2, zx1 = relay((x2, zx1), (near,))
    x2_twin, zx1_twin = to_sibling(x2), to_sibling(zx1)
    zx2 = over_z(x2)
    xc37, xc5 = stage1(((3, 7), (5,)), own, tiles, received, (x2,))
    (zx2,) = relay((zx2,), (xc5,))
    zx2_twin = to_sibling(zx2)
    far = stage2(
        "far", 3, (("halves", (0, 0, 0)), ("swap", (1, 0, 1), (1, 1, 2))),
        (xc4, xc37), (x2, x2_twin, zx1, zx1_twin), (near,), (zx2,),
    )
    last = stage2("last", 1, (("halves", (0, 0, 0)),), (xc5,), (zx2, zx2_twin), (far,))
    parts = [last] + [over_y(last[k], k) for k in range(1, 4)]
    return finish((0, 1, 2, 6, 4, 3, 7, 5), parts)


def solution(mesh):
    placed = (P(None, "vir", None), P("occ", None, None, None), P("occ"))
    return jax.shard_map(
        shards, mesh=mesh, in_specs=placed, out_specs=P("occ", "vir", None), check_vma=False
    )
```

time: 460 us -> 61.2 us (0.13); the launches traced: 453 us -> 61 us
  waiting for transfers between devices: 204 us -> 17 us
  local copies, waits for them, and re-layouts: 116 us -> 2.01 us
  matrix products: 113 us -> 0 us
  Pallas kernels: 0 us -> 24.8 us
  between operations: 14.4 us -> 0.12 us
  starting transfers between devices: 5.43 us -> 17.2 us
    all_gather x1 -> x0, waiting for transfers between devices: 194 us -> none  [shards(): gathered = lax.all_gather(cholesky, 'vir', axis=1, tiled=True)]
    dot_general x16 -> x0, matrix products: 113 us -> none  [the longest x8 57.9 us: shards(): jnp.einsum('lac,lbd->abcd', cholesky, b_block, preferred_element_type=jnp...]
    convert_element_type x8 -> x0, local copies, waits for them, and re-layouts: 102 us -> none  [shards(): v_slab = jnp.einsum('lac,lbd->abcd', cholesky, b_block, preferred_element...]
    pallas_call x0 -> x12, Pallas kernels: none -> 24.8 us  [the longest x2 9.95 us: stage1(): pl.pallas_call(functools.partial(stage1_kernel, groups, len(tokens)), out...]
    ppermute x1 -> x16, starting transfers between devices: 0.04 us -> 17.2 us  [permute(): return lax.ppermute(value, ('occ', 'vir'), pairs)]
    ppermute x1 -> x16, waiting for transfers between devices: 1.51 us -> 17 us  [permute(): return lax.ppermute(value, ('occ', 'vir'), pairs)]
    all_to_all x1 -> x0, waiting for transfers between devices: 8.47 us -> none  [shards(): lax.all_to_all(outgoing, 'vir', split_axis=0, concat_axis=0, tiled=True)]
    all_to_all x1 -> x0, starting transfers between devices: 5.38 us -> none  [shards(): lax.all_to_all(outgoing, 'vir', split_axis=0, concat_axis=0, tiled=True)]
  transfers between devices with their start and end apart: 3 -> 16, of which waited for: 3 -> 8; matrix products, arithmetic and copies ran while one was open for 1% -> 0% of each run, Pallas kernels for 0% -> 30%
where the time goes in v3:
time: 61.2 us; the launch traced here: 61 us
  Pallas kernels  24.8 us (41%)
  starting transfers between devices  17.2 us (28%)
  waiting for transfers between devices  17 us (28%)
  local copies, waits for them, and re-layouts  2.01 us (3%)
    ppermute x16, starting transfers between devices, permute(): return lax.ppermute(value, ('occ', 'vir'), pairs)  17.2 us
    ppermute x16, waiting for transfers between devices, permute(): return lax.ppermute(value, ('occ', 'vir'), pairs)  17 us
    pallas_call x2, Pallas kernels, stage1(): pl.pallas_call(functools.partial(stage1_kernel, groups, len(tokens)), out...  9.95 us
    pallas_call x3, Pallas kernels, stage2(): pl.pallas_call(kernel, out_shape=jax.ShapeDtypeStruct((4, 64, lanes), F32...  9.45 us
    pallas_call x1, Pallas kernels, pack_tiles(): pl.pallas_call(pack_kernel, out_shape=(jax.ShapeDtypeStruct(shape, BF16),...  4.29 us
    unnamed x8, local copies, waits for them, and re-layouts  1.95 us
  transfers between devices with their start and end apart: 16, of which 8 were waited for; matrix products, arithmetic and copies ran while one was open for 0% of the time, Pallas kernels for 30%

profile of v3, /device:TPU:0, one launch (start us, length us, event | category | flops | bytes accessed | tf_op | source)
XLA Modules:
  0.0 61.0 jit_solution(4144058813290931857)
XLA Ops:
  0.0 0.7 %copy-done = s32[64]{0:T(128)S(1)} copy-done((s32[64]{0:T(128)S(1)}, s32[64]{0:T(128)}, u32[]{:S(2)}) %copy-start) | copy-done | bytes 280
  0.7 4.3 %pack_tiles.1 = (bf16[8,8,128,128]{3,2,1,0:T(8,128)(2,1)S(1)}, bf16[8,8,128,128]{3,2,1,0:T(8,128)(2,1)}) custom-call(s32[64]{0:T(128)S(1)} %copy-done, bf16[64,8,128,128]{3,2,1,0:T(8,128)(2,1)} %amp_ref.1), custom_call_target="tpu_custom_call" | custom-call | tf_op jit(solution)/shard_map/pack_tiles/pallas_call | solution.py:77
  5.0 1.3 %copy-done.1 = bf16[8,8,128,128]{3,2,1,0:T(8,128)(2,1)} copy-done((bf16[8,8,128,128]{3,2,1,0:T(8,128)(2,1)}, bf16[8,8,128,128]{3,2,1,0:T(8,128)(2,1)S(1)}, u32[]{:S(2)}) %copy-start.1) | copy-done | bytes 2097176
  6.3 3.2 %collective-permute-start.2 = (bf16[512,128]{1,0:T(8,128)(2,1)S(1)}, bf16[512,128]{1,0:T(8,128)(2,1)S(1)}, u32[]{:S(2)}, u32[]{:S(2)}) collective-permute-start(bf16[512,128]{1,0:T(8,128)(2,1)S(1)} %get-tuple-element.29), channel_id=1, source_target_pairs={{0,3},{1,2},{2,1},{3,0},{4,7},{5,6},{6,5},{7,4},{8,11},{9,10},{10,... | collective-permute-start | bytes 393224 | tf_op jit(solution)/shard_map/ppermute | solution.py:25
  10.5 5.2 %collective-permute-done.2.r3_ref = bf16[512,128]{1,0:T(8,128)(2,1)S(1)} collective-permute-done((bf16[512,128]{1,0:T(8,128)(2,1)S(1)}, bf16[512,128]{1,0:T(8,128)(2,1)S(1)}, u32[]{:S(2)}, u32[]{:S(2)}) %collective-permute-start.2) | collective-permute-done | bytes 131104 | tf_op jit(solution)/shard_map/ppermute | solution.py:25
  15.7 1.6 %collective-permute-done.1.r2_ref = bf16[512,128]{1,0:T(8,128)(2,1)S(1)} collective-permute-done((bf16[512,128]{1,0:T(8,128)(2,1)S(1)}, bf16[512,128]{1,0:T(8,128)(2,1)S(1)}, u32[]{:S(2)}, u32[]{:S(2)}) %collective-permute-start.1) | collective-permute-done | bytes 131104 | tf_op jit(solution)/shard_map/ppermute | solution.py:25
  17.5 2.0 %collective-permute-start.5 = (bf16[2048,128]{1,0:T(8,128)(2,1)S(1)}, bf16[2048,128]{1,0:T(8,128)(2,1)S(1)}, u32[]{:S(2)}, u32[]{:S(2)}) collective-permute-start(bf16[2048,128]{1,0:T(8,128)(2,1)S(1)} %order_rows.1.own_ref.refs_3_), channel_id=1, source_target_pairs={{0,4},{1,5},{2,6},{3,7},{4,0},{5,1},{6,2},{7,3},{8,12},{9,13},{10,... | collective-permute-start | bytes 1572872 | tf_op jit(solution)/shard_map/ppermute | solution.py:25
  19.5 1.5 %collective-permute-start.4 = (bf16[2048,128]{1,0:T(8,128)(2,1)S(1)}, bf16[2048,128]{1,0:T(8,128)(2,1)S(1)}, u32[]{:S(2)}, u32[]{:S(2)}) collective-permute-start(bf16[2048,128]{1,0:T(8,128)(2,1)S(1)} %order_rows.1.own_ref.refs_3_), channel_id=1, source_target_pairs={{0,8},{1,9},{2,10},{3,11},{4,12},{5,13},{6,14},{7,15},{8,0},{9,1},... | collective-permute-start | bytes 1572872 | tf_op jit(solution)/shard_map/ppermute | solution.py:25
  21.0 6.2 %stage1_0_1_2_6_4.1 = (bf16[1,256,8192]{2,1,0:T(8,128)(2,1)S(1)}, bf16[1,256,8192]{2,1,0:T(8,128)(2,1)S(1)}, bf16[2,256,8192]{2,1,0:T(8,128)(2,1)S(1)}, bf16[1,256,8192]{2,1,0:T(8,128)(2,1)S(1)}) custom-call(bf16[2048,128]{1,0:T(8,128)(2,1)S(1)} %order_rows.1.own_ref.refs_3_, bf16[8,8,128,128]{3,2,1,0:T(8,128)(2,1)S(1)} %copy-done.2, ...), custom_call_target="tpu_custom_call" | custom-call | flops 5368709120 | bytes 1310720 | tf_op jit(solution)/shard_map/stage1_0_1_2_6_4/pallas_call | solution.py:171
  27.2 1.5 %collective-permute-done.4.refs_0_ = bf16[2048,128]{1,0:T(8,128)(2,1)S(1)} collective-permute-done((bf16[2048,128]{1,0:T(8,128)(2,1)S(1)}, bf16[2048,128]{1,0:T(8,128)(2,1)S(1)}, u32[]{:S(2)}, u32[]{:S(2)}) %collective-permute-start.4) | collective-permute-done | bytes 524320 | tf_op jit(solution)/shard_map/ppermute | solution.py:25
  28.7 1.3 %collective-permute-start.8 = (bf16[2048,128]{1,0:T(8,128)(2,1)S(1)}, bf16[2048,128]{1,0:T(8,128)(2,1)S(1)}, u32[]{:S(2)}, u32[]{:S(2)}) collective-permute-start(bf16[2048,128]{1,0:T(8,128)(2,1)S(1)} %get-tuple-element.20.value_ref.refs_5_), channel_id=1, source_target_pairs={{0,32},{1,33},{2,34},{3,35},{4,36},{5,37},{6,38},{7,39},{8,40},{9,... | collective-permute-start | bytes 1572872 | tf_op jit(solution)/shard_map/ppermute | solution.py:25
  30.0 2.8 %collective-permute-start.6 = (bf16[1024,128]{1,0:T(8,128)(2,1)S(1)}, bf16[1024,128]{1,0:T(8,128)(2,1)S(1)}, u32[]{:S(2)}, u32[]{:S(2)}) collective-permute-start(bf16[1024,128]{1,0:T(8,128)(2,1)S(1)} %own_half.1), channel_id=1, source_target_pairs={{0,24},{1,25},{2,26},{3,27},{4,28},{5,29},{6,30},{7,31},{8,16},{9,... | collective-permute-start | bytes 786440 | tf_op jit(solution)/shard_map/ppermute | solution.py:25
  32.9 4.6 %stage2_near.1.refs_2_.refs_6_ = f32[4,64,128]{2,1,0:T(8,128)S(1)} custom-call(bf16[1,256,8192]{2,1,0:T(8,128)(2,1)S(1)} %get-tuple-element.19.refs_2_._.refs_0_, bf16[1,256,8192]{2,1,0:T(8,128)(2,1)S(1)} %get-tuple-element.21.refs_1_, bf16[2,256,8192]{2,1,0:T(8,128)(2,1)S(1)} %get-tuple-element.22.refs_2_, bf16[2048,128]{1,0:T(8,128)(2,1)S(1)} %order_rows.1.own_ref.refs_3_, ...), custom_call_target="tpu_custom_call" | custom-call | flops 4294967296 | bytes 1048576 | tf_op jit(solution)/shard_map/stage2_near/pallas_call | solution.py:236
  37.7 1.5 %collective-permute-done.7.refs_1_ = bf16[2048,128]{1,0:T(8,128)(2,1)S(1)} collective-permute-done((bf16[2048,128]{1,0:T(8,128)(2,1)S(1)}, bf16[2048,128]{1,0:T(8,128)(2,1)S(1)}, u32[]{:S(2)}, u32[]{:S(2)}) %collective-permute-start.7) | collective-permute-done | bytes 524320 | tf_op jit(solution)/shard_map/ppermute | solution.py:25
  40.2 3.8 %stage1_3_7_5.1 = (bf16[2,256,8192]{2,1,0:T(8,128)(2,1)S(1)}, bf16[1,256,8192]{2,1,0:T(8,128)(2,1)S(1)}) custom-call(bf16[2048,128]{1,0:T(8,128)(2,1)S(1)} %order_rows.1.own_ref.refs_3_, bf16[8,8,128,128]{3,2,1,0:T(8,128)(2,1)S(1)} %copy-done.2, bf16[8,8,128,128]{3,2,1,0:T(8,128)(2,1)S(1)} %collective-permute-done.3._.tp_ref, ...), custom_call_target="tpu_custom_call" | custom-call | flops 3221225472 | bytes 786432 | tf_op jit(solution)/shard_map/stage1_3_7_5/pallas_call | solution.py:171
  44.0 2.1 %collective-permute-done.9.refs_0_ = bf16[1024,128]{1,0:T(8,128)(2,1)S(1)} collective-permute-done((bf16[1024,128]{1,0:T(8,128)(2,1)S(1)}, bf16[1024,128]{1,0:T(8,128)(2,1)S(1)}, u32[]{:S(2)}, u32[]{:S(2)}) %collective-permute-start.9) | collective-permute-done | bytes 262176 | tf_op jit(solution)/shard_map/ppermute | solution.py:25
  46.2 3.5 %stage2_far.1.refs_3_ = f32[4,64,224]{2,1,0:T(8,128)S(1)} custom-call(bf16[1,256,8192]{2,1,0:T(8,128)(2,1)S(1)} %get-tuple-element.26.refs_0_, bf16[2,256,8192]{2,1,0:T(8,128)(2,1)S(1)} %get-tuple-element.27.refs_1_, bf16[1024,128]{1,0:T(8,128)(2,1)S(1)} %get-tuple-element.24.refs_0_.refs_2_, bf16[1024,128]{1,0:T(8,128)(2,1)S(1)} %collective-permute-done.11.refs_3_, ...), custom_call_target="tpu_custom_call" | custom-call | flops 3221225472 | bytes 786432 | tf_op jit(solution)/shard_map/stage2_far/pallas_call | solution.py:236
  49.7 1.3 %stage2_last.1.own_ref = f32[4,64,256]{2,1,0:T(8,128)S(1)} custom-call(bf16[1,256,8192]{2,1,0:T(8,128)(2,1)S(1)} %get-tuple-element.25.refs_1_.refs_0_, bf16[1024,128]{1,0:T(8,128)(2,1)S(1)} %relay.5.refs_7_.refs_1_, bf16[1024,128]{1,0:T(8,128)(2,1)S(1)} %collective-permute-done.10.refs_2_, f32[4,64,224]{2,1,0:T(8,128)S(1)} %stage2_far.1.refs_3_), custom_call_target="tpu_custom_call" | custom-call | flops 1073741824 | bytes 262144 | tf_op jit(solution)/shard_map/stage2_last/pallas_call | solution.py:236
  51.1 2.8 %collective-permute-start.15 = (f32[64,256]{1,0:T(8,128)S(1)}, f32[64,256]{1,0:T(8,128)S(1)}, u32[]{:S(2)}, u32[]{:S(2)}) collective-permute-start(f32[64,256]{1,0:T(8,128)S(1)} %get-tuple-element.33), channel_id=1, source_target_pairs={{0,3},{1,2},{2,1},{3,0},{4,7},{5,6},{6,5},{7,4},{8,11},{9,10},{10,... | collective-permute-start | bytes 196616 | tf_op jit(solution)/shard_map/ppermute | solution.py:25
  53.9 0.7 %collective-permute-start.14 = (f32[64,256]{1,0:T(8,128)S(1)}, f32[64,256]{1,0:T(8,128)S(1)}, u32[]{:S(2)}, u32[]{:S(2)}) collective-permute-start(f32[64,256]{1,0:T(8,128)S(1)} %get-tuple-element.34), channel_id=1, source_target_pairs={{0,2},{1,3},{2,0},{3,1},{4,6},{5,7},{6,4},{7,5},{8,10},{9,11},{10,... | collective-permute-start | bytes 196616 | tf_op jit(solution)/shard_map/ppermute | solution.py:25
  54.5 0.7 %collective-permute-start.13 = (f32[64,256]{1,0:T(8,128)S(1)}, f32[64,256]{1,0:T(8,128)S(1)}, u32[]{:S(2)}, u32[]{:S(2)}) collective-permute-start(f32[64,256]{1,0:T(8,128)S(1)} %get-tuple-element.35), channel_id=1, source_target_pairs={{0,1},{1,0},{2,3},{3,2},{4,5},{5,4},{6,7},{7,6},{8,9},{9,8},{10,11... | collective-permute-start | bytes 196616 | tf_op jit(solution)/shard_map/ppermute | solution.py:25
  55.3 1.7 %collective-permute-done.15.r3_ref = f32[64,256]{1,0:T(8,128)S(1)} collective-permute-done((f32[64,256]{1,0:T(8,128)S(1)}, f32[64,256]{1,0:T(8,128)S(1)}, u32[]{:S(2)}, u32[]{:S(2)}) %collective-permute-start.15) | collective-permute-done | bytes 65568 | tf_op jit(solution)/shard_map/ppermute | solution.py:25
  57.0 3.1 %collective-permute-done.14.r2_ref = f32[64,256]{1,0:T(8,128)S(1)} collective-permute-done((f32[64,256]{1,0:T(8,128)S(1)}, f32[64,256]{1,0:T(8,128)S(1)}, u32[]{:S(2)}, u32[]{:S(2)}) %collective-permute-start.14) | collective-permute-done | bytes 65568 | tf_op jit(solution)/shard_map/ppermute | solution.py:25
  60.1 0.9 %finish.1 = f32[8,32,64]{2,1,0:T(8,128)} custom-call(f32[4,64,256]{2,1,0:T(8,128)S(1)} %stage2_last.1.own_ref, f32[64,256]{1,0:T(8,128)S(1)} %collective-permute-done.13.r1_ref, f32[64,256]{1,0:T(8,128)S(1)} %collective-permute-done.14.r2_ref, f32[64,256]{1,0:T(8,128)S(1)} %collective-permute-done.15.r3_ref), custom_call_target="tpu_custom_call" | custom-call | tf_op jit(solution)/shard_map/finish/pallas_call | solution.py:262
  (30 shorter events, 2.7 us)
Async XLA Ops:
  0.0 0.7 %copy-start = (s32[64]{0:T(128)S(1)}, s32[64]{0:T(128)}, u32[]{:S(2)}) copy-start(s32[64]{0:T(128)} %mirror_ref.1) | copy-start | bytes 772
  0.7 5.6 %copy-start.3 = (bf16[256,8,128]{2,1,0:T(8,128)(2,1)S(1)}, bf16[256,8,128]{2,1,0:T(8,128)(2,1)}, u32[]{:S(2)}) copy-start(bf16[256,8,128]{2,1,0:T(8,128)(2,1)} %param.3) | copy-start | bytes 1572868
  5.0 1.3 %copy-start.1 = (bf16[8,8,128,128]{3,2,1,0:T(8,128)(2,1)}, bf16[8,8,128,128]{3,2,1,0:T(8,128)(2,1)S(1)}, u32[]{:S(2)}) copy-start(bf16[8,8,128,128]{3,2,1,0:T(8,128)(2,1)S(1)} %get-tuple-element.18.t_ref) | copy-start | bytes 6291460
  6.3 11.1 %collective-permute-start.3 = (bf16[8,8,128,128]{3,2,1,0:T(8,128)(2,1)}, bf16[8,8,128,128]{3,2,1,0:T(8,128)(2,1)S(1)}, u32[]{:S(2)}, u32[]{:S(2)}) collective-permute-start(bf16[8,8,128,128]{3,2,1,0:T(8,128)(2,1)} %get-tuple-element.17), channel_id=1, source_target_pairs={{0,32},{1,33},{2,34},{3,35},{4,36},{5,37},{6,38},{7,39},{8,40},{9,... | collective-permute-start | bytes 6291464 | tf_op jit(solution)/shard_map/ppermute | solution.py:25
  6.3 14.7 %copy-start.2 = (bf16[8,8,128,128]{3,2,1,0:T(8,128)(2,1)S(1)}, bf16[8,8,128,128]{3,2,1,0:T(8,128)(2,1)}, u32[]{:S(2)}) copy-start(bf16[8,8,128,128]{3,2,1,0:T(8,128)(2,1)} %copy-done.1) | copy-start | bytes 6291460
  6.3 9.4 %collective-permute-start.2 = (bf16[512,128]{1,0:T(8,128)(2,1)S(1)}, bf16[512,128]{1,0:T(8,128)(2,1)S(1)}, u32[]{:S(2)}, u32[]{:S(2)}) collective-permute-start(bf16[512,128]{1,0:T(8,128)(2,1)S(1)} %get-tuple-element.29), channel_id=1, source_target_pairs={{0,3},{1,2},{2,1},{3,0},{4,7},{5,6},{6,5},{7,4},{8,11},{9,10},{10,... | collective-permute-start | bytes 393224 | tf_op jit(solution)/shard_map/ppermute | solution.py:25
  9.5 7.8 %collective-permute-start.1 = (bf16[512,128]{1,0:T(8,128)(2,1)S(1)}, bf16[512,128]{1,0:T(8,128)(2,1)S(1)}, u32[]{:S(2)}, u32[]{:S(2)}) collective-permute-start(bf16[512,128]{1,0:T(8,128)(2,1)S(1)} %get-tuple-element.30), channel_id=1, source_target_pairs={{0,2},{1,3},{2,0},{3,1},{4,6},{5,7},{6,4},{7,5},{8,10},{9,11},{10,... | collective-permute-start | bytes 393224 | tf_op jit(solution)/shard_map/ppermute | solution.py:25
  10.1 7.2 %collective-permute-start = (bf16[512,128]{1,0:T(8,128)(2,1)S(1)}, bf16[512,128]{1,0:T(8,128)(2,1)S(1)}, u32[]{:S(2)}, u32[]{:S(2)}) collective-permute-start(bf16[512,128]{1,0:T(8,128)(2,1)S(1)} %get-tuple-element.31), channel_id=1, source_target_pairs={{0,1},{1,0},{2,3},{3,2},{4,5},{5,4},{6,7},{7,6},{8,9},{9,8},{10,11... | collective-permute-start | bytes 393224 | tf_op jit(solution)/shard_map/ppermute | solution.py:25
  17.5 9.7 %collective-permute-start.5 = (bf16[2048,128]{1,0:T(8,128)(2,1)S(1)}, bf16[2048,128]{1,0:T(8,128)(2,1)S(1)}, u32[]{:S(2)}, u32[]{:S(2)}) collective-permute-start(bf16[2048,128]{1,0:T(8,128)(2,1)S(1)} %order_rows.1.own_ref.refs_3_), channel_id=1, source_target_pairs={{0,4},{1,5},{2,6},{3,7},{4,0},{5,1},{6,2},{7,3},{8,12},{9,13},{10,... | collective-permute-start | bytes 1572872 | tf_op jit(solution)/shard_map/ppermute | solution.py:25
  19.5 9.2 %collective-permute-start.4 = (bf16[2048,128]{1,0:T(8,128)(2,1)S(1)}, bf16[2048,128]{1,0:T(8,128)(2,1)S(1)}, u32[]{:S(2)}, u32[]{:S(2)}) collective-permute-start(bf16[2048,128]{1,0:T(8,128)(2,1)S(1)} %order_rows.1.own_ref.refs_3_), channel_id=1, source_target_pairs={{0,8},{1,9},{2,10},{3,11},{4,12},{5,13},{6,14},{7,15},{8,0},{9,1},... | collective-permute-start | bytes 1572872 | tf_op jit(solution)/shard_map/ppermute | solution.py:25
  28.7 4.2 %collective-permute-start.8 = (bf16[2048,128]{1,0:T(8,128)(2,1)S(1)}, bf16[2048,128]{1,0:T(8,128)(2,1)S(1)}, u32[]{:S(2)}, u32[]{:S(2)}) collective-permute-start(bf16[2048,128]{1,0:T(8,128)(2,1)S(1)} %get-tuple-element.20.value_ref.refs_5_), channel_id=1, source_target_pairs={{0,32},{1,33},{2,34},{3,35},{4,36},{5,37},{6,38},{7,39},{8,40},{9,... | collective-permute-start | bytes 1572872 | tf_op jit(solution)/shard_map/ppermute | solution.py:25
  30.0 9.2 %collective-permute-start.7 = (bf16[2048,128]{1,0:T(8,128)(2,1)S(1)}, bf16[2048,128]{1,0:T(8,128)(2,1)S(1)}, u32[]{:S(2)}, u32[]{:S(2)}) collective-permute-start(bf16[2048,128]{1,0:T(8,128)(2,1)S(1)} %get-tuple-element.20.value_ref.refs_5_), channel_id=1, source_target_pairs={{0,4},{1,5},{2,6},{3,7},{4,0},{5,1},{6,2},{7,3},{8,12},{9,13},{10,... | collective-permute-start | bytes 1572872 | tf_op jit(solution)/shard_map/ppermute | solution.py:25
  30.0 7.7 %collective-permute-start.6 = (bf16[1024,128]{1,0:T(8,128)(2,1)S(1)}, bf16[1024,128]{1,0:T(8,128)(2,1)S(1)}, u32[]{:S(2)}, u32[]{:S(2)}) collective-permute-start(bf16[1024,128]{1,0:T(8,128)(2,1)S(1)} %own_half.1), channel_id=1, source_target_pairs={{0,24},{1,25},{2,26},{3,27},{4,28},{5,29},{6,30},{7,31},{8,16},{9,... | collective-permute-start | bytes 786440 | tf_op jit(solution)/shard_map/ppermute | solution.py:25
  39.2 7.0 %collective-permute-start.12 = (bf16[2048,128]{1,0:T(8,128)(2,1)S(1)}, bf16[2048,128]{1,0:T(8,128)(2,1)S(1)}, u32[]{:S(2)}, u32[]{:S(2)}) collective-permute-start(bf16[2048,128]{1,0:T(8,128)(2,1)S(1)} %get-tuple-element.28.refs_4_), channel_id=1, source_target_pairs={{0,32},{1,33},{2,34},{3,35},{4,36},{5,37},{6,38},{7,39},{8,40},{9,... | collective-permute-start | bytes 1572872 | tf_op jit(solution)/shard_map/ppermute | solution.py:25
  39.2 6.9 %collective-permute-start.11 = (bf16[1024,128]{1,0:T(8,128)(2,1)S(1)}, bf16[1024,128]{1,0:T(8,128)(2,1)S(1)}, u32[]{:S(2)}, u32[]{:S(2)}) collective-permute-start(bf16[1024,128]{1,0:T(8,128)(2,1)S(1)} %get-tuple-element.24.refs_0_.refs_2_), channel_id=1, source_target_pairs={{0,32},{1,33},{2,34},{3,35},{4,36},{5,37},{6,38},{7,39},{8,40},{9,... | collective-permute-start | bytes 786440 | tf_op jit(solution)/shard_map/ppermute | solution.py:25
  39.7 6.4 %collective-permute-start.9 = (bf16[1024,128]{1,0:T(8,128)(2,1)S(1)}, bf16[1024,128]{1,0:T(8,128)(2,1)S(1)}, u32[]{:S(2)}, u32[]{:S(2)}) collective-permute-start(bf16[1024,128]{1,0:T(8,128)(2,1)S(1)} %get-tuple-element.24.refs_0_.refs_2_), channel_id=1, source_target_pairs={{0,4},{1,5},{2,6},{3,7},{4,0},{5,1},{6,2},{7,3},{8,12},{9,13},{10,... | collective-permute-start | bytes 786440 | tf_op jit(solution)/shard_map/ppermute | solution.py:25
  46.1 3.7 %collective-permute-start.10 = (bf16[1024,128]{1,0:T(8,128)(2,1)S(1)}, bf16[1024,128]{1,0:T(8,128)(2,1)S(1)}, u32[]{:S(2)}, u32[]{:S(2)}) collective-permute-start(bf16[1024,128]{1,0:T(8,128)(2,1)S(1)} %relay.5.refs_7_.refs_1_), channel_id=1, source_target_pairs={{0,32},{1,33},{2,34},{3,35},{4,36},{5,37},{6,38},{7,39},{8,40},{9,... | collective-permute-start | bytes 786440 | tf_op jit(solution)/shard_map/ppermute | solution.py:25
  51.1 5.9 %collective-permute-start.15 = (f32[64,256]{1,0:T(8,128)S(1)}, f32[64,256]{1,0:T(8,128)S(1)}, u32[]{:S(2)}, u32[]{:S(2)}) collective-permute-start(f32[64,256]{1,0:T(8,128)S(1)} %get-tuple-element.33), channel_id=1, source_target_pairs={{0,3},{1,2},{2,1},{3,0},{4,7},{5,6},{6,5},{7,4},{8,11},{9,10},{10,... | collective-permute-start | bytes 196616 | tf_op jit(solution)/shard_map/ppermute | solution.py:25
  53.9 6.3 %collective-permute-start.14 = (f32[64,256]{1,0:T(8,128)S(1)}, f32[64,256]{1,0:T(8,128)S(1)}, u32[]{:S(2)}, u32[]{:S(2)}) collective-permute-start(f32[64,256]{1,0:T(8,128)S(1)} %get-tuple-element.34), channel_id=1, source_target_pairs={{0,2},{1,3},{2,0},{3,1},{4,6},{5,7},{6,4},{7,5},{8,10},{9,11},{10,... | collective-permute-start | bytes 196616 | tf_op jit(solution)/shard_map/ppermute | solution.py:25
  54.5 5.6 %collective-permute-start.13 = (f32[64,256]{1,0:T(8,128)S(1)}, f32[64,256]{1,0:T(8,128)S(1)}, u32[]{:S(2)}, u32[]{:S(2)}) collective-permute-start(f32[64,256]{1,0:T(8,128)S(1)} %get-tuple-element.35), channel_id=1, source_target_pairs={{0,1},{1,0},{2,3},{3,2},{4,5},{5,4},{6,7},{7,6},{8,9},{9,8},{10,11... | collective-permute-start | bytes 196616 | tf_op jit(solution)/shard_map/ppermute | solution.py:25

commit v4 on v3

v4 whole, which is shorter than its diff:
```python
import functools

import jax
import jax.numpy as jnp
from jax import lax
from jax.experimental import pallas as pl
from jax.experimental.pallas import tpu as pltpu
from jax.sharding import PartitionSpec as P

IRREPS = 8
CLS = 8
ROWS = IRREPS * CLS
NT = (((1,), (1,)), ((), ()))
BF16 = jnp.bfloat16
F32 = jnp.float32
MIB = 2**20


def permute(value, move):
    pairs = []
    for occ in range(4):
        for vir in range(32):
            to_occ, to_vir = move(occ, vir)
            pairs.append((occ * 32 + vir, to_occ * 32 + to_vir))
    return lax.ppermute(value, ("occ", "vir"), pairs)


def over_y(value, k):
    return permute(value, lambda occ, vir: (occ, vir ^ k))


def over_x(value, even, odd):
    return permute(value, lambda occ, vir: (occ, vir ^ (8 * (odd if occ & 1 else even))))


def over_z(value):
    return permute(value, lambda occ, vir: (occ ^ (2 if occ & 1 else 0), vir ^ 4))


def to_sibling(value):
    return permute(value, lambda occ, vir: (occ ^ 1, vir))


def spec(space):
    return pl.BlockSpec(memory_space=space)


def params(mib):
    return pltpu.CompilerParams(vmem_limit_bytes=mib * MIB)


def place():
    vir, core = lax.axis_index("vir"), lax.axis_index("occ") & 1
    return lax.shift_right_logical(vir, 2), vir & 3, core


def cut_kernel(chol_ref, *outs):
    _, y, core = place()
    for k, out_ref in enumerate(outs):
        out_ref[...] = chol_ref[pl.ds(pl.multiple_of((y ^ k) * 512 + core * 256, 256), 256), :]


def cut_chunks(cholesky):
    return pl.pallas_call(
        cut_kernel,
        out_shape=tuple(jax.ShapeDtypeStruct((256, 128), BF16) for _ in range(4)),
        in_specs=[spec(pltpu.VMEM)],
        out_specs=tuple(spec(pltpu.VMEM) for _ in range(4)),
        compiler_params=params(4),
        name="cut_chunks",
    )(cholesky.reshape(2048, 128))


def pack_kernel(amp_ref, _, own_ref, *refs):
    outs, sems, own_sems = refs[:-2], refs[-2], refs[-1]
    h = place()[0]
    per = IRREPS // len(outs)
    copies = []
    for g in range(IRREPS):
        rows = amp_ref.at[pl.ds(g * CLS, CLS)]
        copies.append(pltpu.make_async_copy(rows.at[:, h ^ g], outs[g // per].at[g % per], sems.at[g]))
        copies.append(pltpu.make_async_copy(rows.at[:, h], own_ref.at[g], own_sems.at[g]))
    for copy in copies:
        copy.start()
    for copy in copies:
        copy.wait()


def pack_tiles(amplitudes, token, pieces):
    shape = (IRREPS, CLS, 128, 128)
    piece = jax.ShapeDtypeStruct((IRREPS // pieces, CLS, 128, 128), BF16)
    outs = pl.pallas_call(
        pack_kernel,
        out_shape=(jax.ShapeDtypeStruct(shape, BF16),) + (piece,) * pieces,
        in_specs=[spec(pltpu.HBM), spec(pl.ANY)],
        out_specs=(spec(pltpu.VMEM),) * (1 + pieces),
        scratch_shapes=[pltpu.SemaphoreType.DMA((IRREPS,)), pltpu.SemaphoreType.DMA((IRREPS,))],
        compiler_params=params(46),
        name="pack_tiles",
    )(amplitudes, token)
    return outs[0], outs[1:]


def rows_kernel(r0_ref, r1_ref, r2_ref, r3_ref, _, out_ref, all_ref):
    y = place()[1]
    for k, ref in enumerate((r0_ref, r1_ref, r2_ref, r3_ref)):
        all_ref[k ^ y] = ref[...]

    def step(i, _):
        start = pl.multiple_of(i * 16, 16)
        parts = [all_ref[q, pl.ds(start, 16), :].astype(F32) for q in range(4)]
        both = [p[0:8] for p in parts] + [p[8:16] for p in parts]
        out_ref[pl.ds(pl.multiple_of(i * 64, 64), 64), :] = jnp.concatenate(both, axis=0).astype(BF16)
        return 0

    lax.fori_loop(0, 16, step, 0, unroll=8)


def order_rows(quarters, token):
    return pl.pallas_call(
        rows_kernel,
        out_shape=jax.ShapeDtypeStruct((1024, 128), BF16),
        in_specs=[spec(pltpu.VMEM)] * 4 + [spec(pl.ANY)],
        out_specs=spec(pltpu.VMEM),
        scratch_shapes=[pltpu.VMEM((4, 256, 128), BF16)],
        compiler_params=params(6),
        name="order_rows",
    )(*quarters, token)


def relay(values, tokens):
    n = len(values)
    outs = pl.pallas_call(
        lambda *refs: None,
        out_shape=tuple(jax.ShapeDtypeStruct(v.shape, v.dtype) for v in values),
        in_specs=[spec(pl.ANY)] * (n + len(tokens)),
        out_specs=tuple(spec(pl.ANY) for _ in values),
        input_output_aliases={i: i for i in range(n)},
        compiler_params=params(1),
        name="relay",
    )(*values, *tokens)
    return outs


def join_kernel(first_ref, second_ref, _, both_ref, chosen_ref):
    core = place()[2]
    both_ref[0] = first_ref[...]
    both_ref[1] = second_ref[...]
    chosen_ref[...] = both_ref[core]


def join(first, second, token):
    return pl.pallas_call(
        join_kernel,
        out_shape=(
            jax.ShapeDtypeStruct((2, *first.shape), first.dtype),
            jax.ShapeDtypeStruct(first.shape, first.dtype),
        ),
        in_specs=[spec(pltpu.VMEM)] * 2 + [spec(pl.ANY)],
        out_specs=(spec(pltpu.VMEM), spec(pltpu.VMEM)),
        compiler_params=params(4),
        name="join",
    )(first, second, token)


def stage1_kernel(classes, pieces, tokens, mirror_ref, mine_ref, other_ref, t_ref, *refs):
    tp_refs, refs = refs[:pieces], refs[pieces + tokens :]
    per = IRREPS // pieces
    for x_ref, g in zip(refs, classes):
        tp_ref = tp_refs[g // per].at[g % per]
        for pair in range(4):
            j0, j1 = 2 * pair, 2 * pair + 1
            twins = [tp_ref[mirror_ref[g * CLS + j] - g * CLS].T for j in (j0, j1)]
            upper = jnp.concatenate([t_ref[g, j0], t_ref[g, j1]], axis=1)
            weights = jnp.concatenate([upper, jnp.concatenate(twins, axis=1)], axis=0)
            for part in range(4):
                own_ref = (mine_ref, other_ref)[part // 2]
                own = own_ref[(part % 2) * 512 : (part % 2 + 1) * 512, :]
                lhs = jnp.concatenate([own, own], axis=1)
                x = jnp.dot(lhs, weights, preferred_element_type=F32).astype(BF16)
                for k in range(2):
                    j = 2 * pair + k
                    for l in range(16):
                        lane = (part * 16 + l) * 128
                        x_ref[j * 32 : (j + 1) * 32, lane : lane + 128] = x[
                            l * 32 : (l + 1) * 32, k * 128 : (k + 1) * 128
                        ]


def stage1(classes, mirror, own, tiles, received, tokens=()):
    n = len(classes)
    return pl.pallas_call(
        functools.partial(stage1_kernel, classes, len(received), len(tokens)),
        out_shape=tuple(jax.ShapeDtypeStruct((256, 8192), BF16) for _ in classes),
        in_specs=[spec(pltpu.SMEM)]
        + [spec(pltpu.VMEM)] * (3 + len(received))
        + [spec(pl.ANY)] * len(tokens),
        out_specs=tuple(spec(pltpu.VMEM) for _ in classes),
        compiler_params=params(8),
        cost_estimate=pl.CostEstimate(flops=n * 2**30, transcendentals=0, bytes_accessed=n * 2**18),
        name="stage1_" + "_".join(str(g) for g in classes),
    )(mirror, *own, tiles, *received, *tokens)


def stage2_kernel(picks, n_b, carried, tokens, *refs):
    n = len(picks)
    x_refs, refs = refs[:n], refs[n:]
    b_refs, refs = refs[:n_b], refs[n_b:]
    carry, refs = refs[:carried], refs[carried:]
    out_ref, r_s = refs[tokens:]
    y = place()[1]
    for i, halves in enumerate(picks):
        total = None
        for half, (at, index) in enumerate(halves):
            b_ref = b_refs[at] if index is None else b_refs[at].at[index]
            for step in range(8):
                b = b_ref[step * 128 : (step + 1) * 128, :]
                bt = jnp.concatenate([b[l * 32 : (l + 1) * 32] for l in range(4)], axis=1)
                lane = half * 4096 + step * 512
                term = lax.dot_general(
                    x_refs[i][:, lane : lane + 512], bt, NT, preferred_element_type=F32
                )
                total = term if total is None else total + term
        r_s[i] = total
    for q in range(4):
        columns = [ref[q ^ y] for ref in carry]
        for i in range(n):
            r = r_s[i]
            columns.append(
                jnp.concatenate([r[j * 32 + q * 8 : j * 32 + q * 8 + 8] for j in range(CLS)], axis=0)
            )
        out_ref[q ^ y] = jnp.concatenate(columns, axis=1) if len(columns) > 1 else columns[0]


def stage2(name, xs, picks, bs, carry=(), tokens=()):
    n = len(xs)
    lanes = 32 * n + sum(c.shape[2] for c in carry)
    return pl.pallas_call(
        functools.partial(stage2_kernel, picks, len(bs), len(carry), len(tokens)),
        out_shape=jax.ShapeDtypeStruct((4, 64, lanes), F32),
        in_specs=[spec(pltpu.VMEM)] * (n + len(bs) + len(carry)) + [spec(pl.ANY)] * len(tokens),
        out_specs=spec(pltpu.VMEM),
        scratch_shapes=[pltpu.VMEM((n, 256, 32), F32)],
        compiler_params=params(8),
        cost_estimate=pl.CostEstimate(flops=n * 2**30, transcendentals=0, bytes_accessed=n * 2**18),
        name="stage2_" + name,
    )(*xs, *bs, *carry, *tokens)


def finish_kernel(order, own_ref, r1_ref, r2_ref, r3_ref, out_ref, sum_s, pos_s):
    total = own_ref[0] + r1_ref[...] + r2_ref[...] + r3_ref[...]
    sum_s[0] = total[:, 0:128]
    sum_s[1] = total[:, 128:256]
    for a8 in range(8):
        for k in range(2):
            strip = sum_s[k, pl.ds(a8, CLS, stride=8), :]
            for c in range(4):
                g = order[k * 4 + c]
                pos_s[g * CLS : (g + 1) * CLS, a8 * 32 : (a8 + 1) * 32] = strip[:, c * 32 : (c + 1) * 32]
    out_ref[...] = pos_s[...].T.reshape(8, 32, ROWS)


def finish(order, parts):
    out = pl.pallas_call(
        functools.partial(finish_kernel, order),
        out_shape=jax.ShapeDtypeStruct((8, 32, ROWS), F32),
        in_specs=[spec(pltpu.VMEM)] * 4,
        out_specs=spec(pltpu.VMEM),
        scratch_shapes=[pltpu.VMEM((2, 64, 128), F32), pltpu.VMEM((ROWS, 256), F32)],
        compiler_params=params(6),
        name="finish",
    )(*parts)
    return jnp.transpose(out, (2, 0, 1))


PIECES = 1


def shards(cholesky, amplitudes, mirror):
    chunks = cut_chunks(cholesky)
    quarters = (chunks[0],) + tuple(over_y(chunks[k], k) for k in range(1, 4))
    tiles, outgoing = pack_tiles(amplitudes, chunks[0], PIECES)
    received = tuple(to_sibling(piece) for piece in outgoing)
    mine = order_rows(quarters, tiles)
    own = (mine, to_sibling(mine))

    x1a, x1b, z0 = over_x(mine, 1, 1), over_x(mine, 3, 3), over_z(mine)
    xc0, xc1, xc2, xc6, xc4 = stage1((0, 1, 2, 6, 4), mirror, own, tiles, received)
    (z0,) = relay((z0,), (xc0,))
    x1, forward = join(x1a, x1b, xc0)
    x1_other, z0_other = to_sibling(x1), to_sibling(z0)
    x2 = over_x(forward, 3, 1)
    zx1 = over_z(x1)
    near = stage2(
        "near",
        (xc0, xc1, xc2, xc6),
        (((0, None), (1, None)), ((2, None), (3, None)), ((4, 0), (5, 0)), ((4, 1), (5, 1))),
        (*own, z0, z0_other, x1, x1_other),
    )
    (x2,) = relay((x2,), (near,))
    x2_other = to_sibling(x2)
    zx2 = over_z(x2)
    xc3, xc7, xc5 = stage1((3, 7, 5), mirror, own, tiles, received, (x2,))
    zx1, zx2 = relay((zx1, zx2), (xc5,))
    zx1_other, zx2_other = to_sibling(zx1), to_sibling(zx2)
    far = stage2("far", (xc4,), (((0, None), (1, None)),), (x2, x2_other), (near,), (zx1,))
    last = stage2(
        "last",
        (xc3, xc7, xc5),
        (((0, 0), (1, 0)), ((0, 1), (1, 1)), ((2, None), (3, None))),
        (zx1, zx1_other, zx2, zx2_other),
        (far,),
    )
    parts = [last] + [over_y(last[k], k) for k in range(1, 4)]
    return finish((0, 1, 2, 6, 4, 3, 7, 5), parts)


def solution(mesh):
    placed = (P(None, "vir", None), P("occ", None, None, None), P("occ"))
    return jax.shard_map(
        shards, mesh=mesh, in_specs=placed, out_specs=P("occ", "vir", None), check_vma=False
    )
```

time: 61.2 us -> 58.2 us (0.951)
  waiting for transfers between devices: 17 us -> 11.6 us
  starting transfers between devices: 17.2 us -> 21.4 us
  Pallas kernels: 24.8 us -> 23.7 us
  local copies, waits for them, and re-layouts: 2.01 us -> 1.06 us
    ppermute x16 -> x19, waiting for transfers between devices: 17 us -> 11.6 us  [permute(): return lax.ppermute(value, ('occ', 'vir'), pairs)]
    ppermute x16 -> x19, starting transfers between devices: 17.2 us -> 21.4 us  [permute(): return lax.ppermute(value, ('occ', 'vir'), pairs)]
    pallas_call x1, Pallas kernels: 4.29 us -> 2.29 us  [pack_tiles(): pl.pallas_call(pack_kernel, out_shape=(jax.ShapeDtypeStruct(shape, BF16),...]
    pallas_call x7 -> x8, Pallas kernels: 19.6 us -> 20.6 us  [the longest x2 11.1 us: stage1(): pl.pallas_call(functools.partial(stage1_kernel, classes, len(received), l...]
    unnamed x8 -> x4, local copies, waits for them, and re-layouts: 1.95 us -> 1.05 us
  transfers between devices with their start and end apart: 16 -> 19, of which waited for: 8 -> 8; matrix products, arithmetic and copies ran while one was open for 0% -> 0% of each run, Pallas kernels for 30% -> 29%
where the time goes in v4:
time: 58.2 us; the launch traced here: 58 us
  Pallas kernels  23.7 us (41%)
  starting transfers between devices  21.4 us (37%)
  waiting for transfers between devices  11.6 us (20%)
  local copies, waits for them, and re-layouts  1.06 us (2%)
    ppermute x19, starting transfers between devices, permute(): return lax.ppermute(value, ('occ', 'vir'), pairs)  21.4 us
    ppermute x19, waiting for transfers between devices, permute(): return lax.ppermute(value, ('occ', 'vir'), pairs)  11.6 us
    pallas_call x2, Pallas kernels, stage1(): pl.pallas_call(functools.partial(stage1_kernel, classes, len(received), l...  11.1 us
    pallas_call x3, Pallas kernels, stage2(): pl.pallas_call(functools.partial(stage2_kernel, picks, len(bs), len(carry...  9.33 us
    pallas_call x1, Pallas kernels, pack_tiles(): pl.pallas_call(pack_kernel, out_shape=(jax.ShapeDtypeStruct(shape, BF16),...  2.29 us
  transfers between devices with their start and end apart: 19, of which 8 were waited for; matrix products, arithmetic and copies ran while one was open for 0% of the time, Pallas kernels for 29%

profile of v4, /device:TPU:0, one launch (start us, length us, event | category | flops | bytes accessed | tf_op | source)
XLA Modules:
  0.0 58.0 jit_solution(10184628152268157464)
XLA Ops:
  0.0 1.0 %copy-done = bf16[256,8,128]{2,1,0:T(8,128)(2,1)S(1)} copy-done((bf16[256,8,128]{2,1,0:T(8,128)(2,1)S(1)}, bf16[256,8,128]{2,1,0:T(8,128)(2,1)}, u32[]{:S(2)}) %copy-start) | copy-done | bytes 524312
  1.1 2.3 %pack_tiles.1 = (bf16[8,8,128,128]{3,2,1,0:T(8,128)(2,1)S(1)}, bf16[8,8,128,128]{3,2,1,0:T(8,128)(2,1)S(1)}) custom-call(bf16[64,8,128,128]{3,2,1,0:T(8,128)(2,1)} %amp_ref.1, bf16[256,128]{1,0:T(8,128)(2,1)S(1)} %get-tuple-element.23._.r0_ref), custom_call_target="tpu_custom_call" | custom-call | tf_op jit(solution)/shard_map/pack_tiles/pallas_call | solution.py:92
  3.5 1.7 %collective-permute-start = (bf16[256,128]{1,0:T(8,128)(2,1)S(1)}, bf16[256,128]{1,0:T(8,128)(2,1)S(1)}, u32[]{:S(2)}, u32[]{:S(2)}) collective-permute-start(bf16[256,128]{1,0:T(8,128)(2,1)S(1)} %get-tuple-element.24), channel_id=1, source_target_pairs={{0,1},{1,0},{2,3},{3,2},{4,5},{5,4},{6,7},{7,6},{8,9},{9,8},{10,11... | collective-permute-start | bytes 196616 | tf_op jit(solution)/shard_map/ppermute | solution.py:25
  5.2 2.9 %collective-permute-start.1 = (bf16[256,128]{1,0:T(8,128)(2,1)S(1)}, bf16[256,128]{1,0:T(8,128)(2,1)S(1)}, u32[]{:S(2)}, u32[]{:S(2)}) collective-permute-start(bf16[256,128]{1,0:T(8,128)(2,1)S(1)} %get-tuple-element.25), channel_id=1, source_target_pairs={{0,2},{1,3},{2,0},{3,1},{4,6},{5,7},{6,4},{7,5},{8,10},{9,11},{10,... | collective-permute-start | bytes 196616 | tf_op jit(solution)/shard_map/ppermute | solution.py:25
  8.3 3.7 %collective-permute-done.1.r2_ref = bf16[256,128]{1,0:T(8,128)(2,1)S(1)} collective-permute-done((bf16[256,128]{1,0:T(8,128)(2,1)S(1)}, bf16[256,128]{1,0:T(8,128)(2,1)S(1)}, u32[]{:S(2)}, u32[]{:S(2)}) %collective-permute-start.1) | collective-permute-done | bytes 65568 | tf_op jit(solution)/shard_map/ppermute | solution.py:25
  11.9 1.7 %collective-permute-done.2.r3_ref = bf16[256,128]{1,0:T(8,128)(2,1)S(1)} collective-permute-done((bf16[256,128]{1,0:T(8,128)(2,1)S(1)}, bf16[256,128]{1,0:T(8,128)(2,1)S(1)}, u32[]{:S(2)}, u32[]{:S(2)}) %collective-permute-start.2) | collective-permute-done | bytes 65568 | tf_op jit(solution)/shard_map/ppermute | solution.py:25
  13.8 1.6 %collective-permute-start.5 = (bf16[1024,128]{1,0:T(8,128)(2,1)S(1)}, bf16[1024,128]{1,0:T(8,128)(2,1)S(1)}, u32[]{:S(2)}, u32[]{:S(2)}) collective-permute-start(bf16[1024,128]{1,0:T(8,128)(2,1)S(1)} %order_rows.1.mine_ref.refs_4_), channel_id=1, source_target_pairs={{0,8},{1,9},{2,10},{3,11},{4,12},{5,13},{6,14},{7,15},{8,0},{9,1},... | collective-permute-start | bytes 786440 | tf_op jit(solution)/shard_map/ppermute | solution.py:25
  15.3 2.1 %collective-permute-start.6 = (bf16[1024,128]{1,0:T(8,128)(2,1)S(1)}, bf16[1024,128]{1,0:T(8,128)(2,1)S(1)}, u32[]{:S(2)}, u32[]{:S(2)}) collective-permute-start(bf16[1024,128]{1,0:T(8,128)(2,1)S(1)} %order_rows.1.mine_ref.refs_4_), channel_id=1, source_target_pairs={{0,24},{1,25},{2,26},{3,27},{4,28},{5,29},{6,30},{7,31},{8,16},{9,... | collective-permute-start | bytes 786440 | tf_op jit(solution)/shard_map/ppermute | solution.py:25
  17.4 1.9 %collective-permute-start.8 = (bf16[1024,128]{1,0:T(8,128)(2,1)S(1)}, bf16[1024,128]{1,0:T(8,128)(2,1)S(1)}, u32[]{:S(2)}, u32[]{:S(2)}) collective-permute-start(bf16[1024,128]{1,0:T(8,128)(2,1)S(1)} %order_rows.1.mine_ref.refs_4_), channel_id=1, source_target_pairs={{0,4},{1,5},{2,6},{3,7},{4,0},{5,1},{6,2},{7,3},{8,12},{9,13},{10,... | collective-permute-start | bytes 786440 | tf_op jit(solution)/shard_map/ppermute | solution.py:25
  19.4 6.7 %stage1_0_1_2_6_4.1 = (bf16[256,8192]{1,0:T(8,128)(2,1)S(1)}, bf16[256,8192]{1,0:T(8,128)(2,1)S(1)}, bf16[256,8192]{1,0:T(8,128)(2,1)S(1)}, bf16[256,8192]{1,0:T(8,128)(2,1)S(1)}, bf16[256,8192]{1,0:T(8,128)(2,1)S(1)}) custom-call(s32[64]{0:T(128)S(1)} %copy-done.1, bf16[1024,128]{1,0:T(8,128)(2,1)S(1)} %order_rows.1.mine_ref.refs_4_, ...), custom_call_target="tpu_custom_call" | custom-call | flops 5368709120 | bytes 1310720 | tf_op jit(solution)/shard_map/stage1_0_1_2_6_4/pallas_call | solution.py:192
  26.2 1.8 %collective-permute-start.10 = (bf16[2,1024,128]{2,1,0:T(8,128)(2,1)S(1)}, bf16[2,1024,128]{2,1,0:T(8,128)(2,1)S(1)}, u32[]{:S(2)}, u32[]{:S(2)}) collective-permute-start(bf16[2,1024,128]{2,1,0:T(8,128)(2,1)S(1)} %get-tuple-element.34.refs_8_), channel_id=1, source_target_pairs={{0,32},{1,33},{2,34},{3,35},{4,36},{5,37},{6,38},{7,39},{8,40},{9,... | collective-permute-start | bytes 1572872 | tf_op jit(solution)/shard_map/ppermute | solution.py:25
  28.1 1.5 %collective-permute-start.7 = (bf16[1024,128]{1,0:T(8,128)(2,1)S(1)}, bf16[1024,128]{1,0:T(8,128)(2,1)S(1)}, u32[]{:S(2)}, u32[]{:S(2)}) collective-permute-start(bf16[1024,128]{1,0:T(8,128)(2,1)S(1)} %get-tuple-element.30), channel_id=1, source_target_pairs={{0,24},{1,25},{2,26},{3,27},{4,28},{5,29},{6,30},{7,31},{8,16},{9,... | collective-permute-start | bytes 786440 | tf_op jit(solution)/shard_map/ppermute | solution.py:25
  29.9 4.6 %stage2_near.1.refs_1_.refs_3_ = f32[4,64,128]{2,1,0:T(8,128)S(1)} custom-call(bf16[256,8192]{1,0:T(8,128)(2,1)S(1)} %get-tuple-element.29._.refs_1_.refs_0_, bf16[256,8192]{1,0:T(8,128)(2,1)S(1)} %get-tuple-element.31.refs_1_, bf16[256,8192]{1,0:T(8,128)(2,1)S(1)} %get-tuple-element.32.refs_2_, bf16[256,8192]{1,0:T(8,128)(2,1)S(1)} %get-tuple-element.33.refs_3_, ...), custom_call_target="tpu_custom_call" | custom-call | flops 4294967296 | bytes 1048576 | tf_op jit(solution)/shard_map/stage2_near/pallas_call | solution.py:238
  34.5 1.2 %collective-permute-done.7.refs_0_ = bf16[1024,128]{1,0:T(8,128)(2,1)S(1)} collective-permute-done((bf16[1024,128]{1,0:T(8,128)(2,1)S(1)}, bf16[1024,128]{1,0:T(8,128)(2,1)S(1)}, u32[]{:S(2)}, u32[]{:S(2)}) %collective-permute-start.7) | collective-permute-done | bytes 262176 | tf_op jit(solution)/shard_map/ppermute | solution.py:25
  35.7 2.0 %collective-permute-start.12 = (bf16[1024,128]{1,0:T(8,128)(2,1)S(1)}, bf16[1024,128]{1,0:T(8,128)(2,1)S(1)}, u32[]{:S(2)}, u32[]{:S(2)}) collective-permute-start(bf16[1024,128]{1,0:T(8,128)(2,1)S(1)} %relay.4.refs_1_), channel_id=1, source_target_pairs={{0,4},{1,5},{2,6},{3,7},{4,0},{5,1},{6,2},{7,3},{8,12},{9,13},{10,... | collective-permute-start | bytes 786440 | tf_op jit(solution)/shard_map/ppermute | solution.py:25
  37.7 4.3 %stage1_3_7_5.1 = (bf16[256,8192]{1,0:T(8,128)(2,1)S(1)}, bf16[256,8192]{1,0:T(8,128)(2,1)S(1)}, bf16[256,8192]{1,0:T(8,128)(2,1)S(1)}) custom-call(s32[64]{0:T(128)S(1)} %copy-done.1, bf16[1024,128]{1,0:T(8,128)(2,1)S(1)} %order_rows.1.mine_ref.refs_4_, bf16[1024,128]{1,0:T(8,128)(2,1)S(1)} %collective-permute-done.3.other_ref.refs_5_, ...), custom_call_target="tpu_custom_call" | custom-call | flops 3221225472 | bytes 786432 | tf_op jit(solution)/shard_map/stage1_3_7_5/pallas_call | solution.py:192
  42.8 1.7 %collective-permute-done.15.refs_2_ = bf16[1024,128]{1,0:T(8,128)(2,1)S(1)} collective-permute-done((bf16[1024,128]{1,0:T(8,128)(2,1)S(1)}, bf16[1024,128]{1,0:T(8,128)(2,1)S(1)}, u32[]{:S(2)}, u32[]{:S(2)}) %collective-permute-start.15) | collective-permute-done | bytes 262176 | tf_op jit(solution)/shard_map/ppermute | solution.py:25
  44.4 1.2 %stage2_far.1.refs_7_ = f32[4,64,160]{2,1,0:T(8,128)S(1)} custom-call(bf16[256,8192]{1,0:T(8,128)(2,1)S(1)} %get-tuple-element.40.refs_0_, bf16[1024,128]{1,0:T(8,128)(2,1)S(1)} %relay.4.refs_1_, bf16[1024,128]{1,0:T(8,128)(2,1)S(1)} %collective-permute-done.15.refs_2_, f32[4,64,128]{2,1,0:T(8,128)S(1)} %stage2_near.1.refs_1_.refs_3_, ...), custom_call_target="tpu_custom_call" | custom-call | flops 1073741824 | bytes 262144 | tf_op jit(solution)/shard_map/stage2_far/pallas_call | solution.py:238
  45.7 3.5 %stage2_last.1.own_ref = f32[4,64,256]{2,1,0:T(8,128)S(1)} custom-call(bf16[256,8192]{1,0:T(8,128)(2,1)S(1)} %get-tuple-element.35.refs_0_, bf16[256,8192]{1,0:T(8,128)(2,1)S(1)} %get-tuple-element.36.refs_1_, bf16[256,8192]{1,0:T(8,128)(2,1)S(1)} %get-tuple-element.37.refs_2_, bf16[2,1024,128]{2,1,0:T(8,128)(2,1)S(1)} %get-tuple-element.38.refs_4_.refs_3_, ...), custom_call_target="tpu_custom_call" | custom-call | flops 3221225472 | bytes 786432 | tf_op jit(solution)/shard_map/stage2_last/pallas_call | solution.py:238
  49.3 2.3 %collective-permute-start.17 = (f32[64,256]{1,0:T(8,128)S(1)}, f32[64,256]{1,0:T(8,128)S(1)}, u32[]{:S(2)}, u32[]{:S(2)}) collective-permute-start(f32[64,256]{1,0:T(8,128)S(1)} %get-tuple-element.42), channel_id=1, source_target_pairs={{0,2},{1,3},{2,0},{3,1},{4,6},{5,7},{6,4},{7,5},{8,10},{9,11},{10,... | collective-permute-start | bytes 196616 | tf_op jit(solution)/shard_map/ppermute | solution.py:25
  51.7 2.4 %collective-permute-start.18 = (f32[64,256]{1,0:T(8,128)S(1)}, f32[64,256]{1,0:T(8,128)S(1)}, u32[]{:S(2)}, u32[]{:S(2)}) collective-permute-start(f32[64,256]{1,0:T(8,128)S(1)} %get-tuple-element.41), channel_id=1, source_target_pairs={{0,3},{1,2},{2,1},{3,0},{4,7},{5,6},{6,5},{7,4},{8,11},{9,10},{10,... | collective-permute-start | bytes 196616 | tf_op jit(solution)/shard_map/ppermute | solution.py:25
  54.2 1.2 %collective-permute-done.17.r2_ref = f32[64,256]{1,0:T(8,128)S(1)} collective-permute-done((f32[64,256]{1,0:T(8,128)S(1)}, f32[64,256]{1,0:T(8,128)S(1)}, u32[]{:S(2)}, u32[]{:S(2)}) %collective-permute-start.17) | collective-permute-done | bytes 65568 | tf_op jit(solution)/shard_map/ppermute | solution.py:25
  55.3 1.8 %collective-permute-done.18.r3_ref = f32[64,256]{1,0:T(8,128)S(1)} collective-permute-done((f32[64,256]{1,0:T(8,128)S(1)}, f32[64,256]{1,0:T(8,128)S(1)}, u32[]{:S(2)}, u32[]{:S(2)}) %collective-permute-start.18) | collective-permute-done | bytes 65568 | tf_op jit(solution)/shard_map/ppermute | solution.py:25
  57.1 0.9 %finish.1 = f32[8,32,64]{2,1,0:T(8,128)} custom-call(f32[4,64,256]{2,1,0:T(8,128)S(1)} %stage2_last.1.own_ref, f32[64,256]{1,0:T(8,128)S(1)} %collective-permute-done.16.r1_ref, f32[64,256]{1,0:T(8,128)S(1)} %collective-permute-done.17.r2_ref, f32[64,256]{1,0:T(8,128)S(1)} %collective-permute-done.18.r3_ref), custom_call_target="tpu_custom_call" | custom-call | tf_op jit(solution)/shard_map/finish/pallas_call | solution.py:264
  (32 shorter events, 1.8 us)
Async XLA Ops:
  0.0 1.0 %copy-start = (bf16[256,8,128]{2,1,0:T(8,128)(2,1)S(1)}, bf16[256,8,128]{2,1,0:T(8,128)(2,1)}, u32[]{:S(2)}) copy-start(bf16[256,8,128]{2,1,0:T(8,128)(2,1)} %param.3) | copy-start | bytes 1572868
  1.1 18.3 %copy-start.1 = (s32[64]{0:T(128)S(1)}, s32[64]{0:T(128)}, u32[]{:S(2)}) copy-start(s32[64]{0:T(128)} %mirror_ref.3) | copy-start | bytes 772
  3.4 16.0 %collective-permute-start.4 = (bf16[8,8,128,128]{3,2,1,0:T(8,128)(2,1)S(1)}, bf16[8,8,128,128]{3,2,1,0:T(8,128)(2,1)S(1)}, u32[]{:S(2)}, u32[]{:S(2)}) collective-permute-start(bf16[8,8,128,128]{3,2,1,0:T(8,128)(2,1)S(1)} %get-tuple-element.28), channel_id=1, source_target_pairs={{0,32},{1,33},{2,34},{3,35},{4,36},{5,37},{6,38},{7,39},{8,40},{9,... | collective-permute-start | bytes 6291464 | tf_op jit(solution)/shard_map/ppermute | solution.py:25
  3.5 4.8 %collective-permute-start = (bf16[256,128]{1,0:T(8,128)(2,1)S(1)}, bf16[256,128]{1,0:T(8,128)(2,1)S(1)}, u32[]{:S(2)}, u32[]{:S(2)}) collective-permute-start(bf16[256,128]{1,0:T(8,128)(2,1)S(1)} %get-tuple-element.24), channel_id=1, source_target_pairs={{0,1},{1,0},{2,3},{3,2},{4,5},{5,4},{6,7},{7,6},{8,9},{9,8},{10,11... | collective-permute-start | bytes 196616 | tf_op jit(solution)/shard_map/ppermute | solution.py:25
  5.2 6.7 %collective-permute-start.1 = (bf16[256,128]{1,0:T(8,128)(2,1)S(1)}, bf16[256,128]{1,0:T(8,128)(2,1)S(1)}, u32[]{:S(2)}, u32[]{:S(2)}) collective-permute-start(bf16[256,128]{1,0:T(8,128)(2,1)S(1)} %get-tuple-element.25), channel_id=1, source_target_pairs={{0,2},{1,3},{2,0},{3,1},{4,6},{5,7},{6,4},{7,5},{8,10},{9,11},{10,... | collective-permute-start | bytes 196616 | tf_op jit(solution)/shard_map/ppermute | solution.py:25
  8.1 5.5 %collective-permute-start.2 = (bf16[256,128]{1,0:T(8,128)(2,1)S(1)}, bf16[256,128]{1,0:T(8,128)(2,1)S(1)}, u32[]{:S(2)}, u32[]{:S(2)}) collective-permute-start(bf16[256,128]{1,0:T(8,128)(2,1)S(1)} %get-tuple-element.26), channel_id=1, source_target_pairs={{0,3},{1,2},{2,1},{3,0},{4,7},{5,6},{6,5},{7,4},{8,11},{9,10},{10,... | collective-permute-start | bytes 196616 | tf_op jit(solution)/shard_map/ppermute | solution.py:25
  13.7 5.7 %collective-permute-start.3 = (bf16[1024,128]{1,0:T(8,128)(2,1)S(1)}, bf16[1024,128]{1,0:T(8,128)(2,1)S(1)}, u32[]{:S(2)}, u32[]{:S(2)}) collective-permute-start(bf16[1024,128]{1,0:T(8,128)(2,1)S(1)} %order_rows.1.mine_ref.refs_4_), channel_id=1, source_target_pairs={{0,32},{1,33},{2,34},{3,35},{4,36},{5,37},{6,38},{7,39},{8,40},{9,... | collective-permute-start | bytes 786440 | tf_op jit(solution)/shard_map/ppermute | solution.py:25
  13.8 12.3 %collective-permute-start.5 = (bf16[1024,128]{1,0:T(8,128)(2,1)S(1)}, bf16[1024,128]{1,0:T(8,128)(2,1)S(1)}, u32[]{:S(2)}, u32[]{:S(2)}) collective-permute-start(bf16[1024,128]{1,0:T(8,128)(2,1)S(1)} %order_rows.1.mine_ref.refs_4_), channel_id=1, source_target_pairs={{0,8},{1,9},{2,10},{3,11},{4,12},{5,13},{6,14},{7,15},{8,0},{9,1},... | collective-permute-start | bytes 786440 | tf_op jit(solution)/shard_map/ppermute | solution.py:25
  15.3 10.8 %collective-permute-start.6 = (bf16[1024,128]{1,0:T(8,128)(2,1)S(1)}, bf16[1024,128]{1,0:T(8,128)(2,1)S(1)}, u32[]{:S(2)}, u32[]{:S(2)}) collective-permute-start(bf16[1024,128]{1,0:T(8,128)(2,1)S(1)} %order_rows.1.mine_ref.refs_4_), channel_id=1, source_target_pairs={{0,24},{1,25},{2,26},{3,27},{4,28},{5,29},{6,30},{7,31},{8,16},{9,... | collective-permute-start | bytes 786440 | tf_op jit(solution)/shard_map/ppermute | solution.py:25
  17.4 10.5 %collective-permute-start.8 = (bf16[1024,128]{1,0:T(8,128)(2,1)S(1)}, bf16[1024,128]{1,0:T(8,128)(2,1)S(1)}, u32[]{:S(2)}, u32[]{:S(2)}) collective-permute-start(bf16[1024,128]{1,0:T(8,128)(2,1)S(1)} %order_rows.1.mine_ref.refs_4_), channel_id=1, source_target_pairs={{0,4},{1,5},{2,6},{3,7},{4,0},{5,1},{6,2},{7,3},{8,12},{9,13},{10,... | collective-permute-start | bytes 786440 | tf_op jit(solution)/shard_map/ppermute | solution.py:25
  26.2 3.7 %collective-permute-start.10 = (bf16[2,1024,128]{2,1,0:T(8,128)(2,1)S(1)}, bf16[2,1024,128]{2,1,0:T(8,128)(2,1)S(1)}, u32[]{:S(2)}, u32[]{:S(2)}) collective-permute-start(bf16[2,1024,128]{2,1,0:T(8,128)(2,1)S(1)} %get-tuple-element.34.refs_8_), channel_id=1, source_target_pairs={{0,32},{1,33},{2,34},{3,35},{4,36},{5,37},{6,38},{7,39},{8,40},{9,... | collective-permute-start | bytes 1572872 | tf_op jit(solution)/shard_map/ppermute | solution.py:25
  28.0 1.9 %collective-permute-start.9 = (bf16[1024,128]{1,0:T(8,128)(2,1)S(1)}, bf16[1024,128]{1,0:T(8,128)(2,1)S(1)}, u32[]{:S(2)}, u32[]{:S(2)}) collective-permute-start(bf16[1024,128]{1,0:T(8,128)(2,1)S(1)} %relay.3.refs_6_), channel_id=1, source_target_pairs={{0,32},{1,33},{2,34},{3,35},{4,36},{5,37},{6,38},{7,39},{8,40},{9,... | collective-permute-start | bytes 786440 | tf_op jit(solution)/shard_map/ppermute | solution.py:25
  28.1 13.9 %collective-permute-start.11 = (bf16[2,1024,128]{2,1,0:T(8,128)(2,1)S(1)}, bf16[2,1024,128]{2,1,0:T(8,128)(2,1)S(1)}, u32[]{:S(2)}, u32[]{:S(2)}) collective-permute-start(bf16[2,1024,128]{2,1,0:T(8,128)(2,1)S(1)} %get-tuple-element.34.refs_8_), channel_id=1, source_target_pairs={{0,4},{1,5},{2,6},{3,7},{4,0},{5,1},{6,2},{7,3},{8,12},{9,13},{10,... | collective-permute-start | bytes 1572872 | tf_op jit(solution)/shard_map/ppermute | solution.py:25
  28.1 7.6 %collective-permute-start.7 = (bf16[1024,128]{1,0:T(8,128)(2,1)S(1)}, bf16[1024,128]{1,0:T(8,128)(2,1)S(1)}, u32[]{:S(2)}, u32[]{:S(2)}) collective-permute-start(bf16[1024,128]{1,0:T(8,128)(2,1)S(1)} %get-tuple-element.30), channel_id=1, source_target_pairs={{0,24},{1,25},{2,26},{3,27},{4,28},{5,29},{6,30},{7,31},{8,16},{9,... | collective-permute-start | bytes 786440 | tf_op jit(solution)/shard_map/ppermute | solution.py:25
  35.7 6.4 %collective-permute-start.12 = (bf16[1024,128]{1,0:T(8,128)(2,1)S(1)}, bf16[1024,128]{1,0:T(8,128)(2,1)S(1)}, u32[]{:S(2)}, u32[]{:S(2)}) collective-permute-start(bf16[1024,128]{1,0:T(8,128)(2,1)S(1)} %relay.4.refs_1_), channel_id=1, source_target_pairs={{0,4},{1,5},{2,6},{3,7},{4,0},{5,1},{6,2},{7,3},{8,12},{9,13},{10,... | collective-permute-start | bytes 786440 | tf_op jit(solution)/shard_map/ppermute | solution.py:25
  42.1 3.6 %collective-permute-start.13 = (bf16[2,1024,128]{2,1,0:T(8,128)(2,1)S(1)}, bf16[2,1024,128]{2,1,0:T(8,128)(2,1)S(1)}, u32[]{:S(2)}, u32[]{:S(2)}) collective-permute-start(bf16[2,1024,128]{2,1,0:T(8,128)(2,1)S(1)} %get-tuple-element.38.refs_4_.refs_3_), channel_id=1, source_target_pairs={{0,32},{1,33},{2,34},{3,35},{4,36},{5,37},{6,38},{7,39},{8,40},{9,... | collective-permute-start | bytes 1572872 | tf_op jit(solution)/shard_map/ppermute | solution.py:25
  42.2 2.3 %collective-permute-start.15 = (bf16[1024,128]{1,0:T(8,128)(2,1)S(1)}, bf16[1024,128]{1,0:T(8,128)(2,1)S(1)}, u32[]{:S(2)}, u32[]{:S(2)}) collective-permute-start(bf16[1024,128]{1,0:T(8,128)(2,1)S(1)} %relay.4.refs_1_), channel_id=1, source_target_pairs={{0,32},{1,33},{2,34},{3,35},{4,36},{5,37},{6,38},{7,39},{8,40},{9,... | collective-permute-start | bytes 786440 | tf_op jit(solution)/shard_map/ppermute | solution.py:25
  42.7 3.0 %collective-permute-start.14 = (bf16[1024,128]{1,0:T(8,128)(2,1)S(1)}, bf16[1024,128]{1,0:T(8,128)(2,1)S(1)}, u32[]{:S(2)}, u32[]{:S(2)}) collective-permute-start(bf16[1024,128]{1,0:T(8,128)(2,1)S(1)} %get-tuple-element.39.refs_5_), channel_id=1, source_target_pairs={{0,32},{1,33},{2,34},{3,35},{4,36},{5,37},{6,38},{7,39},{8,40},{9,... | collective-permute-start | bytes 786440 | tf_op jit(solution)/shard_map/ppermute | solution.py:25
  49.2 4.9 %collective-permute-start.16 = (f32[64,256]{1,0:T(8,128)S(1)}, f32[64,256]{1,0:T(8,128)S(1)}, u32[]{:S(2)}, u32[]{:S(2)}) collective-permute-start(f32[64,256]{1,0:T(8,128)S(1)} %get-tuple-element.43), channel_id=1, source_target_pairs={{0,1},{1,0},{2,3},{3,2},{4,5},{5,4},{6,7},{7,6},{8,9},{9,8},{10,11... | collective-permute-start | bytes 196616 | tf_op jit(solution)/shard_map/ppermute | solution.py:25
  49.3 6.0 %collective-permute-start.17 = (f32[64,256]{1,0:T(8,128)S(1)}, f32[64,256]{1,0:T(8,128)S(1)}, u32[]{:S(2)}, u32[]{:S(2)}) collective-permute-start(f32[64,256]{1,0:T(8,128)S(1)} %get-tuple-element.42), channel_id=1, source_target_pairs={{0,2},{1,3},{2,0},{3,1},{4,6},{5,7},{6,4},{7,5},{8,10},{9,11},{10,... | collective-permute-start | bytes 196616 | tf_op jit(solution)/shard_map/ppermute | solution.py:25
  51.7 5.5 %collective-permute-start.18 = (f32[64,256]{1,0:T(8,128)S(1)}, f32[64,256]{1,0:T(8,128)S(1)}, u32[]{:S(2)}, u32[]{:S(2)}) collective-permute-start(f32[64,256]{1,0:T(8,128)S(1)} %get-tuple-element.41), channel_id=1, source_target_pairs={{0,3},{1,2},{2,1},{3,0},{4,7},{5,6},{6,5},{7,4},{8,11},{9,10},{10,... | collective-permute-start | bytes 196616 | tf_op jit(solution)/shard_map/ppermute | solution.py:25

commit v5 on v4

--- a/solution.py
+++ b/solution.py
@@ -54,51 +54,61 @@
     return lax.shift_right_logical(vir, 2), vir & 3, core
 
 
-def cut_kernel(chol_ref, *outs):
-    _, y, core = place()
-    for k, out_ref in enumerate(outs):
-        out_ref[...] = chol_ref[pl.ds(pl.multiple_of((y ^ k) * 512 + core * 256, 256), 256), :]
-
-
-def cut_chunks(cholesky):
-    return pl.pallas_call(
-        cut_kernel,
-        out_shape=tuple(jax.ShapeDtypeStruct((256, 128), BF16) for _ in range(4)),
-        in_specs=[spec(pltpu.VMEM)],
-        out_specs=tuple(spec(pltpu.VMEM) for _ in range(4)),
-        compiler_params=params(4),
-        name="cut_chunks",
-    )(cholesky.reshape(2048, 128))
-
-
-def pack_kernel(amp_ref, _, own_ref, *refs):
-    outs, sems, own_sems = refs[:-2], refs[-2], refs[-1]
-    h = place()[0]
-    per = IRREPS // len(outs)
+def send_kernel(chol_ref, amp_ref, *refs):
+    chunks, tiles_ref, chunk_sems, tile_sems = refs[:4], refs[4], refs[5], refs[6]
+    h, y, core = place()
     copies = []
+    for k, out_ref in enumerate(chunks):
+        start = pl.multiple_of((y ^ k) * 512 + core * 256, 256)
+        copies.append(pltpu.make_async_copy(chol_ref.at[pl.ds(start, 256)], out_ref, chunk_sems.at[k]))
     for g in range(IRREPS):
-        rows = amp_ref.at[pl.ds(g * CLS, CLS)]
-        copies.append(pltpu.make_async_copy(rows.at[:, h ^ g], outs[g // per].at[g % per], sems.at[g]))
-        copies.append(pltpu.make_async_copy(rows.at[:, h], own_ref.at[g], own_sems.at[g]))
+        source = amp_ref.at[pl.ds(g * CLS, CLS), h ^ g]
+        copies.append(pltpu.make_async_copy(source, tiles_ref.at[g], tile_sems.at[g]))
     for copy in copies:
         copy.start()
     for copy in copies:
         copy.wait()
 
 
-def pack_tiles(amplitudes, token, pieces):
-    shape = (IRREPS, CLS, 128, 128)
-    piece = jax.ShapeDtypeStruct((IRREPS // pieces, CLS, 128, 128), BF16)
+def cut_to_send(cholesky, amplitudes):
+    chunk = jax.ShapeDtypeStruct((256, 128), BF16)
     outs = pl.pallas_call(
-        pack_kernel,
-        out_shape=(jax.ShapeDtypeStruct(shape, BF16),) + (piece,) * pieces,
-        in_specs=[spec(pltpu.HBM), spec(pl.ANY)],
-        out_specs=(spec(pltpu.VMEM),) * (1 + pieces),
-        scratch_shapes=[pltpu.SemaphoreType.DMA((IRREPS,)), pltpu.SemaphoreType.DMA((IRREPS,))],
+        send_kernel,
+        out_shape=(chunk,) * 4 + (jax.ShapeDtypeStruct((IRREPS, CLS, 128, 128), BF16),),
+        in_specs=[spec(pltpu.HBM)] * 2,
+        out_specs=(spec(pltpu.VMEM),) * 5,
+        scratch_shapes=[pltpu.SemaphoreType.DMA((4,)), pltpu.SemaphoreType.DMA((IRREPS,))],
         compiler_params=params(46),
-        name="pack_tiles",
-    )(amplitudes, token)
-    return outs[0], outs[1:]
+        name="cut_to_send",
+    )(pltpu.with_memory_space_constraint(cholesky.reshape(2048, 128), pltpu.HBM), amplitudes)
+    return outs[:4], outs[4]
+
+
+def twist_kernel(mirror_ref, amp_ref, received_ref, own_ref, out_ref, sems):
+    h = place()[0]
+    copies = []
+    for g in range(IRREPS):
+        source = amp_ref.at[pl.ds(g * CLS, CLS), h]
+        copies.append(pltpu.make_async_copy(source, own_ref.at[g], sems.at[g]))
+        copies[-1].start()
+    for g in range(IRREPS):
+        for j in range(CLS):
+            out_ref[g, j] = received_ref[g, mirror_ref[g * CLS + j] - g * CLS].T
+    for copy in copies:
+        copy.wait()
+
+
+def twist_tiles(mirror, amplitudes, received):
+    shape = jax.ShapeDtypeStruct((IRREPS, CLS, 128, 128), BF16)
+    return pl.pallas_call(
+        twist_kernel,
+        out_shape=(shape, shape),
+        in_specs=[spec(pltpu.SMEM), spec(pltpu.HBM), spec(pltpu.VMEM)],
+        out_specs=(spec(pltpu.VMEM), spec(pltpu.VMEM)),
+        scratch_shapes=[pltpu.SemaphoreType.DMA((IRREPS,))],
+        compiler_params=params(46),
+        name="twist_tiles",
+    )(mirror, amplitudes, received)
 
 
 def rows_kernel(r0_ref, r1_ref, r2_ref, r3_ref, _, out_ref, all_ref):
@@ -163,16 +173,13 @@
     )(first, second, token)
 
 
-def stage1_kernel(classes, pieces, tokens, mirror_ref, mine_ref, other_ref, t_ref, *refs):
-    tp_refs, refs = refs[:pieces], refs[pieces + tokens :]
-    per = IRREPS // pieces
-    for x_ref, g in zip(refs, classes):
-        tp_ref = tp_refs[g // per].at[g % per]
+def stage1_kernel(classes, tokens, mine_ref, other_ref, t_ref, tp_ref, *refs):
+    for x_ref, g in zip(refs[tokens:], classes):
         for pair in range(4):
             j0, j1 = 2 * pair, 2 * pair + 1
-            twins = [tp_ref[mirror_ref[g * CLS + j] - g * CLS].T for j in (j0, j1)]
             upper = jnp.concatenate([t_ref[g, j0], t_ref[g, j1]], axis=1)
-            weights = jnp.concatenate([upper, jnp.concatenate(twins, axis=1)], axis=0)
+            lower = jnp.concatenate([tp_ref[g, j0], tp_ref[g, j1]], axis=1)
+            weights = jnp.concatenate([upper, lower], axis=0)
             for part in range(4):
                 own_ref = (mine_ref, other_ref)[part // 2]
                 own = own_ref[(part % 2) * 512 : (part % 2 + 1) * 512, :]
@@ -187,19 +194,17 @@
                         ]
 
 
-def stage1(classes, mirror, own, tiles, received, tokens=()):
+def stage1(classes, own, tiles, tokens=()):
     n = len(classes)
     return pl.pallas_call(
-        functools.partial(stage1_kernel, classes, len(received), len(tokens)),
+        functools.partial(stage1_kernel, classes, len(tokens)),
         out_shape=tuple(jax.ShapeDtypeStruct((256, 8192), BF16) for _ in classes),
-        in_specs=[spec(pltpu.SMEM)]
-        + [spec(pltpu.VMEM)] * (3 + len(received))
-        + [spec(pl.ANY)] * len(tokens),
+        in_specs=[spec(pltpu.VMEM)] * 4 + [spec(pl.ANY)] * len(tokens),
         out_specs=tuple(spec(pltpu.VMEM) for _ in classes),
         compiler_params=params(8),
         cost_estimate=pl.CostEstimate(flops=n * 2**30, transcendentals=0, bytes_accessed=n * 2**18),
         name="stage1_" + "_".join(str(g) for g in classes),
-    )(mirror, *own, tiles, *received, *tokens)
+    )(*own, *tiles, *tokens)
 
 
 def stage2_kernel(picks, n_b, carried, tokens, *refs):
@@ -273,19 +278,15 @@
     return jnp.transpose(out, (2, 0, 1))
 
 
-PIECES = 1
-
-
 def shards(cholesky, amplitudes, mirror):
-    chunks = cut_chunks(cholesky)
-    quarters = (chunks[0],) + tuple(over_y(chunks[k], k) for k in range(1, 4))
-    tiles, outgoing = pack_tiles(amplitudes, chunks[0], PIECES)
-    received = tuple(to_sibling(piece) for piece in outgoing)
-    mine = order_rows(quarters, tiles)
+    chunks, outgoing = cut_to_send(cholesky, amplitudes)
+    quarters = {k: over_y(chunks[k], k) for k in (2, 1, 3)}
+    tiles = twist_tiles(mirror, amplitudes, to_sibling(outgoing))
+    mine = order_rows((chunks[0], quarters[1], quarters[2], quarters[3]), tiles[1])
     own = (mine, to_sibling(mine))
 
     x1a, x1b, z0 = over_x(mine, 1, 1), over_x(mine, 3, 3), over_z(mine)
-    xc0, xc1, xc2, xc6, xc4 = stage1((0, 1, 2, 6, 4), mirror, own, tiles, received)
+    xc0, xc1, xc2, xc6, xc4 = stage1((0, 1, 2, 6, 4), own, tiles)
     (z0,) = relay((z0,), (xc0,))
     x1, forward = join(x1a, x1b, xc0)
     x1_other, z0_other = to_sibling(x1), to_sibling(z0)
@@ -300,10 +301,13 @@
     (x2,) = relay((x2,), (near,))
     x2_other = to_sibling(x2)
     zx2 = over_z(x2)
-    xc3, xc7, xc5 = stage1((3, 7, 5), mirror, own, tiles, received, (x2,))
-    zx1, zx2 = relay((zx1, zx2), (xc5,))
-    zx1_other, zx2_other = to_sibling(zx1), to_sibling(zx2)
-    far = stage2("far", (xc4,), (((0, None), (1, None)),), (x2, x2_other), (near,), (zx1,))
+    xc3, xc7 = stage1((3, 7), own, tiles, (x2,))
+    (zx1,) = relay((zx1,), (xc3,))
+    zx1_other = to_sibling(zx1)
+    (xc5,) = stage1((5,), own, tiles, (zx1, x2_other))
+    (zx2,) = relay((zx2,), (xc5,))
+    zx2_other = to_sibling(zx2)
+    far = stage2("far", (xc4,), (((0, None), (1, None)),), (x2, x2_other), (near,), (zx2,))
     last = stage2(
         "last",
         (xc3, xc7, xc5),
@@ -311,8 +315,8 @@
         (zx1, zx1_other, zx2, zx2_other),
         (far,),
     )
-    parts = [last] + [over_y(last[k], k) for k in range(1, 4)]
-    return finish((0, 1, 2, 6, 4, 3, 7, 5), parts)
+    parts = {k: over_y(last[k], k) for k in (2, 1, 3)}
+    return finish((0, 1, 2, 6, 4, 3, 7, 5), (last, parts[1], parts[2], parts[3]))
 
 
 def solution(mesh):

time: 58.2 us -> 54.6 us (0.938)
  waiting for transfers between devices: 11.6 us -> 7.11 us
  local copies, waits for them, and re-layouts: 1.06 us -> 0.02 us
  Pallas kernels: 23.7 us -> 24.7 us
  starting transfers between devices: 21.4 us -> 22.4 us
    ppermute x19, waiting for transfers between devices: 11.6 us -> 7.11 us  [permute(): return lax.ppermute(value, ('occ', 'vir'), pairs)]
    unnamed x4 -> x2, local copies, waits for them, and re-layouts: 1.05 us -> 0.01 us
    ppermute x19, starting transfers between devices: 21.4 us -> 22.4 us  [permute(): return lax.ppermute(value, ('occ', 'vir'), pairs)]
    pallas_call x4 -> x5, Pallas kernels: 13.4 us -> 14.3 us  [the longest x3 10 us: stage1(): pl.pallas_call(functools.partial(stage1_kernel, classes, len(tokens)), ou...]
  transfers between devices with their start and end apart: 19 -> 19, of which waited for: 8 -> 7; matrix products, arithmetic and copies ran while one was open for 0% -> 0% of each run, Pallas kernels for 29% -> 34%
where the time goes in v5:
time: 54.6 us; the launch traced here: 54.4 us
  Pallas kernels  24.7 us (45%)
  starting transfers between devices  22.4 us (41%)
  waiting for transfers between devices  7.11 us (13%)
    ppermute x19, starting transfers between devices, permute(): return lax.ppermute(value, ('occ', 'vir'), pairs)  22.4 us
    pallas_call x3, Pallas kernels, stage1(): pl.pallas_call(functools.partial(stage1_kernel, classes, len(tokens)), ou...  10 us
    pallas_call x3, Pallas kernels, stage2(): pl.pallas_call(functools.partial(stage2_kernel, picks, len(bs), len(carry...  9.32 us
    ppermute x19, waiting for transfers between devices, permute(): return lax.ppermute(value, ('occ', 'vir'), pairs)  7.11 us
    pallas_call x1, Pallas kernels, twist_tiles(): pl.pallas_call(twist_kernel, out_shape=(shape, shape), in_specs=[spec(plt...  2.63 us
    pallas_call x1, Pallas kernels, cut_to_send(): pl.pallas_call(send_kernel, out_shape=(chunk,) * 4 + (jax.ShapeDtypeStruc...  1.7 us
  transfers between devices with their start and end apart: 19, of which 7 were waited for; matrix products, arithmetic and copies ran while one was open for 0% of the time, Pallas kernels for 34%

profile of v5, /device:TPU:0, one launch (start us, length us, event | category | flops | bytes accessed | tf_op | source)
XLA Modules:
  0.0 54.4 jit_solution(3697581420436797577)
XLA Ops:
  0.0 1.7 %cut_to_send.1 = (bf16[256,128]{1,0:T(8,128)(2,1)S(1)}, bf16[256,128]{1,0:T(8,128)(2,1)S(1)}, bf16[256,128]{1,0:T(8,128)(2,1)S(1)}, bf16[256,128]{1,0:T(8,128)(2,1)S(1)}, bf16[8,8,128,128]{3,2,1,0:T(8,128)(2,1)S(1)}) custom-call(bf16[2048,128]{1,0:T(8,128)(2,1)} %bitcast.8, bf16[64,8,128,128]{3,2,1,0:T(8,128)(2,1)} %amp_ref.3), custom_call_target="tpu_custom_call" | custom-call | tf_op jit(solution)/shard_map/cut_to_send/pallas_call | solution.py:75
  1.8 1.7 %collective-permute-start = (bf16[256,128]{1,0:T(8,128)(2,1)S(1)}, bf16[256,128]{1,0:T(8,128)(2,1)S(1)}, u32[]{:S(2)}, u32[]{:S(2)}) collective-permute-start(bf16[256,128]{1,0:T(8,128)(2,1)S(1)} %get-tuple-element.22), channel_id=1, source_target_pairs={{0,1},{1,0},{2,3},{3,2},{4,5},{5,4},{6,7},{7,6},{8,9},{9,8},{10,11... | collective-permute-start | bytes 196616 | tf_op jit(solution)/shard_map/ppermute | solution.py:25
  3.5 2.9 %collective-permute-start.1 = (bf16[256,128]{1,0:T(8,128)(2,1)S(1)}, bf16[256,128]{1,0:T(8,128)(2,1)S(1)}, u32[]{:S(2)}, u32[]{:S(2)}) collective-permute-start(bf16[256,128]{1,0:T(8,128)(2,1)S(1)} %get-tuple-element.23), channel_id=1, source_target_pairs={{0,2},{1,3},{2,0},{3,1},{4,6},{5,7},{6,4},{7,5},{8,10},{9,11},{10,... | collective-permute-start | bytes 196616 | tf_op jit(solution)/shard_map/ppermute | solution.py:25
  6.6 2.6 %twist_tiles.1 = (bf16[8,8,128,128]{3,2,1,0:T(8,128)(2,1)S(1)}, bf16[8,8,128,128]{3,2,1,0:T(8,128)(2,1)S(1)}) custom-call(s32[64]{0:T(128)S(1)} %copy-done, bf16[64,8,128,128]{3,2,1,0:T(8,128)(2,1)} %amp_ref.3, bf16[8,8,128,128]{3,2,1,0:T(8,128)(2,1)S(1)} %collective-permute-done.3.received_ref), custom_call_target="tpu_custom_call" | custom-call | tf_op jit(solution)/shard_map/twist_tiles/pallas_call | solution.py:103
  9.2 1.0 %collective-permute-done.1.r2_ref = bf16[256,128]{1,0:T(8,128)(2,1)S(1)} collective-permute-done((bf16[256,128]{1,0:T(8,128)(2,1)S(1)}, bf16[256,128]{1,0:T(8,128)(2,1)S(1)}, u32[]{:S(2)}, u32[]{:S(2)}) %collective-permute-start.1) | collective-permute-done | bytes 65568 | tf_op jit(solution)/shard_map/ppermute | solution.py:25
  10.3 1.7 %collective-permute-done.2.r3_ref = bf16[256,128]{1,0:T(8,128)(2,1)S(1)} collective-permute-done((bf16[256,128]{1,0:T(8,128)(2,1)S(1)}, bf16[256,128]{1,0:T(8,128)(2,1)S(1)}, u32[]{:S(2)}, u32[]{:S(2)}) %collective-permute-start.2) | collective-permute-done | bytes 65568 | tf_op jit(solution)/shard_map/ppermute | solution.py:25
  12.1 1.6 %collective-permute-start.5 = (bf16[1024,128]{1,0:T(8,128)(2,1)S(1)}, bf16[1024,128]{1,0:T(8,128)(2,1)S(1)}, u32[]{:S(2)}, u32[]{:S(2)}) collective-permute-start(bf16[1024,128]{1,0:T(8,128)(2,1)S(1)} %order_rows.1.mine_ref.refs_4_), channel_id=1, source_target_pairs={{0,8},{1,9},{2,10},{3,11},{4,12},{5,13},{6,14},{7,15},{8,0},{9,1},... | collective-permute-start | bytes 786440 | tf_op jit(solution)/shard_map/ppermute | solution.py:25
  13.7 2.1 %collective-permute-start.6 = (bf16[1024,128]{1,0:T(8,128)(2,1)S(1)}, bf16[1024,128]{1,0:T(8,128)(2,1)S(1)}, u32[]{:S(2)}, u32[]{:S(2)}) collective-permute-start(bf16[1024,128]{1,0:T(8,128)(2,1)S(1)} %order_rows.1.mine_ref.refs_4_), channel_id=1, source_target_pairs={{0,24},{1,25},{2,26},{3,27},{4,28},{5,29},{6,30},{7,31},{8,16},{9,... | collective-permute-start | bytes 786440 | tf_op jit(solution)/shard_map/ppermute | solution.py:25
  15.8 1.9 %collective-permute-start.8 = (bf16[1024,128]{1,0:T(8,128)(2,1)S(1)}, bf16[1024,128]{1,0:T(8,128)(2,1)S(1)}, u32[]{:S(2)}, u32[]{:S(2)}) collective-permute-start(bf16[1024,128]{1,0:T(8,128)(2,1)S(1)} %order_rows.1.mine_ref.refs_4_), channel_id=1, source_target_pairs={{0,4},{1,5},{2,6},{3,7},{4,0},{5,1},{6,2},{7,3},{8,12},{9,13},{10,... | collective-permute-start | bytes 786440 | tf_op jit(solution)/shard_map/ppermute | solution.py:25
  17.7 6.1 %stage1_0_1_2_6_4.1 = (bf16[256,8192]{1,0:T(8,128)(2,1)S(1)}, bf16[256,8192]{1,0:T(8,128)(2,1)S(1)}, bf16[256,8192]{1,0:T(8,128)(2,1)S(1)}, bf16[256,8192]{1,0:T(8,128)(2,1)S(1)}, bf16[256,8192]{1,0:T(8,128)(2,1)S(1)}) custom-call(bf16[1024,128]{1,0:T(8,128)(2,1)S(1)} %order_rows.1.mine_ref.refs_4_, ...), custom_call_target="tpu_custom_call" | custom-call | flops 5368709120 | bytes 1310720 | tf_op jit(solution)/shard_map/stage1_0_1_2_6_4/pallas_call | solution.py:199
  23.9 1.8 %collective-permute-start.10 = (bf16[2,1024,128]{2,1,0:T(8,128)(2,1)S(1)}, bf16[2,1024,128]{2,1,0:T(8,128)(2,1)S(1)}, u32[]{:S(2)}, u32[]{:S(2)}) collective-permute-start(bf16[2,1024,128]{2,1,0:T(8,128)(2,1)S(1)} %get-tuple-element.33.refs_8_), channel_id=1, source_target_pairs={{0,32},{1,33},{2,34},{3,35},{4,36},{5,37},{6,38},{7,39},{8,40},{9,... | collective-permute-start | bytes 1572872 | tf_op jit(solution)/shard_map/ppermute | solution.py:25
  25.8 2.1 %collective-permute-start.7 = (bf16[1024,128]{1,0:T(8,128)(2,1)S(1)}, bf16[1024,128]{1,0:T(8,128)(2,1)S(1)}, u32[]{:S(2)}, u32[]{:S(2)}) collective-permute-start(bf16[1024,128]{1,0:T(8,128)(2,1)S(1)} %get-tuple-element.29), channel_id=1, source_target_pairs={{0,24},{1,25},{2,26},{3,27},{4,28},{5,29},{6,30},{7,31},{8,16},{9,... | collective-permute-start | bytes 786440 | tf_op jit(solution)/shard_map/ppermute | solution.py:25
  27.9 4.6 %stage2_near.1.refs_1_.refs_3_ = f32[4,64,128]{2,1,0:T(8,128)S(1)} custom-call(bf16[256,8192]{1,0:T(8,128)(2,1)S(1)} %get-tuple-element.28._.refs_1_.refs_0_, bf16[256,8192]{1,0:T(8,128)(2,1)S(1)} %get-tuple-element.30.refs_1_, bf16[256,8192]{1,0:T(8,128)(2,1)S(1)} %get-tuple-element.31.refs_2_, bf16[256,8192]{1,0:T(8,128)(2,1)S(1)} %get-tuple-element.32.refs_3_, ...), custom_call_target="tpu_custom_call" | custom-call | flops 4294967296 | bytes 1048576 | tf_op jit(solution)/shard_map/stage2_near/pallas_call | solution.py:243
  32.5 1.0 %collective-permute-done.7.refs_0_ = bf16[1024,128]{1,0:T(8,128)(2,1)S(1)} collective-permute-done((bf16[1024,128]{1,0:T(8,128)(2,1)S(1)}, bf16[1024,128]{1,0:T(8,128)(2,1)S(1)}, u32[]{:S(2)}, u32[]{:S(2)}) %collective-permute-start.7) | collective-permute-done | bytes 262176 | tf_op jit(solution)/shard_map/ppermute | solution.py:25
  33.6 1.9 %collective-permute-start.14 = (bf16[1024,128]{1,0:T(8,128)(2,1)S(1)}, bf16[1024,128]{1,0:T(8,128)(2,1)S(1)}, u32[]{:S(2)}, u32[]{:S(2)}) collective-permute-start(bf16[1024,128]{1,0:T(8,128)(2,1)S(1)} %relay.5.refs_0_.refs_1_), channel_id=1, source_target_pairs={{0,4},{1,5},{2,6},{3,7},{4,0},{5,1},{6,2},{7,3},{8,12},{9,13},{10,... | collective-permute-start | bytes 786440 | tf_op jit(solution)/shard_map/ppermute | solution.py:25
  35.4 2.5 %stage1_3_7.1 = (bf16[256,8192]{1,0:T(8,128)(2,1)S(1)}, bf16[256,8192]{1,0:T(8,128)(2,1)S(1)}) custom-call(bf16[1024,128]{1,0:T(8,128)(2,1)S(1)} %order_rows.1.mine_ref.refs_4_, bf16[1024,128]{1,0:T(8,128)(2,1)S(1)} %collective-permute-done.4.other_ref.refs_5_, bf16[8,8,128,128]{3,2,1,0:T(8,128)(2,1)S(1)} %get-tuple-element.27.t_ref, ...), custom_call_target="tpu_custom_call" | custom-call | flops 2147483648 | bytes 524288 | tf_op jit(solution)/shard_map/stage1_3_7/pallas_call | solution.py:199
  38.0 1.1 %collective-permute-start.13 = (bf16[2,1024,128]{2,1,0:T(8,128)(2,1)S(1)}, bf16[2,1024,128]{2,1,0:T(8,128)(2,1)S(1)}, u32[]{:S(2)}, u32[]{:S(2)}) collective-permute-start(bf16[2,1024,128]{2,1,0:T(8,128)(2,1)S(1)} %relay.6.refs_0_.refs_3_), channel_id=1, source_target_pairs={{0,32},{1,33},{2,34},{3,35},{4,36},{5,37},{6,38},{7,39},{8,40},{9,... | collective-permute-start | bytes 1572872 | tf_op jit(solution)/shard_map/ppermute | solution.py:25
  39.1 1.3 %stage1_5.1.refs_1_.refs_2_ = bf16[256,8192]{1,0:T(8,128)(2,1)S(1)} custom-call(bf16[1024,128]{1,0:T(8,128)(2,1)S(1)} %order_rows.1.mine_ref.refs_4_, bf16[1024,128]{1,0:T(8,128)(2,1)S(1)} %collective-permute-done.4.other_ref.refs_5_, bf16[8,8,128,128]{3,2,1,0:T(8,128)(2,1)S(1)} %get-tuple-element.27.t_ref, ...), custom_call_target="tpu_custom_call" | custom-call | flops 1073741824 | bytes 262144 | tf_op jit(solution)/shard_map/stage1_5/pallas_call | solution.py:199
  40.6 1.2 %stage2_far.1.refs_7_ = f32[4,64,160]{2,1,0:T(8,128)S(1)} custom-call(bf16[256,8192]{1,0:T(8,128)(2,1)S(1)} %get-tuple-element.36.refs_0_, bf16[1024,128]{1,0:T(8,128)(2,1)S(1)} %relay.5.refs_0_.refs_1_, bf16[1024,128]{1,0:T(8,128)(2,1)S(1)} %collective-permute-done.12.refs_1_.refs_2_, f32[4,64,128]{2,1,0:T(8,128)S(1)} %stage2_near.1.refs_1_.refs_3_, ...), custom_call_target="tpu_custom_call" | custom-call | flops 1073741824 | bytes 262144 | tf_op jit(solution)/shard_map/stage2_far/pallas_call | solution.py:243
  42.1 3.5 %stage2_last.1.own_ref = f32[4,64,256]{2,1,0:T(8,128)S(1)} custom-call(bf16[256,8192]{1,0:T(8,128)(2,1)S(1)} %get-tuple-element.34.refs_1_.refs_0_, bf16[256,8192]{1,0:T(8,128)(2,1)S(1)} %get-tuple-element.35.refs_1_, bf16[256,8192]{1,0:T(8,128)(2,1)S(1)} %stage1_5.1.refs_1_.refs_2_, bf16[2,1024,128]{2,1,0:T(8,128)(2,1)S(1)} %relay.6.refs_0_.refs_3_, ...), custom_call_target="tpu_custom_call" | custom-call | flops 3221225472 | bytes 786432 | tf_op jit(solution)/shard_map/stage2_last/pallas_call | solution.py:243
  45.7 2.3 %collective-permute-start.17 = (f32[64,256]{1,0:T(8,128)S(1)}, f32[64,256]{1,0:T(8,128)S(1)}, u32[]{:S(2)}, u32[]{:S(2)}) collective-permute-start(f32[64,256]{1,0:T(8,128)S(1)} %get-tuple-element.38), channel_id=1, source_target_pairs={{0,2},{1,3},{2,0},{3,1},{4,6},{5,7},{6,4},{7,5},{8,10},{9,11},{10,... | collective-permute-start | bytes 196616 | tf_op jit(solution)/shard_map/ppermute | solution.py:25
  48.0 2.4 %collective-permute-start.18 = (f32[64,256]{1,0:T(8,128)S(1)}, f32[64,256]{1,0:T(8,128)S(1)}, u32[]{:S(2)}, u32[]{:S(2)}) collective-permute-start(f32[64,256]{1,0:T(8,128)S(1)} %get-tuple-element.37), channel_id=1, source_target_pairs={{0,3},{1,2},{2,1},{3,0},{4,7},{5,6},{6,5},{7,4},{8,11},{9,10},{10,... | collective-permute-start | bytes 196616 | tf_op jit(solution)/shard_map/ppermute | solution.py:25
  50.6 1.1 %collective-permute-done.17.r2_ref = f32[64,256]{1,0:T(8,128)S(1)} collective-permute-done((f32[64,256]{1,0:T(8,128)S(1)}, f32[64,256]{1,0:T(8,128)S(1)}, u32[]{:S(2)}, u32[]{:S(2)}) %collective-permute-start.17) | collective-permute-done | bytes 65568 | tf_op jit(solution)/shard_map/ppermute | solution.py:25
  51.7 1.8 %collective-permute-done.18.r3_ref = f32[64,256]{1,0:T(8,128)S(1)} collective-permute-done((f32[64,256]{1,0:T(8,128)S(1)}, f32[64,256]{1,0:T(8,128)S(1)}, u32[]{:S(2)}, u32[]{:S(2)}) %collective-permute-start.18) | collective-permute-done | bytes 65568 | tf_op jit(solution)/shard_map/ppermute | solution.py:25
  (32 shorter events, 2.2 us)
Async XLA Ops:
  0.0 6.6 %copy-start = (s32[64]{0:T(128)S(1)}, s32[64]{0:T(128)}, u32[]{:S(2)}) copy-start(s32[64]{0:T(128)} %mirror_ref.1) | copy-start | bytes 772
  1.7 4.9 %collective-permute-start.3 = (bf16[8,8,128,128]{3,2,1,0:T(8,128)(2,1)S(1)}, bf16[8,8,128,128]{3,2,1,0:T(8,128)(2,1)S(1)}, u32[]{:S(2)}, u32[]{:S(2)}) collective-permute-start(bf16[8,8,128,128]{3,2,1,0:T(8,128)(2,1)S(1)} %get-tuple-element.25), channel_id=1, source_target_pairs={{0,32},{1,33},{2,34},{3,35},{4,36},{5,37},{6,38},{7,39},{8,40},{9,... | collective-permute-start | bytes 6291464 | tf_op jit(solution)/shard_map/ppermute | solution.py:25
  1.8 7.4 %collective-permute-start = (bf16[256,128]{1,0:T(8,128)(2,1)S(1)}, bf16[256,128]{1,0:T(8,128)(2,1)S(1)}, u32[]{:S(2)}, u32[]{:S(2)}) collective-permute-start(bf16[256,128]{1,0:T(8,128)(2,1)S(1)} %get-tuple-element.22), channel_id=1, source_target_pairs={{0,1},{1,0},{2,3},{3,2},{4,5},{5,4},{6,7},{7,6},{8,9},{9,8},{10,11... | collective-permute-start | bytes 196616 | tf_op jit(solution)/shard_map/ppermute | solution.py:25
  3.5 6.7 %collective-permute-start.1 = (bf16[256,128]{1,0:T(8,128)(2,1)S(1)}, bf16[256,128]{1,0:T(8,128)(2,1)S(1)}, u32[]{:S(2)}, u32[]{:S(2)}) collective-permute-start(bf16[256,128]{1,0:T(8,128)(2,1)S(1)} %get-tuple-element.23), channel_id=1, source_target_pairs={{0,2},{1,3},{2,0},{3,1},{4,6},{5,7},{6,4},{7,5},{8,10},{9,11},{10,... | collective-permute-start | bytes 196616 | tf_op jit(solution)/shard_map/ppermute | solution.py:25
  6.4 5.5 %collective-permute-start.2 = (bf16[256,128]{1,0:T(8,128)(2,1)S(1)}, bf16[256,128]{1,0:T(8,128)(2,1)S(1)}, u32[]{:S(2)}, u32[]{:S(2)}) collective-permute-start(bf16[256,128]{1,0:T(8,128)(2,1)S(1)} %get-tuple-element.24), channel_id=1, source_target_pairs={{0,3},{1,2},{2,1},{3,0},{4,7},{5,6},{6,5},{7,4},{8,11},{9,10},{10,... | collective-permute-start | bytes 196616 | tf_op jit(solution)/shard_map/ppermute | solution.py:25
  12.0 5.7 %collective-permute-start.4 = (bf16[1024,128]{1,0:T(8,128)(2,1)S(1)}, bf16[1024,128]{1,0:T(8,128)(2,1)S(1)}, u32[]{:S(2)}, u32[]{:S(2)}) collective-permute-start(bf16[1024,128]{1,0:T(8,128)(2,1)S(1)} %order_rows.1.mine_ref.refs_4_), channel_id=1, source_target_pairs={{0,32},{1,33},{2,34},{3,35},{4,36},{5,37},{6,38},{7,39},{8,40},{9,... | collective-permute-start | bytes 786440 | tf_op jit(solution)/shard_map/ppermute | solution.py:25
  12.1 11.7 %collective-permute-start.5 = (bf16[1024,128]{1,0:T(8,128)(2,1)S(1)}, bf16[1024,128]{1,0:T(8,128)(2,1)S(1)}, u32[]{:S(2)}, u32[]{:S(2)}) collective-permute-start(bf16[1024,128]{1,0:T(8,128)(2,1)S(1)} %order_rows.1.mine_ref.refs_4_), channel_id=1, source_target_pairs={{0,8},{1,9},{2,10},{3,11},{4,12},{5,13},{6,14},{7,15},{8,0},{9,1},... | collective-permute-start | bytes 786440 | tf_op jit(solution)/shard_map/ppermute | solution.py:25
  13.7 10.2 %collective-permute-start.6 = (bf16[1024,128]{1,0:T(8,128)(2,1)S(1)}, bf16[1024,128]{1,0:T(8,128)(2,1)S(1)}, u32[]{:S(2)}, u32[]{:S(2)}) collective-permute-start(bf16[1024,128]{1,0:T(8,128)(2,1)S(1)} %order_rows.1.mine_ref.refs_4_), channel_id=1, source_target_pairs={{0,24},{1,25},{2,26},{3,27},{4,28},{5,29},{6,30},{7,31},{8,16},{9,... | collective-permute-start | bytes 786440 | tf_op jit(solution)/shard_map/ppermute | solution.py:25
  15.8 9.9 %collective-permute-start.8 = (bf16[1024,128]{1,0:T(8,128)(2,1)S(1)}, bf16[1024,128]{1,0:T(8,128)(2,1)S(1)}, u32[]{:S(2)}, u32[]{:S(2)}) collective-permute-start(bf16[1024,128]{1,0:T(8,128)(2,1)S(1)} %order_rows.1.mine_ref.refs_4_), channel_id=1, source_target_pairs={{0,4},{1,5},{2,6},{3,7},{4,0},{5,1},{6,2},{7,3},{8,12},{9,13},{10,... | collective-permute-start | bytes 786440 | tf_op jit(solution)/shard_map/ppermute | solution.py:25
  23.9 4.0 %collective-permute-start.10 = (bf16[2,1024,128]{2,1,0:T(8,128)(2,1)S(1)}, bf16[2,1024,128]{2,1,0:T(8,128)(2,1)S(1)}, u32[]{:S(2)}, u32[]{:S(2)}) collective-permute-start(bf16[2,1024,128]{2,1,0:T(8,128)(2,1)S(1)} %get-tuple-element.33.refs_8_), channel_id=1, source_target_pairs={{0,32},{1,33},{2,34},{3,35},{4,36},{5,37},{6,38},{7,39},{8,40},{9,... | collective-permute-start | bytes 1572872 | tf_op jit(solution)/shard_map/ppermute | solution.py:25
  25.7 2.2 %collective-permute-start.9 = (bf16[1024,128]{1,0:T(8,128)(2,1)S(1)}, bf16[1024,128]{1,0:T(8,128)(2,1)S(1)}, u32[]{:S(2)}, u32[]{:S(2)}) collective-permute-start(bf16[1024,128]{1,0:T(8,128)(2,1)S(1)} %relay.4.refs_6_), channel_id=1, source_target_pairs={{0,32},{1,33},{2,34},{3,35},{4,36},{5,37},{6,38},{7,39},{8,40},{9,... | collective-permute-start | bytes 786440 | tf_op jit(solution)/shard_map/ppermute | solution.py:25
  25.8 12.2 %collective-permute-start.11 = (bf16[2,1024,128]{2,1,0:T(8,128)(2,1)S(1)}, bf16[2,1024,128]{2,1,0:T(8,128)(2,1)S(1)}, u32[]{:S(2)}, u32[]{:S(2)}) collective-permute-start(bf16[2,1024,128]{2,1,0:T(8,128)(2,1)S(1)} %get-tuple-element.33.refs_8_), channel_id=1, source_target_pairs={{0,4},{1,5},{2,6},{3,7},{4,0},{5,1},{6,2},{7,3},{8,12},{9,13},{10,... | collective-permute-start | bytes 1572872 | tf_op jit(solution)/shard_map/ppermute | solution.py:25
  25.8 7.7 %collective-permute-start.7 = (bf16[1024,128]{1,0:T(8,128)(2,1)S(1)}, bf16[1024,128]{1,0:T(8,128)(2,1)S(1)}, u32[]{:S(2)}, u32[]{:S(2)}) collective-permute-start(bf16[1024,128]{1,0:T(8,128)(2,1)S(1)} %get-tuple-element.29), channel_id=1, source_target_pairs={{0,24},{1,25},{2,26},{3,27},{4,28},{5,29},{6,30},{7,31},{8,16},{9,... | collective-permute-start | bytes 786440 | tf_op jit(solution)/shard_map/ppermute | solution.py:25
  33.6 5.6 %collective-permute-start.12 = (bf16[1024,128]{1,0:T(8,128)(2,1)S(1)}, bf16[1024,128]{1,0:T(8,128)(2,1)S(1)}, u32[]{:S(2)}, u32[]{:S(2)}) collective-permute-start(bf16[1024,128]{1,0:T(8,128)(2,1)S(1)} %relay.5.refs_0_.refs_1_), channel_id=1, source_target_pairs={{0,32},{1,33},{2,34},{3,35},{4,36},{5,37},{6,38},{7,39},{8,40},{9,... | collective-permute-start | bytes 786440 | tf_op jit(solution)/shard_map/ppermute | solution.py:25
  33.6 6.9 %collective-permute-start.14 = (bf16[1024,128]{1,0:T(8,128)(2,1)S(1)}, bf16[1024,128]{1,0:T(8,128)(2,1)S(1)}, u32[]{:S(2)}, u32[]{:S(2)}) collective-permute-start(bf16[1024,128]{1,0:T(8,128)(2,1)S(1)} %relay.5.refs_0_.refs_1_), channel_id=1, source_target_pairs={{0,4},{1,5},{2,6},{3,7},{4,0},{5,1},{6,2},{7,3},{8,12},{9,13},{10,... | collective-permute-start | bytes 786440 | tf_op jit(solution)/shard_map/ppermute | solution.py:25
  38.0 3.8 %collective-permute-start.13 = (bf16[2,1024,128]{2,1,0:T(8,128)(2,1)S(1)}, bf16[2,1024,128]{2,1,0:T(8,128)(2,1)S(1)}, u32[]{:S(2)}, u32[]{:S(2)}) collective-permute-start(bf16[2,1024,128]{2,1,0:T(8,128)(2,1)S(1)} %relay.6.refs_0_.refs_3_), channel_id=1, source_target_pairs={{0,32},{1,33},{2,34},{3,35},{4,36},{5,37},{6,38},{7,39},{8,40},{9,... | collective-permute-start | bytes 1572872 | tf_op jit(solution)/shard_map/ppermute | solution.py:25
  40.5 1.6 %collective-permute-start.15 = (bf16[1024,128]{1,0:T(8,128)(2,1)S(1)}, bf16[1024,128]{1,0:T(8,128)(2,1)S(1)}, u32[]{:S(2)}, u32[]{:S(2)}) collective-permute-start(bf16[1024,128]{1,0:T(8,128)(2,1)S(1)} %relay.7.refs_4_.refs_5_), channel_id=1, source_target_pairs={{0,32},{1,33},{2,34},{3,35},{4,36},{5,37},{6,38},{7,39},{8,40},{9,... | collective-permute-start | bytes 786440 | tf_op jit(solution)/shard_map/ppermute | solution.py:25
  45.6 5.0 %collective-permute-start.16 = (f32[64,256]{1,0:T(8,128)S(1)}, f32[64,256]{1,0:T(8,128)S(1)}, u32[]{:S(2)}, u32[]{:S(2)}) collective-permute-start(f32[64,256]{1,0:T(8,128)S(1)} %get-tuple-element.39), channel_id=1, source_target_pairs={{0,1},{1,0},{2,3},{3,2},{4,5},{5,4},{6,7},{7,6},{8,9},{9,8},{10,11... | collective-permute-start | bytes 196616 | tf_op jit(solution)/shard_map/ppermute | solution.py:25
  45.7 6.0 %collective-permute-start.17 = (f32[64,256]{1,0:T(8,128)S(1)}, f32[64,256]{1,0:T(8,128)S(1)}, u32[]{:S(2)}, u32[]{:S(2)}) collective-permute-start(f32[64,256]{1,0:T(8,128)S(1)} %get-tuple-element.38), channel_id=1, source_target_pairs={{0,2},{1,3},{2,0},{3,1},{4,6},{5,7},{6,4},{7,5},{8,10},{9,11},{10,... | collective-permute-start | bytes 196616 | tf_op jit(solution)/shard_map/ppermute | solution.py:25
  48.0 5.5 %collective-permute-start.18 = (f32[64,256]{1,0:T(8,128)S(1)}, f32[64,256]{1,0:T(8,128)S(1)}, u32[]{:S(2)}, u32[]{:S(2)}) collective-permute-start(f32[64,256]{1,0:T(8,128)S(1)} %get-tuple-element.37), channel_id=1, source_target_pairs={{0,3},{1,2},{2,1},{3,0},{4,7},{5,6},{6,5},{7,4},{8,11},{9,10},{10,... | collective-permute-start | bytes 196616 | tf_op jit(solution)/shard_map/ppermute | solution.py:25

commit v6 on v5

--- a/solution.py
+++ b/solution.py
@@ -27,6 +27,10 @@
 
 def over_y(value, k):
     return permute(value, lambda occ, vir: (occ, vir ^ k))
+
+
+def over_ring(value, even, odd):
+    return permute(value, lambda occ, vir: (occ, vir ^ (odd if occ & 1 else even)))
 
 
 def over_x(value, even, odd):
@@ -212,8 +216,9 @@
     x_refs, refs = refs[:n], refs[n:]
     b_refs, refs = refs[:n_b], refs[n_b:]
     carry, refs = refs[:carried], refs[carried:]
-    out_ref, r_s = refs[tokens:]
-    y = place()[1]
+    *outs, r_s = refs[tokens:]
+    out_ref = outs[0]
+    _, y, core = place()
     for i, halves in enumerate(picks):
         total = None
         for half, (at, index) in enumerate(halves):
@@ -235,25 +240,49 @@
                 jnp.concatenate([r[j * 32 + q * 8 : j * 32 + q * 8 + 8] for j in range(CLS)], axis=0)
             )
         out_ref[q ^ y] = jnp.concatenate(columns, axis=1) if len(columns) > 1 else columns[0]
-
-
-def stage2(name, xs, picks, bs, carry=(), tokens=()):
+    if len(outs) > 1:
+        outs[1][0] = out_ref[1 + 2 * core]
+        outs[1][1] = out_ref[2]
+        outs[2][...] = out_ref[3 - 2 * core]
+
+
+def stage2(name, xs, picks, bs, carry=(), tokens=(), split=False):
     n = len(xs)
     lanes = 32 * n + sum(c.shape[2] for c in carry)
-    return pl.pallas_call(
+    shapes = tuple(
+        jax.ShapeDtypeStruct(shape, F32)
+        for shape in ((4, 64, lanes), (2, 64, lanes), (64, lanes))[: 3 if split else 1]
+    )
+    outs = pl.pallas_call(
         functools.partial(stage2_kernel, picks, len(bs), len(carry), len(tokens)),
-        out_shape=jax.ShapeDtypeStruct((4, 64, lanes), F32),
+        out_shape=shapes,
         in_specs=[spec(pltpu.VMEM)] * (n + len(bs) + len(carry)) + [spec(pl.ANY)] * len(tokens),
-        out_specs=spec(pltpu.VMEM),
+        out_specs=tuple(spec(pltpu.VMEM) for _ in shapes),
         scratch_shapes=[pltpu.VMEM((n, 256, 32), F32)],
         compiler_params=params(8),
         cost_estimate=pl.CostEstimate(flops=n * 2**30, transcendentals=0, bytes_accessed=n * 2**18),
         name="stage2_" + name,
     )(*xs, *bs, *carry, *tokens)
-
-
-def finish_kernel(order, own_ref, r1_ref, r2_ref, r3_ref, out_ref, sum_s, pos_s):
-    total = own_ref[0] + r1_ref[...] + r2_ref[...] + r3_ref[...]
+    return outs if split else outs[0]
+
+
+def pass_kernel(held_ref, first_ref, out_ref):
+    out_ref[...] = held_ref[...] + first_ref[1]
+
+
+def pass_on(held, first):
+    return pl.pallas_call(
+        pass_kernel,
+        out_shape=jax.ShapeDtypeStruct(held.shape, F32),
+        in_specs=[spec(pltpu.VMEM)] * 2,
+        out_specs=spec(pltpu.VMEM),
+        compiler_params=params(2),
+        name="pass_on",
+    )(held, first)
+
+
+def finish_kernel(order, own_ref, first_ref, second_ref, out_ref, sum_s, pos_s):
+    total = own_ref[0] + first_ref[0] + second_ref[...]
     sum_s[0] = total[:, 0:128]
     sum_s[1] = total[:, 128:256]
     for a8 in range(8):
@@ -269,7 +298,7 @@
     out = pl.pallas_call(
         functools.partial(finish_kernel, order),
         out_shape=jax.ShapeDtypeStruct((8, 32, ROWS), F32),
-        in_specs=[spec(pltpu.VMEM)] * 4,
+        in_specs=[spec(pltpu.VMEM)] * 3,
         out_specs=spec(pltpu.VMEM),
         scratch_shapes=[pltpu.VMEM((2, 64, 128), F32), pltpu.VMEM((ROWS, 256), F32)],
         compiler_params=params(6),
@@ -308,15 +337,17 @@
     (zx2,) = relay((zx2,), (xc5,))
     zx2_other = to_sibling(zx2)
     far = stage2("far", (xc4,), (((0, None), (1, None)),), (x2, x2_other), (near,), (zx2,))
-    last = stage2(
+    last, offer, held = stage2(
         "last",
         (xc3, xc7, xc5),
         (((0, 0), (1, 0)), ((0, 1), (1, 1)), ((2, None), (3, None))),
         (zx1, zx1_other, zx2, zx2_other),
         (far,),
+        split=True,
     )
-    parts = {k: over_y(last[k], k) for k in (2, 1, 3)}
-    return finish((0, 1, 2, 6, 4, 3, 7, 5), (last, parts[1], parts[2], parts[3]))
+    first = over_ring(offer, 1, 3)
+    second = over_ring(pass_on(held, first), 3, 1)
+    return finish((0, 1, 2, 6, 4, 3, 7, 5), (last, first, second))
 
 
 def solution(mesh):

time: 54.6 us -> 57.3 us (1.049)
  waiting for transfers between devices: 7.11 us -> 13.6 us
  starting transfers between devices: 22.4 us -> 18.6 us
    ppermute x19 -> x18, waiting for transfers between devices: 7.11 us -> 13.6 us  [permute(): return lax.ppermute(value, ('occ', 'vir'), pairs)]
    ppermute x19 -> x18, starting transfers between devices: 22.4 us -> 18.6 us  [permute(): return lax.ppermute(value, ('occ', 'vir'), pairs)]
  transfers between devices with their start and end apart: 19 -> 18, of which waited for: 7 -> 6; matrix products, arithmetic and copies ran while one was open for 0% -> 0% of each run, Pallas kernels for 34% -> 32%
where the time goes in v6:
time: 57.3 us; the launch traced here: 57.1 us
  Pallas kernels  24.7 us (43%)
  starting transfers between devices  18.6 us (32%)
  waiting for transfers between devices  13.6 us (24%)
    ppermute x18, starting transfers between devices, permute(): return lax.ppermute(value, ('occ', 'vir'), pairs)  18.6 us
    ppermute x18, waiting for transfers between devices, permute(): return lax.ppermute(value, ('occ', 'vir'), pairs)  13.6 us
    pallas_call x3, Pallas kernels, stage1(): pl.pallas_call(functools.partial(stage1_kernel, classes, len(tokens)), ou...  10 us
    pallas_call x3, Pallas kernels, stage2(): pl.pallas_call(functools.partial(stage2_kernel, picks, len(bs), len(carry...  9.33 us
    pallas_call x1, Pallas kernels, twist_tiles(): pl.pallas_call(twist_kernel, out_shape=(shape, shape), in_specs=[spec(plt...  2.63 us
    pallas_call x1, Pallas kernels, cut_to_send(): pl.pallas_call(send_kernel, out_shape=(chunk,) * 4 + (jax.ShapeDtypeStruc...  1.7 us
  transfers between devices with their start and end apart: 18, of which 6 were waited for; matrix products, arithmetic and copies ran while one was open for 0% of the time, Pallas kernels for 32%

profile of v6, /device:TPU:0, one launch (start us, length us, event | category | flops | bytes accessed | tf_op | source)
XLA Modules:
  0.0 57.1 jit_solution(15745015350037121931)
XLA Ops:
  0.0 1.7 %cut_to_send.1 = (bf16[256,128]{1,0:T(8,128)(2,1)S(1)}, bf16[256,128]{1,0:T(8,128)(2,1)S(1)}, bf16[256,128]{1,0:T(8,128)(2,1)S(1)}, bf16[256,128]{1,0:T(8,128)(2,1)S(1)}, bf16[8,8,128,128]{3,2,1,0:T(8,128)(2,1)S(1)}) custom-call(bf16[2048,128]{1,0:T(8,128)(2,1)} %bitcast.2, bf16[64,8,128,128]{3,2,1,0:T(8,128)(2,1)} %amp_ref.3), custom_call_target="tpu_custom_call" | custom-call | tf_op jit(solution)/shard_map/cut_to_send/pallas_call | solution.py:79
  1.8 1.7 %collective-permute-start = (bf16[256,128]{1,0:T(8,128)(2,1)S(1)}, bf16[256,128]{1,0:T(8,128)(2,1)S(1)}, u32[]{:S(2)}, u32[]{:S(2)}) collective-permute-start(bf16[256,128]{1,0:T(8,128)(2,1)S(1)} %get-tuple-element.25), channel_id=1, source_target_pairs={{0,1},{1,0},{2,3},{3,2},{4,5},{5,4},{6,7},{7,6},{8,9},{9,8},{10,11... | collective-permute-start | bytes 196616 | tf_op jit(solution)/shard_map/ppermute | solution.py:25
  3.5 2.9 %collective-permute-start.1 = (bf16[256,128]{1,0:T(8,128)(2,1)S(1)}, bf16[256,128]{1,0:T(8,128)(2,1)S(1)}, u32[]{:S(2)}, u32[]{:S(2)}) collective-permute-start(bf16[256,128]{1,0:T(8,128)(2,1)S(1)} %get-tuple-element.26), channel_id=1, source_target_pairs={{0,2},{1,3},{2,0},{3,1},{4,6},{5,7},{6,4},{7,5},{8,10},{9,11},{10,... | collective-permute-start | bytes 196616 | tf_op jit(solution)/shard_map/ppermute | solution.py:25
  6.6 2.6 %twist_tiles.1 = (bf16[8,8,128,128]{3,2,1,0:T(8,128)(2,1)S(1)}, bf16[8,8,128,128]{3,2,1,0:T(8,128)(2,1)S(1)}) custom-call(s32[64]{0:T(128)S(1)} %copy-done, bf16[64,8,128,128]{3,2,1,0:T(8,128)(2,1)} %amp_ref.3, bf16[8,8,128,128]{3,2,1,0:T(8,128)(2,1)S(1)} %collective-permute-done.3.received_ref), custom_call_target="tpu_custom_call" | custom-call | tf_op jit(solution)/shard_map/twist_tiles/pallas_call | solution.py:107
  9.2 1.0 %collective-permute-done.1.r2_ref = bf16[256,128]{1,0:T(8,128)(2,1)S(1)} collective-permute-done((bf16[256,128]{1,0:T(8,128)(2,1)S(1)}, bf16[256,128]{1,0:T(8,128)(2,1)S(1)}, u32[]{:S(2)}, u32[]{:S(2)}) %collective-permute-start.1) | collective-permute-done | bytes 65568 | tf_op jit(solution)/shard_map/ppermute | solution.py:25
  10.3 1.7 %collective-permute-done.2.r3_ref = bf16[256,128]{1,0:T(8,128)(2,1)S(1)} collective-permute-done((bf16[256,128]{1,0:T(8,128)(2,1)S(1)}, bf16[256,128]{1,0:T(8,128)(2,1)S(1)}, u32[]{:S(2)}, u32[]{:S(2)}) %collective-permute-start.2) | collective-permute-done | bytes 65568 | tf_op jit(solution)/shard_map/ppermute | solution.py:25
  12.1 1.6 %collective-permute-start.5 = (bf16[1024,128]{1,0:T(8,128)(2,1)S(1)}, bf16[1024,128]{1,0:T(8,128)(2,1)S(1)}, u32[]{:S(2)}, u32[]{:S(2)}) collective-permute-start(bf16[1024,128]{1,0:T(8,128)(2,1)S(1)} %order_rows.1.mine_ref.refs_4_), channel_id=1, source_target_pairs={{0,8},{1,9},{2,10},{3,11},{4,12},{5,13},{6,14},{7,15},{8,0},{9,1},... | collective-permute-start | bytes 786440 | tf_op jit(solution)/shard_map/ppermute | solution.py:25
  13.7 2.1 %collective-permute-start.6 = (bf16[1024,128]{1,0:T(8,128)(2,1)S(1)}, bf16[1024,128]{1,0:T(8,128)(2,1)S(1)}, u32[]{:S(2)}, u32[]{:S(2)}) collective-permute-start(bf16[1024,128]{1,0:T(8,128)(2,1)S(1)} %order_rows.1.mine_ref.refs_4_), channel_id=1, source_target_pairs={{0,24},{1,25},{2,26},{3,27},{4,28},{5,29},{6,30},{7,31},{8,16},{9,... | collective-permute-start | bytes 786440 | tf_op jit(solution)/shard_map/ppermute | solution.py:25
  15.8 1.9 %collective-permute-start.8 = (bf16[1024,128]{1,0:T(8,128)(2,1)S(1)}, bf16[1024,128]{1,0:T(8,128)(2,1)S(1)}, u32[]{:S(2)}, u32[]{:S(2)}) collective-permute-start(bf16[1024,128]{1,0:T(8,128)(2,1)S(1)} %order_rows.1.mine_ref.refs_4_), channel_id=1, source_target_pairs={{0,4},{1,5},{2,6},{3,7},{4,0},{5,1},{6,2},{7,3},{8,12},{9,13},{10,... | collective-permute-start | bytes 786440 | tf_op jit(solution)/shard_map/ppermute | solution.py:25
  17.7 6.1 %stage1_0_1_2_6_4.1 = (bf16[256,8192]{1,0:T(8,128)(2,1)S(1)}, bf16[256,8192]{1,0:T(8,128)(2,1)S(1)}, bf16[256,8192]{1,0:T(8,128)(2,1)S(1)}, bf16[256,8192]{1,0:T(8,128)(2,1)S(1)}, bf16[256,8192]{1,0:T(8,128)(2,1)S(1)}) custom-call(bf16[1024,128]{1,0:T(8,128)(2,1)S(1)} %order_rows.1.mine_ref.refs_4_, ...), custom_call_target="tpu_custom_call" | custom-call | flops 5368709120 | bytes 1310720 | tf_op jit(solution)/shard_map/stage1_0_1_2_6_4/pallas_call | solution.py:203
  23.9 1.8 %collective-permute-start.10 = (bf16[2,1024,128]{2,1,0:T(8,128)(2,1)S(1)}, bf16[2,1024,128]{2,1,0:T(8,128)(2,1)S(1)}, u32[]{:S(2)}, u32[]{:S(2)}) collective-permute-start(bf16[2,1024,128]{2,1,0:T(8,128)(2,1)S(1)} %get-tuple-element.36.refs_8_), channel_id=1, source_target_pairs={{0,32},{1,33},{2,34},{3,35},{4,36},{5,37},{6,38},{7,39},{8,40},{9,... | collective-permute-start | bytes 1572872 | tf_op jit(solution)/shard_map/ppermute | solution.py:25
  25.8 2.1 %collective-permute-start.7 = (bf16[1024,128]{1,0:T(8,128)(2,1)S(1)}, bf16[1024,128]{1,0:T(8,128)(2,1)S(1)}, u32[]{:S(2)}, u32[]{:S(2)}) collective-permute-start(bf16[1024,128]{1,0:T(8,128)(2,1)S(1)} %get-tuple-element.32), channel_id=1, source_target_pairs={{0,24},{1,25},{2,26},{3,27},{4,28},{5,29},{6,30},{7,31},{8,16},{9,... | collective-permute-start | bytes 786440 | tf_op jit(solution)/shard_map/ppermute | solution.py:25
  27.9 4.6 %stage2_near.1.refs_1_.refs_3_ = f32[4,64,128]{2,1,0:T(8,128)S(1)} custom-call(bf16[256,8192]{1,0:T(8,128)(2,1)S(1)} %get-tuple-element.31._.refs_1_.refs_0_, bf16[256,8192]{1,0:T(8,128)(2,1)S(1)} %get-tuple-element.33.refs_1_, bf16[256,8192]{1,0:T(8,128)(2,1)S(1)} %get-tuple-element.34.refs_2_, bf16[256,8192]{1,0:T(8,128)(2,1)S(1)} %get-tuple-element.35.refs_3_, ...), custom_call_target="tpu_custom_call" | custom-call | flops 4294967296 | bytes 1048576 | tf_op jit(solution)/shard_map/stage2_near/pallas_call | solution.py:256
  32.5 1.0 %collective-permute-done.7.refs_0_ = bf16[1024,128]{1,0:T(8,128)(2,1)S(1)} collective-permute-done((bf16[1024,128]{1,0:T(8,128)(2,1)S(1)}, bf16[1024,128]{1,0:T(8,128)(2,1)S(1)}, u32[]{:S(2)}, u32[]{:S(2)}) %collective-permute-start.7) | collective-permute-done | bytes 262176 | tf_op jit(solution)/shard_map/ppermute | solution.py:25
  33.6 1.9 %collective-permute-start.14 = (bf16[1024,128]{1,0:T(8,128)(2,1)S(1)}, bf16[1024,128]{1,0:T(8,128)(2,1)S(1)}, u32[]{:S(2)}, u32[]{:S(2)}) collective-permute-start(bf16[1024,128]{1,0:T(8,128)(2,1)S(1)} %relay.5.refs_0_.refs_1_), channel_id=1, source_target_pairs={{0,4},{1,5},{2,6},{3,7},{4,0},{5,1},{6,2},{7,3},{8,12},{9,13},{10,... | collective-permute-start | bytes 786440 | tf_op jit(solution)/shard_map/ppermute | solution.py:25
  35.4 2.5 %stage1_3_7.1 = (bf16[256,8192]{1,0:T(8,128)(2,1)S(1)}, bf16[256,8192]{1,0:T(8,128)(2,1)S(1)}) custom-call(bf16[1024,128]{1,0:T(8,128)(2,1)S(1)} %order_rows.1.mine_ref.refs_4_, bf16[1024,128]{1,0:T(8,128)(2,1)S(1)} %collective-permute-done.4.other_ref.refs_5_, bf16[8,8,128,128]{3,2,1,0:T(8,128)(2,1)S(1)} %get-tuple-element.30.t_ref, ...), custom_call_target="tpu_custom_call" | custom-call | flops 2147483648 | bytes 524288 | tf_op jit(solution)/shard_map/stage1_3_7/pallas_call | solution.py:203
  38.0 1.1 %collective-permute-start.13 = (bf16[2,1024,128]{2,1,0:T(8,128)(2,1)S(1)}, bf16[2,1024,128]{2,1,0:T(8,128)(2,1)S(1)}, u32[]{:S(2)}, u32[]{:S(2)}) collective-permute-start(bf16[2,1024,128]{2,1,0:T(8,128)(2,1)S(1)} %relay.6.refs_0_.refs_3_), channel_id=1, source_target_pairs={{0,32},{1,33},{2,34},{3,35},{4,36},{5,37},{6,38},{7,39},{8,40},{9,... | collective-permute-start | bytes 1572872 | tf_op jit(solution)/shard_map/ppermute | solution.py:25
  39.1 1.3 %stage1_5.1.refs_1_.refs_2_ = bf16[256,8192]{1,0:T(8,128)(2,1)S(1)} custom-call(bf16[1024,128]{1,0:T(8,128)(2,1)S(1)} %order_rows.1.mine_ref.refs_4_, bf16[1024,128]{1,0:T(8,128)(2,1)S(1)} %collective-permute-done.4.other_ref.refs_5_, bf16[8,8,128,128]{3,2,1,0:T(8,128)(2,1)S(1)} %get-tuple-element.30.t_ref, ...), custom_call_target="tpu_custom_call" | custom-call | flops 1073741824 | bytes 262144 | tf_op jit(solution)/shard_map/stage1_5/pallas_call | solution.py:203
  40.6 1.2 %stage2_far.1.refs_7_ = f32[4,64,160]{2,1,0:T(8,128)S(1)} custom-call(bf16[256,8192]{1,0:T(8,128)(2,1)S(1)} %get-tuple-element.39.refs_0_, bf16[1024,128]{1,0:T(8,128)(2,1)S(1)} %relay.5.refs_0_.refs_1_, bf16[1024,128]{1,0:T(8,128)(2,1)S(1)} %collective-permute-done.12.refs_1_.refs_2_, f32[4,64,128]{2,1,0:T(8,128)S(1)} %stage2_near.1.refs_1_.refs_3_, ...), custom_call_target="tpu_custom_call" | custom-call | flops 1073741824 | bytes 262144 | tf_op jit(solution)/shard_map/stage2_far/pallas_call | solution.py:256
  42.1 3.5 %stage2_last.1 = (f32[4,64,256]{2,1,0:T(8,128)S(1)}, f32[2,64,256]{2,1,0:T(8,128)S(1)}, f32[64,256]{1,0:T(8,128)S(1)}) custom-call(bf16[256,8192]{1,0:T(8,128)(2,1)S(1)} %get-tuple-element.37.refs_1_.refs_0_, bf16[256,8192]{1,0:T(8,128)(2,1)S(1)} %get-tuple-element.38.refs_1_, bf16[256,8192]{1,0:T(8,128)(2,1)S(1)} %stage1_5.1.refs_1_.refs_2_, ...), custom_call_target="tpu_custom_call" | custom-call | flops 3221225472 | bytes 786432 | tf_op jit(solution)/shard_map/stage2_last/pallas_call | solution.py:256
  45.7 5.0 %collective-permute-done.16.first_ref = f32[2,64,256]{2,1,0:T(8,128)S(1)} collective-permute-done((f32[2,64,256]{2,1,0:T(8,128)S(1)}, f32[2,64,256]{2,1,0:T(8,128)S(1)}, u32[]{:S(2)}, u32[]{:S(2)}) %collective-permute-start.16) | collective-permute-done | bytes 131104 | tf_op jit(solution)/shard_map/ppermute | solution.py:25
  50.7 0.9 %collective-permute-start.17 = (f32[64,256]{1,0:T(8,128)S(1)}, f32[64,256]{1,0:T(8,128)S(1)}, u32[]{:S(2)}, u32[]{:S(2)}) collective-permute-start(f32[64,256]{1,0:T(8,128)S(1)} %pass_on.1), channel_id=1, source_target_pairs={{0,3},{1,2},{2,1},{3,0},{4,7},{5,6},{6,5},{7,4},{8,11},{9,10},{10,... | collective-permute-start | bytes 196616 | tf_op jit(solution)/shard_map/ppermute | solution.py:25
  51.6 4.6 %collective-permute-done.17.second_ref = f32[64,256]{1,0:T(8,128)S(1)} collective-permute-done((f32[64,256]{1,0:T(8,128)S(1)}, f32[64,256]{1,0:T(8,128)S(1)}, u32[]{:S(2)}, u32[]{:S(2)}) %collective-permute-start.17) | collective-permute-done | bytes 65568 | tf_op jit(solution)/shard_map/ppermute | solution.py:25
  56.2 0.9 %finish.1 = f32[8,32,64]{2,1,0:T(8,128)} custom-call(f32[4,64,256]{2,1,0:T(8,128)S(1)} %get-tuple-element.40.own_ref, f32[2,64,256]{2,1,0:T(8,128)S(1)} %collective-permute-done.16.first_ref, f32[64,256]{1,0:T(8,128)S(1)} %collective-permute-done.17.second_ref), custom_call_target="tpu_custom_call" | custom-call | tf_op jit(solution)/shard_map/finish/pallas_call | solution.py:298
  (30 shorter events, 1.1 us)
Async XLA Ops:
  0.0 6.6 %copy-start = (s32[64]{0:T(128)S(1)}, s32[64]{0:T(128)}, u32[]{:S(2)}) copy-start(s32[64]{0:T(128)} %mirror_ref.1) | copy-start | bytes 772
  1.7 4.9 %collective-permute-start.3 = (bf16[8,8,128,128]{3,2,1,0:T(8,128)(2,1)S(1)}, bf16[8,8,128,128]{3,2,1,0:T(8,128)(2,1)S(1)}, u32[]{:S(2)}, u32[]{:S(2)}) collective-permute-start(bf16[8,8,128,128]{3,2,1,0:T(8,128)(2,1)S(1)} %get-tuple-element.28), channel_id=1, source_target_pairs={{0,32},{1,33},{2,34},{3,35},{4,36},{5,37},{6,38},{7,39},{8,40},{9,... | collective-permute-start | bytes 6291464 | tf_op jit(solution)/shard_map/ppermute | solution.py:25
  1.8 7.4 %collective-permute-start = (bf16[256,128]{1,0:T(8,128)(2,1)S(1)}, bf16[256,128]{1,0:T(8,128)(2,1)S(1)}, u32[]{:S(2)}, u32[]{:S(2)}) collective-permute-start(bf16[256,128]{1,0:T(8,128)(2,1)S(1)} %get-tuple-element.25), channel_id=1, source_target_pairs={{0,1},{1,0},{2,3},{3,2},{4,5},{5,4},{6,7},{7,6},{8,9},{9,8},{10,11... | collective-permute-start | bytes 196616 | tf_op jit(solution)/shard_map/ppermute | solution.py:25
  3.5 6.7 %collective-permute-start.1 = (bf16[256,128]{1,0:T(8,128)(2,1)S(1)}, bf16[256,128]{1,0:T(8,128)(2,1)S(1)}, u32[]{:S(2)}, u32[]{:S(2)}) collective-permute-start(bf16[256,128]{1,0:T(8,128)(2,1)S(1)} %get-tuple-element.26), channel_id=1, source_target_pairs={{0,2},{1,3},{2,0},{3,1},{4,6},{5,7},{6,4},{7,5},{8,10},{9,11},{10,... | collective-permute-start | bytes 196616 | tf_op jit(solution)/shard_map/ppermute | solution.py:25
  6.4 5.5 %collective-permute-start.2 = (bf16[256,128]{1,0:T(8,128)(2,1)S(1)}, bf16[256,128]{1,0:T(8,128)(2,1)S(1)}, u32[]{:S(2)}, u32[]{:S(2)}) collective-permute-start(bf16[256,128]{1,0:T(8,128)(2,1)S(1)} %get-tuple-element.27), channel_id=1, source_target_pairs={{0,3},{1,2},{2,1},{3,0},{4,7},{5,6},{6,5},{7,4},{8,11},{9,10},{10,... | collective-permute-start | bytes 196616 | tf_op jit(solution)/shard_map/ppermute | solution.py:25
  12.0 5.7 %collective-permute-start.4 = (bf16[1024,128]{1,0:T(8,128)(2,1)S(1)}, bf16[1024,128]{1,0:T(8,128)(2,1)S(1)}, u32[]{:S(2)}, u32[]{:S(2)}) collective-permute-start(bf16[1024,128]{1,0:T(8,128)(2,1)S(1)} %order_rows.1.mine_ref.refs_4_), channel_id=1, source_target_pairs={{0,32},{1,33},{2,34},{3,35},{4,36},{5,37},{6,38},{7,39},{8,40},{9,... | collective-permute-start | bytes 786440 | tf_op jit(solution)/shard_map/ppermute | solution.py:25
  12.1 11.7 %collective-permute-start.5 = (bf16[1024,128]{1,0:T(8,128)(2,1)S(1)}, bf16[1024,128]{1,0:T(8,128)(2,1)S(1)}, u32[]{:S(2)}, u32[]{:S(2)}) collective-permute-start(bf16[1024,128]{1,0:T(8,128)(2,1)S(1)} %order_rows.1.mine_ref.refs_4_), channel_id=1, source_target_pairs={{0,8},{1,9},{2,10},{3,11},{4,12},{5,13},{6,14},{7,15},{8,0},{9,1},... | collective-permute-start | bytes 786440 | tf_op jit(solution)/shard_map/ppermute | solution.py:25
  13.7 10.2 %collective-permute-start.6 = (bf16[1024,128]{1,0:T(8,128)(2,1)S(1)}, bf16[1024,128]{1,0:T(8,128)(2,1)S(1)}, u32[]{:S(2)}, u32[]{:S(2)}) collective-permute-start(bf16[1024,128]{1,0:T(8,128)(2,1)S(1)} %order_rows.1.mine_ref.refs_4_), channel_id=1, source_target_pairs={{0,24},{1,25},{2,26},{3,27},{4,28},{5,29},{6,30},{7,31},{8,16},{9,... | collective-permute-start | bytes 786440 | tf_op jit(solution)/shard_map/ppermute | solution.py:25
  15.8 9.9 %collective-permute-start.8 = (bf16[1024,128]{1,0:T(8,128)(2,1)S(1)}, bf16[1024,128]{1,0:T(8,128)(2,1)S(1)}, u32[]{:S(2)}, u32[]{:S(2)}) collective-permute-start(bf16[1024,128]{1,0:T(8,128)(2,1)S(1)} %order_rows.1.mine_ref.refs_4_), channel_id=1, source_target_pairs={{0,4},{1,5},{2,6},{3,7},{4,0},{5,1},{6,2},{7,3},{8,12},{9,13},{10,... | collective-permute-start | bytes 786440 | tf_op jit(solution)/shard_map/ppermute | solution.py:25
  23.9 4.0 %collective-permute-start.10 = (bf16[2,1024,128]{2,1,0:T(8,128)(2,1)S(1)}, bf16[2,1024,128]{2,1,0:T(8,128)(2,1)S(1)}, u32[]{:S(2)}, u32[]{:S(2)}) collective-permute-start(bf16[2,1024,128]{2,1,0:T(8,128)(2,1)S(1)} %get-tuple-element.36.refs_8_), channel_id=1, source_target_pairs={{0,32},{1,33},{2,34},{3,35},{4,36},{5,37},{6,38},{7,39},{8,40},{9,... | collective-permute-start | bytes 1572872 | tf_op jit(solution)/shard_map/ppermute | solution.py:25
  25.7 2.2 %collective-permute-start.9 = (bf16[1024,128]{1,0:T(8,128)(2,1)S(1)}, bf16[1024,128]{1,0:T(8,128)(2,1)S(1)}, u32[]{:S(2)}, u32[]{:S(2)}) collective-permute-start(bf16[1024,128]{1,0:T(8,128)(2,1)S(1)} %relay.4.refs_6_), channel_id=1, source_target_pairs={{0,32},{1,33},{2,34},{3,35},{4,36},{5,37},{6,38},{7,39},{8,40},{9,... | collective-permute-start | bytes 786440 | tf_op jit(solution)/shard_map/ppermute | solution.py:25
  25.8 12.2 %collective-permute-start.11 = (bf16[2,1024,128]{2,1,0:T(8,128)(2,1)S(1)}, bf16[2,1024,128]{2,1,0:T(8,128)(2,1)S(1)}, u32[]{:S(2)}, u32[]{:S(2)}) collective-permute-start(bf16[2,1024,128]{2,1,0:T(8,128)(2,1)S(1)} %get-tuple-element.36.refs_8_), channel_id=1, source_target_pairs={{0,4},{1,5},{2,6},{3,7},{4,0},{5,1},{6,2},{7,3},{8,12},{9,13},{10,... | collective-permute-start | bytes 1572872 | tf_op jit(solution)/shard_map/ppermute | solution.py:25
  25.8 7.7 %collective-permute-start.7 = (bf16[1024,128]{1,0:T(8,128)(2,1)S(1)}, bf16[1024,128]{1,0:T(8,128)(2,1)S(1)}, u32[]{:S(2)}, u32[]{:S(2)}) collective-permute-start(bf16[1024,128]{1,0:T(8,128)(2,1)S(1)} %get-tuple-element.32), channel_id=1, source_target_pairs={{0,24},{1,25},{2,26},{3,27},{4,28},{5,29},{6,30},{7,31},{8,16},{9,... | collective-permute-start | bytes 786440 | tf_op jit(solution)/shard_map/ppermute | solution.py:25
  33.6 5.6 %collective-permute-start.12 = (bf16[1024,128]{1,0:T(8,128)(2,1)S(1)}, bf16[1024,128]{1,0:T(8,128)(2,1)S(1)}, u32[]{:S(2)}, u32[]{:S(2)}) collective-permute-start(bf16[1024,128]{1,0:T(8,128)(2,1)S(1)} %relay.5.refs_0_.refs_1_), channel_id=1, source_target_pairs={{0,32},{1,33},{2,34},{3,35},{4,36},{5,37},{6,38},{7,39},{8,40},{9,... | collective-permute-start | bytes 786440 | tf_op jit(solution)/shard_map/ppermute | solution.py:25
  33.6 6.9 %collective-permute-start.14 = (bf16[1024,128]{1,0:T(8,128)(2,1)S(1)}, bf16[1024,128]{1,0:T(8,128)(2,1)S(1)}, u32[]{:S(2)}, u32[]{:S(2)}) collective-permute-start(bf16[1024,128]{1,0:T(8,128)(2,1)S(1)} %relay.5.refs_0_.refs_1_), channel_id=1, source_target_pairs={{0,4},{1,5},{2,6},{3,7},{4,0},{5,1},{6,2},{7,3},{8,12},{9,13},{10,... | collective-permute-start | bytes 786440 | tf_op jit(solution)/shard_map/ppermute | solution.py:25
  38.0 3.8 %collective-permute-start.13 = (bf16[2,1024,128]{2,1,0:T(8,128)(2,1)S(1)}, bf16[2,1024,128]{2,1,0:T(8,128)(2,1)S(1)}, u32[]{:S(2)}, u32[]{:S(2)}) collective-permute-start(bf16[2,1024,128]{2,1,0:T(8,128)(2,1)S(1)} %relay.6.refs_0_.refs_3_), channel_id=1, source_target_pairs={{0,32},{1,33},{2,34},{3,35},{4,36},{5,37},{6,38},{7,39},{8,40},{9,... | collective-permute-start | bytes 1572872 | tf_op jit(solution)/shard_map/ppermute | solution.py:25
  40.5 1.6 %collective-permute-start.15 = (bf16[1024,128]{1,0:T(8,128)(2,1)S(1)}, bf16[1024,128]{1,0:T(8,128)(2,1)S(1)}, u32[]{:S(2)}, u32[]{:S(2)}) collective-permute-start(bf16[1024,128]{1,0:T(8,128)(2,1)S(1)} %relay.7.refs_4_.refs_5_), channel_id=1, source_target_pairs={{0,32},{1,33},{2,34},{3,35},{4,36},{5,37},{6,38},{7,39},{8,40},{9,... | collective-permute-start | bytes 786440 | tf_op jit(solution)/shard_map/ppermute | solution.py:25
  45.6 5.0 %collective-permute-start.16 = (f32[2,64,256]{2,1,0:T(8,128)S(1)}, f32[2,64,256]{2,1,0:T(8,128)S(1)}, u32[]{:S(2)}, u32[]{:S(2)}) collective-permute-start(f32[2,64,256]{2,1,0:T(8,128)S(1)} %get-tuple-element.41), channel_id=1, source_target_pairs={{0,1},{1,0},{2,3},{3,2},{4,5},{5,4},{6,7},{7,6},{8,9},{9,8},{10,11... | collective-permute-start | bytes 393224 | tf_op jit(solution)/shard_map/ppermute | solution.py:25
  50.7 5.6 %collective-permute-start.17 = (f32[64,256]{1,0:T(8,128)S(1)}, f32[64,256]{1,0:T(8,128)S(1)}, u32[]{:S(2)}, u32[]{:S(2)}) collective-permute-start(f32[64,256]{1,0:T(8,128)S(1)} %pass_on.1), channel_id=1, source_target_pairs={{0,3},{1,2},{2,1},{3,0},{4,7},{5,6},{6,5},{7,4},{8,11},{9,10},{10,... | collective-permute-start | bytes 196616 | tf_op jit(solution)/shard_map/ppermute | solution.py:25

commit v7 on v5

--- a/solution.py
+++ b/solution.py
@@ -111,7 +111,7 @@
     )(mirror, amplitudes, received)
 
 
-def rows_kernel(r0_ref, r1_ref, r2_ref, r3_ref, _, out_ref, all_ref):
+def rows_kernel(r0_ref, r2_ref, r1_ref, r3_ref, _, out_ref, all_ref):
     y = place()[1]
     for k, ref in enumerate((r0_ref, r1_ref, r2_ref, r3_ref)):
         all_ref[k ^ y] = ref[...]
@@ -282,7 +282,7 @@
     chunks, outgoing = cut_to_send(cholesky, amplitudes)
     quarters = {k: over_y(chunks[k], k) for k in (2, 1, 3)}
     tiles = twist_tiles(mirror, amplitudes, to_sibling(outgoing))
-    mine = order_rows((chunks[0], quarters[1], quarters[2], quarters[3]), tiles[1])
+    mine = order_rows((chunks[0], quarters[2], quarters[1], quarters[3]), tiles[1])
     own = (mine, to_sibling(mine))
 
     x1a, x1b, z0 = over_x(mine, 1, 1), over_x(mine, 3, 3), over_z(mine)
@@ -316,7 +316,7 @@
         (far,),
     )
     parts = {k: over_y(last[k], k) for k in (2, 1, 3)}
-    return finish((0, 1, 2, 6, 4, 3, 7, 5), (last, parts[1], parts[2], parts[3]))
+    return finish((0, 1, 2, 6, 4, 3, 7, 5), (last, parts[2], parts[1], parts[3]))
 
 
 def solution(mesh):

time: 54.6 us -> 53.6 us (0.982)
  starting transfers between devices: 22.4 us -> 21.4 us
    ppermute x19, starting transfers between devices: 22.4 us -> 21.4 us  [permute(): return lax.ppermute(value, ('occ', 'vir'), pairs)]
  transfers between devices with their start and end apart: 19 -> 19, of which waited for: 7 -> 6; matrix products, arithmetic and copies ran while one was open for 0% -> 0% of each run, Pallas kernels for 34% -> 35%
where the time goes in v7:
time: 53.6 us; the launch traced here: 53.3 us
  Pallas kernels  24.7 us (46%)
  starting transfers between devices  21.4 us (40%)
  waiting for transfers between devices  7.02 us (13%)
    ppermute x19, starting transfers between devices, permute(): return lax.ppermute(value, ('occ', 'vir'), pairs)  21.4 us
    pallas_call x3, Pallas kernels, stage1(): pl.pallas_call(functools.partial(stage1_kernel, classes, len(tokens)), ou...  10 us
    pallas_call x3, Pallas kernels, stage2(): pl.pallas_call(functools.partial(stage2_kernel, picks, len(bs), len(carry...  9.31 us
    ppermute x19, waiting for transfers between devices, permute(): return lax.ppermute(value, ('occ', 'vir'), pairs)  7.02 us
    pallas_call x1, Pallas kernels, twist_tiles(): pl.pallas_call(twist_kernel, out_shape=(shape, shape), in_specs=[spec(plt...  2.63 us
    pallas_call x1, Pallas kernels, cut_to_send(): pl.pallas_call(send_kernel, out_shape=(chunk,) * 4 + (jax.ShapeDtypeStruc...  1.7 us
  transfers between devices with their start and end apart: 19, of which 6 were waited for; matrix products, arithmetic and copies ran while one was open for 0% of the time, Pallas kernels for 35%

profile of v7, /device:TPU:0, one launch (start us, length us, event | category | flops | bytes accessed | tf_op | source)
XLA Modules:
  0.0 53.3 jit_solution(7470378894171977412)
XLA Ops:
  0.0 1.7 %cut_to_send.1 = (bf16[256,128]{1,0:T(8,128)(2,1)S(1)}, bf16[256,128]{1,0:T(8,128)(2,1)S(1)}, bf16[256,128]{1,0:T(8,128)(2,1)S(1)}, bf16[256,128]{1,0:T(8,128)(2,1)S(1)}, bf16[8,8,128,128]{3,2,1,0:T(8,128)(2,1)S(1)}) custom-call(bf16[2048,128]{1,0:T(8,128)(2,1)} %bitcast.8, bf16[64,8,128,128]{3,2,1,0:T(8,128)(2,1)} %amp_ref.3), custom_call_target="tpu_custom_call" | custom-call | tf_op jit(solution)/shard_map/cut_to_send/pallas_call | solution.py:75
  1.8 3.4 %collective-permute-start = (bf16[256,128]{1,0:T(8,128)(2,1)S(1)}, bf16[256,128]{1,0:T(8,128)(2,1)S(1)}, u32[]{:S(2)}, u32[]{:S(2)}) collective-permute-start(bf16[256,128]{1,0:T(8,128)(2,1)S(1)} %get-tuple-element.22), channel_id=1, source_target_pairs={{0,2},{1,3},{2,0},{3,1},{4,6},{5,7},{6,4},{7,5},{8,10},{9,11},{10,... | collective-permute-start | bytes 196616 | tf_op jit(solution)/shard_map/ppermute | solution.py:25
  6.2 2.6 %twist_tiles.1 = (bf16[8,8,128,128]{3,2,1,0:T(8,128)(2,1)S(1)}, bf16[8,8,128,128]{3,2,1,0:T(8,128)(2,1)S(1)}) custom-call(s32[64]{0:T(128)S(1)} %copy-done, bf16[64,8,128,128]{3,2,1,0:T(8,128)(2,1)} %amp_ref.3, bf16[8,8,128,128]{3,2,1,0:T(8,128)(2,1)S(1)} %collective-permute-done.3.received_ref), custom_call_target="tpu_custom_call" | custom-call | tf_op jit(solution)/shard_map/twist_tiles/pallas_call | solution.py:103
  8.9 0.8 %collective-permute-done.1.r1_ref = bf16[256,128]{1,0:T(8,128)(2,1)S(1)} collective-permute-done((bf16[256,128]{1,0:T(8,128)(2,1)S(1)}, bf16[256,128]{1,0:T(8,128)(2,1)S(1)}, u32[]{:S(2)}, u32[]{:S(2)}) %collective-permute-start.1) | collective-permute-done | bytes 65568 | tf_op jit(solution)/shard_map/ppermute | solution.py:25
  9.6 1.7 %collective-permute-done.2.r3_ref = bf16[256,128]{1,0:T(8,128)(2,1)S(1)} collective-permute-done((bf16[256,128]{1,0:T(8,128)(2,1)S(1)}, bf16[256,128]{1,0:T(8,128)(2,1)S(1)}, u32[]{:S(2)}, u32[]{:S(2)}) %collective-permute-start.2) | collective-permute-done | bytes 65568 | tf_op jit(solution)/shard_map/ppermute | solution.py:25
  11.5 1.6 %collective-permute-start.5 = (bf16[1024,128]{1,0:T(8,128)(2,1)S(1)}, bf16[1024,128]{1,0:T(8,128)(2,1)S(1)}, u32[]{:S(2)}, u32[]{:S(2)}) collective-permute-start(bf16[1024,128]{1,0:T(8,128)(2,1)S(1)} %order_rows.1.mine_ref.refs_4_), channel_id=1, source_target_pairs={{0,8},{1,9},{2,10},{3,11},{4,12},{5,13},{6,14},{7,15},{8,0},{9,1},... | collective-permute-start | bytes 786440 | tf_op jit(solution)/shard_map/ppermute | solution.py:25
  13.1 2.1 %collective-permute-start.6 = (bf16[1024,128]{1,0:T(8,128)(2,1)S(1)}, bf16[1024,128]{1,0:T(8,128)(2,1)S(1)}, u32[]{:S(2)}, u32[]{:S(2)}) collective-permute-start(bf16[1024,128]{1,0:T(8,128)(2,1)S(1)} %order_rows.1.mine_ref.refs_4_), channel_id=1, source_target_pairs={{0,24},{1,25},{2,26},{3,27},{4,28},{5,29},{6,30},{7,31},{8,16},{9,... | collective-permute-start | bytes 786440 | tf_op jit(solution)/shard_map/ppermute | solution.py:25
  15.2 1.9 %collective-permute-start.8 = (bf16[1024,128]{1,0:T(8,128)(2,1)S(1)}, bf16[1024,128]{1,0:T(8,128)(2,1)S(1)}, u32[]{:S(2)}, u32[]{:S(2)}) collective-permute-start(bf16[1024,128]{1,0:T(8,128)(2,1)S(1)} %order_rows.1.mine_ref.refs_4_), channel_id=1, source_target_pairs={{0,4},{1,5},{2,6},{3,7},{4,0},{5,1},{6,2},{7,3},{8,12},{9,13},{10,... | collective-permute-start | bytes 786440 | tf_op jit(solution)/shard_map/ppermute | solution.py:25
  17.1 6.1 %stage1_0_1_2_6_4.1 = (bf16[256,8192]{1,0:T(8,128)(2,1)S(1)}, bf16[256,8192]{1,0:T(8,128)(2,1)S(1)}, bf16[256,8192]{1,0:T(8,128)(2,1)S(1)}, bf16[256,8192]{1,0:T(8,128)(2,1)S(1)}, bf16[256,8192]{1,0:T(8,128)(2,1)S(1)}) custom-call(bf16[1024,128]{1,0:T(8,128)(2,1)S(1)} %order_rows.1.mine_ref.refs_4_, ...), custom_call_target="tpu_custom_call" | custom-call | flops 5368709120 | bytes 1310720 | tf_op jit(solution)/shard_map/stage1_0_1_2_6_4/pallas_call | solution.py:199
  23.3 1.8 %collective-permute-start.10 = (bf16[2,1024,128]{2,1,0:T(8,128)(2,1)S(1)}, bf16[2,1024,128]{2,1,0:T(8,128)(2,1)S(1)}, u32[]{:S(2)}, u32[]{:S(2)}) collective-permute-start(bf16[2,1024,128]{2,1,0:T(8,128)(2,1)S(1)} %get-tuple-element.33.refs_8_), channel_id=1, source_target_pairs={{0,32},{1,33},{2,34},{3,35},{4,36},{5,37},{6,38},{7,39},{8,40},{9,... | collective-permute-start | bytes 1572872 | tf_op jit(solution)/shard_map/ppermute | solution.py:25
  25.2 2.1 %collective-permute-start.7 = (bf16[1024,128]{1,0:T(8,128)(2,1)S(1)}, bf16[1024,128]{1,0:T(8,128)(2,1)S(1)}, u32[]{:S(2)}, u32[]{:S(2)}) collective-permute-start(bf16[1024,128]{1,0:T(8,128)(2,1)S(1)} %get-tuple-element.29), channel_id=1, source_target_pairs={{0,24},{1,25},{2,26},{3,27},{4,28},{5,29},{6,30},{7,31},{8,16},{9,... | collective-permute-start | bytes 786440 | tf_op jit(solution)/shard_map/ppermute | solution.py:25
  27.3 4.6 %stage2_near.1.refs_1_.refs_3_ = f32[4,64,128]{2,1,0:T(8,128)S(1)} custom-call(bf16[256,8192]{1,0:T(8,128)(2,1)S(1)} %get-tuple-element.28._.refs_1_.refs_0_, bf16[256,8192]{1,0:T(8,128)(2,1)S(1)} %get-tuple-element.30.refs_1_, bf16[256,8192]{1,0:T(8,128)(2,1)S(1)} %get-tuple-element.31.refs_2_, bf16[256,8192]{1,0:T(8,128)(2,1)S(1)} %get-tuple-element.32.refs_3_, ...), custom_call_target="tpu_custom_call" | custom-call | flops 4294967296 | bytes 1048576 | tf_op jit(solution)/shard_map/stage2_near/pallas_call | solution.py:243
  31.9 1.0 %collective-permute-done.7.refs_0_ = bf16[1024,128]{1,0:T(8,128)(2,1)S(1)} collective-permute-done((bf16[1024,128]{1,0:T(8,128)(2,1)S(1)}, bf16[1024,128]{1,0:T(8,128)(2,1)S(1)}, u32[]{:S(2)}, u32[]{:S(2)}) %collective-permute-start.7) | collective-permute-done | bytes 262176 | tf_op jit(solution)/shard_map/ppermute | solution.py:25
  33.0 1.9 %collective-permute-start.14 = (bf16[1024,128]{1,0:T(8,128)(2,1)S(1)}, bf16[1024,128]{1,0:T(8,128)(2,1)S(1)}, u32[]{:S(2)}, u32[]{:S(2)}) collective-permute-start(bf16[1024,128]{1,0:T(8,128)(2,1)S(1)} %relay.5.refs_0_.refs_1_), channel_id=1, source_target_pairs={{0,4},{1,5},{2,6},{3,7},{4,0},{5,1},{6,2},{7,3},{8,12},{9,13},{10,... | collective-permute-start | bytes 786440 | tf_op jit(solution)/shard_map/ppermute | solution.py:25
  34.8 2.5 %stage1_3_7.1 = (bf16[256,8192]{1,0:T(8,128)(2,1)S(1)}, bf16[256,8192]{1,0:T(8,128)(2,1)S(1)}) custom-call(bf16[1024,128]{1,0:T(8,128)(2,1)S(1)} %order_rows.1.mine_ref.refs_4_, bf16[1024,128]{1,0:T(8,128)(2,1)S(1)} %collective-permute-done.4.other_ref.refs_5_, bf16[8,8,128,128]{3,2,1,0:T(8,128)(2,1)S(1)} %get-tuple-element.27.t_ref, ...), custom_call_target="tpu_custom_call" | custom-call | flops 2147483648 | bytes 524288 | tf_op jit(solution)/shard_map/stage1_3_7/pallas_call | solution.py:199
  37.4 1.1 %collective-permute-start.13 = (bf16[2,1024,128]{2,1,0:T(8,128)(2,1)S(1)}, bf16[2,1024,128]{2,1,0:T(8,128)(2,1)S(1)}, u32[]{:S(2)}, u32[]{:S(2)}) collective-permute-start(bf16[2,1024,128]{2,1,0:T(8,128)(2,1)S(1)} %relay.6.refs_0_.refs_3_), channel_id=1, source_target_pairs={{0,32},{1,33},{2,34},{3,35},{4,36},{5,37},{6,38},{7,39},{8,40},{9,... | collective-permute-start | bytes 1572872 | tf_op jit(solution)/shard_map/ppermute | solution.py:25
  38.5 1.3 %stage1_5.1.refs_1_.refs_2_ = bf16[256,8192]{1,0:T(8,128)(2,1)S(1)} custom-call(bf16[1024,128]{1,0:T(8,128)(2,1)S(1)} %order_rows.1.mine_ref.refs_4_, bf16[1024,128]{1,0:T(8,128)(2,1)S(1)} %collective-permute-done.4.other_ref.refs_5_, bf16[8,8,128,128]{3,2,1,0:T(8,128)(2,1)S(1)} %get-tuple-element.27.t_ref, ...), custom_call_target="tpu_custom_call" | custom-call | flops 1073741824 | bytes 262144 | tf_op jit(solution)/shard_map/stage1_5/pallas_call | solution.py:199
  40.0 1.2 %stage2_far.1.refs_7_ = f32[4,64,160]{2,1,0:T(8,128)S(1)} custom-call(bf16[256,8192]{1,0:T(8,128)(2,1)S(1)} %get-tuple-element.36.refs_0_, bf16[1024,128]{1,0:T(8,128)(2,1)S(1)} %relay.5.refs_0_.refs_1_, bf16[1024,128]{1,0:T(8,128)(2,1)S(1)} %collective-permute-done.12.refs_1_.refs_2_, f32[4,64,128]{2,1,0:T(8,128)S(1)} %stage2_near.1.refs_1_.refs_3_, ...), custom_call_target="tpu_custom_call" | custom-call | flops 1073741824 | bytes 262144 | tf_op jit(solution)/shard_map/stage2_far/pallas_call | solution.py:243
  41.5 3.5 %stage2_last.1.own_ref = f32[4,64,256]{2,1,0:T(8,128)S(1)} custom-call(bf16[256,8192]{1,0:T(8,128)(2,1)S(1)} %get-tuple-element.34.refs_1_.refs_0_, bf16[256,8192]{1,0:T(8,128)(2,1)S(1)} %get-tuple-element.35.refs_1_, bf16[256,8192]{1,0:T(8,128)(2,1)S(1)} %stage1_5.1.refs_1_.refs_2_, bf16[2,1024,128]{2,1,0:T(8,128)(2,1)S(1)} %relay.6.refs_0_.refs_3_, ...), custom_call_target="tpu_custom_call" | custom-call | flops 3221225472 | bytes 786432 | tf_op jit(solution)/shard_map/stage2_last/pallas_call | solution.py:243
  45.0 1.3 %collective-permute-start.16 = (f32[64,256]{1,0:T(8,128)S(1)}, f32[64,256]{1,0:T(8,128)S(1)}, u32[]{:S(2)}, u32[]{:S(2)}) collective-permute-start(f32[64,256]{1,0:T(8,128)S(1)} %get-tuple-element.39), channel_id=1, source_target_pairs={{0,2},{1,3},{2,0},{3,1},{4,6},{5,7},{6,4},{7,5},{8,10},{9,11},{10,... | collective-permute-start | bytes 196616 | tf_op jit(solution)/shard_map/ppermute | solution.py:25
  47.0 2.2 %collective-permute-start.18 = (f32[64,256]{1,0:T(8,128)S(1)}, f32[64,256]{1,0:T(8,128)S(1)}, u32[]{:S(2)}, u32[]{:S(2)}) collective-permute-start(f32[64,256]{1,0:T(8,128)S(1)} %get-tuple-element.37), channel_id=1, source_target_pairs={{0,3},{1,2},{2,1},{3,0},{4,7},{5,6},{6,5},{7,4},{8,11},{9,10},{10,... | collective-permute-start | bytes 196616 | tf_op jit(solution)/shard_map/ppermute | solution.py:25
  49.2 2.3 %collective-permute-done.16.r1_ref = f32[64,256]{1,0:T(8,128)S(1)} collective-permute-done((f32[64,256]{1,0:T(8,128)S(1)}, f32[64,256]{1,0:T(8,128)S(1)}, u32[]{:S(2)}, u32[]{:S(2)}) %collective-permute-start.16) | collective-permute-done | bytes 65568 | tf_op jit(solution)/shard_map/ppermute | solution.py:25
  51.5 0.9 %collective-permute-done.18.r3_ref = f32[64,256]{1,0:T(8,128)S(1)} collective-permute-done((f32[64,256]{1,0:T(8,128)S(1)}, f32[64,256]{1,0:T(8,128)S(1)}, u32[]{:S(2)}, u32[]{:S(2)}) %collective-permute-start.18) | collective-permute-done | bytes 65568 | tf_op jit(solution)/shard_map/ppermute | solution.py:25
  52.4 0.9 %finish.1 = f32[8,32,64]{2,1,0:T(8,128)} custom-call(f32[4,64,256]{2,1,0:T(8,128)S(1)} %stage2_last.1.own_ref, f32[64,256]{1,0:T(8,128)S(1)} %collective-permute-done.16.r1_ref, f32[64,256]{1,0:T(8,128)S(1)} %collective-permute-done.17.r2_ref, f32[64,256]{1,0:T(8,128)S(1)} %collective-permute-done.18.r3_ref), custom_call_target="tpu_custom_call" | custom-call | tf_op jit(solution)/shard_map/finish/pallas_call | solution.py:269
  (32 shorter events, 2.6 us)
Async XLA Ops:
  0.0 6.2 %copy-start = (s32[64]{0:T(128)S(1)}, s32[64]{0:T(128)}, u32[]{:S(2)}) copy-start(s32[64]{0:T(128)} %mirror_ref.1) | copy-start | bytes 772
  1.7 4.5 %collective-permute-start.3 = (bf16[8,8,128,128]{3,2,1,0:T(8,128)(2,1)S(1)}, bf16[8,8,128,128]{3,2,1,0:T(8,128)(2,1)S(1)}, u32[]{:S(2)}, u32[]{:S(2)}) collective-permute-start(bf16[8,8,128,128]{3,2,1,0:T(8,128)(2,1)S(1)} %get-tuple-element.25), channel_id=1, source_target_pairs={{0,32},{1,33},{2,34},{3,35},{4,36},{5,37},{6,38},{7,39},{8,40},{9,... | collective-permute-start | bytes 6291464 | tf_op jit(solution)/shard_map/ppermute | solution.py:25
  1.8 7.1 %collective-permute-start = (bf16[256,128]{1,0:T(8,128)(2,1)S(1)}, bf16[256,128]{1,0:T(8,128)(2,1)S(1)}, u32[]{:S(2)}, u32[]{:S(2)}) collective-permute-start(bf16[256,128]{1,0:T(8,128)(2,1)S(1)} %get-tuple-element.22), channel_id=1, source_target_pairs={{0,2},{1,3},{2,0},{3,1},{4,6},{5,7},{6,4},{7,5},{8,10},{9,11},{10,... | collective-permute-start | bytes 196616 | tf_op jit(solution)/shard_map/ppermute | solution.py:25
  5.2 4.5 %collective-permute-start.1 = (bf16[256,128]{1,0:T(8,128)(2,1)S(1)}, bf16[256,128]{1,0:T(8,128)(2,1)S(1)}, u32[]{:S(2)}, u32[]{:S(2)}) collective-permute-start(bf16[256,128]{1,0:T(8,128)(2,1)S(1)} %get-tuple-element.23), channel_id=1, source_target_pairs={{0,1},{1,0},{2,3},{3,2},{4,5},{5,4},{6,7},{7,6},{8,9},{9,8},{10,11... | collective-permute-start | bytes 196616 | tf_op jit(solution)/shard_map/ppermute | solution.py:25
  5.8 5.5 %collective-permute-start.2 = (bf16[256,128]{1,0:T(8,128)(2,1)S(1)}, bf16[256,128]{1,0:T(8,128)(2,1)S(1)}, u32[]{:S(2)}, u32[]{:S(2)}) collective-permute-start(bf16[256,128]{1,0:T(8,128)(2,1)S(1)} %get-tuple-element.24), channel_id=1, source_target_pairs={{0,3},{1,2},{2,1},{3,0},{4,7},{5,6},{6,5},{7,4},{8,11},{9,10},{10,... | collective-permute-start | bytes 196616 | tf_op jit(solution)/shard_map/ppermute | solution.py:25
  11.4 5.7 %collective-permute-start.4 = (bf16[1024,128]{1,0:T(8,128)(2,1)S(1)}, bf16[1024,128]{1,0:T(8,128)(2,1)S(1)}, u32[]{:S(2)}, u32[]{:S(2)}) collective-permute-start(bf16[1024,128]{1,0:T(8,128)(2,1)S(1)} %order_rows.1.mine_ref.refs_4_), channel_id=1, source_target_pairs={{0,32},{1,33},{2,34},{3,35},{4,36},{5,37},{6,38},{7,39},{8,40},{9,... | collective-permute-start | bytes 786440 | tf_op jit(solution)/shard_map/ppermute | solution.py:25
  11.5 11.7 %collective-permute-start.5 = (bf16[1024,128]{1,0:T(8,128)(2,1)S(1)}, bf16[1024,128]{1,0:T(8,128)(2,1)S(1)}, u32[]{:S(2)}, u32[]{:S(2)}) collective-permute-start(bf16[1024,128]{1,0:T(8,128)(2,1)S(1)} %order_rows.1.mine_ref.refs_4_), channel_id=1, source_target_pairs={{0,8},{1,9},{2,10},{3,11},{4,12},{5,13},{6,14},{7,15},{8,0},{9,1},... | collective-permute-start | bytes 786440 | tf_op jit(solution)/shard_map/ppermute | solution.py:25
  13.1 10.2 %collective-permute-start.6 = (bf16[1024,128]{1,0:T(8,128)(2,1)S(1)}, bf16[1024,128]{1,0:T(8,128)(2,1)S(1)}, u32[]{:S(2)}, u32[]{:S(2)}) collective-permute-start(bf16[1024,128]{1,0:T(8,128)(2,1)S(1)} %order_rows.1.mine_ref.refs_4_), channel_id=1, source_target_pairs={{0,24},{1,25},{2,26},{3,27},{4,28},{5,29},{6,30},{7,31},{8,16},{9,... | collective-permute-start | bytes 786440 | tf_op jit(solution)/shard_map/ppermute | solution.py:25
  15.2 9.9 %collective-permute-start.8 = (bf16[1024,128]{1,0:T(8,128)(2,1)S(1)}, bf16[1024,128]{1,0:T(8,128)(2,1)S(1)}, u32[]{:S(2)}, u32[]{:S(2)}) collective-permute-start(bf16[1024,128]{1,0:T(8,128)(2,1)S(1)} %order_rows.1.mine_ref.refs_4_), channel_id=1, source_target_pairs={{0,4},{1,5},{2,6},{3,7},{4,0},{5,1},{6,2},{7,3},{8,12},{9,13},{10,... | collective-permute-start | bytes 786440 | tf_op jit(solution)/shard_map/ppermute | solution.py:25
  23.3 4.0 %collective-permute-start.10 = (bf16[2,1024,128]{2,1,0:T(8,128)(2,1)S(1)}, bf16[2,1024,128]{2,1,0:T(8,128)(2,1)S(1)}, u32[]{:S(2)}, u32[]{:S(2)}) collective-permute-start(bf16[2,1024,128]{2,1,0:T(8,128)(2,1)S(1)} %get-tuple-element.33.refs_8_), channel_id=1, source_target_pairs={{0,32},{1,33},{2,34},{3,35},{4,36},{5,37},{6,38},{7,39},{8,40},{9,... | collective-permute-start | bytes 1572872 | tf_op jit(solution)/shard_map/ppermute | solution.py:25
  25.1 2.2 %collective-permute-start.9 = (bf16[1024,128]{1,0:T(8,128)(2,1)S(1)}, bf16[1024,128]{1,0:T(8,128)(2,1)S(1)}, u32[]{:S(2)}, u32[]{:S(2)}) collective-permute-start(bf16[1024,128]{1,0:T(8,128)(2,1)S(1)} %relay.4.refs_6_), channel_id=1, source_target_pairs={{0,32},{1,33},{2,34},{3,35},{4,36},{5,37},{6,38},{7,39},{8,40},{9,... | collective-permute-start | bytes 786440 | tf_op jit(solution)/shard_map/ppermute | solution.py:25
  25.2 12.2 %collective-permute-start.11 = (bf16[2,1024,128]{2,1,0:T(8,128)(2,1)S(1)}, bf16[2,1024,128]{2,1,0:T(8,128)(2,1)S(1)}, u32[]{:S(2)}, u32[]{:S(2)}) collective-permute-start(bf16[2,1024,128]{2,1,0:T(8,128)(2,1)S(1)} %get-tuple-element.33.refs_8_), channel_id=1, source_target_pairs={{0,4},{1,5},{2,6},{3,7},{4,0},{5,1},{6,2},{7,3},{8,12},{9,13},{10,... | collective-permute-start | bytes 1572872 | tf_op jit(solution)/shard_map/ppermute | solution.py:25
  25.2 7.7 %collective-permute-start.7 = (bf16[1024,128]{1,0:T(8,128)(2,1)S(1)}, bf16[1024,128]{1,0:T(8,128)(2,1)S(1)}, u32[]{:S(2)}, u32[]{:S(2)}) collective-permute-start(bf16[1024,128]{1,0:T(8,128)(2,1)S(1)} %get-tuple-element.29), channel_id=1, source_target_pairs={{0,24},{1,25},{2,26},{3,27},{4,28},{5,29},{6,30},{7,31},{8,16},{9,... | collective-permute-start | bytes 786440 | tf_op jit(solution)/shard_map/ppermute | solution.py:25
  33.0 5.6 %collective-permute-start.12 = (bf16[1024,128]{1,0:T(8,128)(2,1)S(1)}, bf16[1024,128]{1,0:T(8,128)(2,1)S(1)}, u32[]{:S(2)}, u32[]{:S(2)}) collective-permute-start(bf16[1024,128]{1,0:T(8,128)(2,1)S(1)} %relay.5.refs_0_.refs_1_), channel_id=1, source_target_pairs={{0,32},{1,33},{2,34},{3,35},{4,36},{5,37},{6,38},{7,39},{8,40},{9,... | collective-permute-start | bytes 786440 | tf_op jit(solution)/shard_map/ppermute | solution.py:25
  33.0 6.9 %collective-permute-start.14 = (bf16[1024,128]{1,0:T(8,128)(2,1)S(1)}, bf16[1024,128]{1,0:T(8,128)(2,1)S(1)}, u32[]{:S(2)}, u32[]{:S(2)}) collective-permute-start(bf16[1024,128]{1,0:T(8,128)(2,1)S(1)} %relay.5.refs_0_.refs_1_), channel_id=1, source_target_pairs={{0,4},{1,5},{2,6},{3,7},{4,0},{5,1},{6,2},{7,3},{8,12},{9,13},{10,... | collective-permute-start | bytes 786440 | tf_op jit(solution)/shard_map/ppermute | solution.py:25
  37.4 3.8 %collective-permute-start.13 = (bf16[2,1024,128]{2,1,0:T(8,128)(2,1)S(1)}, bf16[2,1024,128]{2,1,0:T(8,128)(2,1)S(1)}, u32[]{:S(2)}, u32[]{:S(2)}) collective-permute-start(bf16[2,1024,128]{2,1,0:T(8,128)(2,1)S(1)} %relay.6.refs_0_.refs_3_), channel_id=1, source_target_pairs={{0,32},{1,33},{2,34},{3,35},{4,36},{5,37},{6,38},{7,39},{8,40},{9,... | collective-permute-start | bytes 1572872 | tf_op jit(solution)/shard_map/ppermute | solution.py:25
  39.9 1.6 %collective-permute-start.15 = (bf16[1024,128]{1,0:T(8,128)(2,1)S(1)}, bf16[1024,128]{1,0:T(8,128)(2,1)S(1)}, u32[]{:S(2)}, u32[]{:S(2)}) collective-permute-start(bf16[1024,128]{1,0:T(8,128)(2,1)S(1)} %relay.7.refs_4_.refs_5_), channel_id=1, source_target_pairs={{0,32},{1,33},{2,34},{3,35},{4,36},{5,37},{6,38},{7,39},{8,40},{9,... | collective-permute-start | bytes 786440 | tf_op jit(solution)/shard_map/ppermute | solution.py:25
  45.0 6.5 %collective-permute-start.16 = (f32[64,256]{1,0:T(8,128)S(1)}, f32[64,256]{1,0:T(8,128)S(1)}, u32[]{:S(2)}, u32[]{:S(2)}) collective-permute-start(f32[64,256]{1,0:T(8,128)S(1)} %get-tuple-element.39), channel_id=1, source_target_pairs={{0,2},{1,3},{2,0},{3,1},{4,6},{5,7},{6,4},{7,5},{8,10},{9,11},{10,... | collective-permute-start | bytes 196616 | tf_op jit(solution)/shard_map/ppermute | solution.py:25
  46.3 5.3 %collective-permute-start.17 = (f32[64,256]{1,0:T(8,128)S(1)}, f32[64,256]{1,0:T(8,128)S(1)}, u32[]{:S(2)}, u32[]{:S(2)}) collective-permute-start(f32[64,256]{1,0:T(8,128)S(1)} %get-tuple-element.38), channel_id=1, source_target_pairs={{0,1},{1,0},{2,3},{3,2},{4,5},{5,4},{6,7},{7,6},{8,9},{9,8},{10,11... | collective-permute-start | bytes 196616 | tf_op jit(solution)/shard_map/ppermute | solution.py:25
  47.0 5.5 %collective-permute-start.18 = (f32[64,256]{1,0:T(8,128)S(1)}, f32[64,256]{1,0:T(8,128)S(1)}, u32[]{:S(2)}, u32[]{:S(2)}) collective-permute-start(f32[64,256]{1,0:T(8,128)S(1)} %get-tuple-element.37), channel_id=1, source_target_pairs={{0,3},{1,2},{2,1},{3,0},{4,7},{5,6},{6,5},{7,4},{8,11},{9,10},{10,... | collective-permute-start | bytes 196616 | tf_op jit(solution)/shard_map/ppermute | solution.py:25

commit v8 on v7

--- a/solution.py
+++ b/solution.py
@@ -180,21 +180,21 @@
             upper = jnp.concatenate([t_ref[g, j0], t_ref[g, j1]], axis=1)
             lower = jnp.concatenate([tp_ref[g, j0], tp_ref[g, j1]], axis=1)
             weights = jnp.concatenate([upper, lower], axis=0)
-            for part in range(4):
-                own_ref = (mine_ref, other_ref)[part // 2]
-                own = own_ref[(part % 2) * 512 : (part % 2 + 1) * 512, :]
+            for part in range(16):
+                own_ref = (mine_ref, other_ref)[part // 8]
+                own = own_ref[(part % 8) * 128 : (part % 8 + 1) * 128, :]
                 lhs = jnp.concatenate([own, own], axis=1)
                 x = jnp.dot(lhs, weights, preferred_element_type=F32).astype(BF16)
                 for k in range(2):
                     j = 2 * pair + k
-                    for l in range(16):
-                        lane = (part * 16 + l) * 128
+                    for l in range(4):
+                        lane = (part * 4 + l) * 128
                         x_ref[j * 32 : (j + 1) * 32, lane : lane + 128] = x[
                             l * 32 : (l + 1) * 32, k * 128 : (k + 1) * 128
                         ]
 
 
-def stage1(classes, own, tiles, tokens=()):
+def stage1(classes, own, tiles, tokens=(), weight=1):
     n = len(classes)
     return pl.pallas_call(
         functools.partial(stage1_kernel, classes, len(tokens)),
@@ -202,7 +202,7 @@
         in_specs=[spec(pltpu.VMEM)] * 4 + [spec(pl.ANY)] * len(tokens),
         out_specs=tuple(spec(pltpu.VMEM) for _ in classes),
         compiler_params=params(8),
-        cost_estimate=pl.CostEstimate(flops=n * 2**30, transcendentals=0, bytes_accessed=n * 2**18),
+        cost_estimate=pl.CostEstimate(flops=int(n * weight * 2**30), transcendentals=0, bytes_accessed=2**10),
         name="stage1_" + "_".join(str(g) for g in classes),
     )(*own, *tiles, *tokens)
 
@@ -218,12 +218,12 @@
         total = None
         for half, (at, index) in enumerate(halves):
             b_ref = b_refs[at] if index is None else b_refs[at].at[index]
-            for step in range(8):
-                b = b_ref[step * 128 : (step + 1) * 128, :]
-                bt = jnp.concatenate([b[l * 32 : (l + 1) * 32] for l in range(4)], axis=1)
-                lane = half * 4096 + step * 512
+            for step in range(16):
+                b = b_ref[step * 64 : (step + 1) * 64, :]
+                bt = jnp.concatenate([b[0:32], b[32:64]], axis=1)
+                lane = half * 4096 + step * 256
                 term = lax.dot_general(
-                    x_refs[i][:, lane : lane + 512], bt, NT, preferred_element_type=F32
+                    x_refs[i][:, lane : lane + 256], bt, NT, preferred_element_type=F32
                 )
                 total = term if total is None else total + term
         r_s[i] = total
@@ -237,7 +237,7 @@
         out_ref[q ^ y] = jnp.concatenate(columns, axis=1) if len(columns) > 1 else columns[0]
 
 
-def stage2(name, xs, picks, bs, carry=(), tokens=()):
+def stage2(name, xs, picks, bs, carry=(), tokens=(), weight=1):
     n = len(xs)
     lanes = 32 * n + sum(c.shape[2] for c in carry)
     return pl.pallas_call(
@@ -247,7 +247,7 @@
         out_specs=spec(pltpu.VMEM),
         scratch_shapes=[pltpu.VMEM((n, 256, 32), F32)],
         compiler_params=params(8),
-        cost_estimate=pl.CostEstimate(flops=n * 2**30, transcendentals=0, bytes_accessed=n * 2**18),
+        cost_estimate=pl.CostEstimate(flops=int(n * weight * 2**30), transcendentals=0, bytes_accessed=2**10),
         name="stage2_" + name,
     )(*xs, *bs, *carry, *tokens)
 
@@ -278,6 +278,9 @@
     return jnp.transpose(out, (2, 0, 1))
 
 
+SA, NEAR, SB, SC = 1, 0, 4, 1
+
+
 def shards(cholesky, amplitudes, mirror):
     chunks, outgoing = cut_to_send(cholesky, amplitudes)
     quarters = {k: over_y(chunks[k], k) for k in (2, 1, 3)}
@@ -286,7 +289,7 @@
     own = (mine, to_sibling(mine))
 
     x1a, x1b, z0 = over_x(mine, 1, 1), over_x(mine, 3, 3), over_z(mine)
-    xc0, xc1, xc2, xc6, xc4 = stage1((0, 1, 2, 6, 4), own, tiles)
+    xc0, xc1, xc2, xc6, xc4 = stage1((0, 1, 2, 6, 4), own, tiles, (), SA)
     (z0,) = relay((z0,), (xc0,))
     x1, forward = join(x1a, x1b, xc0)
     x1_other, z0_other = to_sibling(x1), to_sibling(z0)
@@ -297,14 +300,15 @@
         (xc0, xc1, xc2, xc6),
         (((0, None), (1, None)), ((2, None), (3, None)), ((4, 0), (5, 0)), ((4, 1), (5, 1))),
         (*own, z0, z0_other, x1, x1_other),
+        weight=NEAR,
     )
     (x2,) = relay((x2,), (near,))
     x2_other = to_sibling(x2)
     zx2 = over_z(x2)
-    xc3, xc7 = stage1((3, 7), own, tiles, (x2,))
+    xc3, xc7 = stage1((3, 7), own, tiles, (x2,), SB)
     (zx1,) = relay((zx1,), (xc3,))
     zx1_other = to_sibling(zx1)
-    (xc5,) = stage1((5,), own, tiles, (zx1, x2_other))
+    (xc5,) = stage1((5,), own, tiles, (zx1, x2_other), SC)
     (zx2,) = relay((zx2,), (xc5,))
     zx2_other = to_sibling(zx2)
     far = stage2("far", (xc4,), (((0, None), (1, None)),), (x2, x2_other), (near,), (zx2,))

time: 53.6 us -> 52.7 us (0.983)
  waiting for transfers between devices: 7.02 us -> 6.14 us
  Pallas kernels: 24.7 us -> 24 us
  starting transfers between devices: 21.4 us -> 22 us
    ppermute x19, waiting for transfers between devices: 7.02 us -> 6.14 us  [permute(): return lax.ppermute(value, ('occ', 'vir'), pairs)]
    pallas_call x3, Pallas kernels: 10 us -> 9.31 us  [stage1(): pl.pallas_call(functools.partial(stage1_kernel, classes, len(tokens)), ou...]
    ppermute x19, starting transfers between devices: 21.4 us -> 22 us  [permute(): return lax.ppermute(value, ('occ', 'vir'), pairs)]
  transfers between devices with their start and end apart: 19 -> 19, of which waited for: 6 -> 5; matrix products, arithmetic and copies ran while one was open for 0% -> 0% of each run, Pallas kernels for 35% -> 34%
where the time goes in v8:
time: 52.7 us; the launch traced here: 52.4 us
  Pallas kernels  24 us (46%)
  starting transfers between devices  22 us (42%)
  waiting for transfers between devices  6.14 us (12%)
    ppermute x19, starting transfers between devices, permute(): return lax.ppermute(value, ('occ', 'vir'), pairs)  22 us
    pallas_call x3, Pallas kernels, stage2(): pl.pallas_call(functools.partial(stage2_kernel, picks, len(bs), len(carry...  9.33 us
    pallas_call x3, Pallas kernels, stage1(): pl.pallas_call(functools.partial(stage1_kernel, classes, len(tokens)), ou...  9.31 us
    ppermute x19, waiting for transfers between devices, permute(): return lax.ppermute(value, ('occ', 'vir'), pairs)  6.14 us
    pallas_call x1, Pallas kernels, twist_tiles(): pl.pallas_call(twist_kernel, out_shape=(shape, shape), in_specs=[spec(plt...  2.63 us
    pallas_call x1, Pallas kernels, cut_to_send(): pl.pallas_call(send_kernel, out_shape=(chunk,) * 4 + (jax.ShapeDtypeStruc...  1.7 us
  transfers between devices with their start and end apart: 19, of which 5 were waited for; matrix products, arithmetic and copies ran while one was open for 0% of the time, Pallas kernels for 34%

profile of v8, /device:TPU:0, one launch (start us, length us, event | category | flops | bytes accessed | tf_op | source)
XLA Modules:
  0.0 52.4 jit_solution(10894705750106520612)
XLA Ops:
  0.0 1.7 %cut_to_send.1 = (bf16[256,128]{1,0:T(8,128)(2,1)S(1)}, bf16[256,128]{1,0:T(8,128)(2,1)S(1)}, bf16[256,128]{1,0:T(8,128)(2,1)S(1)}, bf16[256,128]{1,0:T(8,128)(2,1)S(1)}, bf16[8,8,128,128]{3,2,1,0:T(8,128)(2,1)S(1)}) custom-call(bf16[2048,128]{1,0:T(8,128)(2,1)} %bitcast.8, bf16[64,8,128,128]{3,2,1,0:T(8,128)(2,1)} %amp_ref.3), custom_call_target="tpu_custom_call" | custom-call | tf_op jit(solution)/shard_map/cut_to_send/pallas_call | solution.py:75
  1.8 3.4 %collective-permute-start = (bf16[256,128]{1,0:T(8,128)(2,1)S(1)}, bf16[256,128]{1,0:T(8,128)(2,1)S(1)}, u32[]{:S(2)}, u32[]{:S(2)}) collective-permute-start(bf16[256,128]{1,0:T(8,128)(2,1)S(1)} %get-tuple-element.22), channel_id=1, source_target_pairs={{0,2},{1,3},{2,0},{3,1},{4,6},{5,7},{6,4},{7,5},{8,10},{9,11},{10,... | collective-permute-start | bytes 196616 | tf_op jit(solution)/shard_map/ppermute | solution.py:25
  5.2 0.7 %collective-permute-start.1 = (bf16[256,128]{1,0:T(8,128)(2,1)S(1)}, bf16[256,128]{1,0:T(8,128)(2,1)S(1)}, u32[]{:S(2)}, u32[]{:S(2)}) collective-permute-start(bf16[256,128]{1,0:T(8,128)(2,1)S(1)} %get-tuple-element.23), channel_id=1, source_target_pairs={{0,1},{1,0},{2,3},{3,2},{4,5},{5,4},{6,7},{7,6},{8,9},{9,8},{10,11... | collective-permute-start | bytes 196616 | tf_op jit(solution)/shard_map/ppermute | solution.py:25
  6.2 2.6 %twist_tiles.1 = (bf16[8,8,128,128]{3,2,1,0:T(8,128)(2,1)S(1)}, bf16[8,8,128,128]{3,2,1,0:T(8,128)(2,1)S(1)}) custom-call(s32[64]{0:T(128)S(1)} %copy-done, bf16[64,8,128,128]{3,2,1,0:T(8,128)(2,1)} %amp_ref.3, bf16[8,8,128,128]{3,2,1,0:T(8,128)(2,1)S(1)} %collective-permute-done.3.received_ref), custom_call_target="tpu_custom_call" | custom-call | tf_op jit(solution)/shard_map/twist_tiles/pallas_call | solution.py:103
  8.9 0.8 %collective-permute-done.1.r1_ref = bf16[256,128]{1,0:T(8,128)(2,1)S(1)} collective-permute-done((bf16[256,128]{1,0:T(8,128)(2,1)S(1)}, bf16[256,128]{1,0:T(8,128)(2,1)S(1)}, u32[]{:S(2)}, u32[]{:S(2)}) %collective-permute-start.1) | collective-permute-done | bytes 65568 | tf_op jit(solution)/shard_map/ppermute | solution.py:25
  9.6 1.7 %collective-permute-done.2.r3_ref = bf16[256,128]{1,0:T(8,128)(2,1)S(1)} collective-permute-done((bf16[256,128]{1,0:T(8,128)(2,1)S(1)}, bf16[256,128]{1,0:T(8,128)(2,1)S(1)}, u32[]{:S(2)}, u32[]{:S(2)}) %collective-permute-start.2) | collective-permute-done | bytes 65568 | tf_op jit(solution)/shard_map/ppermute | solution.py:25
  11.5 1.6 %collective-permute-start.5 = (bf16[1024,128]{1,0:T(8,128)(2,1)S(1)}, bf16[1024,128]{1,0:T(8,128)(2,1)S(1)}, u32[]{:S(2)}, u32[]{:S(2)}) collective-permute-start(bf16[1024,128]{1,0:T(8,128)(2,1)S(1)} %order_rows.1.mine_ref.refs_4_), channel_id=1, source_target_pairs={{0,8},{1,9},{2,10},{3,11},{4,12},{5,13},{6,14},{7,15},{8,0},{9,1},... | collective-permute-start | bytes 786440 | tf_op jit(solution)/shard_map/ppermute | solution.py:25
  13.1 2.1 %collective-permute-start.6 = (bf16[1024,128]{1,0:T(8,128)(2,1)S(1)}, bf16[1024,128]{1,0:T(8,128)(2,1)S(1)}, u32[]{:S(2)}, u32[]{:S(2)}) collective-permute-start(bf16[1024,128]{1,0:T(8,128)(2,1)S(1)} %order_rows.1.mine_ref.refs_4_), channel_id=1, source_target_pairs={{0,24},{1,25},{2,26},{3,27},{4,28},{5,29},{6,30},{7,31},{8,16},{9,... | collective-permute-start | bytes 786440 | tf_op jit(solution)/shard_map/ppermute | solution.py:25
  15.2 1.9 %collective-permute-start.8 = (bf16[1024,128]{1,0:T(8,128)(2,1)S(1)}, bf16[1024,128]{1,0:T(8,128)(2,1)S(1)}, u32[]{:S(2)}, u32[]{:S(2)}) collective-permute-start(bf16[1024,128]{1,0:T(8,128)(2,1)S(1)} %order_rows.1.mine_ref.refs_4_), channel_id=1, source_target_pairs={{0,4},{1,5},{2,6},{3,7},{4,0},{5,1},{6,2},{7,3},{8,12},{9,13},{10,... | collective-permute-start | bytes 786440 | tf_op jit(solution)/shard_map/ppermute | solution.py:25
  17.1 5.7 %stage1_0_1_2_6_4.1 = (bf16[256,8192]{1,0:T(8,128)(2,1)S(1)}, bf16[256,8192]{1,0:T(8,128)(2,1)S(1)}, bf16[256,8192]{1,0:T(8,128)(2,1)S(1)}, bf16[256,8192]{1,0:T(8,128)(2,1)S(1)}, bf16[256,8192]{1,0:T(8,128)(2,1)S(1)}) custom-call(bf16[1024,128]{1,0:T(8,128)(2,1)S(1)} %order_rows.1.mine_ref.refs_4_, ...), custom_call_target="tpu_custom_call" | custom-call | flops 5368709120 | bytes 1024 | tf_op jit(solution)/shard_map/stage1_0_1_2_6_4/pallas_call | solution.py:199
  22.9 1.8 %collective-permute-start.10 = (bf16[2,1024,128]{2,1,0:T(8,128)(2,1)S(1)}, bf16[2,1024,128]{2,1,0:T(8,128)(2,1)S(1)}, u32[]{:S(2)}, u32[]{:S(2)}) collective-permute-start(bf16[2,1024,128]{2,1,0:T(8,128)(2,1)S(1)} %get-tuple-element.33.refs_8_), channel_id=1, source_target_pairs={{0,32},{1,33},{2,34},{3,35},{4,36},{5,37},{6,38},{7,39},{8,40},{9,... | collective-permute-start | bytes 1572872 | tf_op jit(solution)/shard_map/ppermute | solution.py:25
  24.8 1.1 %collective-permute-start.7 = (bf16[1024,128]{1,0:T(8,128)(2,1)S(1)}, bf16[1024,128]{1,0:T(8,128)(2,1)S(1)}, u32[]{:S(2)}, u32[]{:S(2)}) collective-permute-start(bf16[1024,128]{1,0:T(8,128)(2,1)S(1)} %get-tuple-element.29), channel_id=1, source_target_pairs={{0,24},{1,25},{2,26},{3,27},{4,28},{5,29},{6,30},{7,31},{8,16},{9,... | collective-permute-start | bytes 786440 | tf_op jit(solution)/shard_map/ppermute | solution.py:25
  25.9 1.4 %collective-permute-start.11 = (bf16[2,1024,128]{2,1,0:T(8,128)(2,1)S(1)}, bf16[2,1024,128]{2,1,0:T(8,128)(2,1)S(1)}, u32[]{:S(2)}, u32[]{:S(2)}) collective-permute-start(bf16[2,1024,128]{2,1,0:T(8,128)(2,1)S(1)} %get-tuple-element.33.refs_8_), channel_id=1, source_target_pairs={{0,4},{1,5},{2,6},{3,7},{4,0},{5,1},{6,2},{7,3},{8,12},{9,13},{10,... | collective-permute-start | bytes 1572872 | tf_op jit(solution)/shard_map/ppermute | solution.py:25
  27.3 4.6 %stage2_near.1.refs_1_.refs_3_ = f32[4,64,128]{2,1,0:T(8,128)S(1)} custom-call(bf16[256,8192]{1,0:T(8,128)(2,1)S(1)} %get-tuple-element.28._.refs_1_.refs_0_, bf16[256,8192]{1,0:T(8,128)(2,1)S(1)} %get-tuple-element.30.refs_1_, bf16[256,8192]{1,0:T(8,128)(2,1)S(1)} %get-tuple-element.31.refs_2_, bf16[256,8192]{1,0:T(8,128)(2,1)S(1)} %get-tuple-element.32.refs_3_, ...), custom_call_target="tpu_custom_call" | custom-call | bytes 1024 | tf_op jit(solution)/shard_map/stage2_near/pallas_call | solution.py:243
  32.8 2.4 %stage1_3_7.1 = (bf16[256,8192]{1,0:T(8,128)(2,1)S(1)}, bf16[256,8192]{1,0:T(8,128)(2,1)S(1)}) custom-call(bf16[1024,128]{1,0:T(8,128)(2,1)S(1)} %order_rows.1.mine_ref.refs_4_, bf16[1024,128]{1,0:T(8,128)(2,1)S(1)} %collective-permute-done.4.other_ref.refs_5_, bf16[8,8,128,128]{3,2,1,0:T(8,128)(2,1)S(1)} %get-tuple-element.27.t_ref, ...), custom_call_target="tpu_custom_call" | custom-call | flops 8589934592 | bytes 1024 | tf_op jit(solution)/shard_map/stage1_3_7/pallas_call | solution.py:199
  35.2 2.4 %collective-permute-start.13 = (bf16[2,1024,128]{2,1,0:T(8,128)(2,1)S(1)}, bf16[2,1024,128]{2,1,0:T(8,128)(2,1)S(1)}, u32[]{:S(2)}, u32[]{:S(2)}) collective-permute-start(bf16[2,1024,128]{2,1,0:T(8,128)(2,1)S(1)} %relay.6.refs_0_.refs_3_), channel_id=1, source_target_pairs={{0,32},{1,33},{2,34},{3,35},{4,36},{5,37},{6,38},{7,39},{8,40},{9,... | collective-permute-start | bytes 1572872 | tf_op jit(solution)/shard_map/ppermute | solution.py:25
  37.6 1.3 %stage1_5.1.refs_1_.refs_2_ = bf16[256,8192]{1,0:T(8,128)(2,1)S(1)} custom-call(bf16[1024,128]{1,0:T(8,128)(2,1)S(1)} %order_rows.1.mine_ref.refs_4_, bf16[1024,128]{1,0:T(8,128)(2,1)S(1)} %collective-permute-done.4.other_ref.refs_5_, bf16[8,8,128,128]{3,2,1,0:T(8,128)(2,1)S(1)} %get-tuple-element.27.t_ref, ...), custom_call_target="tpu_custom_call" | custom-call | flops 1073741824 | bytes 1024 | tf_op jit(solution)/shard_map/stage1_5/pallas_call | solution.py:199
  39.3 1.2 %stage2_far.1.refs_7_ = f32[4,64,160]{2,1,0:T(8,128)S(1)} custom-call(bf16[256,8192]{1,0:T(8,128)(2,1)S(1)} %get-tuple-element.36.refs_0_, bf16[1024,128]{1,0:T(8,128)(2,1)S(1)} %relay.5.refs_0_.refs_1_, bf16[1024,128]{1,0:T(8,128)(2,1)S(1)} %collective-permute-done.12.refs_1_.refs_2_, f32[4,64,128]{2,1,0:T(8,128)S(1)} %stage2_near.1.refs_1_.refs_3_, ...), custom_call_target="tpu_custom_call" | custom-call | flops 1073741824 | bytes 1024 | tf_op jit(solution)/shard_map/stage2_far/pallas_call | solution.py:243
  40.6 3.5 %stage2_last.1.own_ref = f32[4,64,256]{2,1,0:T(8,128)S(1)} custom-call(bf16[256,8192]{1,0:T(8,128)(2,1)S(1)} %get-tuple-element.34.refs_1_.refs_0_, bf16[256,8192]{1,0:T(8,128)(2,1)S(1)} %get-tuple-element.35.refs_1_, bf16[256,8192]{1,0:T(8,128)(2,1)S(1)} %stage1_5.1.refs_1_.refs_2_, bf16[2,1024,128]{2,1,0:T(8,128)(2,1)S(1)} %relay.6.refs_0_.refs_3_, ...), custom_call_target="tpu_custom_call" | custom-call | flops 3221225472 | bytes 1024 | tf_op jit(solution)/shard_map/stage2_last/pallas_call | solution.py:243
  44.1 1.3 %collective-permute-start.16 = (f32[64,256]{1,0:T(8,128)S(1)}, f32[64,256]{1,0:T(8,128)S(1)}, u32[]{:S(2)}, u32[]{:S(2)}) collective-permute-start(f32[64,256]{1,0:T(8,128)S(1)} %get-tuple-element.39), channel_id=1, source_target_pairs={{0,2},{1,3},{2,0},{3,1},{4,6},{5,7},{6,4},{7,5},{8,10},{9,11},{10,... | collective-permute-start | bytes 196616 | tf_op jit(solution)/shard_map/ppermute | solution.py:25
  46.0 2.2 %collective-permute-start.18 = (f32[64,256]{1,0:T(8,128)S(1)}, f32[64,256]{1,0:T(8,128)S(1)}, u32[]{:S(2)}, u32[]{:S(2)}) collective-permute-start(f32[64,256]{1,0:T(8,128)S(1)} %get-tuple-element.37), channel_id=1, source_target_pairs={{0,3},{1,2},{2,1},{3,0},{4,7},{5,6},{6,5},{7,4},{8,11},{9,10},{10,... | collective-permute-start | bytes 196616 | tf_op jit(solution)/shard_map/ppermute | solution.py:25
  48.3 2.3 %collective-permute-done.16.r1_ref = f32[64,256]{1,0:T(8,128)S(1)} collective-permute-done((f32[64,256]{1,0:T(8,128)S(1)}, f32[64,256]{1,0:T(8,128)S(1)}, u32[]{:S(2)}, u32[]{:S(2)}) %collective-permute-start.16) | collective-permute-done | bytes 65568 | tf_op jit(solution)/shard_map/ppermute | solution.py:25
  50.6 0.9 %collective-permute-done.18.r3_ref = f32[64,256]{1,0:T(8,128)S(1)} collective-permute-done((f32[64,256]{1,0:T(8,128)S(1)}, f32[64,256]{1,0:T(8,128)S(1)}, u32[]{:S(2)}, u32[]{:S(2)}) %collective-permute-start.18) | collective-permute-done | bytes 65568 | tf_op jit(solution)/shard_map/ppermute | solution.py:25
  51.5 0.9 %finish.1 = f32[8,32,64]{2,1,0:T(8,128)} custom-call(f32[4,64,256]{2,1,0:T(8,128)S(1)} %stage2_last.1.own_ref, f32[64,256]{1,0:T(8,128)S(1)} %collective-permute-done.16.r1_ref, f32[64,256]{1,0:T(8,128)S(1)} %collective-permute-done.17.r2_ref, f32[64,256]{1,0:T(8,128)S(1)} %collective-permute-done.18.r3_ref), custom_call_target="tpu_custom_call" | custom-call | tf_op jit(solution)/shard_map/finish/pallas_call | solution.py:269
  (32 shorter events, 2.8 us)
Async XLA Ops:
  0.0 6.2 %copy-start = (s32[64]{0:T(128)S(1)}, s32[64]{0:T(128)}, u32[]{:S(2)}) copy-start(s32[64]{0:T(128)} %mirror_ref.1) | copy-start | bytes 772
  1.7 4.5 %collective-permute-start.3 = (bf16[8,8,128,128]{3,2,1,0:T(8,128)(2,1)S(1)}, bf16[8,8,128,128]{3,2,1,0:T(8,128)(2,1)S(1)}, u32[]{:S(2)}, u32[]{:S(2)}) collective-permute-start(bf16[8,8,128,128]{3,2,1,0:T(8,128)(2,1)S(1)} %get-tuple-element.25), channel_id=1, source_target_pairs={{0,32},{1,33},{2,34},{3,35},{4,36},{5,37},{6,38},{7,39},{8,40},{9,... | collective-permute-start | bytes 6291464 | tf_op jit(solution)/shard_map/ppermute | solution.py:25
  1.8 7.1 %collective-permute-start = (bf16[256,128]{1,0:T(8,128)(2,1)S(1)}, bf16[256,128]{1,0:T(8,128)(2,1)S(1)}, u32[]{:S(2)}, u32[]{:S(2)}) collective-permute-start(bf16[256,128]{1,0:T(8,128)(2,1)S(1)} %get-tuple-element.22), channel_id=1, source_target_pairs={{0,2},{1,3},{2,0},{3,1},{4,6},{5,7},{6,4},{7,5},{8,10},{9,11},{10,... | collective-permute-start | bytes 196616 | tf_op jit(solution)/shard_map/ppermute | solution.py:25
  5.2 4.5 %collective-permute-start.1 = (bf16[256,128]{1,0:T(8,128)(2,1)S(1)}, bf16[256,128]{1,0:T(8,128)(2,1)S(1)}, u32[]{:S(2)}, u32[]{:S(2)}) collective-permute-start(bf16[256,128]{1,0:T(8,128)(2,1)S(1)} %get-tuple-element.23), channel_id=1, source_target_pairs={{0,1},{1,0},{2,3},{3,2},{4,5},{5,4},{6,7},{7,6},{8,9},{9,8},{10,11... | collective-permute-start | bytes 196616 | tf_op jit(solution)/shard_map/ppermute | solution.py:25
  5.8 5.5 %collective-permute-start.2 = (bf16[256,128]{1,0:T(8,128)(2,1)S(1)}, bf16[256,128]{1,0:T(8,128)(2,1)S(1)}, u32[]{:S(2)}, u32[]{:S(2)}) collective-permute-start(bf16[256,128]{1,0:T(8,128)(2,1)S(1)} %get-tuple-element.24), channel_id=1, source_target_pairs={{0,3},{1,2},{2,1},{3,0},{4,7},{5,6},{6,5},{7,4},{8,11},{9,10},{10,... | collective-permute-start | bytes 196616 | tf_op jit(solution)/shard_map/ppermute | solution.py:25
  11.4 5.7 %collective-permute-start.4 = (bf16[1024,128]{1,0:T(8,128)(2,1)S(1)}, bf16[1024,128]{1,0:T(8,128)(2,1)S(1)}, u32[]{:S(2)}, u32[]{:S(2)}) collective-permute-start(bf16[1024,128]{1,0:T(8,128)(2,1)S(1)} %order_rows.1.mine_ref.refs_4_), channel_id=1, source_target_pairs={{0,32},{1,33},{2,34},{3,35},{4,36},{5,37},{6,38},{7,39},{8,40},{9,... | collective-permute-start | bytes 786440 | tf_op jit(solution)/shard_map/ppermute | solution.py:25
  11.5 11.3 %collective-permute-start.5 = (bf16[1024,128]{1,0:T(8,128)(2,1)S(1)}, bf16[1024,128]{1,0:T(8,128)(2,1)S(1)}, u32[]{:S(2)}, u32[]{:S(2)}) collective-permute-start(bf16[1024,128]{1,0:T(8,128)(2,1)S(1)} %order_rows.1.mine_ref.refs_4_), channel_id=1, source_target_pairs={{0,8},{1,9},{2,10},{3,11},{4,12},{5,13},{6,14},{7,15},{8,0},{9,1},... | collective-permute-start | bytes 786440 | tf_op jit(solution)/shard_map/ppermute | solution.py:25
  13.1 9.7 %collective-permute-start.6 = (bf16[1024,128]{1,0:T(8,128)(2,1)S(1)}, bf16[1024,128]{1,0:T(8,128)(2,1)S(1)}, u32[]{:S(2)}, u32[]{:S(2)}) collective-permute-start(bf16[1024,128]{1,0:T(8,128)(2,1)S(1)} %order_rows.1.mine_ref.refs_4_), channel_id=1, source_target_pairs={{0,24},{1,25},{2,26},{3,27},{4,28},{5,29},{6,30},{7,31},{8,16},{9,... | collective-permute-start | bytes 786440 | tf_op jit(solution)/shard_map/ppermute | solution.py:25
  15.2 9.5 %collective-permute-start.8 = (bf16[1024,128]{1,0:T(8,128)(2,1)S(1)}, bf16[1024,128]{1,0:T(8,128)(2,1)S(1)}, u32[]{:S(2)}, u32[]{:S(2)}) collective-permute-start(bf16[1024,128]{1,0:T(8,128)(2,1)S(1)} %order_rows.1.mine_ref.refs_4_), channel_id=1, source_target_pairs={{0,4},{1,5},{2,6},{3,7},{4,0},{5,1},{6,2},{7,3},{8,12},{9,13},{10,... | collective-permute-start | bytes 786440 | tf_op jit(solution)/shard_map/ppermute | solution.py:25
  22.9 4.5 %collective-permute-start.10 = (bf16[2,1024,128]{2,1,0:T(8,128)(2,1)S(1)}, bf16[2,1024,128]{2,1,0:T(8,128)(2,1)S(1)}, u32[]{:S(2)}, u32[]{:S(2)}) collective-permute-start(bf16[2,1024,128]{2,1,0:T(8,128)(2,1)S(1)} %get-tuple-element.33.refs_8_), channel_id=1, source_target_pairs={{0,32},{1,33},{2,34},{3,35},{4,36},{5,37},{6,38},{7,39},{8,40},{9,... | collective-permute-start | bytes 1572872 | tf_op jit(solution)/shard_map/ppermute | solution.py:25
  24.6 2.7 %collective-permute-start.9 = (bf16[1024,128]{1,0:T(8,128)(2,1)S(1)}, bf16[1024,128]{1,0:T(8,128)(2,1)S(1)}, u32[]{:S(2)}, u32[]{:S(2)}) collective-permute-start(bf16[1024,128]{1,0:T(8,128)(2,1)S(1)} %relay.4.refs_6_), channel_id=1, source_target_pairs={{0,32},{1,33},{2,34},{3,35},{4,36},{5,37},{6,38},{7,39},{8,40},{9,... | collective-permute-start | bytes 786440 | tf_op jit(solution)/shard_map/ppermute | solution.py:25
  24.8 7.6 %collective-permute-start.7 = (bf16[1024,128]{1,0:T(8,128)(2,1)S(1)}, bf16[1024,128]{1,0:T(8,128)(2,1)S(1)}, u32[]{:S(2)}, u32[]{:S(2)}) collective-permute-start(bf16[1024,128]{1,0:T(8,128)(2,1)S(1)} %get-tuple-element.29), channel_id=1, source_target_pairs={{0,24},{1,25},{2,26},{3,27},{4,28},{5,29},{6,30},{7,31},{8,16},{9,... | collective-permute-start | bytes 786440 | tf_op jit(solution)/shard_map/ppermute | solution.py:25
  25.9 9.3 %collective-permute-start.11 = (bf16[2,1024,128]{2,1,0:T(8,128)(2,1)S(1)}, bf16[2,1024,128]{2,1,0:T(8,128)(2,1)S(1)}, u32[]{:S(2)}, u32[]{:S(2)}) collective-permute-start(bf16[2,1024,128]{2,1,0:T(8,128)(2,1)S(1)} %get-tuple-element.33.refs_8_), channel_id=1, source_target_pairs={{0,4},{1,5},{2,6},{3,7},{4,0},{5,1},{6,2},{7,3},{8,12},{9,13},{10,... | collective-permute-start | bytes 1572872 | tf_op jit(solution)/shard_map/ppermute | solution.py:25
  32.3 5.3 %collective-permute-start.12 = (bf16[1024,128]{1,0:T(8,128)(2,1)S(1)}, bf16[1024,128]{1,0:T(8,128)(2,1)S(1)}, u32[]{:S(2)}, u32[]{:S(2)}) collective-permute-start(bf16[1024,128]{1,0:T(8,128)(2,1)S(1)} %relay.5.refs_0_.refs_1_), channel_id=1, source_target_pairs={{0,32},{1,33},{2,34},{3,35},{4,36},{5,37},{6,38},{7,39},{8,40},{9,... | collective-permute-start | bytes 786440 | tf_op jit(solution)/shard_map/ppermute | solution.py:25
  32.3 6.6 %collective-permute-start.14 = (bf16[1024,128]{1,0:T(8,128)(2,1)S(1)}, bf16[1024,128]{1,0:T(8,128)(2,1)S(1)}, u32[]{:S(2)}, u32[]{:S(2)}) collective-permute-start(bf16[1024,128]{1,0:T(8,128)(2,1)S(1)} %relay.5.refs_0_.refs_1_), channel_id=1, source_target_pairs={{0,4},{1,5},{2,6},{3,7},{4,0},{5,1},{6,2},{7,3},{8,12},{9,13},{10,... | collective-permute-start | bytes 786440 | tf_op jit(solution)/shard_map/ppermute | solution.py:25
  35.2 5.3 %collective-permute-start.13 = (bf16[2,1024,128]{2,1,0:T(8,128)(2,1)S(1)}, bf16[2,1024,128]{2,1,0:T(8,128)(2,1)S(1)}, u32[]{:S(2)}, u32[]{:S(2)}) collective-permute-start(bf16[2,1024,128]{2,1,0:T(8,128)(2,1)S(1)} %relay.6.refs_0_.refs_3_), channel_id=1, source_target_pairs={{0,32},{1,33},{2,34},{3,35},{4,36},{5,37},{6,38},{7,39},{8,40},{9,... | collective-permute-start | bytes 1572872 | tf_op jit(solution)/shard_map/ppermute | solution.py:25
  38.9 1.6 %collective-permute-start.15 = (bf16[1024,128]{1,0:T(8,128)(2,1)S(1)}, bf16[1024,128]{1,0:T(8,128)(2,1)S(1)}, u32[]{:S(2)}, u32[]{:S(2)}) collective-permute-start(bf16[1024,128]{1,0:T(8,128)(2,1)S(1)} %relay.7.refs_4_.refs_5_), channel_id=1, source_target_pairs={{0,32},{1,33},{2,34},{3,35},{4,36},{5,37},{6,38},{7,39},{8,40},{9,... | collective-permute-start | bytes 786440 | tf_op jit(solution)/shard_map/ppermute | solution.py:25
  44.1 6.5 %collective-permute-start.16 = (f32[64,256]{1,0:T(8,128)S(1)}, f32[64,256]{1,0:T(8,128)S(1)}, u32[]{:S(2)}, u32[]{:S(2)}) collective-permute-start(f32[64,256]{1,0:T(8,128)S(1)} %get-tuple-element.39), channel_id=1, source_target_pairs={{0,2},{1,3},{2,0},{3,1},{4,6},{5,7},{6,4},{7,5},{8,10},{9,11},{10,... | collective-permute-start | bytes 196616 | tf_op jit(solution)/shard_map/ppermute | solution.py:25
  45.4 5.2 %collective-permute-start.17 = (f32[64,256]{1,0:T(8,128)S(1)}, f32[64,256]{1,0:T(8,128)S(1)}, u32[]{:S(2)}, u32[]{:S(2)}) collective-permute-start(f32[64,256]{1,0:T(8,128)S(1)} %get-tuple-element.38), channel_id=1, source_target_pairs={{0,1},{1,0},{2,3},{3,2},{4,5},{5,4},{6,7},{7,6},{8,9},{9,8},{10,11... | collective-permute-start | bytes 196616 | tf_op jit(solution)/shard_map/ppermute | solution.py:25
  46.0 5.5 %collective-permute-start.18 = (f32[64,256]{1,0:T(8,128)S(1)}, f32[64,256]{1,0:T(8,128)S(1)}, u32[]{:S(2)}, u32[]{:S(2)}) collective-permute-start(f32[64,256]{1,0:T(8,128)S(1)} %get-tuple-element.37), channel_id=1, source_target_pairs={{0,3},{1,2},{2,1},{3,0},{4,7},{5,6},{6,5},{7,4},{8,11},{9,10},{10,... | collective-permute-start | bytes 196616 | tf_op jit(solution)/shard_map/ppermute | solution.py:25

commit v9 on v8

--- a/solution.py
+++ b/solution.py
@@ -173,43 +173,55 @@
     )(first, second, token)
 
 
-def stage1_kernel(classes, tokens, mine_ref, other_ref, t_ref, tp_ref, *refs):
-    for x_ref, g in zip(refs[tokens:], classes):
+def stage1_kernel(work, tokens, mine_ref, *refs):
+    both = any(half == 1 for _, half in work)
+    other_ref, refs = (refs[0], refs[1:]) if both else (None, refs)
+    t_ref, tp_ref, x_refs = refs[0], refs[1], refs[2 + tokens :]
+    for g in dict.fromkeys(g for g, _ in work):
         for pair in range(4):
             j0, j1 = 2 * pair, 2 * pair + 1
             upper = jnp.concatenate([t_ref[g, j0], t_ref[g, j1]], axis=1)
             lower = jnp.concatenate([tp_ref[g, j0], tp_ref[g, j1]], axis=1)
             weights = jnp.concatenate([upper, lower], axis=0)
-            for part in range(16):
-                own_ref = (mine_ref, other_ref)[part // 8]
-                own = own_ref[(part % 8) * 128 : (part % 8 + 1) * 128, :]
-                lhs = jnp.concatenate([own, own], axis=1)
-                x = jnp.dot(lhs, weights, preferred_element_type=F32).astype(BF16)
-                for k in range(2):
-                    j = 2 * pair + k
-                    for l in range(4):
-                        lane = (part * 4 + l) * 128
-                        x_ref[j * 32 : (j + 1) * 32, lane : lane + 128] = x[
-                            l * 32 : (l + 1) * 32, k * 128 : (k + 1) * 128
-                        ]
-
-
-def stage1(classes, own, tiles, tokens=(), weight=1):
-    n = len(classes)
-    return pl.pallas_call(
-        functools.partial(stage1_kernel, classes, len(tokens)),
-        out_shape=tuple(jax.ShapeDtypeStruct((256, 8192), BF16) for _ in classes),
-        in_specs=[spec(pltpu.VMEM)] * 4 + [spec(pl.ANY)] * len(tokens),
-        out_specs=tuple(spec(pltpu.VMEM) for _ in classes),
+            for x_ref, (own_g, half) in zip(x_refs, work):
+                if own_g != g:
+                    continue
+                own_ref = (mine_ref, other_ref)[half]
+                for part in range(8):
+                    own = own_ref[part * 128 : (part + 1) * 128, :]
+                    lhs = jnp.concatenate([own, own], axis=1)
+                    x = jnp.dot(lhs, weights, preferred_element_type=F32).astype(BF16)
+                    for k in range(2):
+                        j = 2 * pair + k
+                        for l in range(4):
+                            lane = (part * 4 + l) * 128
+                            x_ref[j * 32 : (j + 1) * 32, lane : lane + 128] = x[
+                                l * 32 : (l + 1) * 32, k * 128 : (k + 1) * 128
+                            ]
+
+
+def stage1(work, own, tiles, tokens=(), weight=1):
+    if all(half == 0 for _, half in work):
+        own = own[:1]
+    flops = int(len(work) * weight * 2**29)
+    return pl.pallas_call(
+        functools.partial(stage1_kernel, work, len(tokens)),
+        out_shape=tuple(jax.ShapeDtypeStruct((256, 4096), BF16) for _ in work),
+        in_specs=[spec(pltpu.VMEM)] * (len(own) + 2) + [spec(pl.ANY)] * len(tokens),
+        out_specs=tuple(spec(pltpu.VMEM) for _ in work),
         compiler_params=params(8),
-        cost_estimate=pl.CostEstimate(flops=int(n * weight * 2**30), transcendentals=0, bytes_accessed=2**10),
-        name="stage1_" + "_".join(str(g) for g in classes),
+        cost_estimate=pl.CostEstimate(flops=flops, transcendentals=0, bytes_accessed=2**10),
+        name="stage1_" + "_".join(str(g) for g in dict.fromkeys(g for g, _ in work)),
     )(*own, *tiles, *tokens)
+
+
+def halves(*classes):
+    return tuple((g, half) for g in classes for half in range(2))
 
 
 def stage2_kernel(picks, n_b, carried, tokens, *refs):
     n = len(picks)
-    x_refs, refs = refs[:n], refs[n:]
+    x_refs, refs = refs[: 2 * n], refs[2 * n :]
     b_refs, refs = refs[:n_b], refs[n_b:]
     carry, refs = refs[:carried], refs[carried:]
     out_ref, r_s = refs[tokens:]
@@ -221,10 +233,8 @@
             for step in range(16):
                 b = b_ref[step * 64 : (step + 1) * 64, :]
                 bt = jnp.concatenate([b[0:32], b[32:64]], axis=1)
-                lane = half * 4096 + step * 256
-                term = lax.dot_general(
-                    x_refs[i][:, lane : lane + 256], bt, NT, preferred_element_type=F32
-                )
+                x = x_refs[2 * i + half][:, step * 256 : (step + 1) * 256]
+                term = lax.dot_general(x, bt, NT, preferred_element_type=F32)
                 total = term if total is None else total + term
         r_s[i] = total
     for q in range(4):
@@ -238,12 +248,12 @@
 
 
 def stage2(name, xs, picks, bs, carry=(), tokens=(), weight=1):
-    n = len(xs)
+    n = len(picks)
     lanes = 32 * n + sum(c.shape[2] for c in carry)
     return pl.pallas_call(
         functools.partial(stage2_kernel, picks, len(bs), len(carry), len(tokens)),
         out_shape=jax.ShapeDtypeStruct((4, 64, lanes), F32),
-        in_specs=[spec(pltpu.VMEM)] * (n + len(bs) + len(carry)) + [spec(pl.ANY)] * len(tokens),
+        in_specs=[spec(pltpu.VMEM)] * (2 * n + len(bs) + len(carry)) + [spec(pl.ANY)] * len(tokens),
         out_specs=spec(pltpu.VMEM),
         scratch_shapes=[pltpu.VMEM((n, 256, 32), F32)],
         compiler_params=params(8),
@@ -278,7 +288,7 @@
     return jnp.transpose(out, (2, 0, 1))
 
 
-SA, NEAR, SB, SC = 1, 0, 4, 1
+FAST, SLOW = 0, 8
 
 
 def shards(cholesky, amplitudes, mirror):
@@ -289,32 +299,35 @@
     own = (mine, to_sibling(mine))
 
     x1a, x1b, z0 = over_x(mine, 1, 1), over_x(mine, 3, 3), over_z(mine)
-    xc0, xc1, xc2, xc6, xc4 = stage1((0, 1, 2, 6, 4), own, tiles, (), SA)
-    (z0,) = relay((z0,), (xc0,))
-    x1, forward = join(x1a, x1b, xc0)
-    x1_other, z0_other = to_sibling(x1), to_sibling(z0)
+    x0m, x0o, *xs = stage1(halves(0, 1, 2, 6, 4), own, tiles)
+    (z0,) = relay((z0,), (x0o,))
+    x1, forward = join(x1a, x1b, x0o)
     x2 = over_x(forward, 3, 1)
     zx1 = over_z(x1)
+    x1_other, z0_other = to_sibling(x1), to_sibling(z0)
+    x37 = stage1(halves(3, 7), own, tiles, (forward,), FAST)
+    self0 = stage2("self", (x0m, x0o), (((0, None), (1, None)),), own, (), (x37[0],), FAST)
+    (x2,) = relay((x2,), (self0,))
+    zx2 = over_z(x2)
+    x2_other = to_sibling(x2)
     near = stage2(
         "near",
-        (xc0, xc1, xc2, xc6),
-        (((0, None), (1, None)), ((2, None), (3, None)), ((4, 0), (5, 0)), ((4, 1), (5, 1))),
-        (*own, z0, z0_other, x1, x1_other),
-        weight=NEAR,
+        xs[0:6],
+        (((0, None), (1, None)), ((2, 0), (3, 0)), ((2, 1), (3, 1))),
+        (z0, z0_other, x1, x1_other),
+        (self0,),
+        (x2,),
+        SLOW,
     )
-    (x2,) = relay((x2,), (near,))
-    x2_other = to_sibling(x2)
-    zx2 = over_z(x2)
-    xc3, xc7 = stage1((3, 7), own, tiles, (x2,), SB)
-    (zx1,) = relay((zx1,), (xc3,))
+    (zx1,) = relay((zx1,), (near,))
     zx1_other = to_sibling(zx1)
-    (xc5,) = stage1((5,), own, tiles, (zx1, x2_other), SC)
-    (zx2,) = relay((zx2,), (xc5,))
+    x5 = stage1(halves(5), own, tiles, (zx1,))
+    (zx2,) = relay((zx2,), (x5[0],))
     zx2_other = to_sibling(zx2)
-    far = stage2("far", (xc4,), (((0, None), (1, None)),), (x2, x2_other), (near,), (zx2,))
+    far = stage2("far", xs[6:8], (((0, None), (1, None)),), (x2, x2_other), (near,), (zx2,))
     last = stage2(
         "last",
-        (xc3, xc7, xc5),
+        (*x37, *x5),
         (((0, 0), (1, 0)), ((0, 1), (1, 1)), ((2, None), (3, None))),
         (zx1, zx1_other, zx2, zx2_other),
         (far,),

time: 52.7 us -> 52.8 us (level)
  waiting for transfers between devices: 6.14 us -> 8.05 us
  starting transfers between devices: 22 us -> 20.1 us
    ppermute x19, starting transfers between devices: 22 us -> 20.1 us  [permute(): return lax.ppermute(value, ('occ', 'vir'), pairs)]
    ppermute x19, waiting for transfers between devices: 6.14 us -> 8.05 us  [permute(): return lax.ppermute(value, ('occ', 'vir'), pairs)]
    pallas_call x3 -> x4, Pallas kernels: 9.33 us -> 9.48 us  [stage2(): pl.pallas_call(functools.partial(stage2_kernel, picks, len(bs), len(carry...]
  transfers between devices with their start and end apart: 19 -> 19, of which waited for: 5 -> 6; matrix products, arithmetic and copies ran while one was open for 0% -> 0% of each run, Pallas kernels for 34% -> 34%
where the time goes in v9:
time: 52.8 us; the launch traced here: 52.5 us
  Pallas kernels  24.2 us (46%)
  starting transfers between devices  20.1 us (38%)
  waiting for transfers between devices  8.05 us (15%)
    ppermute x19, starting transfers between devices, permute(): return lax.ppermute(value, ('occ', 'vir'), pairs)  20.1 us
    pallas_call x4, Pallas kernels, stage2(): pl.pallas_call(functools.partial(stage2_kernel, picks, len(bs), len(carry...  9.48 us
    pallas_call x3, Pallas kernels, stage1(): pl.pallas_call(functools.partial(stage1_kernel, work, len(tokens)), out_s...  9.32 us
    ppermute x19, waiting for transfers between devices, permute(): return lax.ppermute(value, ('occ', 'vir'), pairs)  8.05 us
    pallas_call x1, Pallas kernels, twist_tiles(): pl.pallas_call(twist_kernel, out_shape=(shape, shape), in_specs=[spec(plt...  2.63 us
    pallas_call x1, Pallas kernels, cut_to_send(): pl.pallas_call(send_kernel, out_shape=(chunk,) * 4 + (jax.ShapeDtypeStruc...  1.7 us
  transfers between devices with their start and end apart: 19, of which 6 were waited for; matrix products, arithmetic and copies ran while one was open for 0% of the time, Pallas kernels for 34%

profile of v9, /device:TPU:0, one launch (start us, length us, event | category | flops | bytes accessed | tf_op | source)
XLA Modules:
  0.0 52.5 jit_solution(17707895703577518611)
XLA Ops:
  0.0 1.7 %cut_to_send.1 = (bf16[256,128]{1,0:T(8,128)(2,1)S(1)}, bf16[256,128]{1,0:T(8,128)(2,1)S(1)}, bf16[256,128]{1,0:T(8,128)(2,1)S(1)}, bf16[256,128]{1,0:T(8,128)(2,1)S(1)}, bf16[8,8,128,128]{3,2,1,0:T(8,128)(2,1)S(1)}) custom-call(bf16[2048,128]{1,0:T(8,128)(2,1)} %bitcast.8, bf16[64,8,128,128]{3,2,1,0:T(8,128)(2,1)} %amp_ref.3), custom_call_target="tpu_custom_call" | custom-call | tf_op jit(solution)/shard_map/cut_to_send/pallas_call | solution.py:75
  1.8 3.4 %collective-permute-start = (bf16[256,128]{1,0:T(8,128)(2,1)S(1)}, bf16[256,128]{1,0:T(8,128)(2,1)S(1)}, u32[]{:S(2)}, u32[]{:S(2)}) collective-permute-start(bf16[256,128]{1,0:T(8,128)(2,1)S(1)} %get-tuple-element.31), channel_id=1, source_target_pairs={{0,2},{1,3},{2,0},{3,1},{4,6},{5,7},{6,4},{7,5},{8,10},{9,11},{10,... | collective-permute-start | bytes 196616 | tf_op jit(solution)/shard_map/ppermute | solution.py:25
  6.2 2.6 %twist_tiles.1 = (bf16[8,8,128,128]{3,2,1,0:T(8,128)(2,1)S(1)}, bf16[8,8,128,128]{3,2,1,0:T(8,128)(2,1)S(1)}) custom-call(s32[64]{0:T(128)S(1)} %copy-done, bf16[64,8,128,128]{3,2,1,0:T(8,128)(2,1)} %amp_ref.3, bf16[8,8,128,128]{3,2,1,0:T(8,128)(2,1)S(1)} %collective-permute-done.3.received_ref), custom_call_target="tpu_custom_call" | custom-call | tf_op jit(solution)/shard_map/twist_tiles/pallas_call | solution.py:103
  9.6 1.7 %collective-permute-done.2.r3_ref = bf16[256,128]{1,0:T(8,128)(2,1)S(1)} collective-permute-done((bf16[256,128]{1,0:T(8,128)(2,1)S(1)}, bf16[256,128]{1,0:T(8,128)(2,1)S(1)}, u32[]{:S(2)}, u32[]{:S(2)}) %collective-permute-start.2) | collective-permute-done | bytes 65568 | tf_op jit(solution)/shard_map/ppermute | solution.py:25
  11.5 1.6 %collective-permute-start.5 = (bf16[1024,128]{1,0:T(8,128)(2,1)S(1)}, bf16[1024,128]{1,0:T(8,128)(2,1)S(1)}, u32[]{:S(2)}, u32[]{:S(2)}) collective-permute-start(bf16[1024,128]{1,0:T(8,128)(2,1)S(1)} %order_rows.1.mine_ref.refs_2_), channel_id=1, source_target_pairs={{0,8},{1,9},{2,10},{3,11},{4,12},{5,13},{6,14},{7,15},{8,0},{9,1},... | collective-permute-start | bytes 786440 | tf_op jit(solution)/shard_map/ppermute | solution.py:25
  13.1 2.1 %collective-permute-start.6 = (bf16[1024,128]{1,0:T(8,128)(2,1)S(1)}, bf16[1024,128]{1,0:T(8,128)(2,1)S(1)}, u32[]{:S(2)}, u32[]{:S(2)}) collective-permute-start(bf16[1024,128]{1,0:T(8,128)(2,1)S(1)} %order_rows.1.mine_ref.refs_2_), channel_id=1, source_target_pairs={{0,24},{1,25},{2,26},{3,27},{4,28},{5,29},{6,30},{7,31},{8,16},{9,... | collective-permute-start | bytes 786440 | tf_op jit(solution)/shard_map/ppermute | solution.py:25
  15.2 1.9 %collective-permute-start.8 = (bf16[1024,128]{1,0:T(8,128)(2,1)S(1)}, bf16[1024,128]{1,0:T(8,128)(2,1)S(1)}, u32[]{:S(2)}, u32[]{:S(2)}) collective-permute-start(bf16[1024,128]{1,0:T(8,128)(2,1)S(1)} %order_rows.1.mine_ref.refs_2_), channel_id=1, source_target_pairs={{0,4},{1,5},{2,6},{3,7},{4,0},{5,1},{6,2},{7,3},{8,12},{9,13},{10,... | collective-permute-start | bytes 786440 | tf_op jit(solution)/shard_map/ppermute | solution.py:25
  17.1 5.7 %stage1_0_1_2_6_4.1 = (bf16[256,4096]{1,0:T(8,128)(2,1)S(1)}, bf16[256,4096]{1,0:T(8,128)(2,1)S(1)}, bf16[256,4096]{1,0:T(8,128)(2,1)S(1)}, bf16[256,4096]{1,0:T...) custom-call(bf16[1024,128]{1,0:T(8,128)(2,1)S(1)} %order_rows.1.mine, ...), custom_call_target="tpu_custom_call" | custom-call | flops 5368709120 | bytes 1024 | tf_op jit(solution)/shard_map/stage1_0_1_2_6_4/pallas_call | solution.py:207
  22.9 1.8 %collective-permute-start.10 = (bf16[2,1024,128]{2,1,0:T(8,128)(2,1)S(1)}, bf16[2,1024,128]{2,1,0:T(8,128)(2,1)S(1)}, u32[]{:S(2)}, u32[]{:S(2)}) collective-permute-start(bf16[2,1024,128]{2,1,0:T(8,128)(2,1)S(1)} %get-tuple-element.43.refs_8_), channel_id=1, source_target_pairs={{0,32},{1,33},{2,34},{3,35},{4,36},{5,37},{6,38},{7,39},{8,40},{9,... | collective-permute-start | bytes 1572872 | tf_op jit(solution)/shard_map/ppermute | solution.py:25
  24.7 1.1 %collective-permute-start.11 = (bf16[1024,128]{1,0:T(8,128)(2,1)S(1)}, bf16[1024,128]{1,0:T(8,128)(2,1)S(1)}, u32[]{:S(2)}, u32[]{:S(2)}) collective-permute-start(bf16[1024,128]{1,0:T(8,128)(2,1)S(1)} %get-tuple-element.38.refs_3_), channel_id=1, source_target_pairs={{0,24},{1,25},{2,26},{3,27},{4,28},{5,29},{6,30},{7,31},{8,16},{9,... | collective-permute-start | bytes 786440 | tf_op jit(solution)/shard_map/ppermute | solution.py:25
  25.8 1.1 %collective-permute-start.7 = (bf16[2,1024,128]{2,1,0:T(8,128)(2,1)S(1)}, bf16[2,1024,128]{2,1,0:T(8,128)(2,1)S(1)}, u32[]{:S(2)}, u32[]{:S(2)}) collective-permute-start(bf16[2,1024,128]{2,1,0:T(8,128)(2,1)S(1)} %get-tuple-element.43.refs_8_), channel_id=1, source_target_pairs={{0,4},{1,5},{2,6},{3,7},{4,0},{5,1},{6,2},{7,3},{8,12},{9,13},{10,... | collective-permute-start | bytes 1572872 | tf_op jit(solution)/shard_map/ppermute | solution.py:25
  26.9 2.4 %stage1_3_7.1 = (bf16[256,4096]{1,0:T(8,128)(2,1)S(1)}, bf16[256,4096]{1,0:T(8,128)(2,1)S(1)}, bf16[256,4096]{1,0:T(8,128)(2,1)S(1)}, bf16[256,4096]{1,0:T(8,128)(2,1)S(1)}) custom-call(bf16[1024,128]{1,0:T(8,128)(2,1)S(1)} %order_rows.1.mine_ref.refs_2_, bf16[1024,128]{1,0:T(8,128)(2,1)S(1)} %collective-permute-done.4.refs_0_.refs_3_, ...), custom_call_target="tpu_custom_call" | custom-call | bytes 1024 | tf_op jit(solution)/shard_map/stage1_3_7/pallas_call | solution.py:207
  29.3 1.2 %stage2_self.1.refs_1_.refs_10_ = f32[4,64,32]{2,1,0:T(8,128)S(1)} custom-call(bf16[256,4096]{1,0:T(8,128)(2,1)S(1)} %get-tuple-element.50.refs_0_, bf16[256,4096]{1,0:T(8,128)(2,1)S(1)} %get-tuple-element.37._.refs_1_, bf16[1024,128]{1,0:T(8,128)(2,1)S(1)} %order_rows.1.mine_ref.refs_2_, bf16[1024,128]{1,0:T(8,128)(2,1)S(1)} %collective-permute-done.4.refs_0_.refs_3_, ...), custom_call_target="tpu_custom_call" | custom-call | bytes 1024 | tf_op jit(solution)/shard_map/stage2_self/pallas_call | solution.py:253
  30.5 1.7 %collective-permute-done.11.refs_0_ = bf16[1024,128]{1,0:T(8,128)(2,1)S(1)} collective-permute-done((bf16[1024,128]{1,0:T(8,128)(2,1)S(1)}, bf16[1024,128]{1,0:T(8,128)(2,1)S(1)}, u32[]{:S(2)}, u32[]{:S(2)}) %collective-permute-start.11) | collective-permute-done | bytes 262176 | tf_op jit(solution)/shard_map/ppermute | solution.py:25
  32.4 3.5 %stage2_near.1.refs_1_.refs_4_ = f32[4,64,128]{2,1,0:T(8,128)S(1)} custom-call(bf16[256,4096]{1,0:T(8,128)(2,1)S(1)} %get-tuple-element.44.refs_0_, bf16[256,4096]{1,0:T(8,128)(2,1)S(1)} %get-tuple-element.45.refs_1_, bf16[256,4096]{1,0:T(8,128)(2,1)S(1)} %get-tuple-element.46.refs_2_, bf16[256,4096]{1,0:T(8,128)(2,1)S(1)} %get-tuple-element.47.refs_3_, ...), custom_call_target="tpu_custom_call" | custom-call | flops 25769803776 | bytes 1024 | tf_op jit(solution)/shard_map/stage2_near/pallas_call | solution.py:253
  36.7 1.3 %stage1_5.1 = (bf16[256,4096]{1,0:T(8,128)(2,1)S(1)}, bf16[256,4096]{1,0:T(8,128)(2,1)S(1)}) custom-call(bf16[1024,128]{1,0:T(8,128)(2,1)S(1)} %order_rows.1.mine_ref.refs_2_, bf16[1024,128]{1,0:T(8,128)(2,1)S(1)} %collective-permute-done.4.refs_0_.refs_3_, bf16[8,8,128,128]{3,2,1,0:T(8,128)(2,1)S(1)} %get-tuple-element.36.refs_1_, ...), custom_call_target="tpu_custom_call" | custom-call | flops 1073741824 | bytes 1024 | tf_op jit(solution)/shard_map/stage1_5/pallas_call | solution.py:207
  38.6 0.8 %collective-permute-start.14 = (bf16[1024,128]{1,0:T(8,128)(2,1)S(1)}, bf16[1024,128]{1,0:T(8,128)(2,1)S(1)}, u32[]{:S(2)}, u32[]{:S(2)}) collective-permute-start(bf16[1024,128]{1,0:T(8,128)(2,1)S(1)} %relay.7.refs_5_.refs_8_), channel_id=1, source_target_pairs={{0,32},{1,33},{2,34},{3,35},{4,36},{5,37},{6,38},{7,39},{8,40},{9,... | collective-permute-start | bytes 786440 | tf_op jit(solution)/shard_map/ppermute | solution.py:25
  39.4 1.2 %stage2_far.1.refs_10_ = f32[4,64,160]{2,1,0:T(8,128)S(1)} custom-call(bf16[256,4096]{1,0:T(8,128)(2,1)S(1)} %get-tuple-element.53.refs_0_, bf16[256,4096]{1,0:T(8,128)(2,1)S(1)} %get-tuple-element.54.refs_1_, bf16[1024,128]{1,0:T(8,128)(2,1)S(1)} %relay.5.refs_11_.refs_2_, bf16[1024,128]{1,0:T(8,128)(2,1)S(1)} %collective-permute-done.15.refs_3_, ...), custom_call_target="tpu_custom_call" | custom-call | flops 1073741824 | bytes 1024 | tf_op jit(solution)/shard_map/stage2_far/pallas_call | solution.py:253
  40.7 3.5 %stage2_last.1.own_ref = f32[4,64,256]{2,1,0:T(8,128)S(1)} custom-call(bf16[256,4096]{1,0:T(8,128)(2,1)S(1)} %get-tuple-element.39.refs_4_.refs_0_, bf16[256,4096]{1,0:T(8,128)(2,1)S(1)} %get-tuple-element.40.refs_1_, bf16[256,4096]{1,0:T(8,128)(2,1)S(1)} %get-tuple-element.41.refs_2_, bf16[256,4096]{1,0:T(8,128)(2,1)S(1)} %get-tuple-element.42.refs_3_, ...), custom_call_target="tpu_custom_call" | custom-call | flops 3221225472 | bytes 1024 | tf_op jit(solution)/shard_map/stage2_last/pallas_call | solution.py:253
  44.2 1.3 %collective-permute-start.16 = (f32[64,256]{1,0:T(8,128)S(1)}, f32[64,256]{1,0:T(8,128)S(1)}, u32[]{:S(2)}, u32[]{:S(2)}) collective-permute-start(f32[64,256]{1,0:T(8,128)S(1)} %get-tuple-element.57), channel_id=1, source_target_pairs={{0,2},{1,3},{2,0},{3,1},{4,6},{5,7},{6,4},{7,5},{8,10},{9,11},{10,... | collective-permute-start | bytes 196616 | tf_op jit(solution)/shard_map/ppermute | solution.py:25
  46.2 2.2 %collective-permute-start.18 = (f32[64,256]{1,0:T(8,128)S(1)}, f32[64,256]{1,0:T(8,128)S(1)}, u32[]{:S(2)}, u32[]{:S(2)}) collective-permute-start(f32[64,256]{1,0:T(8,128)S(1)} %get-tuple-element.55), channel_id=1, source_target_pairs={{0,3},{1,2},{2,1},{3,0},{4,7},{5,6},{6,5},{7,4},{8,11},{9,10},{10,... | collective-permute-start | bytes 196616 | tf_op jit(solution)/shard_map/ppermute | solution.py:25
  48.4 2.3 %collective-permute-done.16.r1_ref = f32[64,256]{1,0:T(8,128)S(1)} collective-permute-done((f32[64,256]{1,0:T(8,128)S(1)}, f32[64,256]{1,0:T(8,128)S(1)}, u32[]{:S(2)}, u32[]{:S(2)}) %collective-permute-start.16) | collective-permute-done | bytes 65568 | tf_op jit(solution)/shard_map/ppermute | solution.py:25
  50.7 0.9 %collective-permute-done.18.r3_ref = f32[64,256]{1,0:T(8,128)S(1)} collective-permute-done((f32[64,256]{1,0:T(8,128)S(1)}, f32[64,256]{1,0:T(8,128)S(1)}, u32[]{:S(2)}, u32[]{:S(2)}) %collective-permute-start.18) | collective-permute-done | bytes 65568 | tf_op jit(solution)/shard_map/ppermute | solution.py:25
  51.6 0.9 %finish.1 = f32[8,32,64]{2,1,0:T(8,128)} custom-call(f32[4,64,256]{2,1,0:T(8,128)S(1)} %stage2_last.1.own_ref, f32[64,256]{1,0:T(8,128)S(1)} %collective-permute-done.16.r1_ref, f32[64,256]{1,0:T(8,128)S(1)} %collective-permute-done.17.r2_ref, f32[64,256]{1,0:T(8,128)S(1)} %collective-permute-done.18.r3_ref), custom_call_target="tpu_custom_call" | custom-call | tf_op jit(solution)/shard_map/finish/pallas_call | solution.py:279
  (33 shorter events, 4.4 us)
Async XLA Ops:
  0.0 6.2 %copy-start = (s32[64]{0:T(128)S(1)}, s32[64]{0:T(128)}, u32[]{:S(2)}) copy-start(s32[64]{0:T(128)} %mirror_ref.1) | copy-start | bytes 772
  1.7 4.5 %collective-permute-start.3 = (bf16[8,8,128,128]{3,2,1,0:T(8,128)(2,1)S(1)}, bf16[8,8,128,128]{3,2,1,0:T(8,128)(2,1)S(1)}, u32[]{:S(2)}, u32[]{:S(2)}) collective-permute-start(bf16[8,8,128,128]{3,2,1,0:T(8,128)(2,1)S(1)} %get-tuple-element.34), channel_id=1, source_target_pairs={{0,32},{1,33},{2,34},{3,35},{4,36},{5,37},{6,38},{7,39},{8,40},{9,... | collective-permute-start | bytes 6291464 | tf_op jit(solution)/shard_map/ppermute | solution.py:25
  1.8 7.1 %collective-permute-start = (bf16[256,128]{1,0:T(8,128)(2,1)S(1)}, bf16[256,128]{1,0:T(8,128)(2,1)S(1)}, u32[]{:S(2)}, u32[]{:S(2)}) collective-permute-start(bf16[256,128]{1,0:T(8,128)(2,1)S(1)} %get-tuple-element.31), channel_id=1, source_target_pairs={{0,2},{1,3},{2,0},{3,1},{4,6},{5,7},{6,4},{7,5},{8,10},{9,11},{10,... | collective-permute-start | bytes 196616 | tf_op jit(solution)/shard_map/ppermute | solution.py:25
  5.2 4.5 %collective-permute-start.1 = (bf16[256,128]{1,0:T(8,128)(2,1)S(1)}, bf16[256,128]{1,0:T(8,128)(2,1)S(1)}, u32[]{:S(2)}, u32[]{:S(2)}) collective-permute-start(bf16[256,128]{1,0:T(8,128)(2,1)S(1)} %get-tuple-element.32), channel_id=1, source_target_pairs={{0,1},{1,0},{2,3},{3,2},{4,5},{5,4},{6,7},{7,6},{8,9},{9,8},{10,11... | collective-permute-start | bytes 196616 | tf_op jit(solution)/shard_map/ppermute | solution.py:25
  5.8 5.5 %collective-permute-start.2 = (bf16[256,128]{1,0:T(8,128)(2,1)S(1)}, bf16[256,128]{1,0:T(8,128)(2,1)S(1)}, u32[]{:S(2)}, u32[]{:S(2)}) collective-permute-start(bf16[256,128]{1,0:T(8,128)(2,1)S(1)} %get-tuple-element.33), channel_id=1, source_target_pairs={{0,3},{1,2},{2,1},{3,0},{4,7},{5,6},{6,5},{7,4},{8,11},{9,10},{10,... | collective-permute-start | bytes 196616 | tf_op jit(solution)/shard_map/ppermute | solution.py:25
  11.4 5.7 %collective-permute-start.4 = (bf16[1024,128]{1,0:T(8,128)(2,1)S(1)}, bf16[1024,128]{1,0:T(8,128)(2,1)S(1)}, u32[]{:S(2)}, u32[]{:S(2)}) collective-permute-start(bf16[1024,128]{1,0:T(8,128)(2,1)S(1)} %order_rows.1.mine_ref.refs_2_), channel_id=1, source_target_pairs={{0,32},{1,33},{2,34},{3,35},{4,36},{5,37},{6,38},{7,39},{8,40},{9,... | collective-permute-start | bytes 786440 | tf_op jit(solution)/shard_map/ppermute | solution.py:25
  11.5 11.3 %collective-permute-start.5 = (bf16[1024,128]{1,0:T(8,128)(2,1)S(1)}, bf16[1024,128]{1,0:T(8,128)(2,1)S(1)}, u32[]{:S(2)}, u32[]{:S(2)}) collective-permute-start(bf16[1024,128]{1,0:T(8,128)(2,1)S(1)} %order_rows.1.mine_ref.refs_2_), channel_id=1, source_target_pairs={{0,8},{1,9},{2,10},{3,11},{4,12},{5,13},{6,14},{7,15},{8,0},{9,1},... | collective-permute-start | bytes 786440 | tf_op jit(solution)/shard_map/ppermute | solution.py:25
  13.1 9.7 %collective-permute-start.6 = (bf16[1024,128]{1,0:T(8,128)(2,1)S(1)}, bf16[1024,128]{1,0:T(8,128)(2,1)S(1)}, u32[]{:S(2)}, u32[]{:S(2)}) collective-permute-start(bf16[1024,128]{1,0:T(8,128)(2,1)S(1)} %order_rows.1.mine_ref.refs_2_), channel_id=1, source_target_pairs={{0,24},{1,25},{2,26},{3,27},{4,28},{5,29},{6,30},{7,31},{8,16},{9,... | collective-permute-start | bytes 786440 | tf_op jit(solution)/shard_map/ppermute | solution.py:25
  15.2 10.6 %collective-permute-start.8 = (bf16[1024,128]{1,0:T(8,128)(2,1)S(1)}, bf16[1024,128]{1,0:T(8,128)(2,1)S(1)}, u32[]{:S(2)}, u32[]{:S(2)}) collective-permute-start(bf16[1024,128]{1,0:T(8,128)(2,1)S(1)} %order_rows.1.mine_ref.refs_2_), channel_id=1, source_target_pairs={{0,4},{1,5},{2,6},{3,7},{4,0},{5,1},{6,2},{7,3},{8,12},{9,13},{10,... | collective-permute-start | bytes 786440 | tf_op jit(solution)/shard_map/ppermute | solution.py:25
  22.9 9.5 %collective-permute-start.10 = (bf16[2,1024,128]{2,1,0:T(8,128)(2,1)S(1)}, bf16[2,1024,128]{2,1,0:T(8,128)(2,1)S(1)}, u32[]{:S(2)}, u32[]{:S(2)}) collective-permute-start(bf16[2,1024,128]{2,1,0:T(8,128)(2,1)S(1)} %get-tuple-element.43.refs_8_), channel_id=1, source_target_pairs={{0,32},{1,33},{2,34},{3,35},{4,36},{5,37},{6,38},{7,39},{8,40},{9,... | collective-permute-start | bytes 1572872 | tf_op jit(solution)/shard_map/ppermute | solution.py:25
  24.7 7.6 %collective-permute-start.11 = (bf16[1024,128]{1,0:T(8,128)(2,1)S(1)}, bf16[1024,128]{1,0:T(8,128)(2,1)S(1)}, u32[]{:S(2)}, u32[]{:S(2)}) collective-permute-start(bf16[1024,128]{1,0:T(8,128)(2,1)S(1)} %get-tuple-element.38.refs_3_), channel_id=1, source_target_pairs={{0,24},{1,25},{2,26},{3,27},{4,28},{5,29},{6,30},{7,31},{8,16},{9,... | collective-permute-start | bytes 786440 | tf_op jit(solution)/shard_map/ppermute | solution.py:25
  25.8 6.6 %collective-permute-start.9 = (bf16[1024,128]{1,0:T(8,128)(2,1)S(1)}, bf16[1024,128]{1,0:T(8,128)(2,1)S(1)}, u32[]{:S(2)}, u32[]{:S(2)}) collective-permute-start(bf16[1024,128]{1,0:T(8,128)(2,1)S(1)} %relay.4.refs_6_), channel_id=1, source_target_pairs={{0,32},{1,33},{2,34},{3,35},{4,36},{5,37},{6,38},{7,39},{8,40},{9,... | collective-permute-start | bytes 786440 | tf_op jit(solution)/shard_map/ppermute | solution.py:25
  25.8 10.1 %collective-permute-start.7 = (bf16[2,1024,128]{2,1,0:T(8,128)(2,1)S(1)}, bf16[2,1024,128]{2,1,0:T(8,128)(2,1)S(1)}, u32[]{:S(2)}, u32[]{:S(2)}) collective-permute-start(bf16[2,1024,128]{2,1,0:T(8,128)(2,1)S(1)} %get-tuple-element.43.refs_8_), channel_id=1, source_target_pairs={{0,4},{1,5},{2,6},{3,7},{4,0},{5,1},{6,2},{7,3},{8,12},{9,13},{10,... | collective-permute-start | bytes 1572872 | tf_op jit(solution)/shard_map/ppermute | solution.py:25
  32.2 6.4 %collective-permute-start.13 = (bf16[1024,128]{1,0:T(8,128)(2,1)S(1)}, bf16[1024,128]{1,0:T(8,128)(2,1)S(1)}, u32[]{:S(2)}, u32[]{:S(2)}) collective-permute-start(bf16[1024,128]{1,0:T(8,128)(2,1)S(1)} %relay.5.refs_11_.refs_2_), channel_id=1, source_target_pairs={{0,4},{1,5},{2,6},{3,7},{4,0},{5,1},{6,2},{7,3},{8,12},{9,13},{10,... | collective-permute-start | bytes 786440 | tf_op jit(solution)/shard_map/ppermute | solution.py:25
  35.9 4.7 %collective-permute-start.12 = (bf16[2,1024,128]{2,1,0:T(8,128)(2,1)S(1)}, bf16[2,1024,128]{2,1,0:T(8,128)(2,1)S(1)}, u32[]{:S(2)}, u32[]{:S(2)}) collective-permute-start(bf16[2,1024,128]{2,1,0:T(8,128)(2,1)S(1)} %relay.6.refs_3_.refs_6_), channel_id=1, source_target_pairs={{0,32},{1,33},{2,34},{3,35},{4,36},{5,37},{6,38},{7,39},{8,40},{9,... | collective-permute-start | bytes 1572872 | tf_op jit(solution)/shard_map/ppermute | solution.py:25
  36.6 2.8 %collective-permute-start.15 = (bf16[1024,128]{1,0:T(8,128)(2,1)S(1)}, bf16[1024,128]{1,0:T(8,128)(2,1)S(1)}, u32[]{:S(2)}, u32[]{:S(2)}) collective-permute-start(bf16[1024,128]{1,0:T(8,128)(2,1)S(1)} %relay.5.refs_11_.refs_2_), channel_id=1, source_target_pairs={{0,32},{1,33},{2,34},{3,35},{4,36},{5,37},{6,38},{7,39},{8,40},{9,... | collective-permute-start | bytes 786440 | tf_op jit(solution)/shard_map/ppermute | solution.py:25
  38.6 2.0 %collective-permute-start.14 = (bf16[1024,128]{1,0:T(8,128)(2,1)S(1)}, bf16[1024,128]{1,0:T(8,128)(2,1)S(1)}, u32[]{:S(2)}, u32[]{:S(2)}) collective-permute-start(bf16[1024,128]{1,0:T(8,128)(2,1)S(1)} %relay.7.refs_5_.refs_8_), channel_id=1, source_target_pairs={{0,32},{1,33},{2,34},{3,35},{4,36},{5,37},{6,38},{7,39},{8,40},{9,... | collective-permute-start | bytes 786440 | tf_op jit(solution)/shard_map/ppermute | solution.py:25
  44.2 6.5 %collective-permute-start.16 = (f32[64,256]{1,0:T(8,128)S(1)}, f32[64,256]{1,0:T(8,128)S(1)}, u32[]{:S(2)}, u32[]{:S(2)}) collective-permute-start(f32[64,256]{1,0:T(8,128)S(1)} %get-tuple-element.57), channel_id=1, source_target_pairs={{0,2},{1,3},{2,0},{3,1},{4,6},{5,7},{6,4},{7,5},{8,10},{9,11},{10,... | collective-permute-start | bytes 196616 | tf_op jit(solution)/shard_map/ppermute | solution.py:25
  45.5 5.2 %collective-permute-start.17 = (f32[64,256]{1,0:T(8,128)S(1)}, f32[64,256]{1,0:T(8,128)S(1)}, u32[]{:S(2)}, u32[]{:S(2)}) collective-permute-start(f32[64,256]{1,0:T(8,128)S(1)} %get-tuple-element.56), channel_id=1, source_target_pairs={{0,1},{1,0},{2,3},{3,2},{4,5},{5,4},{6,7},{7,6},{8,9},{9,8},{10,11... | collective-permute-start | bytes 196616 | tf_op jit(solution)/shard_map/ppermute | solution.py:25
  46.2 5.5 %collective-permute-start.18 = (f32[64,256]{1,0:T(8,128)S(1)}, f32[64,256]{1,0:T(8,128)S(1)}, u32[]{:S(2)}, u32[]{:S(2)}) collective-permute-start(f32[64,256]{1,0:T(8,128)S(1)} %get-tuple-element.55), channel_id=1, source_target_pairs={{0,3},{1,2},{2,1},{3,0},{4,7},{5,6},{6,5},{7,4},{8,11},{9,10},{10,... | collective-permute-start | bytes 196616 | tf_op jit(solution)/shard_map/ppermute | solution.py:25

commit v10 on v9

--- a/solution.py
+++ b/solution.py
@@ -152,39 +152,58 @@
     return outs
 
 
-def join_kernel(first_ref, second_ref, _, both_ref, chosen_ref):
-    core = place()[2]
-    both_ref[0] = first_ref[...]
-    both_ref[1] = second_ref[...]
-    chosen_ref[...] = both_ref[core]
-
-
-def join(first, second, token):
+def join_kernel(mine_ref, other_ref, out_ref):
+    out_ref[0] = mine_ref[...]
+    out_ref[1] = other_ref[...]
+
+
+def join(mine, other):
     return pl.pallas_call(
         join_kernel,
-        out_shape=(
-            jax.ShapeDtypeStruct((2, *first.shape), first.dtype),
-            jax.ShapeDtypeStruct(first.shape, first.dtype),
-        ),
-        in_specs=[spec(pltpu.VMEM)] * 2 + [spec(pl.ANY)],
-        out_specs=(spec(pltpu.VMEM), spec(pltpu.VMEM)),
+        out_shape=jax.ShapeDtypeStruct((2, *mine.shape), mine.dtype),
+        in_specs=[spec(pltpu.VMEM)] * 2,
+        out_specs=spec(pltpu.VMEM),
         compiler_params=params(4),
         name="join",
-    )(first, second, token)
+    )(mine, other)
+
+
+def first_kernel(value_ref, _, out_ref, first_ref):
+    first_ref[...] = value_ref[0]
+
+
+def with_first(value, token):
+    return pl.pallas_call(
+        first_kernel,
+        out_shape=(
+            jax.ShapeDtypeStruct(value.shape, value.dtype),
+            jax.ShapeDtypeStruct(value.shape[1:], value.dtype),
+        ),
+        in_specs=[spec(pltpu.VMEM), spec(pl.ANY)],
+        out_specs=(spec(pl.ANY), spec(pltpu.VMEM)),
+        input_output_aliases={0: 0},
+        compiler_params=params(4),
+        name="with_first",
+    )(value, token)
+
+
+def on_core(pair):
+    return pair[0] if pair[0] == pair[1] else jnp.where(place()[2] == 1, pair[1], pair[0])
 
 
 def stage1_kernel(work, tokens, mine_ref, *refs):
     both = any(half == 1 for _, half in work)
     other_ref, refs = (refs[0], refs[1:]) if both else (None, refs)
     t_ref, tp_ref, x_refs = refs[0], refs[1], refs[2 + tokens :]
-    for g in dict.fromkeys(g for g, _ in work):
+    for slot in dict.fromkeys(slot for slot, _ in work):
+        g = on_core(slot)
         for pair in range(4):
             j0, j1 = 2 * pair, 2 * pair + 1
             upper = jnp.concatenate([t_ref[g, j0], t_ref[g, j1]], axis=1)
             lower = jnp.concatenate([tp_ref[g, j0], tp_ref[g, j1]], axis=1)
             weights = jnp.concatenate([upper, lower], axis=0)
-            for x_ref, (own_g, half) in zip(x_refs, work):
-                if own_g != g:
+            for x_ref, (its_slot, half) in zip(x_refs, work):
+                if its_slot != slot:
                     continue
                 own_ref = (mine_ref, other_ref)[half]
                 for part in range(8):
@@ -211,12 +230,12 @@
         out_specs=tuple(spec(pltpu.VMEM) for _ in work),
         compiler_params=params(8),
         cost_estimate=pl.CostEstimate(flops=flops, transcendentals=0, bytes_accessed=2**10),
-        name="stage1_" + "_".join(str(g) for g in dict.fromkeys(g for g, _ in work)),
+        name="stage1_" + "_".join(str(slot[0]) for slot in dict.fromkeys(slot for slot, _ in work)),
     )(*own, *tiles, *tokens)
 
 
-def halves(*classes):
-    return tuple((g, half) for g in classes for half in range(2))
+def halves(*slots):
+    return tuple((slot, half) for slot in slots for half in range(2))
 
 
 def stage2_kernel(picks, n_b, carried, tokens, *refs):
@@ -270,8 +289,8 @@
         for k in range(2):
             strip = sum_s[k, pl.ds(a8, CLS, stride=8), :]
             for c in range(4):
-                g = order[k * 4 + c]
-                pos_s[g * CLS : (g + 1) * CLS, a8 * 32 : (a8 + 1) * 32] = strip[:, c * 32 : (c + 1) * 32]
+                rows = pl.ds(pl.multiple_of(on_core(order[k * 4 + c]) * CLS, CLS), CLS)
+                pos_s[rows, a8 * 32 : (a8 + 1) * 32] = strip[:, c * 32 : (c + 1) * 32]
     out_ref[...] = pos_s[...].T.reshape(8, 32, ROWS)
 
 
@@ -298,22 +317,25 @@
     mine = order_rows((chunks[0], quarters[2], quarters[1], quarters[3]), tiles[1])
     own = (mine, to_sibling(mine))
 
-    x1a, x1b, z0 = over_x(mine, 1, 1), over_x(mine, 3, 3), over_z(mine)
-    x0m, x0o, *xs = stage1(halves(0, 1, 2, 6, 4), own, tiles)
+    c0, c1, c4, c5 = ((g, g) for g in (0, 1, 4, 5))
+    c26, c62, c37, c73 = (2, 6), (6, 2), (3, 7), (7, 3)
+    z0 = over_z(mine)
+    x1 = over_x(join(*own), 1, 3)
+    x0m, x0o, *xs = stage1(halves(c0, c1, c26, c62, c4, c37), own, tiles)
     (z0,) = relay((z0,), (x0o,))
-    x1, forward = join(x1a, x1b, x0o)
-    x2 = over_x(forward, 3, 1)
+    x1, x1_first = with_first(x1, x0o)
+    x2 = over_x(x1_first, 3, 1)
     zx1 = over_z(x1)
     x1_other, z0_other = to_sibling(x1), to_sibling(z0)
-    x37 = stage1(halves(3, 7), own, tiles, (forward,), FAST)
-    self0 = stage2("self", (x0m, x0o), (((0, None), (1, None)),), own, (), (x37[0],), FAST)
+    x73 = stage1(halves(c73), own, tiles, (x1_first,), FAST)
+    self0 = stage2("self", (x0m, x0o), (((0, None), (1, None)),), own, (), (x73[0],), FAST)
     (x2,) = relay((x2,), (self0,))
     zx2 = over_z(x2)
     x2_other = to_sibling(x2)
     near = stage2(
         "near",
         xs[0:6],
-        (((0, None), (1, None)), ((2, 0), (3, 0)), ((2, 1), (3, 1))),
+        (((0, None), (1, None)), ((2, 0), (2, 1)), ((3, 1), (3, 0))),
         (z0, z0_other, x1, x1_other),
         (self0,),
         (x2,),
@@ -321,19 +343,19 @@
     )
     (zx1,) = relay((zx1,), (near,))
     zx1_other = to_sibling(zx1)
-    x5 = stage1(halves(5), own, tiles, (zx1,))
+    x5 = stage1(halves(c5), own, tiles, (zx1,))
     (zx2,) = relay((zx2,), (x5[0],))
     zx2_other = to_sibling(zx2)
     far = stage2("far", xs[6:8], (((0, None), (1, None)),), (x2, x2_other), (near,), (zx2,))
     last = stage2(
         "last",
-        (*x37, *x5),
-        (((0, 0), (1, 0)), ((0, 1), (1, 1)), ((2, None), (3, None))),
+        (*xs[8:10], *x73, *x5),
+        (((0, 0), (0, 1)), ((1, 1), (1, 0)), ((2, None), (3, None))),
         (zx1, zx1_other, zx2, zx2_other),
         (far,),
     )
     parts = {k: over_y(last[k], k) for k in (2, 1, 3)}
-    return finish((0, 1, 2, 6, 4, 3, 7, 5), (last, parts[2], parts[1], parts[3]))
+    return finish((c0, c1, c26, c62, c4, c37, c73, c5), (last, parts[2], parts[1], parts[3]))
 
 
 def solution(mesh):

time: 52.8 us -> 53.9 us (1.021)
  waiting for transfers between devices: 8.05 us -> 10.7 us
  starting transfers between devices: 20.1 us -> 18.6 us
    ppermute x19 -> x18, waiting for transfers between devices: 8.05 us -> 10.7 us  [permute(): return lax.ppermute(value, ('occ', 'vir'), pairs)]
    ppermute x19 -> x18, starting transfers between devices: 20.1 us -> 18.6 us  [permute(): return lax.ppermute(value, ('occ', 'vir'), pairs)]
  transfers between devices with their start and end apart: 19 -> 18, of which waited for: 6 -> 8; matrix products, arithmetic and copies ran while one was open for 0% -> 0% of each run, Pallas kernels for 34% -> 34%
where the time goes in v10:
time: 53.9 us; the launch traced here: 53.7 us
  Pallas kernels  24.2 us (45%)
  starting transfers between devices  18.6 us (35%)
  waiting for transfers between devices  10.7 us (20%)
    ppermute x18, starting transfers between devices, permute(): return lax.ppermute(value, ('occ', 'vir'), pairs)  18.6 us
    ppermute x18, waiting for transfers between devices, permute(): return lax.ppermute(value, ('occ', 'vir'), pairs)  10.7 us
    pallas_call x4, Pallas kernels, stage2(): pl.pallas_call(functools.partial(stage2_kernel, picks, len(bs), len(carry...  9.48 us
    pallas_call x3, Pallas kernels, stage1(): pl.pallas_call(functools.partial(stage1_kernel, work, len(tokens)), out_s...  9.33 us
    pallas_call x1, Pallas kernels, twist_tiles(): pl.pallas_call(twist_kernel, out_shape=(shape, shape), in_specs=[spec(plt...  2.63 us
    pallas_call x1, Pallas kernels, cut_to_send(): pl.pallas_call(send_kernel, out_shape=(chunk,) * 4 + (jax.ShapeDtypeStruc...  1.7 us
  transfers between devices with their start and end apart: 18, of which 8 were waited for; matrix products, arithmetic and copies ran while one was open for 0% of the time, Pallas kernels for 34%

profile of v10, /device:TPU:0, one launch (start us, length us, event | category | flops | bytes accessed | tf_op | source)
XLA Modules:
  0.0 53.7 jit_solution(977281813938362752)
XLA Ops:
  0.0 1.7 %cut_to_send.1 = (bf16[256,128]{1,0:T(8,128)(2,1)S(1)}, bf16[256,128]{1,0:T(8,128)(2,1)S(1)}, bf16[256,128]{1,0:T(8,128)(2,1)S(1)}, bf16[256,128]{1,0:T(8,128)(2,1)S(1)}, bf16[8,8,128,128]{3,2,1,0:T(8,128)(2,1)S(1)}) custom-call(bf16[2048,128]{1,0:T(8,128)(2,1)} %bitcast.8, bf16[64,8,128,128]{3,2,1,0:T(8,128)(2,1)} %amp_ref.3), custom_call_target="tpu_custom_call" | custom-call | tf_op jit(solution)/shard_map/cut_to_send/pallas_call | solution.py:75
  1.8 3.4 %collective-permute-start = (bf16[256,128]{1,0:T(8,128)(2,1)S(1)}, bf16[256,128]{1,0:T(8,128)(2,1)S(1)}, u32[]{:S(2)}, u32[]{:S(2)}) collective-permute-start(bf16[256,128]{1,0:T(8,128)(2,1)S(1)} %get-tuple-element.31), channel_id=1, source_target_pairs={{0,2},{1,3},{2,0},{3,1},{4,6},{5,7},{6,4},{7,5},{8,10},{9,11},{10,... | collective-permute-start | bytes 196616 | tf_op jit(solution)/shard_map/ppermute | solution.py:25
  6.2 2.6 %twist_tiles.1 = (bf16[8,8,128,128]{3,2,1,0:T(8,128)(2,1)S(1)}, bf16[8,8,128,128]{3,2,1,0:T(8,128)(2,1)S(1)}) custom-call(s32[64]{0:T(128)S(1)} %copy-done, bf16[64,8,128,128]{3,2,1,0:T(8,128)(2,1)} %amp_ref.3, bf16[8,8,128,128]{3,2,1,0:T(8,128)(2,1)S(1)} %collective-permute-done.3.received_ref), custom_call_target="tpu_custom_call" | custom-call | tf_op jit(solution)/shard_map/twist_tiles/pallas_call | solution.py:103
  9.6 1.7 %collective-permute-done.2.r3_ref = bf16[256,128]{1,0:T(8,128)(2,1)S(1)} collective-permute-done((bf16[256,128]{1,0:T(8,128)(2,1)S(1)}, bf16[256,128]{1,0:T(8,128)(2,1)S(1)}, u32[]{:S(2)}, u32[]{:S(2)}) %collective-permute-start.2) | collective-permute-done | bytes 65568 | tf_op jit(solution)/shard_map/ppermute | solution.py:25
  11.5 2.0 %collective-permute-start.7 = (bf16[1024,128]{1,0:T(8,128)(2,1)S(1)}, bf16[1024,128]{1,0:T(8,128)(2,1)S(1)}, u32[]{:S(2)}, u32[]{:S(2)}) collective-permute-start(bf16[1024,128]{1,0:T(8,128)(2,1)S(1)} %order_rows.1.mine_ref.refs_2_), channel_id=1, source_target_pairs={{0,4},{1,5},{2,6},{3,7},{4,0},{5,1},{6,2},{7,3},{8,12},{9,13},{10,... | collective-permute-start | bytes 786440 | tf_op jit(solution)/shard_map/ppermute | solution.py:25
  13.5 1.6 %collective-permute-start.5 = (bf16[2,1024,128]{2,1,0:T(8,128)(2,1)S(1)}, bf16[2,1024,128]{2,1,0:T(8,128)(2,1)S(1)}, u32[]{:S(2)}, u32[]{:S(2)}) collective-permute-start(bf16[2,1024,128]{2,1,0:T(8,128)(2,1)S(1)} %join.1), channel_id=1, source_target_pairs={{0,8},{1,9},{2,10},{3,11},{4,12},{5,13},{6,14},{7,15},{8,0},{9,1},... | collective-permute-start | bytes 1572872 | tf_op jit(solution)/shard_map/ppermute | solution.py:25
  15.1 6.8 %stage1_0_1_2_6_4_3.1 = (bf16[256,4096]{1,0:T(8,128)(2,1)S(1)}, bf16[256,4096]{1,0:T(8,128)(2,1)S(1)}, bf16[256,4096]{1,0:T(8,128)(2,1)S(1)}, bf16[256,4096]{1,0...) custom-call(bf16[1024,128]{1,0:T(8,128)(2,1)S(1)} %order_rows.1.mine, ...), custom_call_target="tpu_custom_call" | custom-call | flops 6442450944 | bytes 1024 | tf_op jit(solution)/shard_map/stage1_0_1_2_6_4_3/pallas_call | solution.py:226
  21.9 0.9 %collective-permute-done.5.value_ref = bf16[2,1024,128]{2,1,0:T(8,128)(2,1)S(1)} collective-permute-done((bf16[2,1024,128]{2,1,0:T(8,128)(2,1)S(1)}, bf16[2,1024,128]{2,1,0:T(8,128)(2,1)S(1)}, u32[]{:S(2)}, u32[]{:S(2)}) %collective-permute-start.5) | collective-permute-done | bytes 524320 | tf_op jit(solution)/shard_map/ppermute | solution.py:25
  22.8 2.4 %collective-permute-start.9 = (bf16[2,1024,128]{2,1,0:T(8,128)(2,1)S(1)}, bf16[2,1024,128]{2,1,0:T(8,128)(2,1)S(1)}, u32[]{:S(2)}, u32[]{:S(2)}) collective-permute-start(bf16[2,1024,128]{2,1,0:T(8,128)(2,1)S(1)} %get-tuple-element.43.refs_8_), channel_id=1, source_target_pairs={{0,32},{1,33},{2,34},{3,35},{4,36},{5,37},{6,38},{7,39},{8,40},{9,... | collective-permute-start | bytes 1572872 | tf_op jit(solution)/shard_map/ppermute | solution.py:25
  25.3 2.7 %collective-permute-start.10 = (bf16[1024,128]{1,0:T(8,128)(2,1)S(1)}, bf16[1024,128]{1,0:T(8,128)(2,1)S(1)}, u32[]{:S(2)}, u32[]{:S(2)}) collective-permute-start(bf16[1024,128]{1,0:T(8,128)(2,1)S(1)} %get-tuple-element.40.refs_3_), channel_id=1, source_target_pairs={{0,24},{1,25},{2,26},{3,27},{4,28},{5,29},{6,30},{7,31},{8,16},{9,... | collective-permute-start | bytes 786440 | tf_op jit(solution)/shard_map/ppermute | solution.py:25
  28.0 1.3 %stage1_7.1 = (bf16[256,4096]{1,0:T(8,128)(2,1)S(1)}, bf16[256,4096]{1,0:T(8,128)(2,1)S(1)}) custom-call(bf16[1024,128]{1,0:T(8,128)(2,1)S(1)} %order_rows.1.mine_ref.refs_2_, bf16[1024,128]{1,0:T(8,128)(2,1)S(1)} %collective-permute-done.4.refs_0_.other_ref.refs_3_, bf16[8,8,128,128]{3,2,1,0:T(8,128)(2,1)S(1)} %get-tuple-element.36.refs_1_, ...), custom_call_target="tpu_custom_call" | custom-call | bytes 1024 | tf_op jit(solution)/shard_map/stage1_7/pallas_call | solution.py:226
  29.3 1.2 %stage2_self.1.refs_1_.refs_10_ = f32[4,64,32]{2,1,0:T(8,128)S(1)} custom-call(bf16[256,4096]{1,0:T(8,128)(2,1)S(1)} %get-tuple-element.50.refs_0_, bf16[256,4096]{1,0:T(8,128)(2,1)S(1)} %get-tuple-element.39._.refs_1_, bf16[1024,128]{1,0:T(8,128)(2,1)S(1)} %order_rows.1.mine_ref.refs_2_, ...), custom_call_target="tpu_custom_call" | custom-call | bytes 1024 | tf_op jit(solution)/shard_map/stage2_self/pallas_call | solution.py:272
  30.5 2.3 %collective-permute-done.10.refs_0_ = bf16[1024,128]{1,0:T(8,128)(2,1)S(1)} collective-permute-done((bf16[1024,128]{1,0:T(8,128)(2,1)S(1)}, bf16[1024,128]{1,0:T(8,128)(2,1)S(1)}, u32[]{:S(2)}, u32[]{:S(2)}) %collective-permute-start.10) | collective-permute-done | bytes 262176 | tf_op jit(solution)/shard_map/ppermute | solution.py:25
  32.9 3.5 %stage2_near.1.refs_1_.refs_4_ = f32[4,64,128]{2,1,0:T(8,128)S(1)} custom-call(bf16[256,4096]{1,0:T(8,128)(2,1)S(1)} %get-tuple-element.44.refs_0_, bf16[256,4096]{1,0:T(8,128)(2,1)S(1)} %get-tuple-element.45.refs_1_, bf16[256,4096]{1,0:T(8,128)(2,1)S(1)} %get-tuple-element.46.refs_2_, bf16[256,4096]{1,0:T(8,128)(2,1)S(1)} %get-tuple-element.47.refs_3_, ...), custom_call_target="tpu_custom_call" | custom-call | flops 25769803776 | bytes 1024 | tf_op jit(solution)/shard_map/stage2_near/pallas_call | solution.py:272
  36.4 0.8 %collective-permute-done.6.refs_0_ = bf16[2,1024,128]{2,1,0:T(8,128)(2,1)S(1)} collective-permute-done((bf16[2,1024,128]{2,1,0:T(8,128)(2,1)S(1)}, bf16[2,1024,128]{2,1,0:T(8,128)(2,1)S(1)}, u32[]{:S(2)}, u32[]{:S(2)}) %collective-permute-start.6) | collective-permute-done | bytes 524320 | tf_op jit(solution)/shard_map/ppermute | solution.py:25
  37.7 1.3 %stage1_5.1 = (bf16[256,4096]{1,0:T(8,128)(2,1)S(1)}, bf16[256,4096]{1,0:T(8,128)(2,1)S(1)}) custom-call(bf16[1024,128]{1,0:T(8,128)(2,1)S(1)} %order_rows.1.mine_ref.refs_2_, bf16[1024,128]{1,0:T(8,128)(2,1)S(1)} %collective-permute-done.4.refs_0_.other_ref.refs_3_, bf16[8,8,128,128]{3,2,1,0:T(8,128)(2,1)S(1)} %get-tuple-element.36.refs_1_, ...), custom_call_target="tpu_custom_call" | custom-call | flops 1073741824 | bytes 1024 | tf_op jit(solution)/shard_map/stage1_5/pallas_call | solution.py:226
  39.0 1.0 %collective-permute-done.12.refs_0_ = bf16[1024,128]{1,0:T(8,128)(2,1)S(1)} collective-permute-done((bf16[1024,128]{1,0:T(8,128)(2,1)S(1)}, bf16[1024,128]{1,0:T(8,128)(2,1)S(1)}, u32[]{:S(2)}, u32[]{:S(2)}) %collective-permute-start.12) | collective-permute-done | bytes 262176 | tf_op jit(solution)/shard_map/ppermute | solution.py:25
  40.6 1.2 %stage2_far.1.refs_10_ = f32[4,64,160]{2,1,0:T(8,128)S(1)} custom-call(bf16[256,4096]{1,0:T(8,128)(2,1)S(1)} %get-tuple-element.53.refs_0_, bf16[256,4096]{1,0:T(8,128)(2,1)S(1)} %get-tuple-element.54.refs_1_, bf16[1024,128]{1,0:T(8,128)(2,1)S(1)} %relay.5.refs_11_.refs_2_, bf16[1024,128]{1,0:T(8,128)(2,1)S(1)} %collective-permute-done.14.refs_3_, ...), custom_call_target="tpu_custom_call" | custom-call | flops 1073741824 | bytes 1024 | tf_op jit(solution)/shard_map/stage2_far/pallas_call | solution.py:272
  41.8 3.5 %stage2_last.1.own_ref = f32[4,64,256]{2,1,0:T(8,128)S(1)} custom-call(bf16[256,4096]{1,0:T(8,128)(2,1)S(1)} %get-tuple-element.37.refs_0_, bf16[256,4096]{1,0:T(8,128)(2,1)S(1)} %get-tuple-element.38.refs_1_, bf16[256,4096]{1,0:T(8,128)(2,1)S(1)} %get-tuple-element.41.refs_4_.refs_2_, bf16[256,4096]{1,0:T(8,128)(2,1)S(1)} %get-tuple-element.42.refs_3_, ...), custom_call_target="tpu_custom_call" | custom-call | flops 3221225472 | bytes 1024 | tf_op jit(solution)/shard_map/stage2_last/pallas_call | solution.py:272
  45.4 1.3 %collective-permute-start.15 = (f32[64,256]{1,0:T(8,128)S(1)}, f32[64,256]{1,0:T(8,128)S(1)}, u32[]{:S(2)}, u32[]{:S(2)}) collective-permute-start(f32[64,256]{1,0:T(8,128)S(1)} %get-tuple-element.57), channel_id=1, source_target_pairs={{0,2},{1,3},{2,0},{3,1},{4,6},{5,7},{6,4},{7,5},{8,10},{9,11},{10,... | collective-permute-start | bytes 196616 | tf_op jit(solution)/shard_map/ppermute | solution.py:25
  47.3 2.2 %collective-permute-start.17 = (f32[64,256]{1,0:T(8,128)S(1)}, f32[64,256]{1,0:T(8,128)S(1)}, u32[]{:S(2)}, u32[]{:S(2)}) collective-permute-start(f32[64,256]{1,0:T(8,128)S(1)} %get-tuple-element.55), channel_id=1, source_target_pairs={{0,3},{1,2},{2,1},{3,0},{4,7},{5,6},{6,5},{7,4},{8,11},{9,10},{10,... | collective-permute-start | bytes 196616 | tf_op jit(solution)/shard_map/ppermute | solution.py:25
  49.5 2.3 %collective-permute-done.15.r1_ref = f32[64,256]{1,0:T(8,128)S(1)} collective-permute-done((f32[64,256]{1,0:T(8,128)S(1)}, f32[64,256]{1,0:T(8,128)S(1)}, u32[]{:S(2)}, u32[]{:S(2)}) %collective-permute-start.15) | collective-permute-done | bytes 65568 | tf_op jit(solution)/shard_map/ppermute | solution.py:25
  51.9 0.9 %collective-permute-done.17.r3_ref = f32[64,256]{1,0:T(8,128)S(1)} collective-permute-done((f32[64,256]{1,0:T(8,128)S(1)}, f32[64,256]{1,0:T(8,128)S(1)}, u32[]{:S(2)}, u32[]{:S(2)}) %collective-permute-start.17) | collective-permute-done | bytes 65568 | tf_op jit(solution)/shard_map/ppermute | solution.py:25
  52.8 0.9 %finish.1 = f32[8,32,64]{2,1,0:T(8,128)} custom-call(f32[4,64,256]{2,1,0:T(8,128)S(1)} %stage2_last.1.own_ref, f32[64,256]{1,0:T(8,128)S(1)} %collective-permute-done.15.r1_ref, f32[64,256]{1,0:T(8,128)S(1)} %collective-permute-done.16.r2_ref, f32[64,256]{1,0:T(8,128)S(1)} %collective-permute-done.17.r3_ref), custom_call_target="tpu_custom_call" | custom-call | tf_op jit(solution)/shard_map/finish/pallas_call | solution.py:298
  (32 shorter events, 4.0 us)
Async XLA Ops:
  0.0 6.2 %copy-start = (s32[64]{0:T(128)S(1)}, s32[64]{0:T(128)}, u32[]{:S(2)}) copy-start(s32[64]{0:T(128)} %mirror_ref.1) | copy-start | bytes 772
  1.7 4.5 %collective-permute-start.3 = (bf16[8,8,128,128]{3,2,1,0:T(8,128)(2,1)S(1)}, bf16[8,8,128,128]{3,2,1,0:T(8,128)(2,1)S(1)}, u32[]{:S(2)}, u32[]{:S(2)}) collective-permute-start(bf16[8,8,128,128]{3,2,1,0:T(8,128)(2,1)S(1)} %get-tuple-element.34), channel_id=1, source_target_pairs={{0,32},{1,33},{2,34},{3,35},{4,36},{5,37},{6,38},{7,39},{8,40},{9,... | collective-permute-start | bytes 6291464 | tf_op jit(solution)/shard_map/ppermute | solution.py:25
  1.8 7.1 %collective-permute-start = (bf16[256,128]{1,0:T(8,128)(2,1)S(1)}, bf16[256,128]{1,0:T(8,128)(2,1)S(1)}, u32[]{:S(2)}, u32[]{:S(2)}) collective-permute-start(bf16[256,128]{1,0:T(8,128)(2,1)S(1)} %get-tuple-element.31), channel_id=1, source_target_pairs={{0,2},{1,3},{2,0},{3,1},{4,6},{5,7},{6,4},{7,5},{8,10},{9,11},{10,... | collective-permute-start | bytes 196616 | tf_op jit(solution)/shard_map/ppermute | solution.py:25
  5.2 4.5 %collective-permute-start.1 = (bf16[256,128]{1,0:T(8,128)(2,1)S(1)}, bf16[256,128]{1,0:T(8,128)(2,1)S(1)}, u32[]{:S(2)}, u32[]{:S(2)}) collective-permute-start(bf16[256,128]{1,0:T(8,128)(2,1)S(1)} %get-tuple-element.32), channel_id=1, source_target_pairs={{0,1},{1,0},{2,3},{3,2},{4,5},{5,4},{6,7},{7,6},{8,9},{9,8},{10,11... | collective-permute-start | bytes 196616 | tf_op jit(solution)/shard_map/ppermute | solution.py:25
  5.8 5.5 %collective-permute-start.2 = (bf16[256,128]{1,0:T(8,128)(2,1)S(1)}, bf16[256,128]{1,0:T(8,128)(2,1)S(1)}, u32[]{:S(2)}, u32[]{:S(2)}) collective-permute-start(bf16[256,128]{1,0:T(8,128)(2,1)S(1)} %get-tuple-element.33), channel_id=1, source_target_pairs={{0,3},{1,2},{2,1},{3,0},{4,7},{5,6},{6,5},{7,4},{8,11},{9,10},{10,... | collective-permute-start | bytes 196616 | tf_op jit(solution)/shard_map/ppermute | solution.py:25
  11.4 2.1 %collective-permute-start.4 = (bf16[1024,128]{1,0:T(8,128)(2,1)S(1)}, bf16[1024,128]{1,0:T(8,128)(2,1)S(1)}, u32[]{:S(2)}, u32[]{:S(2)}) collective-permute-start(bf16[1024,128]{1,0:T(8,128)(2,1)S(1)} %order_rows.1.mine_ref.refs_2_), channel_id=1, source_target_pairs={{0,32},{1,33},{2,34},{3,35},{4,36},{5,37},{6,38},{7,39},{8,40},{9,... | collective-permute-start | bytes 786440 | tf_op jit(solution)/shard_map/ppermute | solution.py:25
  11.5 16.5 %collective-permute-start.7 = (bf16[1024,128]{1,0:T(8,128)(2,1)S(1)}, bf16[1024,128]{1,0:T(8,128)(2,1)S(1)}, u32[]{:S(2)}, u32[]{:S(2)}) collective-permute-start(bf16[1024,128]{1,0:T(8,128)(2,1)S(1)} %order_rows.1.mine_ref.refs_2_), channel_id=1, source_target_pairs={{0,4},{1,5},{2,6},{3,7},{4,0},{5,1},{6,2},{7,3},{8,12},{9,13},{10,... | collective-permute-start | bytes 786440 | tf_op jit(solution)/shard_map/ppermute | solution.py:25
  13.5 9.3 %collective-permute-start.5 = (bf16[2,1024,128]{2,1,0:T(8,128)(2,1)S(1)}, bf16[2,1024,128]{2,1,0:T(8,128)(2,1)S(1)}, u32[]{:S(2)}, u32[]{:S(2)}) collective-permute-start(bf16[2,1024,128]{2,1,0:T(8,128)(2,1)S(1)} %join.1), channel_id=1, source_target_pairs={{0,8},{1,9},{2,10},{3,11},{4,12},{5,13},{6,14},{7,15},{8,0},{9,1},... | collective-permute-start | bytes 1572872 | tf_op jit(solution)/shard_map/ppermute | solution.py:25
  22.8 10.0 %collective-permute-start.9 = (bf16[2,1024,128]{2,1,0:T(8,128)(2,1)S(1)}, bf16[2,1024,128]{2,1,0:T(8,128)(2,1)S(1)}, u32[]{:S(2)}, u32[]{:S(2)}) collective-permute-start(bf16[2,1024,128]{2,1,0:T(8,128)(2,1)S(1)} %get-tuple-element.43.refs_8_), channel_id=1, source_target_pairs={{0,32},{1,33},{2,34},{3,35},{4,36},{5,37},{6,38},{7,39},{8,40},{9,... | collective-permute-start | bytes 1572872 | tf_op jit(solution)/shard_map/ppermute | solution.py:25
  25.3 7.6 %collective-permute-start.10 = (bf16[1024,128]{1,0:T(8,128)(2,1)S(1)}, bf16[1024,128]{1,0:T(8,128)(2,1)S(1)}, u32[]{:S(2)}, u32[]{:S(2)}) collective-permute-start(bf16[1024,128]{1,0:T(8,128)(2,1)S(1)} %get-tuple-element.40.refs_3_), channel_id=1, source_target_pairs={{0,24},{1,25},{2,26},{3,27},{4,28},{5,29},{6,30},{7,31},{8,16},{9,... | collective-permute-start | bytes 786440 | tf_op jit(solution)/shard_map/ppermute | solution.py:25
  28.0 4.9 %collective-permute-start.8 = (bf16[1024,128]{1,0:T(8,128)(2,1)S(1)}, bf16[1024,128]{1,0:T(8,128)(2,1)S(1)}, u32[]{:S(2)}, u32[]{:S(2)}) collective-permute-start(bf16[1024,128]{1,0:T(8,128)(2,1)S(1)} %relay.4.refs_6_), channel_id=1, source_target_pairs={{0,32},{1,33},{2,34},{3,35},{4,36},{5,37},{6,38},{7,39},{8,40},{9,... | collective-permute-start | bytes 786440 | tf_op jit(solution)/shard_map/ppermute | solution.py:25
  28.0 9.2 %collective-permute-start.6 = (bf16[2,1024,128]{2,1,0:T(8,128)(2,1)S(1)}, bf16[2,1024,128]{2,1,0:T(8,128)(2,1)S(1)}, u32[]{:S(2)}, u32[]{:S(2)}) collective-permute-start(bf16[2,1024,128]{2,1,0:T(8,128)(2,1)S(1)} %get-tuple-element.43.refs_8_), channel_id=1, source_target_pairs={{0,4},{1,5},{2,6},{3,7},{4,0},{5,1},{6,2},{7,3},{8,12},{9,13},{10,... | collective-permute-start | bytes 1572872 | tf_op jit(solution)/shard_map/ppermute | solution.py:25
  32.8 7.1 %collective-permute-start.12 = (bf16[1024,128]{1,0:T(8,128)(2,1)S(1)}, bf16[1024,128]{1,0:T(8,128)(2,1)S(1)}, u32[]{:S(2)}, u32[]{:S(2)}) collective-permute-start(bf16[1024,128]{1,0:T(8,128)(2,1)S(1)} %relay.5.refs_11_.refs_2_), channel_id=1, source_target_pairs={{0,4},{1,5},{2,6},{3,7},{4,0},{5,1},{6,2},{7,3},{8,12},{9,13},{10,... | collective-permute-start | bytes 786440 | tf_op jit(solution)/shard_map/ppermute | solution.py:25
  37.2 4.6 %collective-permute-start.11 = (bf16[2,1024,128]{2,1,0:T(8,128)(2,1)S(1)}, bf16[2,1024,128]{2,1,0:T(8,128)(2,1)S(1)}, u32[]{:S(2)}, u32[]{:S(2)}) collective-permute-start(bf16[2,1024,128]{2,1,0:T(8,128)(2,1)S(1)} %relay.6.refs_3_.refs_6_), channel_id=1, source_target_pairs={{0,32},{1,33},{2,34},{3,35},{4,36},{5,37},{6,38},{7,39},{8,40},{9,... | collective-permute-start | bytes 1572872 | tf_op jit(solution)/shard_map/ppermute | solution.py:25
  37.7 2.8 %collective-permute-start.14 = (bf16[1024,128]{1,0:T(8,128)(2,1)S(1)}, bf16[1024,128]{1,0:T(8,128)(2,1)S(1)}, u32[]{:S(2)}, u32[]{:S(2)}) collective-permute-start(bf16[1024,128]{1,0:T(8,128)(2,1)S(1)} %relay.5.refs_11_.refs_2_), channel_id=1, source_target_pairs={{0,32},{1,33},{2,34},{3,35},{4,36},{5,37},{6,38},{7,39},{8,40},{9,... | collective-permute-start | bytes 786440 | tf_op jit(solution)/shard_map/ppermute | solution.py:25
  40.0 1.8 %collective-permute-start.13 = (bf16[1024,128]{1,0:T(8,128)(2,1)S(1)}, bf16[1024,128]{1,0:T(8,128)(2,1)S(1)}, u32[]{:S(2)}, u32[]{:S(2)}) collective-permute-start(bf16[1024,128]{1,0:T(8,128)(2,1)S(1)} %relay.7.refs_5_.refs_8_), channel_id=1, source_target_pairs={{0,32},{1,33},{2,34},{3,35},{4,36},{5,37},{6,38},{7,39},{8,40},{9,... | collective-permute-start | bytes 786440 | tf_op jit(solution)/shard_map/ppermute | solution.py:25
  45.4 6.5 %collective-permute-start.15 = (f32[64,256]{1,0:T(8,128)S(1)}, f32[64,256]{1,0:T(8,128)S(1)}, u32[]{:S(2)}, u32[]{:S(2)}) collective-permute-start(f32[64,256]{1,0:T(8,128)S(1)} %get-tuple-element.57), channel_id=1, source_target_pairs={{0,2},{1,3},{2,0},{3,1},{4,6},{5,7},{6,4},{7,5},{8,10},{9,11},{10,... | collective-permute-start | bytes 196616 | tf_op jit(solution)/shard_map/ppermute | solution.py:25
  46.6 5.2 %collective-permute-start.16 = (f32[64,256]{1,0:T(8,128)S(1)}, f32[64,256]{1,0:T(8,128)S(1)}, u32[]{:S(2)}, u32[]{:S(2)}) collective-permute-start(f32[64,256]{1,0:T(8,128)S(1)} %get-tuple-element.56), channel_id=1, source_target_pairs={{0,1},{1,0},{2,3},{3,2},{4,5},{5,4},{6,7},{7,6},{8,9},{9,8},{10,11... | collective-permute-start | bytes 196616 | tf_op jit(solution)/shard_map/ppermute | solution.py:25
  47.3 5.5 %collective-permute-start.17 = (f32[64,256]{1,0:T(8,128)S(1)}, f32[64,256]{1,0:T(8,128)S(1)}, u32[]{:S(2)}, u32[]{:S(2)}) collective-permute-start(f32[64,256]{1,0:T(8,128)S(1)} %get-tuple-element.55), channel_id=1, source_target_pairs={{0,3},{1,2},{2,1},{3,0},{4,7},{5,6},{6,5},{7,4},{8,11},{9,10},{10,... | collective-permute-start | bytes 196616 | tf_op jit(solution)/shard_map/ppermute | solution.py:25

commit v11 on v10

--- a/solution.py
+++ b/solution.py
@@ -147,44 +147,29 @@
         out_specs=tuple(spec(pl.ANY) for _ in values),
         input_output_aliases={i: i for i in range(n)},
         compiler_params=params(1),
+        cost_estimate=pl.CostEstimate(flops=0, transcendentals=0, bytes_accessed=0),
         name="relay",
     )(*values, *tokens)
     return outs
 
 
-def join_kernel(mine_ref, other_ref, out_ref):
-    out_ref[0] = mine_ref[...]
-    out_ref[1] = other_ref[...]
-
-
-def join(mine, other):
+def join_kernel(first_ref, second_ref, third_ref, _, pair_ref, all_ref):
+    for i, ref in enumerate((first_ref, second_ref)):
+        pair_ref[i] = ref[...]
+        all_ref[i] = ref[...]
+    all_ref[2] = third_ref[...]
+
+
+def join(first, second, third, token):
     return pl.pallas_call(
         join_kernel,
-        out_shape=jax.ShapeDtypeStruct((2, *mine.shape), mine.dtype),
-        in_specs=[spec(pltpu.VMEM)] * 2,
-        out_specs=spec(pltpu.VMEM),
+        out_shape=tuple(jax.ShapeDtypeStruct((n, *first.shape), first.dtype) for n in (2, 3)),
+        in_specs=[spec(pltpu.VMEM)] * 3 + [spec(pl.ANY)],
+        out_specs=(spec(pltpu.VMEM), spec(pltpu.VMEM)),
         compiler_params=params(4),
+        cost_estimate=pl.CostEstimate(flops=0, transcendentals=0, bytes_accessed=0),
         name="join",
-    )(mine, other)
-
-
-def first_kernel(value_ref, _, out_ref, first_ref):
-    first_ref[...] = value_ref[0]
-
-
-def with_first(value, token):
-    return pl.pallas_call(
-        first_kernel,
-        out_shape=(
-            jax.ShapeDtypeStruct(value.shape, value.dtype),
-            jax.ShapeDtypeStruct(value.shape[1:], value.dtype),
-        ),
-        in_specs=[spec(pltpu.VMEM), spec(pl.ANY)],
-        out_specs=(spec(pl.ANY), spec(pltpu.VMEM)),
-        input_output_aliases={0: 0},
-        compiler_params=params(4),
-        name="with_first",
-    )(value, token)
+    )(first, second, third, token)
 
 
 def on_core(pair):
@@ -319,24 +304,23 @@
 
     c0, c1, c4, c5 = ((g, g) for g in (0, 1, 4, 5))
     c26, c62, c37, c73 = (2, 6), (6, 2), (3, 7), (7, 3)
-    z0 = over_z(mine)
-    x1 = over_x(join(*own), 1, 3)
-    x0m, x0o, *xs = stage1(halves(c0, c1, c26, c62, c4, c37), own, tiles)
-    (z0,) = relay((z0,), (x0o,))
-    x1, x1_first = with_first(x1, x0o)
-    x2 = over_x(x1_first, 3, 1)
+    x1a, x1b, z0 = over_x(mine, 1, 3), over_x(mine, 3, 1), over_z(mine)
+    x0m, x0o, *xs = stage1(halves(c0, c1, c26, c62, c4), own, tiles)
+    (x1a,) = relay((x1a,), (x0o,))
+    x2 = over_x(x1a, 3, 1)
+    x1, near_blocks = join(x1a, x1b, z0, x0o)
     zx1 = over_z(x1)
-    x1_other, z0_other = to_sibling(x1), to_sibling(z0)
-    x73 = stage1(halves(c73), own, tiles, (x1_first,), FAST)
-    self0 = stage2("self", (x0m, x0o), (((0, None), (1, None)),), own, (), (x73[0],), FAST)
+    other_blocks = to_sibling(near_blocks)
+    x37 = stage1(halves(c37, c73), own, tiles, (x1,), FAST)
+    self0 = stage2("self", (x0m, x0o), (((0, None), (1, None)),), own, (), (x37[0],), FAST)
     (x2,) = relay((x2,), (self0,))
     zx2 = over_z(x2)
     x2_other = to_sibling(x2)
     near = stage2(
         "near",
         xs[0:6],
-        (((0, None), (1, None)), ((2, 0), (2, 1)), ((3, 1), (3, 0))),
-        (z0, z0_other, x1, x1_other),
+        (((0, 2), (1, 2)), ((0, 0), (1, 1)), ((0, 1), (1, 0))),
+        (near_blocks, other_blocks),
         (self0,),
         (x2,),
         SLOW,
@@ -349,8 +333,8 @@
     far = stage2("far", xs[6:8], (((0, None), (1, None)),), (x2, x2_other), (near,), (zx2,))
     last = stage2(
         "last",
-        (*xs[8:10], *x73, *x5),
-        (((0, 0), (0, 1)), ((1, 1), (1, 0)), ((2, None), (3, None))),
+        (*x37, *x5),
+        (((0, 0), (1, 1)), ((0, 1), (1, 0)), ((2, None), (3, None))),
         (zx1, zx1_other, zx2, zx2_other),
         (far,),
     )

time: 53.9 us -> 51.8 us (0.961)
  waiting for transfers between devices: 10.7 us -> 8.71 us
    ppermute x18, waiting for transfers between devices: 10.7 us -> 8.71 us  [permute(): return lax.ppermute(value, ('occ', 'vir'), pairs)]
  transfers between devices with their start and end apart: 18 -> 18, of which waited for: 8 -> 7; matrix products, arithmetic and copies ran while one was open for 0% -> 0% of each run, Pallas kernels for 34% -> 35%
where the time goes in v11:
time: 51.8 us; the launch traced here: 51.5 us
  Pallas kernels  24.3 us (47%)
  starting transfers between devices  18.4 us (36%)
  waiting for transfers between devices  8.71 us (17%)
    ppermute x18, starting transfers between devices, permute(): return lax.ppermute(value, ('occ', 'vir'), pairs)  18.4 us
    pallas_call x4, Pallas kernels, stage2(): pl.pallas_call(functools.partial(stage2_kernel, picks, len(bs), len(carry...  9.48 us
    pallas_call x3, Pallas kernels, stage1(): pl.pallas_call(functools.partial(stage1_kernel, work, len(tokens)), out_s...  9.31 us
    ppermute x18, waiting for transfers between devices, permute(): return lax.ppermute(value, ('occ', 'vir'), pairs)  8.71 us
    pallas_call x1, Pallas kernels, twist_tiles(): pl.pallas_call(twist_kernel, out_shape=(shape, shape), in_specs=[spec(plt...  2.63 us
    pallas_call x1, Pallas kernels, cut_to_send(): pl.pallas_call(send_kernel, out_shape=(chunk,) * 4 + (jax.ShapeDtypeStruc...  1.7 us
  transfers between devices with their start and end apart: 18, of which 7 were waited for; matrix products, arithmetic and copies ran while one was open for 0% of the time, Pallas kernels for 35%

profile of v11, /device:TPU:0, one launch (start us, length us, event | category | flops | bytes accessed | tf_op | source)
XLA Modules:
  0.0 51.5 jit_solution(2136515007205795494)
XLA Ops:
  0.0 1.7 %cut_to_send.1 = (bf16[256,128]{1,0:T(8,128)(2,1)S(1)}, bf16[256,128]{1,0:T(8,128)(2,1)S(1)}, bf16[256,128]{1,0:T(8,128)(2,1)S(1)}, bf16[256,128]{1,0:T(8,128)(2,1)S(1)}, bf16[8,8,128,128]{3,2,1,0:T(8,128)(2,1)S(1)}) custom-call(bf16[2048,128]{1,0:T(8,128)(2,1)} %bitcast.8, bf16[64,8,128,128]{3,2,1,0:T(8,128)(2,1)} %amp_ref.3), custom_call_target="tpu_custom_call" | custom-call | tf_op jit(solution)/shard_map/cut_to_send/pallas_call | solution.py:75
  1.8 3.4 %collective-permute-start = (bf16[256,128]{1,0:T(8,128)(2,1)S(1)}, bf16[256,128]{1,0:T(8,128)(2,1)S(1)}, u32[]{:S(2)}, u32[]{:S(2)}) collective-permute-start(bf16[256,128]{1,0:T(8,128)(2,1)S(1)} %get-tuple-element.31), channel_id=1, source_target_pairs={{0,2},{1,3},{2,0},{3,1},{4,6},{5,7},{6,4},{7,5},{8,10},{9,11},{10,... | collective-permute-start | bytes 196616 | tf_op jit(solution)/shard_map/ppermute | solution.py:25
  6.2 2.6 %twist_tiles.1 = (bf16[8,8,128,128]{3,2,1,0:T(8,128)(2,1)S(1)}, bf16[8,8,128,128]{3,2,1,0:T(8,128)(2,1)S(1)}) custom-call(s32[64]{0:T(128)S(1)} %copy-done, bf16[64,8,128,128]{3,2,1,0:T(8,128)(2,1)} %amp_ref.3, bf16[8,8,128,128]{3,2,1,0:T(8,128)(2,1)S(1)} %collective-permute-done.3.received_ref), custom_call_target="tpu_custom_call" | custom-call | tf_op jit(solution)/shard_map/twist_tiles/pallas_call | solution.py:103
  9.6 1.7 %collective-permute-done.2.r3_ref = bf16[256,128]{1,0:T(8,128)(2,1)S(1)} collective-permute-done((bf16[256,128]{1,0:T(8,128)(2,1)S(1)}, bf16[256,128]{1,0:T(8,128)(2,1)S(1)}, u32[]{:S(2)}, u32[]{:S(2)}) %collective-permute-start.2) | collective-permute-done | bytes 65568 | tf_op jit(solution)/shard_map/ppermute | solution.py:25
  11.5 1.6 %collective-permute-start.5 = (bf16[1024,128]{1,0:T(8,128)(2,1)S(1)}, bf16[1024,128]{1,0:T(8,128)(2,1)S(1)}, u32[]{:S(2)}, u32[]{:S(2)}) collective-permute-start(bf16[1024,128]{1,0:T(8,128)(2,1)S(1)} %order_rows.1.mine_ref.refs_2_), channel_id=1, source_target_pairs={{0,8},{1,9},{2,10},{3,11},{4,12},{5,13},{6,14},{7,15},{8,0},{9,1},... | collective-permute-start | bytes 786440 | tf_op jit(solution)/shard_map/ppermute | solution.py:25
  13.1 2.1 %collective-permute-start.6 = (bf16[1024,128]{1,0:T(8,128)(2,1)S(1)}, bf16[1024,128]{1,0:T(8,128)(2,1)S(1)}, u32[]{:S(2)}, u32[]{:S(2)}) collective-permute-start(bf16[1024,128]{1,0:T(8,128)(2,1)S(1)} %order_rows.1.mine_ref.refs_2_), channel_id=1, source_target_pairs={{0,24},{1,25},{2,26},{3,27},{4,28},{5,29},{6,30},{7,31},{8,16},{9,... | collective-permute-start | bytes 786440 | tf_op jit(solution)/shard_map/ppermute | solution.py:25
  15.2 1.9 %collective-permute-start.7 = (bf16[1024,128]{1,0:T(8,128)(2,1)S(1)}, bf16[1024,128]{1,0:T(8,128)(2,1)S(1)}, u32[]{:S(2)}, u32[]{:S(2)}) collective-permute-start(bf16[1024,128]{1,0:T(8,128)(2,1)S(1)} %order_rows.1.mine_ref.refs_2_), channel_id=1, source_target_pairs={{0,4},{1,5},{2,6},{3,7},{4,0},{5,1},{6,2},{7,3},{8,12},{9,13},{10,... | collective-permute-start | bytes 786440 | tf_op jit(solution)/shard_map/ppermute | solution.py:25
  17.1 5.7 %stage1_0_1_2_6_4.1 = (bf16[256,4096]{1,0:T(8,128)(2,1)S(1)}, bf16[256,4096]{1,0:T(8,128)(2,1)S(1)}, bf16[256,4096]{1,0:T(8,128)(2,1)S(1)}, bf16[256,4096]{1,0:T...) custom-call(bf16[1024,128]{1,0:T(8,128)(2,1)S(1)} %order_rows.1.mine, ...), custom_call_target="tpu_custom_call" | custom-call | flops 5368709120 | bytes 1024 | tf_op jit(solution)/shard_map/stage1_0_1_2_6_4/pallas_call | solution.py:211
  23.0 1.2 %collective-permute-start.9 = (bf16[3,1024,128]{2,1,0:T(8,128)(2,1)S(1)}, bf16[3,1024,128]{2,1,0:T(8,128)(2,1)S(1)}, u32[]{:S(2)}, u32[]{:S(2)}) collective-permute-start(bf16[3,1024,128]{2,1,0:T(8,128)(2,1)S(1)} %get-tuple-element.49.refs_6_), channel_id=1, source_target_pairs={{0,32},{1,33},{2,34},{3,35},{4,36},{5,37},{6,38},{7,39},{8,40},{9,... | collective-permute-start | bytes 2359304 | tf_op jit(solution)/shard_map/ppermute | solution.py:25
  24.2 1.1 %collective-permute-start.10 = (bf16[1024,128]{1,0:T(8,128)(2,1)S(1)}, bf16[1024,128]{1,0:T(8,128)(2,1)S(1)}, u32[]{:S(2)}, u32[]{:S(2)}) collective-permute-start(bf16[1024,128]{1,0:T(8,128)(2,1)S(1)} %relay.4.first_ref), channel_id=1, source_target_pairs={{0,24},{1,25},{2,26},{3,27},{4,28},{5,29},{6,30},{7,31},{8,16},{9,... | collective-permute-start | bytes 786440 | tf_op jit(solution)/shard_map/ppermute | solution.py:25
  25.3 1.1 %collective-permute-start.8 = (bf16[2,1024,128]{2,1,0:T(8,128)(2,1)S(1)}, bf16[2,1024,128]{2,1,0:T(8,128)(2,1)S(1)}, u32[]{:S(2)}, u32[]{:S(2)}) collective-permute-start(bf16[2,1024,128]{2,1,0:T(8,128)(2,1)S(1)} %get-tuple-element.38.refs_3_), channel_id=1, source_target_pairs={{0,4},{1,5},{2,6},{3,7},{4,0},{5,1},{6,2},{7,3},{8,12},{9,13},{10,... | collective-permute-start | bytes 1572872 | tf_op jit(solution)/shard_map/ppermute | solution.py:25
  26.4 2.4 %stage1_3_7.1 = (bf16[256,4096]{1,0:T(8,128)(2,1)S(1)}, bf16[256,4096]{1,0:T(8,128)(2,1)S(1)}, bf16[256,4096]{1,0:T(8,128)(2,1)S(1)}, bf16[256,4096]{1,0:T(8,128)(2,1)S(1)}) custom-call(bf16[1024,128]{1,0:T(8,128)(2,1)S(1)} %order_rows.1.mine_ref.refs_2_, bf16[1024,128]{1,0:T(8,128)(2,1)S(1)} %collective-permute-done.4.refs_0_.refs_3_, ...), custom_call_target="tpu_custom_call" | custom-call | bytes 1024 | tf_op jit(solution)/shard_map/stage1_3_7/pallas_call | solution.py:211
  28.8 1.2 %stage2_self.1.refs_1_.refs_8_ = f32[4,64,32]{2,1,0:T(8,128)S(1)} custom-call(bf16[256,4096]{1,0:T(8,128)(2,1)S(1)} %get-tuple-element.50.refs_0_, bf16[256,4096]{1,0:T(8,128)(2,1)S(1)} %get-tuple-element.37.refs_1_._, bf16[1024,128]{1,0:T(8,128)(2,1)S(1)} %order_rows.1.mine_ref.refs_2_, bf16[1024,128]{1,0:T(8,128)(2,1)S(1)} %collective-permute-done.4.refs_0_.refs_3_, ...), custom_call_target="tpu_custom_call" | custom-call | bytes 1024 | tf_op jit(solution)/shard_map/stage2_self/pallas_call | solution.py:257
  30.1 1.7 %collective-permute-done.10.refs_0_ = bf16[1024,128]{1,0:T(8,128)(2,1)S(1)} collective-permute-done((bf16[1024,128]{1,0:T(8,128)(2,1)S(1)}, bf16[1024,128]{1,0:T(8,128)(2,1)S(1)}, u32[]{:S(2)}, u32[]{:S(2)}) %collective-permute-start.10) | collective-permute-done | bytes 262176 | tf_op jit(solution)/shard_map/ppermute | solution.py:25
  31.8 3.5 %stage2_near.1.refs_1_.refs_4_ = f32[4,64,128]{2,1,0:T(8,128)S(1)} custom-call(bf16[256,4096]{1,0:T(8,128)(2,1)S(1)} %get-tuple-element.43.refs_0_, bf16[256,4096]{1,0:T(8,128)(2,1)S(1)} %get-tuple-element.44.refs_1_, bf16[256,4096]{1,0:T(8,128)(2,1)S(1)} %get-tuple-element.45.refs_2_, bf16[256,4096]{1,0:T(8,128)(2,1)S(1)} %get-tuple-element.46.refs_3_, ...), custom_call_target="tpu_custom_call" | custom-call | flops 25769803776 | bytes 1024 | tf_op jit(solution)/shard_map/stage2_near/pallas_call | solution.py:257
  35.9 1.3 %stage1_5.1 = (bf16[256,4096]{1,0:T(8,128)(2,1)S(1)}, bf16[256,4096]{1,0:T(8,128)(2,1)S(1)}) custom-call(bf16[1024,128]{1,0:T(8,128)(2,1)S(1)} %order_rows.1.mine_ref.refs_2_, bf16[1024,128]{1,0:T(8,128)(2,1)S(1)} %collective-permute-done.4.refs_0_.refs_3_, bf16[8,8,128,128]{3,2,1,0:T(8,128)(2,1)S(1)} %get-tuple-element.36.refs_1_, ...), custom_call_target="tpu_custom_call" | custom-call | flops 1073741824 | bytes 1024 | tf_op jit(solution)/shard_map/stage1_5/pallas_call | solution.py:211
  37.2 1.0 %collective-permute-done.12.refs_0_ = bf16[1024,128]{1,0:T(8,128)(2,1)S(1)} collective-permute-done((bf16[1024,128]{1,0:T(8,128)(2,1)S(1)}, bf16[1024,128]{1,0:T(8,128)(2,1)S(1)}, u32[]{:S(2)}, u32[]{:S(2)}) %collective-permute-start.12) | collective-permute-done | bytes 262176 | tf_op jit(solution)/shard_map/ppermute | solution.py:25
  38.2 1.2 %stage2_far.1.refs_10_ = f32[4,64,160]{2,1,0:T(8,128)S(1)} custom-call(bf16[256,4096]{1,0:T(8,128)(2,1)S(1)} %get-tuple-element.53.refs_0_, bf16[256,4096]{1,0:T(8,128)(2,1)S(1)} %get-tuple-element.54.refs_1_, bf16[1024,128]{1,0:T(8,128)(2,1)S(1)} %relay.5.refs_9_.refs_2_, bf16[1024,128]{1,0:T(8,128)(2,1)S(1)} %collective-permute-done.14.refs_3_, ...), custom_call_target="tpu_custom_call" | custom-call | flops 1073741824 | bytes 1024 | tf_op jit(solution)/shard_map/stage2_far/pallas_call | solution.py:257
  39.7 3.5 %stage2_last.1.own_ref = f32[4,64,256]{2,1,0:T(8,128)S(1)} custom-call(bf16[256,4096]{1,0:T(8,128)(2,1)S(1)} %get-tuple-element.39.refs_4_.refs_0_, bf16[256,4096]{1,0:T(8,128)(2,1)S(1)} %get-tuple-element.40.refs_1_, bf16[256,4096]{1,0:T(8,128)(2,1)S(1)} %get-tuple-element.41.refs_2_, bf16[256,4096]{1,0:T(8,128)(2,1)S(1)} %get-tuple-element.42.refs_3_, ...), custom_call_target="tpu_custom_call" | custom-call | flops 3221225472 | bytes 1024 | tf_op jit(solution)/shard_map/stage2_last/pallas_call | solution.py:257
  43.2 1.3 %collective-permute-start.15 = (f32[64,256]{1,0:T(8,128)S(1)}, f32[64,256]{1,0:T(8,128)S(1)}, u32[]{:S(2)}, u32[]{:S(2)}) collective-permute-start(f32[64,256]{1,0:T(8,128)S(1)} %get-tuple-element.57), channel_id=1, source_target_pairs={{0,2},{1,3},{2,0},{3,1},{4,6},{5,7},{6,4},{7,5},{8,10},{9,11},{10,... | collective-permute-start | bytes 196616 | tf_op jit(solution)/shard_map/ppermute | solution.py:25
  45.2 2.2 %collective-permute-start.17 = (f32[64,256]{1,0:T(8,128)S(1)}, f32[64,256]{1,0:T(8,128)S(1)}, u32[]{:S(2)}, u32[]{:S(2)}) collective-permute-start(f32[64,256]{1,0:T(8,128)S(1)} %get-tuple-element.55), channel_id=1, source_target_pairs={{0,3},{1,2},{2,1},{3,0},{4,7},{5,6},{6,5},{7,4},{8,11},{9,10},{10,... | collective-permute-start | bytes 196616 | tf_op jit(solution)/shard_map/ppermute | solution.py:25
  47.4 2.3 %collective-permute-done.15.r1_ref = f32[64,256]{1,0:T(8,128)S(1)} collective-permute-done((f32[64,256]{1,0:T(8,128)S(1)}, f32[64,256]{1,0:T(8,128)S(1)}, u32[]{:S(2)}, u32[]{:S(2)}) %collective-permute-start.15) | collective-permute-done | bytes 65568 | tf_op jit(solution)/shard_map/ppermute | solution.py:25
  49.8 0.9 %collective-permute-done.17.r3_ref = f32[64,256]{1,0:T(8,128)S(1)} collective-permute-done((f32[64,256]{1,0:T(8,128)S(1)}, f32[64,256]{1,0:T(8,128)S(1)}, u32[]{:S(2)}, u32[]{:S(2)}) %collective-permute-start.17) | collective-permute-done | bytes 65568 | tf_op jit(solution)/shard_map/ppermute | solution.py:25
  50.7 0.9 %finish.1 = f32[8,32,64]{2,1,0:T(8,128)} custom-call(f32[4,64,256]{2,1,0:T(8,128)S(1)} %stage2_last.1.own_ref, f32[64,256]{1,0:T(8,128)S(1)} %collective-permute-done.15.r1_ref, f32[64,256]{1,0:T(8,128)S(1)} %collective-permute-done.16.r2_ref, f32[64,256]{1,0:T(8,128)S(1)} %collective-permute-done.17.r3_ref), custom_call_target="tpu_custom_call" | custom-call | tf_op jit(solution)/shard_map/finish/pallas_call | solution.py:283
  (31 shorter events, 3.9 us)
Async XLA Ops:
  0.0 6.2 %copy-start = (s32[64]{0:T(128)S(1)}, s32[64]{0:T(128)}, u32[]{:S(2)}) copy-start(s32[64]{0:T(128)} %mirror_ref.1) | copy-start | bytes 772
  1.7 4.5 %collective-permute-start.3 = (bf16[8,8,128,128]{3,2,1,0:T(8,128)(2,1)S(1)}, bf16[8,8,128,128]{3,2,1,0:T(8,128)(2,1)S(1)}, u32[]{:S(2)}, u32[]{:S(2)}) collective-permute-start(bf16[8,8,128,128]{3,2,1,0:T(8,128)(2,1)S(1)} %get-tuple-element.34), channel_id=1, source_target_pairs={{0,32},{1,33},{2,34},{3,35},{4,36},{5,37},{6,38},{7,39},{8,40},{9,... | collective-permute-start | bytes 6291464 | tf_op jit(solution)/shard_map/ppermute | solution.py:25
  1.8 7.1 %collective-permute-start = (bf16[256,128]{1,0:T(8,128)(2,1)S(1)}, bf16[256,128]{1,0:T(8,128)(2,1)S(1)}, u32[]{:S(2)}, u32[]{:S(2)}) collective-permute-start(bf16[256,128]{1,0:T(8,128)(2,1)S(1)} %get-tuple-element.31), channel_id=1, source_target_pairs={{0,2},{1,3},{2,0},{3,1},{4,6},{5,7},{6,4},{7,5},{8,10},{9,11},{10,... | collective-permute-start | bytes 196616 | tf_op jit(solution)/shard_map/ppermute | solution.py:25
  5.2 4.5 %collective-permute-start.1 = (bf16[256,128]{1,0:T(8,128)(2,1)S(1)}, bf16[256,128]{1,0:T(8,128)(2,1)S(1)}, u32[]{:S(2)}, u32[]{:S(2)}) collective-permute-start(bf16[256,128]{1,0:T(8,128)(2,1)S(1)} %get-tuple-element.32), channel_id=1, source_target_pairs={{0,1},{1,0},{2,3},{3,2},{4,5},{5,4},{6,7},{7,6},{8,9},{9,8},{10,11... | collective-permute-start | bytes 196616 | tf_op jit(solution)/shard_map/ppermute | solution.py:25
  5.8 5.5 %collective-permute-start.2 = (bf16[256,128]{1,0:T(8,128)(2,1)S(1)}, bf16[256,128]{1,0:T(8,128)(2,1)S(1)}, u32[]{:S(2)}, u32[]{:S(2)}) collective-permute-start(bf16[256,128]{1,0:T(8,128)(2,1)S(1)} %get-tuple-element.33), channel_id=1, source_target_pairs={{0,3},{1,2},{2,1},{3,0},{4,7},{5,6},{6,5},{7,4},{8,11},{9,10},{10,... | collective-permute-start | bytes 196616 | tf_op jit(solution)/shard_map/ppermute | solution.py:25
  11.4 5.7 %collective-permute-start.4 = (bf16[1024,128]{1,0:T(8,128)(2,1)S(1)}, bf16[1024,128]{1,0:T(8,128)(2,1)S(1)}, u32[]{:S(2)}, u32[]{:S(2)}) collective-permute-start(bf16[1024,128]{1,0:T(8,128)(2,1)S(1)} %order_rows.1.mine_ref.refs_2_), channel_id=1, source_target_pairs={{0,32},{1,33},{2,34},{3,35},{4,36},{5,37},{6,38},{7,39},{8,40},{9,... | collective-permute-start | bytes 786440 | tf_op jit(solution)/shard_map/ppermute | solution.py:25
  11.5 11.3 %collective-permute-start.5 = (bf16[1024,128]{1,0:T(8,128)(2,1)S(1)}, bf16[1024,128]{1,0:T(8,128)(2,1)S(1)}, u32[]{:S(2)}, u32[]{:S(2)}) collective-permute-start(bf16[1024,128]{1,0:T(8,128)(2,1)S(1)} %order_rows.1.mine_ref.refs_2_), channel_id=1, source_target_pairs={{0,8},{1,9},{2,10},{3,11},{4,12},{5,13},{6,14},{7,15},{8,0},{9,1},... | collective-permute-start | bytes 786440 | tf_op jit(solution)/shard_map/ppermute | solution.py:25
  13.1 9.7 %collective-permute-start.6 = (bf16[1024,128]{1,0:T(8,128)(2,1)S(1)}, bf16[1024,128]{1,0:T(8,128)(2,1)S(1)}, u32[]{:S(2)}, u32[]{:S(2)}) collective-permute-start(bf16[1024,128]{1,0:T(8,128)(2,1)S(1)} %order_rows.1.mine_ref.refs_2_), channel_id=1, source_target_pairs={{0,24},{1,25},{2,26},{3,27},{4,28},{5,29},{6,30},{7,31},{8,16},{9,... | collective-permute-start | bytes 786440 | tf_op jit(solution)/shard_map/ppermute | solution.py:25
  15.2 7.6 %collective-permute-start.7 = (bf16[1024,128]{1,0:T(8,128)(2,1)S(1)}, bf16[1024,128]{1,0:T(8,128)(2,1)S(1)}, u32[]{:S(2)}, u32[]{:S(2)}) collective-permute-start(bf16[1024,128]{1,0:T(8,128)(2,1)S(1)} %order_rows.1.mine_ref.refs_2_), channel_id=1, source_target_pairs={{0,4},{1,5},{2,6},{3,7},{4,0},{5,1},{6,2},{7,3},{8,12},{9,13},{10,... | collective-permute-start | bytes 786440 | tf_op jit(solution)/shard_map/ppermute | solution.py:25
  23.0 8.8 %collective-permute-start.9 = (bf16[3,1024,128]{2,1,0:T(8,128)(2,1)S(1)}, bf16[3,1024,128]{2,1,0:T(8,128)(2,1)S(1)}, u32[]{:S(2)}, u32[]{:S(2)}) collective-permute-start(bf16[3,1024,128]{2,1,0:T(8,128)(2,1)S(1)} %get-tuple-element.49.refs_6_), channel_id=1, source_target_pairs={{0,32},{1,33},{2,34},{3,35},{4,36},{5,37},{6,38},{7,39},{8,40},{9,... | collective-permute-start | bytes 2359304 | tf_op jit(solution)/shard_map/ppermute | solution.py:25
  24.2 7.6 %collective-permute-start.10 = (bf16[1024,128]{1,0:T(8,128)(2,1)S(1)}, bf16[1024,128]{1,0:T(8,128)(2,1)S(1)}, u32[]{:S(2)}, u32[]{:S(2)}) collective-permute-start(bf16[1024,128]{1,0:T(8,128)(2,1)S(1)} %relay.4.first_ref), channel_id=1, source_target_pairs={{0,24},{1,25},{2,26},{3,27},{4,28},{5,29},{6,30},{7,31},{8,16},{9,... | collective-permute-start | bytes 786440 | tf_op jit(solution)/shard_map/ppermute | solution.py:25
  25.3 10.0 %collective-permute-start.8 = (bf16[2,1024,128]{2,1,0:T(8,128)(2,1)S(1)}, bf16[2,1024,128]{2,1,0:T(8,128)(2,1)S(1)}, u32[]{:S(2)}, u32[]{:S(2)}) collective-permute-start(bf16[2,1024,128]{2,1,0:T(8,128)(2,1)S(1)} %get-tuple-element.38.refs_3_), channel_id=1, source_target_pairs={{0,4},{1,5},{2,6},{3,7},{4,0},{5,1},{6,2},{7,3},{8,12},{9,13},{10,... | collective-permute-start | bytes 1572872 | tf_op jit(solution)/shard_map/ppermute | solution.py:25
  31.8 6.4 %collective-permute-start.12 = (bf16[1024,128]{1,0:T(8,128)(2,1)S(1)}, bf16[1024,128]{1,0:T(8,128)(2,1)S(1)}, u32[]{:S(2)}, u32[]{:S(2)}) collective-permute-start(bf16[1024,128]{1,0:T(8,128)(2,1)S(1)} %relay.5.refs_9_.refs_2_), channel_id=1, source_target_pairs={{0,4},{1,5},{2,6},{3,7},{4,0},{5,1},{6,2},{7,3},{8,12},{9,13},{10,... | collective-permute-start | bytes 786440 | tf_op jit(solution)/shard_map/ppermute | solution.py:25
  35.3 4.4 %collective-permute-start.11 = (bf16[2,1024,128]{2,1,0:T(8,128)(2,1)S(1)}, bf16[2,1024,128]{2,1,0:T(8,128)(2,1)S(1)}, u32[]{:S(2)}, u32[]{:S(2)}) collective-permute-start(bf16[2,1024,128]{2,1,0:T(8,128)(2,1)S(1)} %relay.6.refs_3_.refs_6_), channel_id=1, source_target_pairs={{0,32},{1,33},{2,34},{3,35},{4,36},{5,37},{6,38},{7,39},{8,40},{9,... | collective-permute-start | bytes 1572872 | tf_op jit(solution)/shard_map/ppermute | solution.py:25
  35.8 2.4 %collective-permute-start.14 = (bf16[1024,128]{1,0:T(8,128)(2,1)S(1)}, bf16[1024,128]{1,0:T(8,128)(2,1)S(1)}, u32[]{:S(2)}, u32[]{:S(2)}) collective-permute-start(bf16[1024,128]{1,0:T(8,128)(2,1)S(1)} %relay.5.refs_9_.refs_2_), channel_id=1, source_target_pairs={{0,32},{1,33},{2,34},{3,35},{4,36},{5,37},{6,38},{7,39},{8,40},{9,... | collective-permute-start | bytes 786440 | tf_op jit(solution)/shard_map/ppermute | solution.py:25
  38.2 1.5 %collective-permute-start.13 = (bf16[1024,128]{1,0:T(8,128)(2,1)S(1)}, bf16[1024,128]{1,0:T(8,128)(2,1)S(1)}, u32[]{:S(2)}, u32[]{:S(2)}) collective-permute-start(bf16[1024,128]{1,0:T(8,128)(2,1)S(1)} %relay.7.refs_5_.refs_8_), channel_id=1, source_target_pairs={{0,32},{1,33},{2,34},{3,35},{4,36},{5,37},{6,38},{7,39},{8,40},{9,... | collective-permute-start | bytes 786440 | tf_op jit(solution)/shard_map/ppermute | solution.py:25
  43.2 6.5 %collective-permute-start.15 = (f32[64,256]{1,0:T(8,128)S(1)}, f32[64,256]{1,0:T(8,128)S(1)}, u32[]{:S(2)}, u32[]{:S(2)}) collective-permute-start(f32[64,256]{1,0:T(8,128)S(1)} %get-tuple-element.57), channel_id=1, source_target_pairs={{0,2},{1,3},{2,0},{3,1},{4,6},{5,7},{6,4},{7,5},{8,10},{9,11},{10,... | collective-permute-start | bytes 196616 | tf_op jit(solution)/shard_map/ppermute | solution.py:25
  44.5 5.3 %collective-permute-start.16 = (f32[64,256]{1,0:T(8,128)S(1)}, f32[64,256]{1,0:T(8,128)S(1)}, u32[]{:S(2)}, u32[]{:S(2)}) collective-permute-start(f32[64,256]{1,0:T(8,128)S(1)} %get-tuple-element.56), channel_id=1, source_target_pairs={{0,1},{1,0},{2,3},{3,2},{4,5},{5,4},{6,7},{7,6},{8,9},{9,8},{10,11... | collective-permute-start | bytes 196616 | tf_op jit(solution)/shard_map/ppermute | solution.py:25
  45.2 5.5 %collective-permute-start.17 = (f32[64,256]{1,0:T(8,128)S(1)}, f32[64,256]{1,0:T(8,128)S(1)}, u32[]{:S(2)}, u32[]{:S(2)}) collective-permute-start(f32[64,256]{1,0:T(8,128)S(1)} %get-tuple-element.55), channel_id=1, source_target_pairs={{0,3},{1,2},{2,1},{3,0},{4,7},{5,6},{6,5},{7,4},{8,11},{9,10},{10,... | collective-permute-start | bytes 196616 | tf_op jit(solution)/shard_map/ppermute | solution.py:25

commit v12 on v11

--- a/solution.py
+++ b/solution.py
@@ -138,7 +138,7 @@
     )(*quarters, token)
 
 
-def relay(values, tokens):
+def relay(values, tokens, weight=0):
     n = len(values)
     outs = pl.pallas_call(
         lambda *refs: None,
@@ -147,7 +147,7 @@
         out_specs=tuple(spec(pl.ANY) for _ in values),
         input_output_aliases={i: i for i in range(n)},
         compiler_params=params(1),
-        cost_estimate=pl.CostEstimate(flops=0, transcendentals=0, bytes_accessed=0),
+        cost_estimate=pl.CostEstimate(flops=int(weight * 2**30), transcendentals=0, bytes_accessed=0),
         name="relay",
     )(*values, *tokens)
     return outs
@@ -292,7 +292,7 @@
     return jnp.transpose(out, (2, 0, 1))
 
 
-FAST, SLOW = 0, 8
+FAST, SLOW, HOLD = 0, 8, 16
 
 
 def shards(cholesky, amplitudes, mirror):
@@ -313,7 +313,7 @@
     other_blocks = to_sibling(near_blocks)
     x37 = stage1(halves(c37, c73), own, tiles, (x1,), FAST)
     self0 = stage2("self", (x0m, x0o), (((0, None), (1, None)),), own, (), (x37[0],), FAST)
-    (x2,) = relay((x2,), (self0,))
+    (x2,) = relay((x2,), (self0,), HOLD)
     zx2 = over_z(x2)
     x2_other = to_sibling(x2)
     near = stage2(

time: 51.8 us -> 51.5 us (level)
  waiting for transfers between devices: 8.71 us -> 7.15 us
  starting transfers between devices: 18.4 us -> 19.6 us
    ppermute x18, waiting for transfers between devices: 8.71 us -> 7.15 us  [permute(): return lax.ppermute(value, ('occ', 'vir'), pairs)]
    ppermute x18, starting transfers between devices: 18.4 us -> 19.6 us  [permute(): return lax.ppermute(value, ('occ', 'vir'), pairs)]
  transfers between devices with their start and end apart: 18 -> 18, of which waited for: 7 -> 6; matrix products, arithmetic and copies ran while one was open for 0% -> 0% of each run, Pallas kernels for 35% -> 35%
where the time goes in v12:
time: 51.5 us; the launch traced here: 51.2 us
  Pallas kernels  24.3 us (47%)
  starting transfers between devices  19.6 us (38%)
  waiting for transfers between devices  7.15 us (14%)
    ppermute x18, starting transfers between devices, permute(): return lax.ppermute(value, ('occ', 'vir'), pairs)  19.6 us
    pallas_call x4, Pallas kernels, stage2(): pl.pallas_call(functools.partial(stage2_kernel, picks, len(bs), len(carry...  9.48 us
    pallas_call x3, Pallas kernels, stage1(): pl.pallas_call(functools.partial(stage1_kernel, work, len(tokens)), out_s...  9.32 us
    ppermute x18, waiting for transfers between devices, permute(): return lax.ppermute(value, ('occ', 'vir'), pairs)  7.15 us
    pallas_call x1, Pallas kernels, twist_tiles(): pl.pallas_call(twist_kernel, out_shape=(shape, shape), in_specs=[spec(plt...  2.63 us
    pallas_call x1, Pallas kernels, cut_to_send(): pl.pallas_call(send_kernel, out_shape=(chunk,) * 4 + (jax.ShapeDtypeStruc...  1.7 us
  transfers between devices with their start and end apart: 18, of which 6 were waited for; matrix products, arithmetic and copies ran while one was open for 0% of the time, Pallas kernels for 35%

profile of v12, /device:TPU:0, one launch (start us, length us, event | category | flops | bytes accessed | tf_op | source)
XLA Modules:
  0.0 51.2 jit_solution(7086901960419000312)
XLA Ops:
  0.0 1.7 %cut_to_send.1 = (bf16[256,128]{1,0:T(8,128)(2,1)S(1)}, bf16[256,128]{1,0:T(8,128)(2,1)S(1)}, bf16[256,128]{1,0:T(8,128)(2,1)S(1)}, bf16[256,128]{1,0:T(8,128)(2,1)S(1)}, bf16[8,8,128,128]{3,2,1,0:T(8,128)(2,1)S(1)}) custom-call(bf16[2048,128]{1,0:T(8,128)(2,1)} %bitcast.8, bf16[64,8,128,128]{3,2,1,0:T(8,128)(2,1)} %amp_ref.3), custom_call_target="tpu_custom_call" | custom-call | tf_op jit(solution)/shard_map/cut_to_send/pallas_call | solution.py:75
  1.8 3.4 %collective-permute-start = (bf16[256,128]{1,0:T(8,128)(2,1)S(1)}, bf16[256,128]{1,0:T(8,128)(2,1)S(1)}, u32[]{:S(2)}, u32[]{:S(2)}) collective-permute-start(bf16[256,128]{1,0:T(8,128)(2,1)S(1)} %get-tuple-element.31), channel_id=1, source_target_pairs={{0,2},{1,3},{2,0},{3,1},{4,6},{5,7},{6,4},{7,5},{8,10},{9,11},{10,... | collective-permute-start | bytes 196616 | tf_op jit(solution)/shard_map/ppermute | solution.py:25
  6.2 2.6 %twist_tiles.1 = (bf16[8,8,128,128]{3,2,1,0:T(8,128)(2,1)S(1)}, bf16[8,8,128,128]{3,2,1,0:T(8,128)(2,1)S(1)}) custom-call(s32[64]{0:T(128)S(1)} %copy-done, bf16[64,8,128,128]{3,2,1,0:T(8,128)(2,1)} %amp_ref.3, bf16[8,8,128,128]{3,2,1,0:T(8,128)(2,1)S(1)} %collective-permute-done.3.received_ref), custom_call_target="tpu_custom_call" | custom-call | tf_op jit(solution)/shard_map/twist_tiles/pallas_call | solution.py:103
  9.6 1.7 %collective-permute-done.2.r3_ref = bf16[256,128]{1,0:T(8,128)(2,1)S(1)} collective-permute-done((bf16[256,128]{1,0:T(8,128)(2,1)S(1)}, bf16[256,128]{1,0:T(8,128)(2,1)S(1)}, u32[]{:S(2)}, u32[]{:S(2)}) %collective-permute-start.2) | collective-permute-done | bytes 65568 | tf_op jit(solution)/shard_map/ppermute | solution.py:25
  11.5 1.6 %collective-permute-start.5 = (bf16[1024,128]{1,0:T(8,128)(2,1)S(1)}, bf16[1024,128]{1,0:T(8,128)(2,1)S(1)}, u32[]{:S(2)}, u32[]{:S(2)}) collective-permute-start(bf16[1024,128]{1,0:T(8,128)(2,1)S(1)} %order_rows.1.mine_ref.refs_2_), channel_id=1, source_target_pairs={{0,8},{1,9},{2,10},{3,11},{4,12},{5,13},{6,14},{7,15},{8,0},{9,1},... | collective-permute-start | bytes 786440 | tf_op jit(solution)/shard_map/ppermute | solution.py:25
  13.1 2.1 %collective-permute-start.6 = (bf16[1024,128]{1,0:T(8,128)(2,1)S(1)}, bf16[1024,128]{1,0:T(8,128)(2,1)S(1)}, u32[]{:S(2)}, u32[]{:S(2)}) collective-permute-start(bf16[1024,128]{1,0:T(8,128)(2,1)S(1)} %order_rows.1.mine_ref.refs_2_), channel_id=1, source_target_pairs={{0,24},{1,25},{2,26},{3,27},{4,28},{5,29},{6,30},{7,31},{8,16},{9,... | collective-permute-start | bytes 786440 | tf_op jit(solution)/shard_map/ppermute | solution.py:25
  15.2 1.9 %collective-permute-start.7 = (bf16[1024,128]{1,0:T(8,128)(2,1)S(1)}, bf16[1024,128]{1,0:T(8,128)(2,1)S(1)}, u32[]{:S(2)}, u32[]{:S(2)}) collective-permute-start(bf16[1024,128]{1,0:T(8,128)(2,1)S(1)} %order_rows.1.mine_ref.refs_2_), channel_id=1, source_target_pairs={{0,4},{1,5},{2,6},{3,7},{4,0},{5,1},{6,2},{7,3},{8,12},{9,13},{10,... | collective-permute-start | bytes 786440 | tf_op jit(solution)/shard_map/ppermute | solution.py:25
  17.1 5.7 %stage1_0_1_2_6_4.1 = (bf16[256,4096]{1,0:T(8,128)(2,1)S(1)}, bf16[256,4096]{1,0:T(8,128)(2,1)S(1)}, bf16[256,4096]{1,0:T(8,128)(2,1)S(1)}, bf16[256,4096]{1,0:T...) custom-call(bf16[1024,128]{1,0:T(8,128)(2,1)S(1)} %order_rows.1.mine, ...), custom_call_target="tpu_custom_call" | custom-call | flops 5368709120 | bytes 1024 | tf_op jit(solution)/shard_map/stage1_0_1_2_6_4/pallas_call | solution.py:211
  22.8 1.2 %collective-permute-start.10 = (bf16[1024,128]{1,0:T(8,128)(2,1)S(1)}, bf16[1024,128]{1,0:T(8,128)(2,1)S(1)}, u32[]{:S(2)}, u32[]{:S(2)}) collective-permute-start(bf16[1024,128]{1,0:T(8,128)(2,1)S(1)} %relay.4.first_ref), channel_id=1, source_target_pairs={{0,24},{1,25},{2,26},{3,27},{4,28},{5,29},{6,30},{7,31},{8,16},{9,... | collective-permute-start | bytes 786440 | tf_op jit(solution)/shard_map/ppermute | solution.py:25
  24.2 1.6 %collective-permute-start.9 = (bf16[3,1024,128]{2,1,0:T(8,128)(2,1)S(1)}, bf16[3,1024,128]{2,1,0:T(8,128)(2,1)S(1)}, u32[]{:S(2)}, u32[]{:S(2)}) collective-permute-start(bf16[3,1024,128]{2,1,0:T(8,128)(2,1)S(1)} %get-tuple-element.49.refs_6_), channel_id=1, source_target_pairs={{0,32},{1,33},{2,34},{3,35},{4,36},{5,37},{6,38},{7,39},{8,40},{9,... | collective-permute-start | bytes 2359304 | tf_op jit(solution)/shard_map/ppermute | solution.py:25
  25.7 2.4 %stage1_3_7.1 = (bf16[256,4096]{1,0:T(8,128)(2,1)S(1)}, bf16[256,4096]{1,0:T(8,128)(2,1)S(1)}, bf16[256,4096]{1,0:T(8,128)(2,1)S(1)}, bf16[256,4096]{1,0:T(8,128)(2,1)S(1)}) custom-call(bf16[1024,128]{1,0:T(8,128)(2,1)S(1)} %order_rows.1.mine_ref.refs_2_, bf16[1024,128]{1,0:T(8,128)(2,1)S(1)} %collective-permute-done.4.refs_0_.refs_3_, ...), custom_call_target="tpu_custom_call" | custom-call | bytes 1024 | tf_op jit(solution)/shard_map/stage1_3_7/pallas_call | solution.py:211
  28.1 1.2 %stage2_self.1.refs_1_.refs_8_ = f32[4,64,32]{2,1,0:T(8,128)S(1)} custom-call(bf16[256,4096]{1,0:T(8,128)(2,1)S(1)} %get-tuple-element.50.refs_0_, bf16[256,4096]{1,0:T(8,128)(2,1)S(1)} %get-tuple-element.37.refs_1_._, bf16[1024,128]{1,0:T(8,128)(2,1)S(1)} %order_rows.1.mine_ref.refs_2_, bf16[1024,128]{1,0:T(8,128)(2,1)S(1)} %collective-permute-done.4.refs_0_.refs_3_, ...), custom_call_target="tpu_custom_call" | custom-call | bytes 1024 | tf_op jit(solution)/shard_map/stage2_self/pallas_call | solution.py:257
  29.4 1.1 %collective-permute-done.10.refs_0_ = bf16[1024,128]{1,0:T(8,128)(2,1)S(1)} collective-permute-done((bf16[1024,128]{1,0:T(8,128)(2,1)S(1)}, bf16[1024,128]{1,0:T(8,128)(2,1)S(1)}, u32[]{:S(2)}, u32[]{:S(2)}) %collective-permute-start.10) | collective-permute-done | bytes 262176 | tf_op jit(solution)/shard_map/ppermute | solution.py:25
  30.5 1.0 %collective-permute-start.12 = (bf16[1024,128]{1,0:T(8,128)(2,1)S(1)}, bf16[1024,128]{1,0:T(8,128)(2,1)S(1)}, u32[]{:S(2)}, u32[]{:S(2)}) collective-permute-start(bf16[1024,128]{1,0:T(8,128)(2,1)S(1)} %relay.5.refs_9_.refs_2_), channel_id=1, source_target_pairs={{0,4},{1,5},{2,6},{3,7},{4,0},{5,1},{6,2},{7,3},{8,12},{9,13},{10,... | collective-permute-start | bytes 786440 | tf_op jit(solution)/shard_map/ppermute | solution.py:25
  31.5 3.5 %stage2_near.1.refs_1_.refs_4_ = f32[4,64,128]{2,1,0:T(8,128)S(1)} custom-call(bf16[256,4096]{1,0:T(8,128)(2,1)S(1)} %get-tuple-element.43.refs_0_, bf16[256,4096]{1,0:T(8,128)(2,1)S(1)} %get-tuple-element.44.refs_1_, bf16[256,4096]{1,0:T(8,128)(2,1)S(1)} %get-tuple-element.45.refs_2_, bf16[256,4096]{1,0:T(8,128)(2,1)S(1)} %get-tuple-element.46.refs_3_, ...), custom_call_target="tpu_custom_call" | custom-call | flops 25769803776 | bytes 1024 | tf_op jit(solution)/shard_map/stage2_near/pallas_call | solution.py:257
  35.0 1.0 %collective-permute-start.11 = (bf16[2,1024,128]{2,1,0:T(8,128)(2,1)S(1)}, bf16[2,1024,128]{2,1,0:T(8,128)(2,1)S(1)}, u32[]{:S(2)}, u32[]{:S(2)}) collective-permute-start(bf16[2,1024,128]{2,1,0:T(8,128)(2,1)S(1)} %relay.6.refs_3_.refs_6_), channel_id=1, source_target_pairs={{0,32},{1,33},{2,34},{3,35},{4,36},{5,37},{6,38},{7,39},{8,40},{9,... | collective-permute-start | bytes 1572872 | tf_op jit(solution)/shard_map/ppermute | solution.py:25
  36.1 1.3 %stage1_5.1 = (bf16[256,4096]{1,0:T(8,128)(2,1)S(1)}, bf16[256,4096]{1,0:T(8,128)(2,1)S(1)}) custom-call(bf16[1024,128]{1,0:T(8,128)(2,1)S(1)} %order_rows.1.mine_ref.refs_2_, bf16[1024,128]{1,0:T(8,128)(2,1)S(1)} %collective-permute-done.4.refs_0_.refs_3_, bf16[8,8,128,128]{3,2,1,0:T(8,128)(2,1)S(1)} %get-tuple-element.36.refs_1_, ...), custom_call_target="tpu_custom_call" | custom-call | flops 1073741824 | bytes 1024 | tf_op jit(solution)/shard_map/stage1_5/pallas_call | solution.py:211
  38.1 1.2 %stage2_far.1.refs_10_ = f32[4,64,160]{2,1,0:T(8,128)S(1)} custom-call(bf16[256,4096]{1,0:T(8,128)(2,1)S(1)} %get-tuple-element.53.refs_0_, bf16[256,4096]{1,0:T(8,128)(2,1)S(1)} %get-tuple-element.54.refs_1_, bf16[1024,128]{1,0:T(8,128)(2,1)S(1)} %relay.5.refs_9_.refs_2_, bf16[1024,128]{1,0:T(8,128)(2,1)S(1)} %collective-permute-done.14.refs_3_, ...), custom_call_target="tpu_custom_call" | custom-call | flops 1073741824 | bytes 1024 | tf_op jit(solution)/shard_map/stage2_far/pallas_call | solution.py:257
  39.3 3.5 %stage2_last.1.own_ref = f32[4,64,256]{2,1,0:T(8,128)S(1)} custom-call(bf16[256,4096]{1,0:T(8,128)(2,1)S(1)} %get-tuple-element.39.refs_4_.refs_0_, bf16[256,4096]{1,0:T(8,128)(2,1)S(1)} %get-tuple-element.40.refs_1_, bf16[256,4096]{1,0:T(8,128)(2,1)S(1)} %get-tuple-element.41.refs_2_, bf16[256,4096]{1,0:T(8,128)(2,1)S(1)} %get-tuple-element.42.refs_3_, ...), custom_call_target="tpu_custom_call" | custom-call | flops 3221225472 | bytes 1024 | tf_op jit(solution)/shard_map/stage2_last/pallas_call | solution.py:257
  42.9 1.3 %collective-permute-start.15 = (f32[64,256]{1,0:T(8,128)S(1)}, f32[64,256]{1,0:T(8,128)S(1)}, u32[]{:S(2)}, u32[]{:S(2)}) collective-permute-start(f32[64,256]{1,0:T(8,128)S(1)} %get-tuple-element.57), channel_id=1, source_target_pairs={{0,2},{1,3},{2,0},{3,1},{4,6},{5,7},{6,4},{7,5},{8,10},{9,11},{10,... | collective-permute-start | bytes 196616 | tf_op jit(solution)/shard_map/ppermute | solution.py:25
  44.8 2.2 %collective-permute-start.17 = (f32[64,256]{1,0:T(8,128)S(1)}, f32[64,256]{1,0:T(8,128)S(1)}, u32[]{:S(2)}, u32[]{:S(2)}) collective-permute-start(f32[64,256]{1,0:T(8,128)S(1)} %get-tuple-element.55), channel_id=1, source_target_pairs={{0,3},{1,2},{2,1},{3,0},{4,7},{5,6},{6,5},{7,4},{8,11},{9,10},{10,... | collective-permute-start | bytes 196616 | tf_op jit(solution)/shard_map/ppermute | solution.py:25
  47.0 2.3 %collective-permute-done.15.r1_ref = f32[64,256]{1,0:T(8,128)S(1)} collective-permute-done((f32[64,256]{1,0:T(8,128)S(1)}, f32[64,256]{1,0:T(8,128)S(1)}, u32[]{:S(2)}, u32[]{:S(2)}) %collective-permute-start.15) | collective-permute-done | bytes 65568 | tf_op jit(solution)/shard_map/ppermute | solution.py:25
  49.4 0.9 %collective-permute-done.17.r3_ref = f32[64,256]{1,0:T(8,128)S(1)} collective-permute-done((f32[64,256]{1,0:T(8,128)S(1)}, f32[64,256]{1,0:T(8,128)S(1)}, u32[]{:S(2)}, u32[]{:S(2)}) %collective-permute-start.17) | collective-permute-done | bytes 65568 | tf_op jit(solution)/shard_map/ppermute | solution.py:25
  50.3 0.9 %finish.1 = f32[8,32,64]{2,1,0:T(8,128)} custom-call(f32[4,64,256]{2,1,0:T(8,128)S(1)} %stage2_last.1.own_ref, f32[64,256]{1,0:T(8,128)S(1)} %collective-permute-done.15.r1_ref, f32[64,256]{1,0:T(8,128)S(1)} %collective-permute-done.16.r2_ref, f32[64,256]{1,0:T(8,128)S(1)} %collective-permute-done.17.r3_ref), custom_call_target="tpu_custom_call" | custom-call | tf_op jit(solution)/shard_map/finish/pallas_call | solution.py:283
  (31 shorter events, 3.7 us)
Async XLA Ops:
  0.0 6.2 %copy-start = (s32[64]{0:T(128)S(1)}, s32[64]{0:T(128)}, u32[]{:S(2)}) copy-start(s32[64]{0:T(128)} %mirror_ref.1) | copy-start | bytes 772
  1.7 4.5 %collective-permute-start.3 = (bf16[8,8,128,128]{3,2,1,0:T(8,128)(2,1)S(1)}, bf16[8,8,128,128]{3,2,1,0:T(8,128)(2,1)S(1)}, u32[]{:S(2)}, u32[]{:S(2)}) collective-permute-start(bf16[8,8,128,128]{3,2,1,0:T(8,128)(2,1)S(1)} %get-tuple-element.34), channel_id=1, source_target_pairs={{0,32},{1,33},{2,34},{3,35},{4,36},{5,37},{6,38},{7,39},{8,40},{9,... | collective-permute-start | bytes 6291464 | tf_op jit(solution)/shard_map/ppermute | solution.py:25
  1.8 7.1 %collective-permute-start = (bf16[256,128]{1,0:T(8,128)(2,1)S(1)}, bf16[256,128]{1,0:T(8,128)(2,1)S(1)}, u32[]{:S(2)}, u32[]{:S(2)}) collective-permute-start(bf16[256,128]{1,0:T(8,128)(2,1)S(1)} %get-tuple-element.31), channel_id=1, source_target_pairs={{0,2},{1,3},{2,0},{3,1},{4,6},{5,7},{6,4},{7,5},{8,10},{9,11},{10,... | collective-permute-start | bytes 196616 | tf_op jit(solution)/shard_map/ppermute | solution.py:25
  5.2 4.5 %collective-permute-start.1 = (bf16[256,128]{1,0:T(8,128)(2,1)S(1)}, bf16[256,128]{1,0:T(8,128)(2,1)S(1)}, u32[]{:S(2)}, u32[]{:S(2)}) collective-permute-start(bf16[256,128]{1,0:T(8,128)(2,1)S(1)} %get-tuple-element.32), channel_id=1, source_target_pairs={{0,1},{1,0},{2,3},{3,2},{4,5},{5,4},{6,7},{7,6},{8,9},{9,8},{10,11... | collective-permute-start | bytes 196616 | tf_op jit(solution)/shard_map/ppermute | solution.py:25
  5.8 5.5 %collective-permute-start.2 = (bf16[256,128]{1,0:T(8,128)(2,1)S(1)}, bf16[256,128]{1,0:T(8,128)(2,1)S(1)}, u32[]{:S(2)}, u32[]{:S(2)}) collective-permute-start(bf16[256,128]{1,0:T(8,128)(2,1)S(1)} %get-tuple-element.33), channel_id=1, source_target_pairs={{0,3},{1,2},{2,1},{3,0},{4,7},{5,6},{6,5},{7,4},{8,11},{9,10},{10,... | collective-permute-start | bytes 196616 | tf_op jit(solution)/shard_map/ppermute | solution.py:25
  11.4 5.7 %collective-permute-start.4 = (bf16[1024,128]{1,0:T(8,128)(2,1)S(1)}, bf16[1024,128]{1,0:T(8,128)(2,1)S(1)}, u32[]{:S(2)}, u32[]{:S(2)}) collective-permute-start(bf16[1024,128]{1,0:T(8,128)(2,1)S(1)} %order_rows.1.mine_ref.refs_2_), channel_id=1, source_target_pairs={{0,32},{1,33},{2,34},{3,35},{4,36},{5,37},{6,38},{7,39},{8,40},{9,... | collective-permute-start | bytes 786440 | tf_op jit(solution)/shard_map/ppermute | solution.py:25
  11.5 11.3 %collective-permute-start.5 = (bf16[1024,128]{1,0:T(8,128)(2,1)S(1)}, bf16[1024,128]{1,0:T(8,128)(2,1)S(1)}, u32[]{:S(2)}, u32[]{:S(2)}) collective-permute-start(bf16[1024,128]{1,0:T(8,128)(2,1)S(1)} %order_rows.1.mine_ref.refs_2_), channel_id=1, source_target_pairs={{0,8},{1,9},{2,10},{3,11},{4,12},{5,13},{6,14},{7,15},{8,0},{9,1},... | collective-permute-start | bytes 786440 | tf_op jit(solution)/shard_map/ppermute | solution.py:25
  13.1 10.9 %collective-permute-start.6 = (bf16[1024,128]{1,0:T(8,128)(2,1)S(1)}, bf16[1024,128]{1,0:T(8,128)(2,1)S(1)}, u32[]{:S(2)}, u32[]{:S(2)}) collective-permute-start(bf16[1024,128]{1,0:T(8,128)(2,1)S(1)} %order_rows.1.mine_ref.refs_2_), channel_id=1, source_target_pairs={{0,24},{1,25},{2,26},{3,27},{4,28},{5,29},{6,30},{7,31},{8,16},{9,... | collective-permute-start | bytes 786440 | tf_op jit(solution)/shard_map/ppermute | solution.py:25
  15.2 8.8 %collective-permute-start.7 = (bf16[1024,128]{1,0:T(8,128)(2,1)S(1)}, bf16[1024,128]{1,0:T(8,128)(2,1)S(1)}, u32[]{:S(2)}, u32[]{:S(2)}) collective-permute-start(bf16[1024,128]{1,0:T(8,128)(2,1)S(1)} %order_rows.1.mine_ref.refs_2_), channel_id=1, source_target_pairs={{0,4},{1,5},{2,6},{3,7},{4,0},{5,1},{6,2},{7,3},{8,12},{9,13},{10,... | collective-permute-start | bytes 786440 | tf_op jit(solution)/shard_map/ppermute | solution.py:25
  22.8 7.7 %collective-permute-start.10 = (bf16[1024,128]{1,0:T(8,128)(2,1)S(1)}, bf16[1024,128]{1,0:T(8,128)(2,1)S(1)}, u32[]{:S(2)}, u32[]{:S(2)}) collective-permute-start(bf16[1024,128]{1,0:T(8,128)(2,1)S(1)} %relay.4.first_ref), channel_id=1, source_target_pairs={{0,24},{1,25},{2,26},{3,27},{4,28},{5,29},{6,30},{7,31},{8,16},{9,... | collective-permute-start | bytes 786440 | tf_op jit(solution)/shard_map/ppermute | solution.py:25
  24.2 7.3 %collective-permute-start.9 = (bf16[3,1024,128]{2,1,0:T(8,128)(2,1)S(1)}, bf16[3,1024,128]{2,1,0:T(8,128)(2,1)S(1)}, u32[]{:S(2)}, u32[]{:S(2)}) collective-permute-start(bf16[3,1024,128]{2,1,0:T(8,128)(2,1)S(1)} %get-tuple-element.49.refs_6_), channel_id=1, source_target_pairs={{0,32},{1,33},{2,34},{3,35},{4,36},{5,37},{6,38},{7,39},{8,40},{9,... | collective-permute-start | bytes 2359304 | tf_op jit(solution)/shard_map/ppermute | solution.py:25
  25.7 9.3 %collective-permute-start.8 = (bf16[2,1024,128]{2,1,0:T(8,128)(2,1)S(1)}, bf16[2,1024,128]{2,1,0:T(8,128)(2,1)S(1)}, u32[]{:S(2)}, u32[]{:S(2)}) collective-permute-start(bf16[2,1024,128]{2,1,0:T(8,128)(2,1)S(1)} %get-tuple-element.38.refs_3_), channel_id=1, source_target_pairs={{0,4},{1,5},{2,6},{3,7},{4,0},{5,1},{6,2},{7,3},{8,12},{9,13},{10,... | collective-permute-start | bytes 1572872 | tf_op jit(solution)/shard_map/ppermute | solution.py:25
  30.5 7.3 %collective-permute-start.12 = (bf16[1024,128]{1,0:T(8,128)(2,1)S(1)}, bf16[1024,128]{1,0:T(8,128)(2,1)S(1)}, u32[]{:S(2)}, u32[]{:S(2)}) collective-permute-start(bf16[1024,128]{1,0:T(8,128)(2,1)S(1)} %relay.5.refs_9_.refs_2_), channel_id=1, source_target_pairs={{0,4},{1,5},{2,6},{3,7},{4,0},{5,1},{6,2},{7,3},{8,12},{9,13},{10,... | collective-permute-start | bytes 786440 | tf_op jit(solution)/shard_map/ppermute | solution.py:25
  35.0 4.3 %collective-permute-start.11 = (bf16[2,1024,128]{2,1,0:T(8,128)(2,1)S(1)}, bf16[2,1024,128]{2,1,0:T(8,128)(2,1)S(1)}, u32[]{:S(2)}, u32[]{:S(2)}) collective-permute-start(bf16[2,1024,128]{2,1,0:T(8,128)(2,1)S(1)} %relay.6.refs_3_.refs_6_), channel_id=1, source_target_pairs={{0,32},{1,33},{2,34},{3,35},{4,36},{5,37},{6,38},{7,39},{8,40},{9,... | collective-permute-start | bytes 1572872 | tf_op jit(solution)/shard_map/ppermute | solution.py:25
  36.0 2.0 %collective-permute-start.14 = (bf16[1024,128]{1,0:T(8,128)(2,1)S(1)}, bf16[1024,128]{1,0:T(8,128)(2,1)S(1)}, u32[]{:S(2)}, u32[]{:S(2)}) collective-permute-start(bf16[1024,128]{1,0:T(8,128)(2,1)S(1)} %relay.5.refs_9_.refs_2_), channel_id=1, source_target_pairs={{0,32},{1,33},{2,34},{3,35},{4,36},{5,37},{6,38},{7,39},{8,40},{9,... | collective-permute-start | bytes 786440 | tf_op jit(solution)/shard_map/ppermute | solution.py:25
  37.7 1.6 %collective-permute-start.13 = (bf16[1024,128]{1,0:T(8,128)(2,1)S(1)}, bf16[1024,128]{1,0:T(8,128)(2,1)S(1)}, u32[]{:S(2)}, u32[]{:S(2)}) collective-permute-start(bf16[1024,128]{1,0:T(8,128)(2,1)S(1)} %relay.7.refs_5_.refs_8_), channel_id=1, source_target_pairs={{0,32},{1,33},{2,34},{3,35},{4,36},{5,37},{6,38},{7,39},{8,40},{9,... | collective-permute-start | bytes 786440 | tf_op jit(solution)/shard_map/ppermute | solution.py:25
  42.9 6.5 %collective-permute-start.15 = (f32[64,256]{1,0:T(8,128)S(1)}, f32[64,256]{1,0:T(8,128)S(1)}, u32[]{:S(2)}, u32[]{:S(2)}) collective-permute-start(f32[64,256]{1,0:T(8,128)S(1)} %get-tuple-element.57), channel_id=1, source_target_pairs={{0,2},{1,3},{2,0},{3,1},{4,6},{5,7},{6,4},{7,5},{8,10},{9,11},{10,... | collective-permute-start | bytes 196616 | tf_op jit(solution)/shard_map/ppermute | solution.py:25
  44.1 5.2 %collective-permute-start.16 = (f32[64,256]{1,0:T(8,128)S(1)}, f32[64,256]{1,0:T(8,128)S(1)}, u32[]{:S(2)}, u32[]{:S(2)}) collective-permute-start(f32[64,256]{1,0:T(8,128)S(1)} %get-tuple-element.56), channel_id=1, source_target_pairs={{0,1},{1,0},{2,3},{3,2},{4,5},{5,4},{6,7},{7,6},{8,9},{9,8},{10,11... | collective-permute-start | bytes 196616 | tf_op jit(solution)/shard_map/ppermute | solution.py:25
  44.8 5.5 %collective-permute-start.17 = (f32[64,256]{1,0:T(8,128)S(1)}, f32[64,256]{1,0:T(8,128)S(1)}, u32[]{:S(2)}, u32[]{:S(2)}) collective-permute-start(f32[64,256]{1,0:T(8,128)S(1)} %get-tuple-element.55), channel_id=1, source_target_pairs={{0,3},{1,2},{2,1},{3,0},{4,7},{5,6},{6,5},{7,4},{8,11},{9,10},{10,... | collective-permute-start | bytes 196616 | tf_op jit(solution)/shard_map/ppermute | solution.py:25

commit v13 on v12

--- a/solution.py
+++ b/solution.py
@@ -153,23 +153,22 @@
     return outs
 
 
-def join_kernel(first_ref, second_ref, third_ref, _, pair_ref, all_ref):
-    for i, ref in enumerate((first_ref, second_ref)):
-        pair_ref[i] = ref[...]
-        all_ref[i] = ref[...]
-    all_ref[2] = third_ref[...]
-
-
-def join(first, second, third, token):
+def join_kernel(*refs):
+    for i, ref in enumerate(refs[:-2]):
+        refs[-1][i] = ref[...]
+
+
+def join(values, token):
+    n = len(values)
     return pl.pallas_call(
         join_kernel,
-        out_shape=tuple(jax.ShapeDtypeStruct((n, *first.shape), first.dtype) for n in (2, 3)),
-        in_specs=[spec(pltpu.VMEM)] * 3 + [spec(pl.ANY)],
-        out_specs=(spec(pltpu.VMEM), spec(pltpu.VMEM)),
+        out_shape=jax.ShapeDtypeStruct((n, *values[0].shape), values[0].dtype),
+        in_specs=[spec(pltpu.VMEM)] * n + [spec(pl.ANY)],
+        out_specs=spec(pltpu.VMEM),
         compiler_params=params(4),
         cost_estimate=pl.CostEstimate(flops=0, transcendentals=0, bytes_accessed=0),
         name="join",
-    )(first, second, third, token)
+    )(*values, token)
 
 
 def on_core(pair):
@@ -304,11 +303,15 @@
 
     c0, c1, c4, c5 = ((g, g) for g in (0, 1, 4, 5))
     c26, c62, c37, c73 = (2, 6), (6, 2), (3, 7), (7, 3)
-    x1a, x1b, z0 = over_x(mine, 1, 3), over_x(mine, 3, 1), over_z(mine)
-    x0m, x0o, *xs = stage1(halves(c0, c1, c26, c62, c4), own, tiles)
-    (x1a,) = relay((x1a,), (x0o,))
+    x1a, z0 = over_x(mine, 1, 3), over_z(mine)
+    x0m, x0o = stage1(halves(c0), own, tiles)
+    again = join((mine,), x0o)
+    x1b = over_x(again, 3, 1).reshape(1024, 128)
+    xs = stage1(halves(c1, c26, c62, c4), own, tiles, (again,))
+    (x1a,) = relay((x1a,), (xs[2],))
     x2 = over_x(x1a, 3, 1)
-    x1, near_blocks = join(x1a, x1b, z0, x0o)
+    x1 = join((x1a, x1b), xs[2])
+    near_blocks = join((x1a, x1b, z0), xs[2])
     zx1 = over_z(x1)
     other_blocks = to_sibling(near_blocks)
     x37 = stage1(halves(c37, c73), own, tiles, (x1,), FAST)

time: 51.5 us -> 51.7 us (level)
    pallas_call x3 -> x4, Pallas kernels: 9.32 us -> 9.48 us  [stage1(): pl.pallas_call(functools.partial(stage1_kernel, work, len(tokens)), out_s...]
where the time goes in v13:
time: 51.7 us; the launch traced here: 51.4 us
  Pallas kernels  24.4 us (47%)
  starting transfers between devices  19.6 us (38%)
  waiting for transfers between devices  7.22 us (14%)
    ppermute x18, starting transfers between devices, permute(): return lax.ppermute(value, ('occ', 'vir'), pairs)  19.6 us
    pallas_call x4, Pallas kernels, stage2(): pl.pallas_call(functools.partial(stage2_kernel, picks, len(bs), len(carry...  9.48 us
    pallas_call x4, Pallas kernels, stage1(): pl.pallas_call(functools.partial(stage1_kernel, work, len(tokens)), out_s...  9.48 us
    ppermute x18, waiting for transfers between devices, permute(): return lax.ppermute(value, ('occ', 'vir'), pairs)  7.22 us
    pallas_call x1, Pallas kernels, twist_tiles(): pl.pallas_call(twist_kernel, out_shape=(shape, shape), in_specs=[spec(plt...  2.63 us
    pallas_call x1, Pallas kernels, cut_to_send(): pl.pallas_call(send_kernel, out_shape=(chunk,) * 4 + (jax.ShapeDtypeStruc...  1.7 us
  transfers between devices with their start and end apart: 18, of which 6 were waited for; matrix products, arithmetic and copies ran while one was open for 0% of the time, Pallas kernels for 35%

profile of v13, /device:TPU:0, one launch (start us, length us, event | category | flops | bytes accessed | tf_op | source)
XLA Modules:
  0.0 51.4 jit_solution(1314900491532865045)
XLA Ops:
  0.0 1.7 %cut_to_send.1 = (bf16[256,128]{1,0:T(8,128)(2,1)S(1)}, bf16[256,128]{1,0:T(8,128)(2,1)S(1)}, bf16[256,128]{1,0:T(8,128)(2,1)S(1)}, bf16[256,128]{1,0:T(8,128)(2,1)S(1)}, bf16[8,8,128,128]{3,2,1,0:T(8,128)(2,1)S(1)}) custom-call(bf16[2048,128]{1,0:T(8,128)(2,1)} %bitcast.11, bf16[64,8,128,128]{3,2,1,0:T(8,128)(2,1)} %amp_ref.3), custom_call_target="tpu_custom_call" | custom-call | tf_op jit(solution)/shard_map/cut_to_send/pallas_call | solution.py:75
  1.8 3.4 %collective-permute-start = (bf16[256,128]{1,0:T(8,128)(2,1)S(1)}, bf16[256,128]{1,0:T(8,128)(2,1)S(1)}, u32[]{:S(2)}, u32[]{:S(2)}) collective-permute-start(bf16[256,128]{1,0:T(8,128)(2,1)S(1)} %get-tuple-element.29), channel_id=1, source_target_pairs={{0,2},{1,3},{2,0},{3,1},{4,6},{5,7},{6,4},{7,5},{8,10},{9,11},{10,... | collective-permute-start | bytes 196616 | tf_op jit(solution)/shard_map/ppermute | solution.py:25
  6.2 2.6 %twist_tiles.1 = (bf16[8,8,128,128]{3,2,1,0:T(8,128)(2,1)S(1)}, bf16[8,8,128,128]{3,2,1,0:T(8,128)(2,1)S(1)}) custom-call(s32[64]{0:T(128)S(1)} %copy-done, bf16[64,8,128,128]{3,2,1,0:T(8,128)(2,1)} %amp_ref.3, bf16[8,8,128,128]{3,2,1,0:T(8,128)(2,1)S(1)} %collective-permute-done.3.received_ref), custom_call_target="tpu_custom_call" | custom-call | tf_op jit(solution)/shard_map/twist_tiles/pallas_call | solution.py:103
  9.6 1.7 %collective-permute-done.2.r3_ref = bf16[256,128]{1,0:T(8,128)(2,1)S(1)} collective-permute-done((bf16[256,128]{1,0:T(8,128)(2,1)S(1)}, bf16[256,128]{1,0:T(8,128)(2,1)S(1)}, u32[]{:S(2)}, u32[]{:S(2)}) %collective-permute-start.2) | collective-permute-done | bytes 65568 | tf_op jit(solution)/shard_map/ppermute | solution.py:25
  11.5 1.6 %collective-permute-start.5 = (bf16[1024,128]{1,0:T(8,128)(2,1)S(1)}, bf16[1024,128]{1,0:T(8,128)(2,1)S(1)}, u32[]{:S(2)}, u32[]{:S(2)}) collective-permute-start(bf16[1024,128]{1,0:T(8,128)(2,1)S(1)} %order_rows.1.mine_ref.refs_0_.refs_2_), channel_id=1, source_target_pairs={{0,8},{1,9},{2,10},{3,11},{4,12},{5,13},{6,14},{7,15},{8,0},{9,1},... | collective-permute-start | bytes 786440 | tf_op jit(solution)/shard_map/ppermute | solution.py:25
  13.1 1.9 %collective-permute-start.8 = (bf16[1024,128]{1,0:T(8,128)(2,1)S(1)}, bf16[1024,128]{1,0:T(8,128)(2,1)S(1)}, u32[]{:S(2)}, u32[]{:S(2)}) collective-permute-start(bf16[1024,128]{1,0:T(8,128)(2,1)S(1)} %order_rows.1.mine_ref.refs_0_.refs_2_), channel_id=1, source_target_pairs={{0,4},{1,5},{2,6},{3,7},{4,0},{5,1},{6,2},{7,3},{8,12},{9,13},{10,... | collective-permute-start | bytes 786440 | tf_op jit(solution)/shard_map/ppermute | solution.py:25
  15.0 1.3 %stage1_0.1 = (bf16[256,4096]{1,0:T(8,128)(2,1)S(1)}, bf16[256,4096]{1,0:T(8,128)(2,1)S(1)}) custom-call(bf16[1024,128]{1,0:T(8,128)(2,1)S(1)} %order_rows.1.mine_ref.refs_0_.refs_2_, bf16[1024,128]{1,0:T(8,128)(2,1)S(1)} %collective-permute-done.4.refs_0_.refs_3_, bf16[8,8,128,128]{3,2,1,0:T(8,128)(2,1)S(1)} %get-tuple-element.34.refs_1_, ...), custom_call_target="tpu_custom_call" | custom-call | flops 1073741824 | bytes 1024 | tf_op jit(solution)/shard_map/stage1_0/pallas_call | solution.py:210
  16.3 2.2 %collective-permute-start.6 = (bf16[1,1024,128]{2,1,0:T(8,128)(2,1)S(1)}, bf16[1,1024,128]{2,1,0:T(8,128)(2,1)S(1)}, u32[]{:S(2)}, u32[]{:S(2)}) collective-permute-start(bf16[1,1024,128]{2,1,0:T(8,128)(2,1)S(1)} %join.3.refs_3_), channel_id=1, source_target_pairs={{0,24},{1,25},{2,26},{3,27},{4,28},{5,29},{6,30},{7,31},{8,16},{9,... | collective-permute-start | bytes 786440 | tf_op jit(solution)/shard_map/ppermute | solution.py:25
  18.5 4.6 %stage1_1_2_6_4.1 = (bf16[256,4096]{1,0:T(8,128)(2,1)S(1)}, bf16[256,4096]{1,0:T(8,128)(2,1)S(1)}, bf16[256,4096]{1,0:T(8,128)(2,1)S(1)}, bf16[256,4096]{1,0:T(8...) custom-call(bf16[1024,128]{1,0:T(8,128)(2,1)S(1)} %order_rows.1.mine, ...), custom_call_target="tpu_custom_call" | custom-call | flops 4294967296 | bytes 1024 | tf_op jit(solution)/shard_map/stage1_1_2_6_4/pallas_call | solution.py:210
  23.1 1.2 %collective-permute-start.10 = (bf16[1024,128]{1,0:T(8,128)(2,1)S(1)}, bf16[1024,128]{1,0:T(8,128)(2,1)S(1)}, u32[]{:S(2)}, u32[]{:S(2)}) collective-permute-start(bf16[1024,128]{1,0:T(8,128)(2,1)S(1)} %relay.4.refs_0_), channel_id=1, source_target_pairs={{0,24},{1,25},{2,26},{3,27},{4,28},{5,29},{6,30},{7,31},{8,16},{9,... | collective-permute-start | bytes 786440 | tf_op jit(solution)/shard_map/ppermute | solution.py:25
  24.4 1.5 %collective-permute-start.9 = (bf16[3,1024,128]{2,1,0:T(8,128)(2,1)S(1)}, bf16[3,1024,128]{2,1,0:T(8,128)(2,1)S(1)}, u32[]{:S(2)}, u32[]{:S(2)}) collective-permute-start(bf16[3,1024,128]{2,1,0:T(8,128)(2,1)S(1)} %join.5.refs_6_), channel_id=1, source_target_pairs={{0,32},{1,33},{2,34},{3,35},{4,36},{5,37},{6,38},{7,39},{8,40},{9,... | collective-permute-start | bytes 2359304 | tf_op jit(solution)/shard_map/ppermute | solution.py:25
  26.0 2.4 %stage1_3_7.1 = (bf16[256,4096]{1,0:T(8,128)(2,1)S(1)}, bf16[256,4096]{1,0:T(8,128)(2,1)S(1)}, bf16[256,4096]{1,0:T(8,128)(2,1)S(1)}, bf16[256,4096]{1,0:T(8,128)(2,1)S(1)}) custom-call(bf16[1024,128]{1,0:T(8,128)(2,1)S(1)} %order_rows.1.mine_ref.refs_0_.refs_2_, bf16[1024,128]{1,0:T(8,128)(2,1)S(1)} %collective-permute-done.4.refs_0_.refs_3_, ...), custom_call_target="tpu_custom_call" | custom-call | bytes 1024 | tf_op jit(solution)/shard_map/stage1_3_7/pallas_call | solution.py:210
  28.3 1.2 %stage2_self.1.refs_1_.refs_8_ = f32[4,64,32]{2,1,0:T(8,128)S(1)} custom-call(bf16[256,4096]{1,0:T(8,128)(2,1)S(1)} %get-tuple-element.46.refs_0_, bf16[256,4096]{1,0:T(8,128)(2,1)S(1)} %get-tuple-element.35.refs_1_, bf16[1024,128]{1,0:T(8,128)(2,1)S(1)} %order_rows.1.mine_ref.refs_0_.refs_2_, bf16[1024,128]{1,0:T(8,128)(2,1)S(1)} %collective-permute-done.4.refs_0_.refs_3_, ...), custom_call_target="tpu_custom_call" | custom-call | bytes 1024 | tf_op jit(solution)/shard_map/stage2_self/pallas_call | solution.py:256
  29.6 1.2 %collective-permute-done.10.refs_0_ = bf16[1024,128]{1,0:T(8,128)(2,1)S(1)} collective-permute-done((bf16[1024,128]{1,0:T(8,128)(2,1)S(1)}, bf16[1024,128]{1,0:T(8,128)(2,1)S(1)}, u32[]{:S(2)}, u32[]{:S(2)}) %collective-permute-start.10) | collective-permute-done | bytes 262176 | tf_op jit(solution)/shard_map/ppermute | solution.py:25
  30.7 1.0 %collective-permute-start.12 = (bf16[1024,128]{1,0:T(8,128)(2,1)S(1)}, bf16[1024,128]{1,0:T(8,128)(2,1)S(1)}, u32[]{:S(2)}, u32[]{:S(2)}) collective-permute-start(bf16[1024,128]{1,0:T(8,128)(2,1)S(1)} %relay.5.refs_9_.refs_2_), channel_id=1, source_target_pairs={{0,4},{1,5},{2,6},{3,7},{4,0},{5,1},{6,2},{7,3},{8,12},{9,13},{10,... | collective-permute-start | bytes 786440 | tf_op jit(solution)/shard_map/ppermute | solution.py:25
  31.7 3.5 %stage2_near.1.refs_1_.refs_4_ = f32[4,64,128]{2,1,0:T(8,128)S(1)} custom-call(bf16[256,4096]{1,0:T(8,128)(2,1)S(1)} %get-tuple-element.41.refs_0_, bf16[256,4096]{1,0:T(8,128)(2,1)S(1)} %get-tuple-element.42.refs_1_, bf16[256,4096]{1,0:T(8,128)(2,1)S(1)} %get-tuple-element.36.refs_1_.refs_2_.refs_3_, bf16[256,4096]{1,0:T(8,128)(2,1)S(1)} %get-tuple-element.43.refs_3_, ...), custom_call_target="tpu_custom_call" | custom-call | flops 25769803776 | bytes 1024 | tf_op jit(solution)/shard_map/stage2_near/pallas_call | solution.py:256
  35.2 1.0 %collective-permute-start.11 = (bf16[2,1024,128]{2,1,0:T(8,128)(2,1)S(1)}, bf16[2,1024,128]{2,1,0:T(8,128)(2,1)S(1)}, u32[]{:S(2)}, u32[]{:S(2)}) collective-permute-start(bf16[2,1024,128]{2,1,0:T(8,128)(2,1)S(1)} %relay.6.refs_3_.refs_6_), channel_id=1, source_target_pairs={{0,32},{1,33},{2,34},{3,35},{4,36},{5,37},{6,38},{7,39},{8,40},{9,... | collective-permute-start | bytes 1572872 | tf_op jit(solution)/shard_map/ppermute | solution.py:25
  36.3 1.3 %stage1_5.1 = (bf16[256,4096]{1,0:T(8,128)(2,1)S(1)}, bf16[256,4096]{1,0:T(8,128)(2,1)S(1)}) custom-call(bf16[1024,128]{1,0:T(8,128)(2,1)S(1)} %order_rows.1.mine_ref.refs_0_.refs_2_, bf16[1024,128]{1,0:T(8,128)(2,1)S(1)} %collective-permute-done.4.refs_0_.refs_3_, bf16[8,8,128,128]{3,2,1,0:T(8,128)(2,1)S(1)} %get-tuple-element.34.refs_1_, ...), custom_call_target="tpu_custom_call" | custom-call | flops 1073741824 | bytes 1024 | tf_op jit(solution)/shard_map/stage1_5/pallas_call | solution.py:210
  38.3 1.2 %stage2_far.1.refs_10_ = f32[4,64,160]{2,1,0:T(8,128)S(1)} custom-call(bf16[256,4096]{1,0:T(8,128)(2,1)S(1)} %get-tuple-element.49.refs_0_, bf16[256,4096]{1,0:T(8,128)(2,1)S(1)} %get-tuple-element.50.refs_1_, bf16[1024,128]{1,0:T(8,128)(2,1)S(1)} %relay.5.refs_9_.refs_2_, bf16[1024,128]{1,0:T(8,128)(2,1)S(1)} %collective-permute-done.14.refs_3_, ...), custom_call_target="tpu_custom_call" | custom-call | flops 1073741824 | bytes 1024 | tf_op jit(solution)/shard_map/stage2_far/pallas_call | solution.py:256
  39.6 3.5 %stage2_last.1.own_ref = f32[4,64,256]{2,1,0:T(8,128)S(1)} custom-call(bf16[256,4096]{1,0:T(8,128)(2,1)S(1)} %get-tuple-element.37.refs_4_.refs_0_, bf16[256,4096]{1,0:T(8,128)(2,1)S(1)} %get-tuple-element.38.refs_1_, bf16[256,4096]{1,0:T(8,128)(2,1)S(1)} %get-tuple-element.39.refs_2_, bf16[256,4096]{1,0:T(8,128)(2,1)S(1)} %get-tuple-element.40.refs_3_, ...), custom_call_target="tpu_custom_call" | custom-call | flops 3221225472 | bytes 1024 | tf_op jit(solution)/shard_map/stage2_last/pallas_call | solution.py:256
  43.1 1.3 %collective-permute-start.15 = (f32[64,256]{1,0:T(8,128)S(1)}, f32[64,256]{1,0:T(8,128)S(1)}, u32[]{:S(2)}, u32[]{:S(2)}) collective-permute-start(f32[64,256]{1,0:T(8,128)S(1)} %get-tuple-element.53), channel_id=1, source_target_pairs={{0,2},{1,3},{2,0},{3,1},{4,6},{5,7},{6,4},{7,5},{8,10},{9,11},{10,... | collective-permute-start | bytes 196616 | tf_op jit(solution)/shard_map/ppermute | solution.py:25
  45.0 2.2 %collective-permute-start.17 = (f32[64,256]{1,0:T(8,128)S(1)}, f32[64,256]{1,0:T(8,128)S(1)}, u32[]{:S(2)}, u32[]{:S(2)}) collective-permute-start(f32[64,256]{1,0:T(8,128)S(1)} %get-tuple-element.51), channel_id=1, source_target_pairs={{0,3},{1,2},{2,1},{3,0},{4,7},{5,6},{6,5},{7,4},{8,11},{9,10},{10,... | collective-permute-start | bytes 196616 | tf_op jit(solution)/shard_map/ppermute | solution.py:25
  47.3 2.3 %collective-permute-done.15.r1_ref = f32[64,256]{1,0:T(8,128)S(1)} collective-permute-done((f32[64,256]{1,0:T(8,128)S(1)}, f32[64,256]{1,0:T(8,128)S(1)}, u32[]{:S(2)}, u32[]{:S(2)}) %collective-permute-start.15) | collective-permute-done | bytes 65568 | tf_op jit(solution)/shard_map/ppermute | solution.py:25
  49.6 0.9 %collective-permute-done.17.r3_ref = f32[64,256]{1,0:T(8,128)S(1)} collective-permute-done((f32[64,256]{1,0:T(8,128)S(1)}, f32[64,256]{1,0:T(8,128)S(1)}, u32[]{:S(2)}, u32[]{:S(2)}) %collective-permute-start.17) | collective-permute-done | bytes 65568 | tf_op jit(solution)/shard_map/ppermute | solution.py:25
  (34 shorter events, 4.6 us)
Async XLA Ops:
  0.0 6.2 %copy-start = (s32[64]{0:T(128)S(1)}, s32[64]{0:T(128)}, u32[]{:S(2)}) copy-start(s32[64]{0:T(128)} %mirror_ref.1) | copy-start | bytes 772
  1.7 4.5 %collective-permute-start.3 = (bf16[8,8,128,128]{3,2,1,0:T(8,128)(2,1)S(1)}, bf16[8,8,128,128]{3,2,1,0:T(8,128)(2,1)S(1)}, u32[]{:S(2)}, u32[]{:S(2)}) collective-permute-start(bf16[8,8,128,128]{3,2,1,0:T(8,128)(2,1)S(1)} %get-tuple-element.32), channel_id=1, source_target_pairs={{0,32},{1,33},{2,34},{3,35},{4,36},{5,37},{6,38},{7,39},{8,40},{9,... | collective-permute-start | bytes 6291464 | tf_op jit(solution)/shard_map/ppermute | solution.py:25
  1.8 7.1 %collective-permute-start = (bf16[256,128]{1,0:T(8,128)(2,1)S(1)}, bf16[256,128]{1,0:T(8,128)(2,1)S(1)}, u32[]{:S(2)}, u32[]{:S(2)}) collective-permute-start(bf16[256,128]{1,0:T(8,128)(2,1)S(1)} %get-tuple-element.29), channel_id=1, source_target_pairs={{0,2},{1,3},{2,0},{3,1},{4,6},{5,7},{6,4},{7,5},{8,10},{9,11},{10,... | collective-permute-start | bytes 196616 | tf_op jit(solution)/shard_map/ppermute | solution.py:25
  5.2 4.5 %collective-permute-start.1 = (bf16[256,128]{1,0:T(8,128)(2,1)S(1)}, bf16[256,128]{1,0:T(8,128)(2,1)S(1)}, u32[]{:S(2)}, u32[]{:S(2)}) collective-permute-start(bf16[256,128]{1,0:T(8,128)(2,1)S(1)} %get-tuple-element.30), channel_id=1, source_target_pairs={{0,1},{1,0},{2,3},{3,2},{4,5},{5,4},{6,7},{7,6},{8,9},{9,8},{10,11... | collective-permute-start | bytes 196616 | tf_op jit(solution)/shard_map/ppermute | solution.py:25
  5.8 5.5 %collective-permute-start.2 = (bf16[256,128]{1,0:T(8,128)(2,1)S(1)}, bf16[256,128]{1,0:T(8,128)(2,1)S(1)}, u32[]{:S(2)}, u32[]{:S(2)}) collective-permute-start(bf16[256,128]{1,0:T(8,128)(2,1)S(1)} %get-tuple-element.31), channel_id=1, source_target_pairs={{0,3},{1,2},{2,1},{3,0},{4,7},{5,6},{6,5},{7,4},{8,11},{9,10},{10,... | collective-permute-start | bytes 196616 | tf_op jit(solution)/shard_map/ppermute | solution.py:25
  11.4 3.6 %collective-permute-start.4 = (bf16[1024,128]{1,0:T(8,128)(2,1)S(1)}, bf16[1024,128]{1,0:T(8,128)(2,1)S(1)}, u32[]{:S(2)}, u32[]{:S(2)}) collective-permute-start(bf16[1024,128]{1,0:T(8,128)(2,1)S(1)} %order_rows.1.mine_ref.refs_0_.refs_2_), channel_id=1, source_target_pairs={{0,32},{1,33},{2,34},{3,35},{4,36},{5,37},{6,38},{7,39},{8,40},{9,... | collective-permute-start | bytes 786440 | tf_op jit(solution)/shard_map/ppermute | solution.py:25
  11.5 11.6 %collective-permute-start.5 = (bf16[1024,128]{1,0:T(8,128)(2,1)S(1)}, bf16[1024,128]{1,0:T(8,128)(2,1)S(1)}, u32[]{:S(2)}, u32[]{:S(2)}) collective-permute-start(bf16[1024,128]{1,0:T(8,128)(2,1)S(1)} %order_rows.1.mine_ref.refs_0_.refs_2_), channel_id=1, source_target_pairs={{0,8},{1,9},{2,10},{3,11},{4,12},{5,13},{6,14},{7,15},{8,0},{9,1},... | collective-permute-start | bytes 786440 | tf_op jit(solution)/shard_map/ppermute | solution.py:25
  13.1 11.3 %collective-permute-start.8 = (bf16[1024,128]{1,0:T(8,128)(2,1)S(1)}, bf16[1024,128]{1,0:T(8,128)(2,1)S(1)}, u32[]{:S(2)}, u32[]{:S(2)}) collective-permute-start(bf16[1024,128]{1,0:T(8,128)(2,1)S(1)} %order_rows.1.mine_ref.refs_0_.refs_2_), channel_id=1, source_target_pairs={{0,4},{1,5},{2,6},{3,7},{4,0},{5,1},{6,2},{7,3},{8,12},{9,13},{10,... | collective-permute-start | bytes 786440 | tf_op jit(solution)/shard_map/ppermute | solution.py:25
  16.3 8.0 %collective-permute-start.6 = (bf16[1,1024,128]{2,1,0:T(8,128)(2,1)S(1)}, bf16[1,1024,128]{2,1,0:T(8,128)(2,1)S(1)}, u32[]{:S(2)}, u32[]{:S(2)}) collective-permute-start(bf16[1,1024,128]{2,1,0:T(8,128)(2,1)S(1)} %join.3.refs_3_), channel_id=1, source_target_pairs={{0,24},{1,25},{2,26},{3,27},{4,28},{5,29},{6,30},{7,31},{8,16},{9,... | collective-permute-start | bytes 786440 | tf_op jit(solution)/shard_map/ppermute | solution.py:25
  23.1 7.7 %collective-permute-start.10 = (bf16[1024,128]{1,0:T(8,128)(2,1)S(1)}, bf16[1024,128]{1,0:T(8,128)(2,1)S(1)}, u32[]{:S(2)}, u32[]{:S(2)}) collective-permute-start(bf16[1024,128]{1,0:T(8,128)(2,1)S(1)} %relay.4.refs_0_), channel_id=1, source_target_pairs={{0,24},{1,25},{2,26},{3,27},{4,28},{5,29},{6,30},{7,31},{8,16},{9,... | collective-permute-start | bytes 786440 | tf_op jit(solution)/shard_map/ppermute | solution.py:25
  24.4 7.3 %collective-permute-start.9 = (bf16[3,1024,128]{2,1,0:T(8,128)(2,1)S(1)}, bf16[3,1024,128]{2,1,0:T(8,128)(2,1)S(1)}, u32[]{:S(2)}, u32[]{:S(2)}) collective-permute-start(bf16[3,1024,128]{2,1,0:T(8,128)(2,1)S(1)} %join.5.refs_6_), channel_id=1, source_target_pairs={{0,32},{1,33},{2,34},{3,35},{4,36},{5,37},{6,38},{7,39},{8,40},{9,... | collective-permute-start | bytes 2359304 | tf_op jit(solution)/shard_map/ppermute | solution.py:25
  26.0 9.3 %collective-permute-start.7 = (bf16[2,1024,128]{2,1,0:T(8,128)(2,1)S(1)}, bf16[2,1024,128]{2,1,0:T(8,128)(2,1)S(1)}, u32[]{:S(2)}, u32[]{:S(2)}) collective-permute-start(bf16[2,1024,128]{2,1,0:T(8,128)(2,1)S(1)} %join.4.refs_3_), channel_id=1, source_target_pairs={{0,4},{1,5},{2,6},{3,7},{4,0},{5,1},{6,2},{7,3},{8,12},{9,13},{10,... | collective-permute-start | bytes 1572872 | tf_op jit(solution)/shard_map/ppermute | solution.py:25
  30.7 7.2 %collective-permute-start.12 = (bf16[1024,128]{1,0:T(8,128)(2,1)S(1)}, bf16[1024,128]{1,0:T(8,128)(2,1)S(1)}, u32[]{:S(2)}, u32[]{:S(2)}) collective-permute-start(bf16[1024,128]{1,0:T(8,128)(2,1)S(1)} %relay.5.refs_9_.refs_2_), channel_id=1, source_target_pairs={{0,4},{1,5},{2,6},{3,7},{4,0},{5,1},{6,2},{7,3},{8,12},{9,13},{10,... | collective-permute-start | bytes 786440 | tf_op jit(solution)/shard_map/ppermute | solution.py:25
  35.2 4.3 %collective-permute-start.11 = (bf16[2,1024,128]{2,1,0:T(8,128)(2,1)S(1)}, bf16[2,1024,128]{2,1,0:T(8,128)(2,1)S(1)}, u32[]{:S(2)}, u32[]{:S(2)}) collective-permute-start(bf16[2,1024,128]{2,1,0:T(8,128)(2,1)S(1)} %relay.6.refs_3_.refs_6_), channel_id=1, source_target_pairs={{0,32},{1,33},{2,34},{3,35},{4,36},{5,37},{6,38},{7,39},{8,40},{9,... | collective-permute-start | bytes 1572872 | tf_op jit(solution)/shard_map/ppermute | solution.py:25
  36.2 2.0 %collective-permute-start.14 = (bf16[1024,128]{1,0:T(8,128)(2,1)S(1)}, bf16[1024,128]{1,0:T(8,128)(2,1)S(1)}, u32[]{:S(2)}, u32[]{:S(2)}) collective-permute-start(bf16[1024,128]{1,0:T(8,128)(2,1)S(1)} %relay.5.refs_9_.refs_2_), channel_id=1, source_target_pairs={{0,32},{1,33},{2,34},{3,35},{4,36},{5,37},{6,38},{7,39},{8,40},{9,... | collective-permute-start | bytes 786440 | tf_op jit(solution)/shard_map/ppermute | solution.py:25
  37.9 1.6 %collective-permute-start.13 = (bf16[1024,128]{1,0:T(8,128)(2,1)S(1)}, bf16[1024,128]{1,0:T(8,128)(2,1)S(1)}, u32[]{:S(2)}, u32[]{:S(2)}) collective-permute-start(bf16[1024,128]{1,0:T(8,128)(2,1)S(1)} %relay.7.refs_5_.refs_8_), channel_id=1, source_target_pairs={{0,32},{1,33},{2,34},{3,35},{4,36},{5,37},{6,38},{7,39},{8,40},{9,... | collective-permute-start | bytes 786440 | tf_op jit(solution)/shard_map/ppermute | solution.py:25
  43.1 6.5 %collective-permute-start.15 = (f32[64,256]{1,0:T(8,128)S(1)}, f32[64,256]{1,0:T(8,128)S(1)}, u32[]{:S(2)}, u32[]{:S(2)}) collective-permute-start(f32[64,256]{1,0:T(8,128)S(1)} %get-tuple-element.53), channel_id=1, source_target_pairs={{0,2},{1,3},{2,0},{3,1},{4,6},{5,7},{6,4},{7,5},{8,10},{9,11},{10,... | collective-permute-start | bytes 196616 | tf_op jit(solution)/shard_map/ppermute | solution.py:25
  44.4 5.2 %collective-permute-start.16 = (f32[64,256]{1,0:T(8,128)S(1)}, f32[64,256]{1,0:T(8,128)S(1)}, u32[]{:S(2)}, u32[]{:S(2)}) collective-permute-start(f32[64,256]{1,0:T(8,128)S(1)} %get-tuple-element.52), channel_id=1, source_target_pairs={{0,1},{1,0},{2,3},{3,2},{4,5},{5,4},{6,7},{7,6},{8,9},{9,8},{10,11... | collective-permute-start | bytes 196616 | tf_op jit(solution)/shard_map/ppermute | solution.py:25
  45.0 5.5 %collective-permute-start.17 = (f32[64,256]{1,0:T(8,128)S(1)}, f32[64,256]{1,0:T(8,128)S(1)}, u32[]{:S(2)}, u32[]{:S(2)}) collective-permute-start(f32[64,256]{1,0:T(8,128)S(1)} %get-tuple-element.51), channel_id=1, source_target_pairs={{0,3},{1,2},{2,1},{3,0},{4,7},{5,6},{6,5},{7,4},{8,11},{9,10},{10,... | collective-permute-start | bytes 196616 | tf_op jit(solution)/shard_map/ppermute | solution.py:25

commit v14 on v12

--- a/solution.py
+++ b/solution.py
@@ -266,6 +266,27 @@
     )(*xs, *bs, *carry, *tokens)
 
 
+def mixed_kernel(work, *refs):
+    own, tiles, xs, refs = refs[:2], refs[2:4], refs[4:6], refs[7:]
+    stage1_kernel(work, 0, *own, *tiles, *refs[: len(work)])
+    stage2_kernel((((0, None), (1, None)),), 2, 0, 0, *xs, *own, *refs[len(work) :])
+
+
+def mixed(work, own, tiles, xs, token):
+    outs = pl.pallas_call(
+        functools.partial(mixed_kernel, work),
+        out_shape=tuple(jax.ShapeDtypeStruct((256, 4096), BF16) for _ in work)
+        + (jax.ShapeDtypeStruct((4, 64, 32), F32),),
+        in_specs=[spec(pltpu.VMEM)] * 6 + [spec(pl.ANY)],
+        out_specs=tuple(spec(pltpu.VMEM) for _ in range(len(work) + 1)),
+        scratch_shapes=[pltpu.VMEM((1, 256, 32), F32)],
+        compiler_params=params(8),
+        cost_estimate=pl.CostEstimate(flops=0, transcendentals=0, bytes_accessed=2**10),
+        name="mixed",
+    )(*own, *tiles, *xs, token)
+    return outs[:-1], outs[-1]
+
+
 def finish_kernel(order, own_ref, r1_ref, r2_ref, r3_ref, out_ref, sum_s, pos_s):
     total = own_ref[0] + r1_ref[...] + r2_ref[...] + r3_ref[...]
     sum_s[0] = total[:, 0:128]
@@ -311,8 +332,7 @@
     x1, near_blocks = join(x1a, x1b, z0, x0o)
     zx1 = over_z(x1)
     other_blocks = to_sibling(near_blocks)
-    x37 = stage1(halves(c37, c73), own, tiles, (x1,), FAST)
-    self0 = stage2("self", (x0m, x0o), (((0, None), (1, None)),), own, (), (x37[0],), FAST)
+    x37, self0 = mixed(halves(c37, c73), own, tiles, (x0m, x0o), x1)
     (x2,) = relay((x2,), (self0,), HOLD)
     zx2 = over_z(x2)
     x2_other = to_sibling(x2)

time: 51.5 us -> 51.5 us (level)
    pallas_call x0 -> x1, Pallas kernels: none -> 3.47 us  [mixed(): pl.pallas_call(functools.partial(mixed_kernel, work), out_shape=tuple((ja...]
    pallas_call x3 -> x2, Pallas kernels: 9.32 us -> 6.95 us  [stage1(): pl.pallas_call(functools.partial(stage1_kernel, work, len(tokens)), out_s...]
    pallas_call x4 -> x3, Pallas kernels: 9.48 us -> 8.25 us  [stage2(): pl.pallas_call(functools.partial(stage2_kernel, picks, len(bs), len(carry...]
  transfers between devices with their start and end apart: 18 -> 18, of which waited for: 6 -> 7; matrix products, arithmetic and copies ran while one was open for 0% -> 0% of each run, Pallas kernels for 35% -> 35%
where the time goes in v14:
time: 51.5 us; the launch traced here: 51.2 us
  Pallas kernels  24.1 us (47%)
  starting transfers between devices  19.4 us (38%)
  waiting for transfers between devices  7.51 us (15%)
    ppermute x18, starting transfers between devices, permute(): return lax.ppermute(value, ('occ', 'vir'), pairs)  19.4 us
    pallas_call x3, Pallas kernels, stage2(): pl.pallas_call(functools.partial(stage2_kernel, picks, len(bs), len(carry...  8.25 us
    ppermute x18, waiting for transfers between devices, permute(): return lax.ppermute(value, ('occ', 'vir'), pairs)  7.51 us
    pallas_call x2, Pallas kernels, stage1(): pl.pallas_call(functools.partial(stage1_kernel, work, len(tokens)), out_s...  6.95 us
    pallas_call x1, Pallas kernels, mixed(): pl.pallas_call(functools.partial(mixed_kernel, work), out_shape=tuple((ja...  3.47 us
    pallas_call x1, Pallas kernels, twist_tiles(): pl.pallas_call(twist_kernel, out_shape=(shape, shape), in_specs=[spec(plt...  2.63 us
    pallas_call x1, Pallas kernels, cut_to_send(): pl.pallas_call(send_kernel, out_shape=(chunk,) * 4 + (jax.ShapeDtypeStruc...  1.7 us
  transfers between devices with their start and end apart: 18, of which 7 were waited for; matrix products, arithmetic and copies ran while one was open for 0% of the time, Pallas kernels for 35%

profile of v14, /device:TPU:0, one launch (start us, length us, event | category | flops | bytes accessed | tf_op | source)
XLA Modules:
  0.0 51.2 jit_solution(8369923539338760169)
XLA Ops:
  0.0 1.7 %cut_to_send.1 = (bf16[256,128]{1,0:T(8,128)(2,1)S(1)}, bf16[256,128]{1,0:T(8,128)(2,1)S(1)}, bf16[256,128]{1,0:T(8,128)(2,1)S(1)}, bf16[256,128]{1,0:T(8,128)(2,1)S(1)}, bf16[8,8,128,128]{3,2,1,0:T(8,128)(2,1)S(1)}) custom-call(bf16[2048,128]{1,0:T(8,128)(2,1)} %bitcast.8, bf16[64,8,128,128]{3,2,1,0:T(8,128)(2,1)} %amp_ref.3), custom_call_target="tpu_custom_call" | custom-call | tf_op jit(solution)/shard_map/cut_to_send/pallas_call | solution.py:75
  1.8 3.4 %collective-permute-start = (bf16[256,128]{1,0:T(8,128)(2,1)S(1)}, bf16[256,128]{1,0:T(8,128)(2,1)S(1)}, u32[]{:S(2)}, u32[]{:S(2)}) collective-permute-start(bf16[256,128]{1,0:T(8,128)(2,1)S(1)} %get-tuple-element.32), channel_id=1, source_target_pairs={{0,2},{1,3},{2,0},{3,1},{4,6},{5,7},{6,4},{7,5},{8,10},{9,11},{10,... | collective-permute-start | bytes 196616 | tf_op jit(solution)/shard_map/ppermute | solution.py:25
  6.2 2.6 %twist_tiles.1 = (bf16[8,8,128,128]{3,2,1,0:T(8,128)(2,1)S(1)}, bf16[8,8,128,128]{3,2,1,0:T(8,128)(2,1)S(1)}) custom-call(s32[64]{0:T(128)S(1)} %copy-done, bf16[64,8,128,128]{3,2,1,0:T(8,128)(2,1)} %amp_ref.3, bf16[8,8,128,128]{3,2,1,0:T(8,128)(2,1)S(1)} %collective-permute-done.3.received_ref), custom_call_target="tpu_custom_call" | custom-call | tf_op jit(solution)/shard_map/twist_tiles/pallas_call | solution.py:103
  8.9 0.8 %collective-permute-done.1.r1_ref = bf16[256,128]{1,0:T(8,128)(2,1)S(1)} collective-permute-done((bf16[256,128]{1,0:T(8,128)(2,1)S(1)}, bf16[256,128]{1,0:T(8,128)(2,1)S(1)}, u32[]{:S(2)}, u32[]{:S(2)}) %collective-permute-start.1) | collective-permute-done | bytes 65568 | tf_op jit(solution)/shard_map/ppermute | solution.py:25
  9.6 1.7 %collective-permute-done.2.r3_ref = bf16[256,128]{1,0:T(8,128)(2,1)S(1)} collective-permute-done((bf16[256,128]{1,0:T(8,128)(2,1)S(1)}, bf16[256,128]{1,0:T(8,128)(2,1)S(1)}, u32[]{:S(2)}, u32[]{:S(2)}) %collective-permute-start.2) | collective-permute-done | bytes 65568 | tf_op jit(solution)/shard_map/ppermute | solution.py:25
  11.5 1.6 %collective-permute-start.5 = (bf16[1024,128]{1,0:T(8,128)(2,1)S(1)}, bf16[1024,128]{1,0:T(8,128)(2,1)S(1)}, u32[]{:S(2)}, u32[]{:S(2)}) collective-permute-start(bf16[1024,128]{1,0:T(8,128)(2,1)S(1)} %order_rows.1.mine_ref.refs_0_), channel_id=1, source_target_pairs={{0,8},{1,9},{2,10},{3,11},{4,12},{5,13},{6,14},{7,15},{8,0},{9,1},... | collective-permute-start | bytes 786440 | tf_op jit(solution)/shard_map/ppermute | solution.py:25
  13.1 2.1 %collective-permute-start.6 = (bf16[1024,128]{1,0:T(8,128)(2,1)S(1)}, bf16[1024,128]{1,0:T(8,128)(2,1)S(1)}, u32[]{:S(2)}, u32[]{:S(2)}) collective-permute-start(bf16[1024,128]{1,0:T(8,128)(2,1)S(1)} %order_rows.1.mine_ref.refs_0_), channel_id=1, source_target_pairs={{0,24},{1,25},{2,26},{3,27},{4,28},{5,29},{6,30},{7,31},{8,16},{9,... | collective-permute-start | bytes 786440 | tf_op jit(solution)/shard_map/ppermute | solution.py:25
  15.2 1.9 %collective-permute-start.7 = (bf16[1024,128]{1,0:T(8,128)(2,1)S(1)}, bf16[1024,128]{1,0:T(8,128)(2,1)S(1)}, u32[]{:S(2)}, u32[]{:S(2)}) collective-permute-start(bf16[1024,128]{1,0:T(8,128)(2,1)S(1)} %order_rows.1.mine_ref.refs_0_), channel_id=1, source_target_pairs={{0,4},{1,5},{2,6},{3,7},{4,0},{5,1},{6,2},{7,3},{8,12},{9,13},{10,... | collective-permute-start | bytes 786440 | tf_op jit(solution)/shard_map/ppermute | solution.py:25
  17.1 5.7 %stage1_0_1_2_6_4.1 = (bf16[256,4096]{1,0:T(8,128)(2,1)S(1)}, bf16[256,4096]{1,0:T(8,128)(2,1)S(1)}, bf16[256,4096]{1,0:T(8,128)(2,1)S(1)}, bf16[256,4096]{1,0:T...) custom-call(bf16[1024,128]{1,0:T(8,128)(2,1)S(1)} %order_rows.1.mine, ...), custom_call_target="tpu_custom_call" | custom-call | flops 5368709120 | bytes 1024 | tf_op jit(solution)/shard_map/stage1_0_1_2_6_4/pallas_call | solution.py:211
  22.8 1.2 %collective-permute-start.10 = (bf16[1024,128]{1,0:T(8,128)(2,1)S(1)}, bf16[1024,128]{1,0:T(8,128)(2,1)S(1)}, u32[]{:S(2)}, u32[]{:S(2)}) collective-permute-start(bf16[1024,128]{1,0:T(8,128)(2,1)S(1)} %relay.4.first_ref), channel_id=1, source_target_pairs={{0,24},{1,25},{2,26},{3,27},{4,28},{5,29},{6,30},{7,31},{8,16},{9,... | collective-permute-start | bytes 786440 | tf_op jit(solution)/shard_map/ppermute | solution.py:25
  24.2 1.6 %collective-permute-start.9 = (bf16[3,1024,128]{2,1,0:T(8,128)(2,1)S(1)}, bf16[3,1024,128]{2,1,0:T(8,128)(2,1)S(1)}, u32[]{:S(2)}, u32[]{:S(2)}) collective-permute-start(bf16[3,1024,128]{2,1,0:T(8,128)(2,1)S(1)} %get-tuple-element.51.refs_6_), channel_id=1, source_target_pairs={{0,32},{1,33},{2,34},{3,35},{4,36},{5,37},{6,38},{7,39},{8,40},{9,... | collective-permute-start | bytes 2359304 | tf_op jit(solution)/shard_map/ppermute | solution.py:25
  25.7 3.5 %mixed.1 = (bf16[256,4096]{1,0:T(8,128)(2,1)S(1)}, bf16[256,4096]{1,0:T(8,128)(2,1)S(1)}, bf16[256,4096]{1,0:T(8,128)(2,1)S(1)}, bf16[256,4096]{1,0:T(8,128)(2,1)S(1)}, f32[4,64,32]{2,1,0:T(8,128)S(1)}) custom-call(bf16[1024,128]{1,0:T(8,128)(2,1)S(1)} %order_rows.1.mine_ref.refs_0_, bf16[1024,128]{1,0:T(8,128)(2,1)S(1)} %collective-permute-done.4.refs_0_.refs_1_, ...), custom_call_target="tpu_custom_call" | custom-call | bytes 1024 | tf_op jit(solution)/shard_map/mixed/pallas_call | solution.py:276
  29.2 1.2 %collective-permute-done.10.refs_0_ = bf16[1024,128]{1,0:T(8,128)(2,1)S(1)} collective-permute-done((bf16[1024,128]{1,0:T(8,128)(2,1)S(1)}, bf16[1024,128]{1,0:T(8,128)(2,1)S(1)}, u32[]{:S(2)}, u32[]{:S(2)}) %collective-permute-start.10) | collective-permute-done | bytes 262176 | tf_op jit(solution)/shard_map/ppermute | solution.py:25
  30.5 0.9 %collective-permute-start.12 = (bf16[1024,128]{1,0:T(8,128)(2,1)S(1)}, bf16[1024,128]{1,0:T(8,128)(2,1)S(1)}, u32[]{:S(2)}, u32[]{:S(2)}) collective-permute-start(bf16[1024,128]{1,0:T(8,128)(2,1)S(1)} %relay.5.refs_9_.refs_2_), channel_id=1, source_target_pairs={{0,4},{1,5},{2,6},{3,7},{4,0},{5,1},{6,2},{7,3},{8,12},{9,13},{10,... | collective-permute-start | bytes 786440 | tf_op jit(solution)/shard_map/ppermute | solution.py:25
  31.3 3.5 %stage2_near.1.refs_1_.refs_4_ = f32[4,64,128]{2,1,0:T(8,128)S(1)} custom-call(bf16[256,4096]{1,0:T(8,128)(2,1)S(1)} %get-tuple-element.45.refs_0_, bf16[256,4096]{1,0:T(8,128)(2,1)S(1)} %get-tuple-element.46.refs_1_, bf16[256,4096]{1,0:T(8,128)(2,1)S(1)} %get-tuple-element.47.refs_2_, bf16[256,4096]{1,0:T(8,128)(2,1)S(1)} %get-tuple-element.48.refs_3_, ...), custom_call_target="tpu_custom_call" | custom-call | flops 25769803776 | bytes 1024 | tf_op jit(solution)/shard_map/stage2_near/pallas_call | solution.py:257
  34.9 1.0 %collective-permute-start.11 = (bf16[2,1024,128]{2,1,0:T(8,128)(2,1)S(1)}, bf16[2,1024,128]{2,1,0:T(8,128)(2,1)S(1)}, u32[]{:S(2)}, u32[]{:S(2)}) collective-permute-start(bf16[2,1024,128]{2,1,0:T(8,128)(2,1)S(1)} %relay.6.refs_3_.refs_6_), channel_id=1, source_target_pairs={{0,32},{1,33},{2,34},{3,35},{4,36},{5,37},{6,38},{7,39},{8,40},{9,... | collective-permute-start | bytes 1572872 | tf_op jit(solution)/shard_map/ppermute | solution.py:25
  36.0 1.3 %stage1_5.1 = (bf16[256,4096]{1,0:T(8,128)(2,1)S(1)}, bf16[256,4096]{1,0:T(8,128)(2,1)S(1)}) custom-call(bf16[1024,128]{1,0:T(8,128)(2,1)S(1)} %order_rows.1.mine_ref.refs_0_, bf16[1024,128]{1,0:T(8,128)(2,1)S(1)} %collective-permute-done.4.refs_0_.refs_1_, bf16[8,8,128,128]{3,2,1,0:T(8,128)(2,1)S(1)} %get-tuple-element.37.refs_1_.refs_2_, ...), custom_call_target="tpu_custom_call" | custom-call | flops 1073741824 | bytes 1024 | tf_op jit(solution)/shard_map/stage1_5/pallas_call | solution.py:211
  38.1 1.2 %stage2_far.1.refs_10_ = f32[4,64,160]{2,1,0:T(8,128)S(1)} custom-call(bf16[256,4096]{1,0:T(8,128)(2,1)S(1)} %get-tuple-element.55.refs_0_, bf16[256,4096]{1,0:T(8,128)(2,1)S(1)} %get-tuple-element.56.refs_1_, bf16[1024,128]{1,0:T(8,128)(2,1)S(1)} %relay.5.refs_9_.refs_2_, bf16[1024,128]{1,0:T(8,128)(2,1)S(1)} %collective-permute-done.14.refs_3_, ...), custom_call_target="tpu_custom_call" | custom-call | flops 1073741824 | bytes 1024 | tf_op jit(solution)/shard_map/stage2_far/pallas_call | solution.py:257
  39.3 3.5 %stage2_last.1.own_ref = f32[4,64,256]{2,1,0:T(8,128)S(1)} custom-call(bf16[256,4096]{1,0:T(8,128)(2,1)S(1)} %get-tuple-element.41.refs_0_, bf16[256,4096]{1,0:T(8,128)(2,1)S(1)} %get-tuple-element.42.refs_1_, bf16[256,4096]{1,0:T(8,128)(2,1)S(1)} %get-tuple-element.43.refs_2_, bf16[256,4096]{1,0:T(8,128)(2,1)S(1)} %get-tuple-element.44.refs_3_, ...), custom_call_target="tpu_custom_call" | custom-call | flops 3221225472 | bytes 1024 | tf_op jit(solution)/shard_map/stage2_last/pallas_call | solution.py:257
  42.9 1.3 %collective-permute-start.15 = (f32[64,256]{1,0:T(8,128)S(1)}, f32[64,256]{1,0:T(8,128)S(1)}, u32[]{:S(2)}, u32[]{:S(2)}) collective-permute-start(f32[64,256]{1,0:T(8,128)S(1)} %get-tuple-element.59), channel_id=1, source_target_pairs={{0,2},{1,3},{2,0},{3,1},{4,6},{5,7},{6,4},{7,5},{8,10},{9,11},{10,... | collective-permute-start | bytes 196616 | tf_op jit(solution)/shard_map/ppermute | solution.py:25
  44.8 2.2 %collective-permute-start.17 = (f32[64,256]{1,0:T(8,128)S(1)}, f32[64,256]{1,0:T(8,128)S(1)}, u32[]{:S(2)}, u32[]{:S(2)}) collective-permute-start(f32[64,256]{1,0:T(8,128)S(1)} %get-tuple-element.57), channel_id=1, source_target_pairs={{0,3},{1,2},{2,1},{3,0},{4,7},{5,6},{6,5},{7,4},{8,11},{9,10},{10,... | collective-permute-start | bytes 196616 | tf_op jit(solution)/shard_map/ppermute | solution.py:25
  47.0 2.3 %collective-permute-done.15.r1_ref = f32[64,256]{1,0:T(8,128)S(1)} collective-permute-done((f32[64,256]{1,0:T(8,128)S(1)}, f32[64,256]{1,0:T(8,128)S(1)}, u32[]{:S(2)}, u32[]{:S(2)}) %collective-permute-start.15) | collective-permute-done | bytes 65568 | tf_op jit(solution)/shard_map/ppermute | solution.py:25
  49.4 0.9 %collective-permute-done.17.r3_ref = f32[64,256]{1,0:T(8,128)S(1)} collective-permute-done((f32[64,256]{1,0:T(8,128)S(1)}, f32[64,256]{1,0:T(8,128)S(1)}, u32[]{:S(2)}, u32[]{:S(2)}) %collective-permute-start.17) | collective-permute-done | bytes 65568 | tf_op jit(solution)/shard_map/ppermute | solution.py:25
  50.3 0.9 %finish.1 = f32[8,32,64]{2,1,0:T(8,128)} custom-call(f32[4,64,256]{2,1,0:T(8,128)S(1)} %stage2_last.1.own_ref, f32[64,256]{1,0:T(8,128)S(1)} %collective-permute-done.15.r1_ref, f32[64,256]{1,0:T(8,128)S(1)} %collective-permute-done.16.r2_ref, f32[64,256]{1,0:T(8,128)S(1)} %collective-permute-done.17.r3_ref), custom_call_target="tpu_custom_call" | custom-call | tf_op jit(solution)/shard_map/finish/pallas_call | solution.py:304
  (30 shorter events, 3.2 us)
Async XLA Ops:
  0.0 6.2 %copy-start = (s32[64]{0:T(128)S(1)}, s32[64]{0:T(128)}, u32[]{:S(2)}) copy-start(s32[64]{0:T(128)} %mirror_ref.1) | copy-start | bytes 772
  1.7 4.5 %collective-permute-start.3 = (bf16[8,8,128,128]{3,2,1,0:T(8,128)(2,1)S(1)}, bf16[8,8,128,128]{3,2,1,0:T(8,128)(2,1)S(1)}, u32[]{:S(2)}, u32[]{:S(2)}) collective-permute-start(bf16[8,8,128,128]{3,2,1,0:T(8,128)(2,1)S(1)} %get-tuple-element.35), channel_id=1, source_target_pairs={{0,32},{1,33},{2,34},{3,35},{4,36},{5,37},{6,38},{7,39},{8,40},{9,... | collective-permute-start | bytes 6291464 | tf_op jit(solution)/shard_map/ppermute | solution.py:25
  1.8 7.1 %collective-permute-start = (bf16[256,128]{1,0:T(8,128)(2,1)S(1)}, bf16[256,128]{1,0:T(8,128)(2,1)S(1)}, u32[]{:S(2)}, u32[]{:S(2)}) collective-permute-start(bf16[256,128]{1,0:T(8,128)(2,1)S(1)} %get-tuple-element.32), channel_id=1, source_target_pairs={{0,2},{1,3},{2,0},{3,1},{4,6},{5,7},{6,4},{7,5},{8,10},{9,11},{10,... | collective-permute-start | bytes 196616 | tf_op jit(solution)/shard_map/ppermute | solution.py:25
  5.2 4.5 %collective-permute-start.1 = (bf16[256,128]{1,0:T(8,128)(2,1)S(1)}, bf16[256,128]{1,0:T(8,128)(2,1)S(1)}, u32[]{:S(2)}, u32[]{:S(2)}) collective-permute-start(bf16[256,128]{1,0:T(8,128)(2,1)S(1)} %get-tuple-element.33), channel_id=1, source_target_pairs={{0,1},{1,0},{2,3},{3,2},{4,5},{5,4},{6,7},{7,6},{8,9},{9,8},{10,11... | collective-permute-start | bytes 196616 | tf_op jit(solution)/shard_map/ppermute | solution.py:25
  5.8 5.5 %collective-permute-start.2 = (bf16[256,128]{1,0:T(8,128)(2,1)S(1)}, bf16[256,128]{1,0:T(8,128)(2,1)S(1)}, u32[]{:S(2)}, u32[]{:S(2)}) collective-permute-start(bf16[256,128]{1,0:T(8,128)(2,1)S(1)} %get-tuple-element.34), channel_id=1, source_target_pairs={{0,3},{1,2},{2,1},{3,0},{4,7},{5,6},{6,5},{7,4},{8,11},{9,10},{10,... | collective-permute-start | bytes 196616 | tf_op jit(solution)/shard_map/ppermute | solution.py:25
  11.4 5.7 %collective-permute-start.4 = (bf16[1024,128]{1,0:T(8,128)(2,1)S(1)}, bf16[1024,128]{1,0:T(8,128)(2,1)S(1)}, u32[]{:S(2)}, u32[]{:S(2)}) collective-permute-start(bf16[1024,128]{1,0:T(8,128)(2,1)S(1)} %order_rows.1.mine_ref.refs_0_), channel_id=1, source_target_pairs={{0,32},{1,33},{2,34},{3,35},{4,36},{5,37},{6,38},{7,39},{8,40},{9,... | collective-permute-start | bytes 786440 | tf_op jit(solution)/shard_map/ppermute | solution.py:25
  11.5 11.3 %collective-permute-start.5 = (bf16[1024,128]{1,0:T(8,128)(2,1)S(1)}, bf16[1024,128]{1,0:T(8,128)(2,1)S(1)}, u32[]{:S(2)}, u32[]{:S(2)}) collective-permute-start(bf16[1024,128]{1,0:T(8,128)(2,1)S(1)} %order_rows.1.mine_ref.refs_0_), channel_id=1, source_target_pairs={{0,8},{1,9},{2,10},{3,11},{4,12},{5,13},{6,14},{7,15},{8,0},{9,1},... | collective-permute-start | bytes 786440 | tf_op jit(solution)/shard_map/ppermute | solution.py:25
  13.1 10.9 %collective-permute-start.6 = (bf16[1024,128]{1,0:T(8,128)(2,1)S(1)}, bf16[1024,128]{1,0:T(8,128)(2,1)S(1)}, u32[]{:S(2)}, u32[]{:S(2)}) collective-permute-start(bf16[1024,128]{1,0:T(8,128)(2,1)S(1)} %order_rows.1.mine_ref.refs_0_), channel_id=1, source_target_pairs={{0,24},{1,25},{2,26},{3,27},{4,28},{5,29},{6,30},{7,31},{8,16},{9,... | collective-permute-start | bytes 786440 | tf_op jit(solution)/shard_map/ppermute | solution.py:25
  15.2 8.8 %collective-permute-start.7 = (bf16[1024,128]{1,0:T(8,128)(2,1)S(1)}, bf16[1024,128]{1,0:T(8,128)(2,1)S(1)}, u32[]{:S(2)}, u32[]{:S(2)}) collective-permute-start(bf16[1024,128]{1,0:T(8,128)(2,1)S(1)} %order_rows.1.mine_ref.refs_0_), channel_id=1, source_target_pairs={{0,4},{1,5},{2,6},{3,7},{4,0},{5,1},{6,2},{7,3},{8,12},{9,13},{10,... | collective-permute-start | bytes 786440 | tf_op jit(solution)/shard_map/ppermute | solution.py:25
  22.8 7.7 %collective-permute-start.10 = (bf16[1024,128]{1,0:T(8,128)(2,1)S(1)}, bf16[1024,128]{1,0:T(8,128)(2,1)S(1)}, u32[]{:S(2)}, u32[]{:S(2)}) collective-permute-start(bf16[1024,128]{1,0:T(8,128)(2,1)S(1)} %relay.4.first_ref), channel_id=1, source_target_pairs={{0,24},{1,25},{2,26},{3,27},{4,28},{5,29},{6,30},{7,31},{8,16},{9,... | collective-permute-start | bytes 786440 | tf_op jit(solution)/shard_map/ppermute | solution.py:25
  24.2 7.2 %collective-permute-start.9 = (bf16[3,1024,128]{2,1,0:T(8,128)(2,1)S(1)}, bf16[3,1024,128]{2,1,0:T(8,128)(2,1)S(1)}, u32[]{:S(2)}, u32[]{:S(2)}) collective-permute-start(bf16[3,1024,128]{2,1,0:T(8,128)(2,1)S(1)} %get-tuple-element.51.refs_6_), channel_id=1, source_target_pairs={{0,32},{1,33},{2,34},{3,35},{4,36},{5,37},{6,38},{7,39},{8,40},{9,... | collective-permute-start | bytes 2359304 | tf_op jit(solution)/shard_map/ppermute | solution.py:25
  25.7 9.2 %collective-permute-start.8 = (bf16[2,1024,128]{2,1,0:T(8,128)(2,1)S(1)}, bf16[2,1024,128]{2,1,0:T(8,128)(2,1)S(1)}, u32[]{:S(2)}, u32[]{:S(2)}) collective-permute-start(bf16[2,1024,128]{2,1,0:T(8,128)(2,1)S(1)} %get-tuple-element.40.refs_6_), channel_id=1, source_target_pairs={{0,4},{1,5},{2,6},{3,7},{4,0},{5,1},{6,2},{7,3},{8,12},{9,13},{10,... | collective-permute-start | bytes 1572872 | tf_op jit(solution)/shard_map/ppermute | solution.py:25
  30.5 7.3 %collective-permute-start.12 = (bf16[1024,128]{1,0:T(8,128)(2,1)S(1)}, bf16[1024,128]{1,0:T(8,128)(2,1)S(1)}, u32[]{:S(2)}, u32[]{:S(2)}) collective-permute-start(bf16[1024,128]{1,0:T(8,128)(2,1)S(1)} %relay.5.refs_9_.refs_2_), channel_id=1, source_target_pairs={{0,4},{1,5},{2,6},{3,7},{4,0},{5,1},{6,2},{7,3},{8,12},{9,13},{10,... | collective-permute-start | bytes 786440 | tf_op jit(solution)/shard_map/ppermute | solution.py:25
  34.9 4.4 %collective-permute-start.11 = (bf16[2,1024,128]{2,1,0:T(8,128)(2,1)S(1)}, bf16[2,1024,128]{2,1,0:T(8,128)(2,1)S(1)}, u32[]{:S(2)}, u32[]{:S(2)}) collective-permute-start(bf16[2,1024,128]{2,1,0:T(8,128)(2,1)S(1)} %relay.6.refs_3_.refs_6_), channel_id=1, source_target_pairs={{0,32},{1,33},{2,34},{3,35},{4,36},{5,37},{6,38},{7,39},{8,40},{9,... | collective-permute-start | bytes 1572872 | tf_op jit(solution)/shard_map/ppermute | solution.py:25
  35.9 2.2 %collective-permute-start.14 = (bf16[1024,128]{1,0:T(8,128)(2,1)S(1)}, bf16[1024,128]{1,0:T(8,128)(2,1)S(1)}, u32[]{:S(2)}, u32[]{:S(2)}) collective-permute-start(bf16[1024,128]{1,0:T(8,128)(2,1)S(1)} %relay.5.refs_9_.refs_2_), channel_id=1, source_target_pairs={{0,32},{1,33},{2,34},{3,35},{4,36},{5,37},{6,38},{7,39},{8,40},{9,... | collective-permute-start | bytes 786440 | tf_op jit(solution)/shard_map/ppermute | solution.py:25
  37.7 1.6 %collective-permute-start.13 = (bf16[1024,128]{1,0:T(8,128)(2,1)S(1)}, bf16[1024,128]{1,0:T(8,128)(2,1)S(1)}, u32[]{:S(2)}, u32[]{:S(2)}) collective-permute-start(bf16[1024,128]{1,0:T(8,128)(2,1)S(1)} %relay.7.refs_5_.refs_8_), channel_id=1, source_target_pairs={{0,32},{1,33},{2,34},{3,35},{4,36},{5,37},{6,38},{7,39},{8,40},{9,... | collective-permute-start | bytes 786440 | tf_op jit(solution)/shard_map/ppermute | solution.py:25
  42.9 6.5 %collective-permute-start.15 = (f32[64,256]{1,0:T(8,128)S(1)}, f32[64,256]{1,0:T(8,128)S(1)}, u32[]{:S(2)}, u32[]{:S(2)}) collective-permute-start(f32[64,256]{1,0:T(8,128)S(1)} %get-tuple-element.59), channel_id=1, source_target_pairs={{0,2},{1,3},{2,0},{3,1},{4,6},{5,7},{6,4},{7,5},{8,10},{9,11},{10,... | collective-permute-start | bytes 196616 | tf_op jit(solution)/shard_map/ppermute | solution.py:25
  44.1 5.2 %collective-permute-start.16 = (f32[64,256]{1,0:T(8,128)S(1)}, f32[64,256]{1,0:T(8,128)S(1)}, u32[]{:S(2)}, u32[]{:S(2)}) collective-permute-start(f32[64,256]{1,0:T(8,128)S(1)} %get-tuple-element.58), channel_id=1, source_target_pairs={{0,1},{1,0},{2,3},{3,2},{4,5},{5,4},{6,7},{7,6},{8,9},{9,8},{10,11... | collective-permute-start | bytes 196616 | tf_op jit(solution)/shard_map/ppermute | solution.py:25
  44.8 5.5 %collective-permute-start.17 = (f32[64,256]{1,0:T(8,128)S(1)}, f32[64,256]{1,0:T(8,128)S(1)}, u32[]{:S(2)}, u32[]{:S(2)}) collective-permute-start(f32[64,256]{1,0:T(8,128)S(1)} %get-tuple-element.57), channel_id=1, source_target_pairs={{0,3},{1,2},{2,1},{3,0},{4,7},{5,6},{6,5},{7,4},{8,11},{9,10},{10,... | collective-permute-start | bytes 196616 | tf_op jit(solution)/shard_map/ppermute | solution.py:25

commit v15 on v13

--- a/solution.py
+++ b/solution.py
@@ -265,6 +265,27 @@
     )(*xs, *bs, *carry, *tokens)
 
 
+def mixed_kernel(work, *refs):
+    own, tiles, xs, refs = refs[:2], refs[2:4], refs[4:6], refs[7:]
+    stage1_kernel(work, 0, *own, *tiles, *refs[: len(work)])
+    stage2_kernel((((0, None), (1, None)),), 2, 0, 0, *xs, *own, *refs[len(work) :])
+
+
+def mixed(work, own, tiles, xs, token):
+    outs = pl.pallas_call(
+        functools.partial(mixed_kernel, work),
+        out_shape=tuple(jax.ShapeDtypeStruct((256, 4096), BF16) for _ in work)
+        + (jax.ShapeDtypeStruct((4, 64, 32), F32),),
+        in_specs=[spec(pltpu.VMEM)] * 6 + [spec(pl.ANY)],
+        out_specs=tuple(spec(pltpu.VMEM) for _ in range(len(work) + 1)),
+        scratch_shapes=[pltpu.VMEM((1, 256, 32), F32)],
+        compiler_params=params(8),
+        cost_estimate=pl.CostEstimate(flops=0, transcendentals=0, bytes_accessed=2**10),
+        name="mixed",
+    )(*own, *tiles, *xs, token)
+    return outs[:-1], outs[-1]
+
+
 def finish_kernel(order, own_ref, r1_ref, r2_ref, r3_ref, out_ref, sum_s, pos_s):
     total = own_ref[0] + r1_ref[...] + r2_ref[...] + r3_ref[...]
     sum_s[0] = total[:, 0:128]
@@ -314,8 +335,7 @@
     near_blocks = join((x1a, x1b, z0), xs[2])
     zx1 = over_z(x1)
     other_blocks = to_sibling(near_blocks)
-    x37 = stage1(halves(c37, c73), own, tiles, (x1,), FAST)
-    self0 = stage2("self", (x0m, x0o), (((0, None), (1, None)),), own, (), (x37[0],), FAST)
+    x37, self0 = mixed(halves(c37, c73), own, tiles, (x0m, x0o), x1)
     (x2,) = relay((x2,), (self0,), HOLD)
     zx2 = over_z(x2)
     x2_other = to_sibling(x2)

time: 51.7 us -> 51.7 us (level)
    pallas_call x0 -> x1, Pallas kernels: none -> 3.47 us  [mixed(): pl.pallas_call(functools.partial(mixed_kernel, work), out_shape=tuple((ja...]
    pallas_call x4 -> x3, Pallas kernels: 9.48 us -> 7.11 us  [stage1(): pl.pallas_call(functools.partial(stage1_kernel, work, len(tokens)), out_s...]
    pallas_call x4 -> x3, Pallas kernels: 9.48 us -> 8.25 us  [stage2(): pl.pallas_call(functools.partial(stage2_kernel, picks, len(bs), len(carry...]
  transfers between devices with their start and end apart: 18 -> 18, of which waited for: 6 -> 7; matrix products, arithmetic and copies ran while one was open for 0% -> 0% of each run, Pallas kernels for 35% -> 35%
where the time goes in v15:
time: 51.7 us; the launch traced here: 51.4 us
  Pallas kernels  24.2 us (47%)
  starting transfers between devices  19.4 us (38%)
  waiting for transfers between devices  7.56 us (15%)
    ppermute x18, starting transfers between devices, permute(): return lax.ppermute(value, ('occ', 'vir'), pairs)  19.4 us
    pallas_call x3, Pallas kernels, stage2(): pl.pallas_call(functools.partial(stage2_kernel, picks, len(bs), len(carry...  8.25 us
    ppermute x18, waiting for transfers between devices, permute(): return lax.ppermute(value, ('occ', 'vir'), pairs)  7.56 us
    pallas_call x3, Pallas kernels, stage1(): pl.pallas_call(functools.partial(stage1_kernel, work, len(tokens)), out_s...  7.11 us
    pallas_call x1, Pallas kernels, mixed(): pl.pallas_call(functools.partial(mixed_kernel, work), out_shape=tuple((ja...  3.47 us
    pallas_call x1, Pallas kernels, twist_tiles(): pl.pallas_call(twist_kernel, out_shape=(shape, shape), in_specs=[spec(plt...  2.63 us
    pallas_call x1, Pallas kernels, cut_to_send(): pl.pallas_call(send_kernel, out_shape=(chunk,) * 4 + (jax.ShapeDtypeStruc...  1.7 us
  transfers between devices with their start and end apart: 18, of which 7 were waited for; matrix products, arithmetic and copies ran while one was open for 0% of the time, Pallas kernels for 35%

profile of v15, /device:TPU:0, one launch (start us, length us, event | category | flops | bytes accessed | tf_op | source)
XLA Modules:
  0.0 51.4 jit_solution(11350840046984866720)
XLA Ops:
  0.0 1.7 %cut_to_send.1 = (bf16[256,128]{1,0:T(8,128)(2,1)S(1)}, bf16[256,128]{1,0:T(8,128)(2,1)S(1)}, bf16[256,128]{1,0:T(8,128)(2,1)S(1)}, bf16[256,128]{1,0:T(8,128)(2,1)S(1)}, bf16[8,8,128,128]{3,2,1,0:T(8,128)(2,1)S(1)}) custom-call(bf16[2048,128]{1,0:T(8,128)(2,1)} %bitcast.11, bf16[64,8,128,128]{3,2,1,0:T(8,128)(2,1)} %amp_ref.3), custom_call_target="tpu_custom_call" | custom-call | tf_op jit(solution)/shard_map/cut_to_send/pallas_call | solution.py:75
  1.8 3.4 %collective-permute-start = (bf16[256,128]{1,0:T(8,128)(2,1)S(1)}, bf16[256,128]{1,0:T(8,128)(2,1)S(1)}, u32[]{:S(2)}, u32[]{:S(2)}) collective-permute-start(bf16[256,128]{1,0:T(8,128)(2,1)S(1)} %get-tuple-element.30), channel_id=1, source_target_pairs={{0,2},{1,3},{2,0},{3,1},{4,6},{5,7},{6,4},{7,5},{8,10},{9,11},{10,... | collective-permute-start | bytes 196616 | tf_op jit(solution)/shard_map/ppermute | solution.py:25
  6.2 2.6 %twist_tiles.1 = (bf16[8,8,128,128]{3,2,1,0:T(8,128)(2,1)S(1)}, bf16[8,8,128,128]{3,2,1,0:T(8,128)(2,1)S(1)}) custom-call(s32[64]{0:T(128)S(1)} %copy-done, bf16[64,8,128,128]{3,2,1,0:T(8,128)(2,1)} %amp_ref.3, bf16[8,8,128,128]{3,2,1,0:T(8,128)(2,1)S(1)} %collective-permute-done.3.received_ref), custom_call_target="tpu_custom_call" | custom-call | tf_op jit(solution)/shard_map/twist_tiles/pallas_call | solution.py:103
  9.6 1.7 %collective-permute-done.2.r3_ref = bf16[256,128]{1,0:T(8,128)(2,1)S(1)} collective-permute-done((bf16[256,128]{1,0:T(8,128)(2,1)S(1)}, bf16[256,128]{1,0:T(8,128)(2,1)S(1)}, u32[]{:S(2)}, u32[]{:S(2)}) %collective-permute-start.2) | collective-permute-done | bytes 65568 | tf_op jit(solution)/shard_map/ppermute | solution.py:25
  11.5 1.6 %collective-permute-start.5 = (bf16[1024,128]{1,0:T(8,128)(2,1)S(1)}, bf16[1024,128]{1,0:T(8,128)(2,1)S(1)}, u32[]{:S(2)}, u32[]{:S(2)}) collective-permute-start(bf16[1024,128]{1,0:T(8,128)(2,1)S(1)} %order_rows.1.mine_ref.refs_0_), channel_id=1, source_target_pairs={{0,8},{1,9},{2,10},{3,11},{4,12},{5,13},{6,14},{7,15},{8,0},{9,1},... | collective-permute-start | bytes 786440 | tf_op jit(solution)/shard_map/ppermute | solution.py:25
  13.1 1.9 %collective-permute-start.8 = (bf16[1024,128]{1,0:T(8,128)(2,1)S(1)}, bf16[1024,128]{1,0:T(8,128)(2,1)S(1)}, u32[]{:S(2)}, u32[]{:S(2)}) collective-permute-start(bf16[1024,128]{1,0:T(8,128)(2,1)S(1)} %order_rows.1.mine_ref.refs_0_), channel_id=1, source_target_pairs={{0,4},{1,5},{2,6},{3,7},{4,0},{5,1},{6,2},{7,3},{8,12},{9,13},{10,... | collective-permute-start | bytes 786440 | tf_op jit(solution)/shard_map/ppermute | solution.py:25
  15.0 1.3 %stage1_0.1 = (bf16[256,4096]{1,0:T(8,128)(2,1)S(1)}, bf16[256,4096]{1,0:T(8,128)(2,1)S(1)}) custom-call(bf16[1024,128]{1,0:T(8,128)(2,1)S(1)} %order_rows.1.mine_ref.refs_0_, bf16[1024,128]{1,0:T(8,128)(2,1)S(1)} %collective-permute-done.4.refs_0_.refs_1_, bf16[8,8,128,128]{3,2,1,0:T(8,128)(2,1)S(1)} %get-tuple-element.35.refs_1_.refs_2_, ...), custom_call_target="tpu_custom_call" | custom-call | flops 1073741824 | bytes 1024 | tf_op jit(solution)/shard_map/stage1_0/pallas_call | solution.py:210
  16.3 2.2 %collective-permute-start.6 = (bf16[1,1024,128]{2,1,0:T(8,128)(2,1)S(1)}, bf16[1,1024,128]{2,1,0:T(8,128)(2,1)S(1)}, u32[]{:S(2)}, u32[]{:S(2)}) collective-permute-start(bf16[1,1024,128]{2,1,0:T(8,128)(2,1)S(1)} %join.3.refs_3_), channel_id=1, source_target_pairs={{0,24},{1,25},{2,26},{3,27},{4,28},{5,29},{6,30},{7,31},{8,16},{9,... | collective-permute-start | bytes 786440 | tf_op jit(solution)/shard_map/ppermute | solution.py:25
  18.5 4.6 %stage1_1_2_6_4.1 = (bf16[256,4096]{1,0:T(8,128)(2,1)S(1)}, bf16[256,4096]{1,0:T(8,128)(2,1)S(1)}, bf16[256,4096]{1,0:T(8,128)(2,1)S(1)}, bf16[256,4096]{1,0:T(8...) custom-call(bf16[1024,128]{1,0:T(8,128)(2,1)S(1)} %order_rows.1.mine, ...), custom_call_target="tpu_custom_call" | custom-call | flops 4294967296 | bytes 1024 | tf_op jit(solution)/shard_map/stage1_1_2_6_4/pallas_call | solution.py:210
  23.1 1.2 %collective-permute-start.10 = (bf16[1024,128]{1,0:T(8,128)(2,1)S(1)}, bf16[1024,128]{1,0:T(8,128)(2,1)S(1)}, u32[]{:S(2)}, u32[]{:S(2)}) collective-permute-start(bf16[1024,128]{1,0:T(8,128)(2,1)S(1)} %relay.4.refs_0_), channel_id=1, source_target_pairs={{0,24},{1,25},{2,26},{3,27},{4,28},{5,29},{6,30},{7,31},{8,16},{9,... | collective-permute-start | bytes 786440 | tf_op jit(solution)/shard_map/ppermute | solution.py:25
  24.4 1.5 %collective-permute-start.9 = (bf16[3,1024,128]{2,1,0:T(8,128)(2,1)S(1)}, bf16[3,1024,128]{2,1,0:T(8,128)(2,1)S(1)}, u32[]{:S(2)}, u32[]{:S(2)}) collective-permute-start(bf16[3,1024,128]{2,1,0:T(8,128)(2,1)S(1)} %join.5.refs_6_), channel_id=1, source_target_pairs={{0,32},{1,33},{2,34},{3,35},{4,36},{5,37},{6,38},{7,39},{8,40},{9,... | collective-permute-start | bytes 2359304 | tf_op jit(solution)/shard_map/ppermute | solution.py:25
  26.0 3.5 %mixed.1 = (bf16[256,4096]{1,0:T(8,128)(2,1)S(1)}, bf16[256,4096]{1,0:T(8,128)(2,1)S(1)}, bf16[256,4096]{1,0:T(8,128)(2,1)S(1)}, bf16[256,4096]{1,0:T(8,128)(2,1)S(1)}, f32[4,64,32]{2,1,0:T(8,128)S(1)}) custom-call(bf16[1024,128]{1,0:T(8,128)(2,1)S(1)} %order_rows.1.mine_ref.refs_0_, bf16[1024,128]{1,0:T(8,128)(2,1)S(1)} %collective-permute-done.4.refs_0_.refs_1_, ...), custom_call_target="tpu_custom_call" | custom-call | bytes 1024 | tf_op jit(solution)/shard_map/mixed/pallas_call | solution.py:275
  29.4 1.3 %collective-permute-done.10.refs_0_ = bf16[1024,128]{1,0:T(8,128)(2,1)S(1)} collective-permute-done((bf16[1024,128]{1,0:T(8,128)(2,1)S(1)}, bf16[1024,128]{1,0:T(8,128)(2,1)S(1)}, u32[]{:S(2)}, u32[]{:S(2)}) %collective-permute-start.10) | collective-permute-done | bytes 262176 | tf_op jit(solution)/shard_map/ppermute | solution.py:25
  30.7 0.8 %collective-permute-start.12 = (bf16[1024,128]{1,0:T(8,128)(2,1)S(1)}, bf16[1024,128]{1,0:T(8,128)(2,1)S(1)}, u32[]{:S(2)}, u32[]{:S(2)}) collective-permute-start(bf16[1024,128]{1,0:T(8,128)(2,1)S(1)} %relay.5.refs_9_.refs_2_), channel_id=1, source_target_pairs={{0,4},{1,5},{2,6},{3,7},{4,0},{5,1},{6,2},{7,3},{8,12},{9,13},{10,... | collective-permute-start | bytes 786440 | tf_op jit(solution)/shard_map/ppermute | solution.py:25
  31.6 3.5 %stage2_near.1.refs_1_.refs_4_ = f32[4,64,128]{2,1,0:T(8,128)S(1)} custom-call(bf16[256,4096]{1,0:T(8,128)(2,1)S(1)} %get-tuple-element.43.refs_0_, bf16[256,4096]{1,0:T(8,128)(2,1)S(1)} %get-tuple-element.44.refs_1_, bf16[256,4096]{1,0:T(8,128)(2,1)S(1)} %get-tuple-element.38.refs_1_.refs_2_.refs_3_, bf16[256,4096]{1,0:T(8,128)(2,1)S(1)} %get-tuple-element.45.refs_3_, ...), custom_call_target="tpu_custom_call" | custom-call | flops 25769803776 | bytes 1024 | tf_op jit(solution)/shard_map/stage2_near/pallas_call | solution.py:256
  35.1 1.0 %collective-permute-start.11 = (bf16[2,1024,128]{2,1,0:T(8,128)(2,1)S(1)}, bf16[2,1024,128]{2,1,0:T(8,128)(2,1)S(1)}, u32[]{:S(2)}, u32[]{:S(2)}) collective-permute-start(bf16[2,1024,128]{2,1,0:T(8,128)(2,1)S(1)} %relay.6.refs_3_.refs_6_), channel_id=1, source_target_pairs={{0,32},{1,33},{2,34},{3,35},{4,36},{5,37},{6,38},{7,39},{8,40},{9,... | collective-permute-start | bytes 1572872 | tf_op jit(solution)/shard_map/ppermute | solution.py:25
  36.2 1.3 %stage1_5.1 = (bf16[256,4096]{1,0:T(8,128)(2,1)S(1)}, bf16[256,4096]{1,0:T(8,128)(2,1)S(1)}) custom-call(bf16[1024,128]{1,0:T(8,128)(2,1)S(1)} %order_rows.1.mine_ref.refs_0_, bf16[1024,128]{1,0:T(8,128)(2,1)S(1)} %collective-permute-done.4.refs_0_.refs_1_, bf16[8,8,128,128]{3,2,1,0:T(8,128)(2,1)S(1)} %get-tuple-element.35.refs_1_.refs_2_, ...), custom_call_target="tpu_custom_call" | custom-call | flops 1073741824 | bytes 1024 | tf_op jit(solution)/shard_map/stage1_5/pallas_call | solution.py:210
  38.3 1.2 %stage2_far.1.refs_10_ = f32[4,64,160]{2,1,0:T(8,128)S(1)} custom-call(bf16[256,4096]{1,0:T(8,128)(2,1)S(1)} %get-tuple-element.51.refs_0_, bf16[256,4096]{1,0:T(8,128)(2,1)S(1)} %get-tuple-element.52.refs_1_, bf16[1024,128]{1,0:T(8,128)(2,1)S(1)} %relay.5.refs_9_.refs_2_, bf16[1024,128]{1,0:T(8,128)(2,1)S(1)} %collective-permute-done.14.refs_3_, ...), custom_call_target="tpu_custom_call" | custom-call | flops 1073741824 | bytes 1024 | tf_op jit(solution)/shard_map/stage2_far/pallas_call | solution.py:256
  39.6 3.5 %stage2_last.1.own_ref = f32[4,64,256]{2,1,0:T(8,128)S(1)} custom-call(bf16[256,4096]{1,0:T(8,128)(2,1)S(1)} %get-tuple-element.39.refs_0_, bf16[256,4096]{1,0:T(8,128)(2,1)S(1)} %get-tuple-element.40.refs_1_, bf16[256,4096]{1,0:T(8,128)(2,1)S(1)} %get-tuple-element.41.refs_2_, bf16[256,4096]{1,0:T(8,128)(2,1)S(1)} %get-tuple-element.42.refs_3_, ...), custom_call_target="tpu_custom_call" | custom-call | flops 3221225472 | bytes 1024 | tf_op jit(solution)/shard_map/stage2_last/pallas_call | solution.py:256
  43.1 1.3 %collective-permute-start.15 = (f32[64,256]{1,0:T(8,128)S(1)}, f32[64,256]{1,0:T(8,128)S(1)}, u32[]{:S(2)}, u32[]{:S(2)}) collective-permute-start(f32[64,256]{1,0:T(8,128)S(1)} %get-tuple-element.55), channel_id=1, source_target_pairs={{0,2},{1,3},{2,0},{3,1},{4,6},{5,7},{6,4},{7,5},{8,10},{9,11},{10,... | collective-permute-start | bytes 196616 | tf_op jit(solution)/shard_map/ppermute | solution.py:25
  45.0 2.2 %collective-permute-start.17 = (f32[64,256]{1,0:T(8,128)S(1)}, f32[64,256]{1,0:T(8,128)S(1)}, u32[]{:S(2)}, u32[]{:S(2)}) collective-permute-start(f32[64,256]{1,0:T(8,128)S(1)} %get-tuple-element.53), channel_id=1, source_target_pairs={{0,3},{1,2},{2,1},{3,0},{4,7},{5,6},{6,5},{7,4},{8,11},{9,10},{10,... | collective-permute-start | bytes 196616 | tf_op jit(solution)/shard_map/ppermute | solution.py:25
  47.3 2.3 %collective-permute-done.15.r1_ref = f32[64,256]{1,0:T(8,128)S(1)} collective-permute-done((f32[64,256]{1,0:T(8,128)S(1)}, f32[64,256]{1,0:T(8,128)S(1)}, u32[]{:S(2)}, u32[]{:S(2)}) %collective-permute-start.15) | collective-permute-done | bytes 65568 | tf_op jit(solution)/shard_map/ppermute | solution.py:25
  49.6 0.9 %collective-permute-done.17.r3_ref = f32[64,256]{1,0:T(8,128)S(1)} collective-permute-done((f32[64,256]{1,0:T(8,128)S(1)}, f32[64,256]{1,0:T(8,128)S(1)}, u32[]{:S(2)}, u32[]{:S(2)}) %collective-permute-start.17) | collective-permute-done | bytes 65568 | tf_op jit(solution)/shard_map/ppermute | solution.py:25
  50.5 0.9 %finish.1 = f32[8,32,64]{2,1,0:T(8,128)} custom-call(f32[4,64,256]{2,1,0:T(8,128)S(1)} %stage2_last.1.own_ref, f32[64,256]{1,0:T(8,128)S(1)} %collective-permute-done.15.r1_ref, f32[64,256]{1,0:T(8,128)S(1)} %collective-permute-done.16.r2_ref, f32[64,256]{1,0:T(8,128)S(1)} %collective-permute-done.17.r3_ref), custom_call_target="tpu_custom_call" | custom-call | tf_op jit(solution)/shard_map/finish/pallas_call | solution.py:303
  (33 shorter events, 3.9 us)
Async XLA Ops:
  0.0 6.2 %copy-start = (s32[64]{0:T(128)S(1)}, s32[64]{0:T(128)}, u32[]{:S(2)}) copy-start(s32[64]{0:T(128)} %mirror_ref.1) | copy-start | bytes 772
  1.7 4.5 %collective-permute-start.3 = (bf16[8,8,128,128]{3,2,1,0:T(8,128)(2,1)S(1)}, bf16[8,8,128,128]{3,2,1,0:T(8,128)(2,1)S(1)}, u32[]{:S(2)}, u32[]{:S(2)}) collective-permute-start(bf16[8,8,128,128]{3,2,1,0:T(8,128)(2,1)S(1)} %get-tuple-element.33), channel_id=1, source_target_pairs={{0,32},{1,33},{2,34},{3,35},{4,36},{5,37},{6,38},{7,39},{8,40},{9,... | collective-permute-start | bytes 6291464 | tf_op jit(solution)/shard_map/ppermute | solution.py:25
  1.8 7.1 %collective-permute-start = (bf16[256,128]{1,0:T(8,128)(2,1)S(1)}, bf16[256,128]{1,0:T(8,128)(2,1)S(1)}, u32[]{:S(2)}, u32[]{:S(2)}) collective-permute-start(bf16[256,128]{1,0:T(8,128)(2,1)S(1)} %get-tuple-element.30), channel_id=1, source_target_pairs={{0,2},{1,3},{2,0},{3,1},{4,6},{5,7},{6,4},{7,5},{8,10},{9,11},{10,... | collective-permute-start | bytes 196616 | tf_op jit(solution)/shard_map/ppermute | solution.py:25
  5.2 4.5 %collective-permute-start.1 = (bf16[256,128]{1,0:T(8,128)(2,1)S(1)}, bf16[256,128]{1,0:T(8,128)(2,1)S(1)}, u32[]{:S(2)}, u32[]{:S(2)}) collective-permute-start(bf16[256,128]{1,0:T(8,128)(2,1)S(1)} %get-tuple-element.31), channel_id=1, source_target_pairs={{0,1},{1,0},{2,3},{3,2},{4,5},{5,4},{6,7},{7,6},{8,9},{9,8},{10,11... | collective-permute-start | bytes 196616 | tf_op jit(solution)/shard_map/ppermute | solution.py:25
  5.8 5.5 %collective-permute-start.2 = (bf16[256,128]{1,0:T(8,128)(2,1)S(1)}, bf16[256,128]{1,0:T(8,128)(2,1)S(1)}, u32[]{:S(2)}, u32[]{:S(2)}) collective-permute-start(bf16[256,128]{1,0:T(8,128)(2,1)S(1)} %get-tuple-element.32), channel_id=1, source_target_pairs={{0,3},{1,2},{2,1},{3,0},{4,7},{5,6},{6,5},{7,4},{8,11},{9,10},{10,... | collective-permute-start | bytes 196616 | tf_op jit(solution)/shard_map/ppermute | solution.py:25
  11.4 3.6 %collective-permute-start.4 = (bf16[1024,128]{1,0:T(8,128)(2,1)S(1)}, bf16[1024,128]{1,0:T(8,128)(2,1)S(1)}, u32[]{:S(2)}, u32[]{:S(2)}) collective-permute-start(bf16[1024,128]{1,0:T(8,128)(2,1)S(1)} %order_rows.1.mine_ref.refs_0_), channel_id=1, source_target_pairs={{0,32},{1,33},{2,34},{3,35},{4,36},{5,37},{6,38},{7,39},{8,40},{9,... | collective-permute-start | bytes 786440 | tf_op jit(solution)/shard_map/ppermute | solution.py:25
  11.5 11.6 %collective-permute-start.5 = (bf16[1024,128]{1,0:T(8,128)(2,1)S(1)}, bf16[1024,128]{1,0:T(8,128)(2,1)S(1)}, u32[]{:S(2)}, u32[]{:S(2)}) collective-permute-start(bf16[1024,128]{1,0:T(8,128)(2,1)S(1)} %order_rows.1.mine_ref.refs_0_), channel_id=1, source_target_pairs={{0,8},{1,9},{2,10},{3,11},{4,12},{5,13},{6,14},{7,15},{8,0},{9,1},... | collective-permute-start | bytes 786440 | tf_op jit(solution)/shard_map/ppermute | solution.py:25
  13.1 11.3 %collective-permute-start.8 = (bf16[1024,128]{1,0:T(8,128)(2,1)S(1)}, bf16[1024,128]{1,0:T(8,128)(2,1)S(1)}, u32[]{:S(2)}, u32[]{:S(2)}) collective-permute-start(bf16[1024,128]{1,0:T(8,128)(2,1)S(1)} %order_rows.1.mine_ref.refs_0_), channel_id=1, source_target_pairs={{0,4},{1,5},{2,6},{3,7},{4,0},{5,1},{6,2},{7,3},{8,12},{9,13},{10,... | collective-permute-start | bytes 786440 | tf_op jit(solution)/shard_map/ppermute | solution.py:25
  16.3 8.0 %collective-permute-start.6 = (bf16[1,1024,128]{2,1,0:T(8,128)(2,1)S(1)}, bf16[1,1024,128]{2,1,0:T(8,128)(2,1)S(1)}, u32[]{:S(2)}, u32[]{:S(2)}) collective-permute-start(bf16[1,1024,128]{2,1,0:T(8,128)(2,1)S(1)} %join.3.refs_3_), channel_id=1, source_target_pairs={{0,24},{1,25},{2,26},{3,27},{4,28},{5,29},{6,30},{7,31},{8,16},{9,... | collective-permute-start | bytes 786440 | tf_op jit(solution)/shard_map/ppermute | solution.py:25
  23.1 7.7 %collective-permute-start.10 = (bf16[1024,128]{1,0:T(8,128)(2,1)S(1)}, bf16[1024,128]{1,0:T(8,128)(2,1)S(1)}, u32[]{:S(2)}, u32[]{:S(2)}) collective-permute-start(bf16[1024,128]{1,0:T(8,128)(2,1)S(1)} %relay.4.refs_0_), channel_id=1, source_target_pairs={{0,24},{1,25},{2,26},{3,27},{4,28},{5,29},{6,30},{7,31},{8,16},{9,... | collective-permute-start | bytes 786440 | tf_op jit(solution)/shard_map/ppermute | solution.py:25
  24.4 7.2 %collective-permute-start.9 = (bf16[3,1024,128]{2,1,0:T(8,128)(2,1)S(1)}, bf16[3,1024,128]{2,1,0:T(8,128)(2,1)S(1)}, u32[]{:S(2)}, u32[]{:S(2)}) collective-permute-start(bf16[3,1024,128]{2,1,0:T(8,128)(2,1)S(1)} %join.5.refs_6_), channel_id=1, source_target_pairs={{0,32},{1,33},{2,34},{3,35},{4,36},{5,37},{6,38},{7,39},{8,40},{9,... | collective-permute-start | bytes 2359304 | tf_op jit(solution)/shard_map/ppermute | solution.py:25
  26.0 9.2 %collective-permute-start.7 = (bf16[2,1024,128]{2,1,0:T(8,128)(2,1)S(1)}, bf16[2,1024,128]{2,1,0:T(8,128)(2,1)S(1)}, u32[]{:S(2)}, u32[]{:S(2)}) collective-permute-start(bf16[2,1024,128]{2,1,0:T(8,128)(2,1)S(1)} %join.4.refs_6_), channel_id=1, source_target_pairs={{0,4},{1,5},{2,6},{3,7},{4,0},{5,1},{6,2},{7,3},{8,12},{9,13},{10,... | collective-permute-start | bytes 1572872 | tf_op jit(solution)/shard_map/ppermute | solution.py:25
  30.7 7.2 %collective-permute-start.12 = (bf16[1024,128]{1,0:T(8,128)(2,1)S(1)}, bf16[1024,128]{1,0:T(8,128)(2,1)S(1)}, u32[]{:S(2)}, u32[]{:S(2)}) collective-permute-start(bf16[1024,128]{1,0:T(8,128)(2,1)S(1)} %relay.5.refs_9_.refs_2_), channel_id=1, source_target_pairs={{0,4},{1,5},{2,6},{3,7},{4,0},{5,1},{6,2},{7,3},{8,12},{9,13},{10,... | collective-permute-start | bytes 786440 | tf_op jit(solution)/shard_map/ppermute | solution.py:25
  35.1 4.4 %collective-permute-start.11 = (bf16[2,1024,128]{2,1,0:T(8,128)(2,1)S(1)}, bf16[2,1024,128]{2,1,0:T(8,128)(2,1)S(1)}, u32[]{:S(2)}, u32[]{:S(2)}) collective-permute-start(bf16[2,1024,128]{2,1,0:T(8,128)(2,1)S(1)} %relay.6.refs_3_.refs_6_), channel_id=1, source_target_pairs={{0,32},{1,33},{2,34},{3,35},{4,36},{5,37},{6,38},{7,39},{8,40},{9,... | collective-permute-start | bytes 1572872 | tf_op jit(solution)/shard_map/ppermute | solution.py:25
  36.1 2.2 %collective-permute-start.14 = (bf16[1024,128]{1,0:T(8,128)(2,1)S(1)}, bf16[1024,128]{1,0:T(8,128)(2,1)S(1)}, u32[]{:S(2)}, u32[]{:S(2)}) collective-permute-start(bf16[1024,128]{1,0:T(8,128)(2,1)S(1)} %relay.5.refs_9_.refs_2_), channel_id=1, source_target_pairs={{0,32},{1,33},{2,34},{3,35},{4,36},{5,37},{6,38},{7,39},{8,40},{9,... | collective-permute-start | bytes 786440 | tf_op jit(solution)/shard_map/ppermute | solution.py:25
  37.9 1.6 %collective-permute-start.13 = (bf16[1024,128]{1,0:T(8,128)(2,1)S(1)}, bf16[1024,128]{1,0:T(8,128)(2,1)S(1)}, u32[]{:S(2)}, u32[]{:S(2)}) collective-permute-start(bf16[1024,128]{1,0:T(8,128)(2,1)S(1)} %relay.7.refs_5_.refs_8_), channel_id=1, source_target_pairs={{0,32},{1,33},{2,34},{3,35},{4,36},{5,37},{6,38},{7,39},{8,40},{9,... | collective-permute-start | bytes 786440 | tf_op jit(solution)/shard_map/ppermute | solution.py:25
  43.1 6.5 %collective-permute-start.15 = (f32[64,256]{1,0:T(8,128)S(1)}, f32[64,256]{1,0:T(8,128)S(1)}, u32[]{:S(2)}, u32[]{:S(2)}) collective-permute-start(f32[64,256]{1,0:T(8,128)S(1)} %get-tuple-element.55), channel_id=1, source_target_pairs={{0,2},{1,3},{2,0},{3,1},{4,6},{5,7},{6,4},{7,5},{8,10},{9,11},{10,... | collective-permute-start | bytes 196616 | tf_op jit(solution)/shard_map/ppermute | solution.py:25
  44.4 5.2 %collective-permute-start.16 = (f32[64,256]{1,0:T(8,128)S(1)}, f32[64,256]{1,0:T(8,128)S(1)}, u32[]{:S(2)}, u32[]{:S(2)}) collective-permute-start(f32[64,256]{1,0:T(8,128)S(1)} %get-tuple-element.54), channel_id=1, source_target_pairs={{0,1},{1,0},{2,3},{3,2},{4,5},{5,4},{6,7},{7,6},{8,9},{9,8},{10,11... | collective-permute-start | bytes 196616 | tf_op jit(solution)/shard_map/ppermute | solution.py:25
  45.0 5.5 %collective-permute-start.17 = (f32[64,256]{1,0:T(8,128)S(1)}, f32[64,256]{1,0:T(8,128)S(1)}, u32[]{:S(2)}, u32[]{:S(2)}) collective-permute-start(f32[64,256]{1,0:T(8,128)S(1)} %get-tuple-element.53), channel_id=1, source_target_pairs={{0,3},{1,2},{2,1},{3,0},{4,7},{5,6},{6,5},{7,4},{8,11},{9,10},{10,... | collective-permute-start | bytes 196616 | tf_op jit(solution)/shard_map/ppermute | solution.py:25
